TPU v7x, 32 devices: a whole 2x2x4 slice. The times are simulated.
32 devices in a mesh: groups: 2 (over y), blk: 8 (over z, x), narrow: 2 (over core).
Axes of the slice: x: 2, y: 2, z: 4, core: 2. Of those that a mesh axis runs over, the one named last changes fastest.
Arguments:
- embeddings: bfloat16 [12288, 768], P(('groups', 'blk', 'narrow')), parts along dimension 0, may hold values from -0.16237976 to 0.16237976
- pair_mask: int32 [16, 2], P('groups'), parts along dimension 0, may hold values 0 or 1
- shift_index: int32 [2], P('groups'), parts along dimension 0, may hold values from 0 to 63
- start_seed: int32 [12288, 64], P(('groups', 'blk', 'narrow')), parts along dimension 0, may hold values from -1499 to 1499
Outputs:
- embedding_out: float32 [12288, 64], P(('groups', 'blk', 'narrow')), parts along dimension 0
There are 2 independent parts, one for each index of `groups`. A program takes and returns all parts, laid end to end along the dimension named above; each array names one. Nothing has to cross between parts.
All inputs are finite; a program needn't handle non-finite values.
Results may differ from a plain program's by a relative error of at most 0.0003.
Values may be sent and summed in bfloat16 or wider, within the bound.
No kernel may reach another device: no remote copies, remote signals or barrier semaphores. Data moves between devices by JAX's collectives and lax.ppermute only.
A program may use at most 64 MiB of HBM per device.

v0:
```python
import math

import jax
import jax.numpy as jnp
from jax import lax
from jax.sharding import PartitionSpec as P

ITERS = 2
QSTEPS = 6


kernel_gamma = 2.0
ridge_weight = 1e-05
highest = lax.Precision.HIGHEST


def shifted_2(shard, axis, by):
    length = lax.axis_size(axis)
    return lax.ppermute(shard, axis, [(i, (i + by) % length) for i in range(length)])


def row_squares(values):
    return jnp.einsum("rc,rc->r", values, values, preferred_element_type=jnp.float32)


def inner(left, right):
    return jnp.einsum("ra,rb->ab", left, right, precision=highest)


def times(left, right):
    return jnp.dot(left, right, precision=highest)


def lower_solve(factor, rhs):
    return lax.linalg.triangular_solve(factor, rhs, left_side=True, lower=True)


def upper_solve(factor, rhs):
    return lax.linalg.triangular_solve(factor, rhs, left_side=True, lower=True, transpose_a=True)


def ritz_step(gram, image_gram, shift_value, width):
    total = gram.shape[0]
    identity = jnp.eye(total, dtype=jnp.float32)
    ridged = gram + ridge_weight * jnp.mean(jnp.diagonal(gram)) * identity
    factor = jnp.linalg.cholesky(ridged)
    halfway = lower_solve(factor, image_gram)
    projected = lower_solve(factor, halfway.T).T
    shifted = projected + (3.0 - shift_value) * identity
    coeffs = jnp.eye(total, width, dtype=jnp.float32)
    for repeat in range(QSTEPS):
        coeffs = times(shifted, coeffs)
        norm_factor = jnp.linalg.cholesky(inner(coeffs, coeffs))
        coeffs = lower_solve(norm_factor, coeffs.T).T
    mixing = upper_solve(factor, coeffs)
    return (mixing, coeffs, projected)


def kernel_tile(row_emb, row_sq, col_emb, col_sq):
    inner_prod = jnp.einsum("rc,kc->rk", row_emb, col_emb, preferred_element_type=jnp.float32)
    return jnp.exp(-kernel_gamma * (row_sq[:, None] + col_sq[None, :] - 2.0 * inner_prod))


def masked_tile(keep_flag, row_emb, row_sq, col_emb, col_sq):
    tile_shape = (row_emb.shape[0], col_emb.shape[0])
    return lax.cond(
        keep_flag > 0,
        lambda: kernel_tile(row_emb, row_sq, col_emb, col_sq),
        lambda: jnp.zeros(tile_shape, jnp.float32),
    )


def shards(embeddings, pair_mask, shift_index, start_seed):
    local_rows = embeddings.shape[0]
    blocks = lax.axis_size("blk")
    where = lax.axis_index("blk")
    own_sq = row_squares(embeddings)
    block_emb = lax.all_gather(embeddings, "narrow", axis=0, tiled=True)
    block_sq = row_squares(block_emb)
    own_tile = kernel_tile(block_emb, block_sq, embeddings, own_sq)
    ahead_one = pair_mask[where, 0]
    ahead_two = pair_mask[where, 1]
    behind_one = pair_mask[(where + blocks - 1) % blocks, 0]
    behind_two = pair_mask[(where + blocks - 2) % blocks, 1]
    flag_table = {1: behind_one, 2: behind_two, -1: ahead_one, -2: ahead_two}
    near_tiles = []
    for offset in (1, 2, -1, -2):
        near_emb = shifted_2(embeddings, "blk", offset)
        tile = masked_tile(flag_table[offset], block_emb, block_sq, near_emb, row_squares(near_emb))
        near_tiles.append((offset, tile))

    def apply_fn(scaled):
        total = times(own_tile, scaled)
        for offset, tile in near_tiles:
            near_scaled = shifted_2(scaled, "blk", offset)
            total = total + times(tile, near_scaled)
        return lax.psum_scatter(total, "narrow", scatter_dimension=0, tiled=True)

    total = jnp.sum(own_tile, axis=1)
    for offset, tile in near_tiles:
        total = total + jnp.sum(tile, axis=1)
    degree = lax.psum_scatter(total, "narrow", scatter_dimension=0, tiled=True)
    scale = lax.rsqrt(degree)[:, None]

    def operate(vectors):
        return scale * apply_fn(scale * vectors)

    start = start_seed.astype(jnp.float32) / 1000.0
    start_gram = lax.psum(inner(start, start), ("blk", "narrow"))
    current = lower_solve(jnp.linalg.cholesky(start_gram), start.T).T
    image = operate(current)
    width = current.shape[1]
    previous = current
    previous_image = image
    index_value = shift_index[0]
    for iteration in range(ITERS):
        ritz_block = lax.psum(inner(current, image), ("blk", "narrow"))
        shift_value = ritz_block[index_value, index_value]
        residual = image - times(current, ritz_block)
        residual_image = operate(residual)
        if iteration == 0:
            basis = jnp.concatenate([current, residual], axis=1)
            basis_image = jnp.concatenate([image, residual_image], axis=1)
        else:
            basis = jnp.concatenate([current, residual, previous], axis=1)
            basis_image = jnp.concatenate([image, residual_image, previous_image], axis=1)
        gram, image_gram = lax.psum(
            (inner(basis, basis), inner(basis, basis_image)), ("blk", "narrow")
        )
        mixing, coeffs, projected = ritz_step(gram, image_gram, shift_value, width)
        current = times(basis, mixing)
        image = times(basis_image, mixing)
        previous = times(basis[:, width:], mixing[width:])
        previous_image = times(basis_image[:, width:], mixing[width:])
    total_rows = local_rows * lax.axis_size("blk") * lax.axis_size("narrow")
    return current * math.sqrt(total_rows)


def solution(mesh):
    return jax.shard_map(
        shards,
        mesh=mesh,
        in_specs=(
            P(("groups", "blk", "narrow"), None),
            P("groups", None),
            P("groups"),
            P(("groups", "blk", "narrow"), None),
        ),
        out_specs=P(("groups", "blk", "narrow"), None),
        check_vma=False,
    )
```

profile of v0, /device:TPU:0, one launch (start us, length us, event | category | flops | bytes accessed | tf_op | source)
XLA Modules:
  0.0 857.4 jit_solution(16186465481335730421)
XLA Ops:
  11.9 3.2 collective-permute-start.2
  20.7 84.3 %psum.49 = f32[64,64]{0,1:T(8,128)S(1)} all-reduce(f32[64,64]{0,1:T(8,128)S(1)} %fusion.43), channel_id=1, replica_groups=mesh['groups'=2,'blk'=8,'narrow'=2] {'blk','narrow'}, use_global_device_ids=true, to_apply=%region_0.1 | all-reduce | flops 4096 | bytes 32768 | tf_op jit(solution)/shard_map/psum | solution.py:109
  105.1 5.8 cholesky.338
  112.4 5.5 custom-call.37
  133.1 3.8 conditional.6
  136.9 3.6 conditional.7
  140.5 3.2 fusion.160
  148.8 4.7 collective-permute-start.6
  162.6 6.3 reduce-scatter.4.cloned.1.call-done
  172.2 62.5 %psum.50 = f32[64,64]{1,0:T(8,128)} all-reduce(f32[64,64]{1,0:T(8,128)} %fusion.164), channel_id=1, replica_groups=mesh['groups'=2,'blk'=8,'narrow'=2] {'blk','narrow'}, use_global_device_ids=true, to_apply=%region_18.20 | all-reduce | flops 4096 | bytes 32768 | tf_op jit(solution)/shard_map/psum | solution.py:117
  238.6 4.8 collective-permute-start.10
  254.0 4.2 reduce-scatter.6.cloned.1.call-done
  264.2 86.0 %all-reduce.13.cloned.1.call-done = (f32[128,128]{1,0:T(8,128)}, f32[128,128]{1,0:T(8,128)}) async-done(((f32[128,128]{1,0:T(8,128)}, f32[128,128]{1,0:T(8,128)}), (f32[128,128]{1,0:T(8,128)}, f32[128,128]{1,0:T(8,128)})) %all-reduce.13.cloned.1.call-update) | async-done | bytes 131088 | tf_op jit(solution)/shard_map/psum | solution.py:127
  359.1 13.2 %cholesky.77 = f32[128,128]{1,0:T(8,128)} custom-call(f32[128,128]{1,0:T(8,128)} %fusion.66), custom_call_target="Cholesky" | custom-call | tf_op jit(solution)/shard_map/jit(cholesky)/cholesky | solution.py:46
  376.0 11.3 %custom-call.38 = f32[1,128,128]{1,2,0:T(8,128)} custom-call(f32[1,128,128]{2,1,0:T(8,128)} %fusion.44), custom_call_target="InvertDiagBlocksLowerTriangular" | custom-call | tf_op jit(solution)/shard_map/triangular_solve | solution.py:39
  394.6 7.2 cholesky.349
  405.1 6.3 custom-call.59
  417.7 7.2 cholesky.360
  428.3 6.3 custom-call.60
  440.9 7.4 cholesky.371
  451.6 6.3 custom-call.61
  464.2 7.2 cholesky.382
  474.7 6.3 custom-call.62
  487.3 7.2 cholesky.393
  497.9 6.3 custom-call.63
  510.5 7.2 cholesky.404
  521.2 6.3 custom-call.64
  533.6 60.5 %psum.53 = f32[64,64]{1,0:T(8,128)} all-reduce(f32[64,64]{1,0:T(8,128)} %fusion.179), channel_id=1, replica_groups=mesh['groups'=2,'blk'=8,'narrow'=2] {'blk','narrow'}, use_global_device_ids=true, to_apply=%region_25.29 | all-reduce | flops 4096 | bytes 32768 | tf_op jit(solution)/shard_map/psum | solution.py:117
  598.1 4.8 collective-permute-start.14
  613.1 4.8 reduce-scatter.8.cloned.1.call-done
  621.9 91.2 %all-reduce.11.cloned.1.call-done = (f32[192,192]{1,0:T(8,128)}, f32[192,192]{1,0:T(8,128)}) async-done(((f32[192,192]{1,0:T(8,128)}, f32[192,192]{1,0:T(8,128)}), (f32[192,192]{1,0:T(8,128)}, f32[192,192]{1,0:T(8,128)})) %all-reduce.11.cloned.1.call-update) | async-done | bytes 294928 | tf_op jit(solution)/shard_map/psum | solution.py:127
  713.1 3.3 gather_fusion.1
  717.9 11.7 %cholesky.90 = f32[128,128]{1,0:T(8,128)S(1)} custom-call(f32[128,128]{1,0:T(8,128)S(1)} %cholesky.479), custom_call_target="Cholesky" | custom-call | tf_op jit(solution)/shard_map/jit(cholesky)/cholesky | solution.py:46
  729.6 9.8 %custom-call.39 = f32[1,128,128]{1,2,0:T(8,128)S(1)} custom-call(f32[1,128,128]{2,1,0:T(8,128)S(1)} %get-tuple-element.157), custom_call_target="InvertDiagBlocksLowerTriangular" | custom-call | tf_op jit(solution)/shard_map/jit(cholesky)/cholesky | solution.py:46
  739.8 5.8 cholesky.144
  748.6 19.8 %custom-call.40 = f32[2,128,128]{1,2,0:T(8,128)S(1)} custom-call(f32[2,128,128]{2,1,0:T(8,128)S(1)} %pad_maximum_fusion.5), custom_call_target="InvertDiagBlocksLowerTriangular" | custom-call | tf_op jit(solution)/shard_map/triangular_solve | solution.py:39
  771.1 5.8 cholesky.415
  778.3 4.9 custom-call.67
  784.1 5.8 cholesky.426
  791.3 4.9 custom-call.68
  797.1 5.8 cholesky.437
  804.3 4.9 custom-call.69
  810.2 5.8 cholesky.448
  817.3 4.9 custom-call.70
  823.2 5.8 cholesky.459
  830.3 5.1 custom-call.71
  836.3 5.8 cholesky.470
  843.5 4.9 custom-call.72
  (313 shorter events, 187.1 us)
Async XLA Ops:
  6.5 111.4 %copy-start.36 = (u32[32]{0:T(128)S(1)}, u32[32]{0:T(128)}, u32[]{:S(2)}) copy-start(u32[32]{0:T(128)} %constant.380) | copy-start | bytes 388
  6.5 112.7 %copy-start.10 = (bf16[384,768]{1,0:T(8,128)(2,1)S(1)}, bf16[384,768]{1,0:T(8,128)(2,1)}, u32[]{:S(2)}) copy-start(bf16[384,768]{1,0:T(8,128)(2,1)} %param.21) | copy-start | bytes 1769476
  6.5 118.9 %all-gather.2.cloned.1.call-start = ((), (), s32[]{:S(2)}) async-start(), calls=%async_computation.3 | async-start | bytes 1769472 | tf_op jit(solution)/shard_map/all_gather | solution.py:78
  7.3 161.6 %reduce-scatter.4.cloned.1.call-start = ((), (), s32[]{:S(2)}) async-start(), calls=%async_computation.4 | async-start | bytes 294912 | tf_op jit(solution)/shard_map/reduce_scatter | solution.py:97
  7.3 112.7 %collective-permute-start = (bf16[384,768]{1,0:T(8,128)(2,1)}, bf16[384,768]{1,0:T(8,128)(2,1)S(1)}, u32[]{:S(2)}, u32[]{:S(2)}) collective-permute-start(bf16[384,768]{1,0:T(8,128)(2,1)} %param.21), channel_id=1, source_target_pairs={{0,2},{2,4},{4,6},{6,8},{8,10},{10,12},{12,14},{14,0},{1,3},{3,5},... | collective-permute-start | bytes 1769480 | tf_op jit(solution)/shard_map/ppermute | solution.py:19
  10.3 110.6 %collective-permute-start.1 = (bf16[384,768]{1,0:T(8,128)(2,1)}, bf16[384,768]{1,0:T(8,128)(2,1)}, u32[]{:S(2)}, u32[]{:S(2)}) collective-permute-start(bf16[384,768]{1,0:T(8,128)(2,1)} %param.21), channel_id=1, source_target_pairs={{0,4},{2,6},{4,8},{6,10},{8,12},{10,14},{12,0},{14,2},{1,5},{3,7},... | collective-permute-start | bytes 1769480 | tf_op jit(solution)/shard_map/ppermute | solution.py:19
  11.9 110.1 %collective-permute-start.2 = (bf16[384,768]{1,0:T(8,128)(2,1)}, bf16[384,768]{1,0:T(8,128)(2,1)}, u32[]{:S(2)}, u32[]{:S(2)}) collective-permute-start(bf16[384,768]{1,0:T(8,128)(2,1)} %param.21), channel_id=1, source_target_pairs={{0,14},{2,0},{4,2},{6,4},{8,6},{10,8},{12,10},{14,12},{1,15},{3,1}... | collective-permute-start | bytes 1769480 | tf_op jit(solution)/shard_map/ppermute | solution.py:19
  15.1 109.1 %collective-permute-start.3 = (bf16[384,768]{1,0:T(8,128)(2,1)}, bf16[384,768]{1,0:T(8,128)(2,1)S(1)}, u32[]{:S(2)}, u32[]{:S(2)}) collective-permute-start(bf16[384,768]{1,0:T(8,128)(2,1)} %param.21), channel_id=1, source_target_pairs={{0,12},{2,14},{4,0},{6,2},{8,4},{10,6},{12,8},{14,10},{1,13},{3,15... | collective-permute-start | bytes 1769480 | tf_op jit(solution)/shard_map/ppermute | solution.py:19
  124.2 1.2 copy-start.22
  125.4 1.7 copy-start.13
  127.1 9.8 %copy-start.34 = (f32[768]{0:T(1024)}, f32[768]{0:T(1024)S(1)}, u32[]{:S(2)}) copy-start(f32[768]{0:T(1024)S(1)} %fusion.12) | copy-start | bytes 9220
  127.1 1.1 copy-start.25
  128.9 1.0 copy-start.14
  132.1 1.0 copy-start
  133.1 2.0 copy-start.15
  136.9 2.0 copy-start.35
  136.9 2.0 copy-start.16
  136.9 2.1 copy-start.23
  140.5 3.2 copy-start.33
  148.8 9.0 %collective-permute-start.4 = (f32[384,64]{0,1:T(8,128)S(1)}, f32[384,64]{0,1:T(8,128)S(1)}, u32[]{:S(2)}, u32[]{:S(2)}) collective-permute-start(f32[384,64]{0,1:T(8,128)S(1)} %get-tuple-element.166), channel_id=1, source_target_pairs={{0,2},{2,4},{4,6},{6,8},{8,10},{10,12},{12,14},{14,0},{1,3},{3,5},... | collective-permute-start | bytes 294920 | tf_op jit(solution)/shard_map/ppermute | solution.py:19
  148.8 9.8 %collective-permute-start.6 = (f32[384,64]{0,1:T(8,128)S(1)}, f32[384,64]{0,1:T(8,128)S(1)}, u32[]{:S(2)}, u32[]{:S(2)}) collective-permute-start(f32[384,64]{0,1:T(8,128)S(1)} %get-tuple-element.166), channel_id=1, source_target_pairs={{0,14},{2,0},{4,2},{6,4},{8,6},{10,8},{12,10},{14,12},{1,15},{3,1}... | collective-permute-start | bytes 294920 | tf_op jit(solution)/shard_map/ppermute | solution.py:19
  153.5 6.7 collective-permute-start.7
  153.5 7.5 collective-permute-start.5
  158.6 2.4 copy-start.1
  162.5 95.7 %reduce-scatter.6.cloned.1.call-start = ((), (), s32[]{:S(2)}) async-start(), calls=%async_computation.5 | async-start | bytes 294912 | tf_op jit(solution)/shard_map/reduce_scatter | solution.py:97
  236.5 8.9 %collective-permute-start.8 = (f32[384,64]{0,1:T(8,128)S(1)}, f32[384,64]{0,1:T(8,128)S(1)}, u32[]{:S(2)}, u32[]{:S(2)}) collective-permute-start(f32[384,64]{0,1:T(8,128)S(1)} %get-tuple-element.168), channel_id=1, source_target_pairs={{0,2},{2,4},{4,6},{6,8},{8,10},{10,12},{12,14},{14,0},{1,3},{3,5},... | collective-permute-start | bytes 294920 | tf_op jit(solution)/shard_map/ppermute | solution.py:19
  238.6 7.6 collective-permute-start.10
  243.4 4.6 collective-permute-start.11
  243.4 6.4 collective-permute-start.9
  246.2 3.6 copy-start.2
  251.3 99.0 %all-reduce.13.cloned.1.call-start = ((), (), s32[]{:S(2)}) async-start(), calls=%async_computation.8 | async-start | bytes 262144 | tf_op jit(solution)/shard_map/psum | solution.py:127
  261.8 356.1 %reduce-scatter.8.cloned.1.call-start = ((), (), s32[]{:S(2)}) async-start(), calls=%async_computation.6 | async-start | bytes 294912 | tf_op jit(solution)/shard_map/reduce_scatter | solution.py:97
  529.6 1.2 copy-start.20
  530.9 1.3 copy-start.8
  596.1 8.9 %collective-permute-start.12 = (f32[384,64]{0,1:T(8,128)S(1)}, f32[384,64]{0,1:T(8,128)S(1)}, u32[]{:S(2)}, u32[]{:S(2)}) collective-permute-start(f32[384,64]{0,1:T(8,128)S(1)} %get-tuple-element.170), channel_id=1, source_target_pairs={{0,2},{2,4},{4,6},{6,8},{8,10},{10,12},{12,14},{14,0},{1,3},{3,5},... | collective-permute-start | bytes 294920 | tf_op jit(solution)/shard_map/ppermute | solution.py:19
  598.1 7.6 collective-permute-start.14
  602.9 4.6 collective-permute-start.15
  602.9 6.4 collective-permute-start.13
  605.7 3.6 copy-start.3
  608.3 3.0 copy-start.7
  608.3 3.0 copy-start.21
  608.3 3.3 copy-start.9
  608.3 3.3 copy-start.19
  608.4 4.4 copy-start.12
  610.8 8.0 copy-start.18
  610.8 102.2 %all-reduce.11.cloned.1.call-start = ((), (), s32[]{:S(2)}) async-start(), calls=%async_computation.7 | async-start | bytes 786432 | tf_op jit(solution)/shard_map/psum | solution.py:127
  713.1 4.6 copy-start.4
  717.8 50.6 %copy-start.32 = (f32[192,192]{1,0:T(8,128)S(1)}, f32[192,192]{1,0:T(8,128)}, u32[]{:S(2)}) copy-start(f32[192,192]{1,0:T(8,128)} %get-tuple-element.144) | copy-start | bytes 442372
  (11 other events, 7.0 us)
Sparse Core Ops, SparseCore 0:
  8.9 11.9 all-gather.1
  162.7 6.1 reduce-scatter.3
  251.4 6.8 reduce-scatter.5
  261.9 88.2 all-reduce.12
  611.0 6.8 reduce-scatter.7
  621.1 91.8 all-reduce.10
where the time goes:
time: 867 us; the launch traced here: 857 us
  other arithmetic  291 us (34%)
  blocking collectives  210 us (24%)
  waiting for transfers between devices  198 us (23%)
  matrix products  74.3 us (9%)
  local copies, waits for them, and re-layouts  31.4 us (4%)
  starting transfers between devices  29.7 us (3%)
  between operations  22.6 us (3%)
    psum x2, waiting for transfers between devices, shards(): lax.psum((inner(basis, basis), inner(basis, basis_image)), ('blk', 'narro...  177 us
    psum x2, blocking collectives, shards(): ritz_block = lax.psum(inner(current, image), ('blk', 'narrow'))  123 us
    another operation x36, other arithmetic, ritz_step(): norm_factor = jnp.linalg.cholesky(inner(coeffs, coeffs))  91.1 us
    another operation x26, other arithmetic, lower_solve(): return lax.linalg.triangular_solve(factor, rhs, left_side=True, lower=True)  89 us
    psum x1, blocking collectives, shards(): start_gram = lax.psum(inner(start, start), ('blk', 'narrow'))  84.3 us
    another operation x10, other arithmetic, ritz_step(): factor = jnp.linalg.cholesky(ridged)  43.5 us
    another operation x8, other arithmetic, upper_solve(): lax.linalg.triangular_solve(factor, rhs, left_side=True, lower=True, tran...  33.4 us
    dot_general x34, matrix products, times(): return jnp.dot(left, right, precision=highest)  33 us
  transfers between devices with their start and end apart: 22, of which 10 were waited for; matrix products, arithmetic and copies ran while one was open for 5% of the time, Pallas kernels for 0%

commit v1 on v0

v1 whole, which is shorter than its diff:
```python
import math

import jax
import jax.numpy as jnp
from jax import lax
from jax.experimental import pallas as pl
from jax.experimental.pallas import tpu as pltpu
from jax.sharding import PartitionSpec as P

KERNEL_GAMMA = 2.0
RIDGE_WEIGHT = 1e-05
NVEC = 64
F32 = jnp.float32
BF16 = jnp.bfloat16
VMEM_LIMIT = 48 * 1024 * 1024


def dot(left, right, left_dim=1, right_dim=0):
    precision = lax.Precision.HIGHEST if left.dtype == F32 else None
    return lax.dot_general(
        left, right, (((left_dim,), (right_dim,)), ((), ())),
        precision=precision, preferred_element_type=F32,
    )


def halves(values):
    high = values.astype(BF16)
    return high, (values - high.astype(F32)).astype(BF16)


def call(body, out_shapes, args, smem=(), flops=0, nbytes=0):
    specs = [
        pl.BlockSpec(memory_space=pltpu.SMEM if i in smem else pltpu.VMEM)
        for i in range(len(args))
    ]
    out = pl.pallas_call(
        body,
        out_shape=[jax.ShapeDtypeStruct(shape, dtype) for shape, dtype in out_shapes],
        in_specs=specs,
        out_specs=[pl.BlockSpec(memory_space=pltpu.VMEM) for _ in out_shapes],
        compiler_params=pltpu.CompilerParams(vmem_limit_bytes=VMEM_LIMIT),
        cost_estimate=pl.CostEstimate(flops=flops, bytes_accessed=nbytes, transcendentals=0),
    )(*args)
    return out


def tile_body(keep, own, other, col, high, low, row_sum, col_sum):
    weight = keep[0].astype(F32)
    size = own.shape[0]
    ones = jnp.ones((8, own.shape[1]), BF16)
    ones_rows = jnp.ones((8, size), BF16)
    col_emb = col[...]
    col32 = col_emb.astype(F32)
    sq_high, sq_low = halves(col32 * col32)
    col_sq = (dot(ones, sq_high, 1, 1) + dot(ones, sq_low, 1, 1))[0:1, :]
    total = jnp.zeros((8, size), F32)
    for half, rows in enumerate((own, other)):
        row_emb = rows[...]
        row32 = row_emb.astype(F32)
        row_sq = jnp.sum(row32 * row32, axis=1, keepdims=True)
        inner = dot(row_emb, col_emb, 1, 1)
        tile = jnp.exp(-KERNEL_GAMMA * (row_sq + col_sq - 2.0 * inner)) * weight
        tile_high, tile_low = halves(tile)
        high[half * size:(half + 1) * size, :] = tile_high
        low[half * size:(half + 1) * size, :] = tile_low
        row_sum[half * 8:(half + 1) * 8, :] = dot(ones_rows, tile_high, 1, 1) + dot(ones_rows, tile_low, 1, 1)
        total = total + dot(ones_rows, tile_high) + dot(ones_rows, tile_low)
    col_sum[...] = total


def make_tile(keep, own, other, col):
    rows, depth = own.shape
    return call(
        tile_body,
        [((2 * rows, rows), BF16), ((2 * rows, rows), BF16), ((16, rows), F32), ((8, rows), F32)],
        [keep, own, other, col], smem=(0,),
        flops=4 * rows * rows * depth, nbytes=6 * rows * depth + 8 * rows * rows,
    )


def swapped(values):
    middle = values.shape[0] // 2
    return jnp.concatenate([values[middle:], values[:middle]], axis=0)


def per_row(values, width):
    return jnp.concatenate([
        jnp.broadcast_to(values[0:1, :], (width, values.shape[1])),
        jnp.broadcast_to(values[8:9, :], (width, values.shape[1])),
    ], axis=0)


def send_ahead(vectors, tiles, outs):
    width = vectors.shape[0] // 2
    whole = jnp.concatenate([vectors[:width], vectors[width:]], axis=1)
    high, low = halves(whole)
    both = jnp.concatenate([high, low], axis=0)
    for (tile_high, tile_low), out in zip(tiles, outs):
        product = dot(both, tile_high[...])
        out[...] = product[:width] + product[width:] + dot(high, tile_low[...])


def first_body(sum0, sum1, sum2, other_sum, q0, q1, q2, q3, seed, other_seed, h1, l1, h2, l2,
               degree_out, vectors_out, ahead1, ahead2):
    width = seed.shape[0]
    own_sum = sum0[...] + sum1[...] + sum2[...]
    degree = own_sum + swapped(other_sum[...])
    behind = jnp.concatenate([q0[...] + q1[...], q2[...] + q3[...]], axis=0)
    degree = degree + behind
    degree_out[...] = degree
    scale = lax.rsqrt(degree)
    vectors = jnp.concatenate([seed[...], other_seed[...]], axis=0) * per_row(scale, width)
    vectors_out[...] = vectors
    send_ahead(vectors, ((h1, l1), (h2, l2)), (ahead1, ahead2))


def next_body(total, other_total, degree, h1, l1, h2, l2, vectors_out, ahead1, ahead2):
    width = total.shape[0] // 2
    vectors = (total[...] + swapped(other_total[...])) / per_row(degree[...], width)
    vectors_out[...] = vectors
    send_ahead(vectors, ((h1, l1), (h2, l2)), (ahead1, ahead2))


def product_rows(vectors, tile_high, tile_low):
    width = vectors.shape[0]
    high, low = halves(vectors)
    both = jnp.concatenate([high, low], axis=0)
    product = dot(both, tile_high[...], 1, 1)
    return product[:width] + product[width:] + dot(high, tile_low[...], 1, 1)


def block_body(vectors, near1, near2, q1, q2, h0, l0, h1, l1, h2, l2, total):
    width, size = near1.shape
    product = product_rows(vectors[:width, :], h0, l0)
    product = product + product_rows(near1[...], h1, l1)
    product = product + product_rows(near2[...], h2, l2)
    total[:width, :] = product[:, :size] + q1[...] + q2[...]
    total[width:, :] = product[:, size:]


def moment_body(degree, v0, v1, v2, near1, near2, h0, l0, h1, l1, h2, l2, moments, scaled):
    width, size = near1.shape
    root = jnp.sqrt(degree[0:1, :])
    x0, x1, x2 = v0[:width, :] * root, v1[:width, :] * root, v2[:width, :] * root
    scaled[...] = jnp.concatenate([x0, x1, x2], axis=0)
    low_order = dot(jnp.concatenate([x0, x1], axis=0), jnp.concatenate([x0, x1], axis=0), 1, 1)
    high_order = dot(jnp.concatenate([x1, x2], axis=0), x2, 1, 1)
    last = product_rows(near1[...], h1, l1) + product_rows(near2[...], h2, l2)
    last = 2.0 * last + product_rows(v2[:width, :], h0, l0)
    whole = jnp.concatenate([v2[:width, :], v2[width:, :]], axis=1)
    last = dot(whole, last, 1, 1)
    moments[0:width, :] = low_order[:width, :]
    moments[width:2 * width, :] = jnp.concatenate([low_order[width:, width:], high_order[:width]], axis=1)
    moments[2 * width:, :] = jnp.concatenate([high_order[width:], last], axis=1)


def unit(rows, cols):
    return (lax.broadcasted_iota(jnp.int32, (rows, cols), 0)
            == lax.broadcasted_iota(jnp.int32, (rows, cols), 1)).astype(F32)


def inverse_factor(matrix):
    size = matrix.shape[0]
    work = jnp.concatenate([matrix, unit(size, size)], axis=1)
    blocks = [work[8 * i:8 * i + 8, :] for i in range(size // 8)]
    place = lax.broadcasted_iota(jnp.int32, (8, 2 * size), 0)
    shape = (8, 2 * size)
    for k in range(0, size, 2):
        top, r = divmod(k, 8)
        pivot = blocks[top]
        row0 = jnp.broadcast_to(pivot[r:r + 1, :], shape)
        row1 = jnp.broadcast_to(pivot[r + 1:r + 2, :], shape)
        a = jnp.broadcast_to(row0[:, k:k + 1], shape)
        b = jnp.broadcast_to(row0[:, k + 1:k + 2], shape)
        d = jnp.broadcast_to(row1[:, k + 1:k + 2], shape)
        inv_a = 1.0 / a
        inv_d = a / (a * d - b * b)
        ratio = b * inv_a
        row1 = row1 - ratio * row0
        for i in range(top, size // 8):
            c0 = jnp.broadcast_to(blocks[i][:, k:k + 1], shape)
            c1 = jnp.broadcast_to(blocks[i][:, k + 1:k + 2], shape)
            f0 = c0 * inv_a
            f1 = (c1 - c0 * ratio) * inv_d
            if i == top:
                f0 = jnp.where(place > r, f0, 0.0)
                f1 = jnp.where(place > r + 1, f1, 0.0)
            blocks[i] = blocks[i] - f0 * row0 - f1 * row1
    work = jnp.concatenate(blocks, axis=0)
    diagonal = jnp.sum(work[:, :size] * unit(size, size), axis=1, keepdims=True)
    return work[:, size:] * lax.rsqrt(diagonal)


def trace(matrix):
    return jnp.sum(matrix * unit(*matrix.shape))


def dense(moments, index, rows):
    n = NVEC
    eye = unit(n, n)
    pick = ((lax.broadcasted_iota(jnp.int32, (n, n), 0) == index)
            & (lax.broadcasted_iota(jnp.int32, (n, n), 1) == index)).astype(F32)

    def even(matrix):
        return 0.5 * (matrix + matrix.T)

    base_t = inverse_factor(moments[0])
    base = base_t.T
    wide = dot(base_t, jnp.concatenate(moments[1:], axis=1))
    tall = dot(jnp.concatenate([wide[:, i * n:(i + 1) * n] for i in range(5)], axis=0), base)
    m = [eye] + [even(tall[i * n:(i + 1) * n]) for i in range(5)]

    square = dot(m[1], m[1])
    cross = dot(m[1], jnp.concatenate([m[2], square], axis=1))
    gram_r = m[2] - square
    image_r = m[3] - cross[:, :n] - cross[:, :n].T + cross[:, n:]
    shift = 3.0 - jnp.sum(m[1] * pick)
    ridge = RIDGE_WEIGHT * (n + trace(gram_r)) / (2 * n)
    ridged = gram_r + ridge * eye
    factor_t = inverse_factor(ridged)
    inverse = dot(factor_t, factor_t, 0, 0)
    keep = 1.0 / (1.0 + ridge)
    step = jnp.concatenate([
        jnp.concatenate([m[1] * keep + shift * eye, gram_r * keep], axis=1),
        jnp.concatenate([eye - ridge * inverse, dot(inverse, image_r) + shift * eye], axis=1),
    ], axis=0)
    cube = dot(dot(step, step), step)
    power = dot(cube, cube[:, :n])
    top, bottom = power[:n], power[n:]
    norm = (1.0 + ridge) * dot(top, top, 0, 0) + dot(bottom, dot(ridged, bottom), 0, 0)
    norm_t = inverse_factor(even(norm))
    mixed = dot(power, norm_t, 1, 1)
    top, bottom = mixed[:n], mixed[n:]

    back = dot(m[1], bottom)
    zero = jnp.zeros((n, n), F32)
    current = jnp.concatenate([top - back, bottom, zero], axis=0)
    image = jnp.concatenate([zero, top - back, bottom], axis=0)
    previous = jnp.concatenate([-back, bottom, zero], axis=0)
    hankel = [jnp.concatenate(m[i:i + 3], axis=1) for i in range(4)]
    plain = jnp.concatenate(hankel[:3], axis=0)
    raised = jnp.concatenate(hankel[1:], axis=0)
    ritz = even(dot(dot(current, plain, 0, 0), image))
    shift = 3.0 - jnp.sum(ritz * pick)
    residual = image - dot(current, ritz)
    basis = jnp.concatenate([current, previous, residual], axis=1)
    gram = dot(dot(basis, plain, 0, 0), basis)
    image_gram = dot(dot(basis, raised, 0, 0), basis)
    ridge = RIDGE_WEIGHT * trace(gram) / (3 * n)
    ridged = gram + ridge * unit(3 * n, 3 * n)
    g = [[ridged[i * n:(i + 1) * n, j * n:(j + 1) * n] for j in range(3)] for i in range(3)]
    v0 = inverse_factor(even(g[0][0]))
    l1020 = dot(jnp.concatenate([g[1][0], g[2][0]], axis=0), v0, 1, 1)
    outer = dot(l1020, l1020, 1, 1)
    v1 = inverse_factor(even(g[1][1] - outer[:n, :n]))
    l21 = dot(g[2][1] - outer[n:, :n], v1, 1, 1)
    v2 = inverse_factor(even(g[2][2] - outer[n:, n:] - dot(l21, l21, 1, 1)))
    l10, l20 = l1020[:n], l1020[n:]
    h0 = dot(v0, image_gram[:n])
    h1 = dot(v1, image_gram[n:2 * n] - dot(l10, h0))
    h2 = dot(v2, image_gram[2 * n:] - dot(l20, h0) - dot(l21, h1))
    z2 = dot(v2, h2, 0, 0)
    z1 = dot(v1, h1 - dot(l21, z2, 0, 0), 0, 0)
    z0 = dot(v0, h0 - dot(l10, z1, 0, 0) - dot(l20, z2, 0, 0), 0, 0)
    step = jnp.concatenate([z0, z1, z2], axis=0) + shift * unit(3 * n, 3 * n)
    cube = dot(dot(step, step), step)
    power = dot(cube, cube[:, :n])
    norm_t = inverse_factor(even(dot(power, dot(ridged, power), 0, 0)))
    mixed = dot(basis, dot(power, norm_t, 1, 1)) * math.sqrt(rows)
    return jnp.concatenate([dot(base, mixed[i * n:(i + 1) * n]) for i in range(3)], axis=0)


def dense_body(rows, index, moments, scaled, out):
    n = NVEC
    packed = moments[...]
    parts = [packed[i * n:(i + 1) * n, j * n:(j + 1) * n] for i in range(3) for j in range(2)]
    parts = [0.5 * (part + part.T) for part in parts]
    coeffs = dense(parts, index[0], rows)
    out[...] = dot(scaled[...], coeffs, 0, 0)


def moved(shard, axis, by):
    length = lax.axis_size(axis)
    return lax.ppermute(shard, axis, [(i, (i + by) % length) for i in range(length)])


def moved_both(shard, axis, by):
    blocks, cores = lax.axis_size(axis), lax.axis_size("narrow")
    pairs = []
    for i in range(blocks):
        for j in range(cores):
            pairs.append((i * cores + j, (i + by) % blocks * cores + (j + 1) % cores))
    return lax.ppermute(shard, (axis, "narrow"), pairs)


def total_over_rows(values):
    values = lax.psum(values, "narrow")
    blocks = lax.axis_size("blk")
    span = 1
    while blocks % (2 * span) == 0:
        groups = [[i, i + span] for i in range(blocks) if i // span % 2 == 0]
        values = lax.psum(values, "blk", axis_index_groups=groups)
        span *= 2
    if span < blocks:
        groups = [list(range(i, blocks, span)) for i in range(span)]
        values = lax.psum(values, "blk", axis_index_groups=groups)
    return values


def shards(embeddings, pair_mask, shift_index, start_seed):
    size = embeddings.shape[0]
    blocks = lax.axis_size("blk")
    where = lax.axis_index("blk")
    other_emb = moved(embeddings, "narrow", 1)
    near_emb = [moved(embeddings, "blk", -1), moved(embeddings, "blk", -2)]
    seed = start_seed.astype(F32).T / 1000.0
    other_seed = moved(seed, "narrow", 1)
    keep = lax.dynamic_slice_in_dim(pair_mask, where, 1, 0)[0]
    flags = [jnp.ones((1,), jnp.int32), keep[0:1], keep[1:2]]
    tiles, row_sums, col_sums = [], [], []
    for flag, col in zip(flags, [embeddings] + near_emb):
        high, low, row_sum, col_sum = make_tile(flag, embeddings, other_emb, col)
        tiles += [high, low]
        row_sums.append(row_sum)
        col_sums.append(col_sum)
    other_sum = moved(row_sums[0] + row_sums[1] + row_sums[2], "narrow", 1)
    behind = [moved(col_sums[1], "blk", 1), moved(col_sums[2], "blk", 2),
              moved_both(col_sums[1], "blk", 1), moved_both(col_sums[2], "blk", 2)]
    pair_shape = ((2 * NVEC, size), F32)
    half_shape = ((NVEC, size), F32)
    cost = dict(flops=2 * 3 * 128 * 2 * size * 2 * size, nbytes=16 * size * size)
    degree, vectors, ahead1, ahead2 = call(
        first_body, [((16, size), F32), pair_shape, half_shape, half_shape],
        row_sums + [other_sum] + behind + [seed, other_seed] + tiles[2:], **cost,
    )
    history = [vectors]
    for _ in range(2):
        near1, near2 = moved(vectors[:NVEC], "blk", -1), moved(vectors[:NVEC], "blk", -2)
        q1, q2 = moved(ahead1, "blk", 1), moved(ahead2, "blk", 2)
        (total,) = call(block_body, [pair_shape], [vectors, near1, near2, q1, q2] + tiles, **cost)
        other_total = moved(total, "narrow", 1)
        vectors, ahead1, ahead2 = call(
            next_body, [pair_shape, half_shape, half_shape],
            [total, other_total, degree] + tiles[2:], **cost,
        )
        history.append(vectors)
    near1, near2 = moved(vectors[:NVEC], "blk", -1), moved(vectors[:NVEC], "blk", -2)
    moments, scaled = call(
        moment_body, [((3 * NVEC, 2 * NVEC), F32), ((3 * NVEC, size), F32)],
        [degree] + history + [near1, near2] + tiles, **cost,
    )
    moments = total_over_rows(moments)
    rows = size * blocks * lax.axis_size("narrow")
    (out,) = call(
        lambda *refs: dense_body(rows, *refs), [((size, NVEC), F32)],
        [shift_index, moments, scaled], smem=(0,), flops=10**9, nbytes=10**6,
    )
    return out


def solution(mesh):
    return jax.shard_map(
        shards,
        mesh=mesh,
        in_specs=(
            P(("groups", "blk", "narrow"), None),
            P("groups", None),
            P("groups"),
            P(("groups", "blk", "narrow"), None),
        ),
        out_specs=P(("groups", "blk", "narrow"), None),
        check_vma=False,
    )
```

time: 867 us -> 231 us (0.27); the launches traced: 857 us -> 231 us
  other arithmetic: 291 us -> 0.91 us
  blocking collectives: 210 us -> 0 us
  matrix products: 74.3 us -> 0 us
  waiting for transfers between devices: 198 us -> 130 us
  Pallas kernels: 0 us -> 57.1 us
  local copies, waits for them, and re-layouts: 31.4 us -> 3.41 us
  between operations: 22.6 us -> 13.9 us
    another operation x83 -> x0, other arithmetic: 264 us -> none  [the longest x36 91.1 us: ritz_step(): norm_factor = jnp.linalg.cholesky(inner(coeffs, coeffs))]
    psum x3 -> x0, blocking collectives: 207 us -> none  [the longest x2 123 us: shards(): ritz_block = lax.psum(inner(current, image), ('blk', 'narrow'))]
    psum x2 -> x4, waiting for transfers between devices: 177 us -> 90.6 us  [the longest x3 73.1 us: total_over_rows(): values = lax.psum(values, 'blk', axis_index_groups=groups)]
    dot_general x58 -> x0, matrix products: 58.5 us -> none  [the longest x34 33 us: times(): return jnp.dot(left, right, precision=highest)]
    pallas_call x0 -> x10, Pallas kernels: none -> 57.1 us  [call(): pl.pallas_call(body, out_shape=[jax.ShapeDtypeStruct(shape, dtype) for sh...]
    ppermute x16 -> x21, waiting for transfers between devices: 4.77 us -> 39.3 us  [the longest x19 38.3 us: moved(): lax.ppermute(shard, axis, [(i, (i + by) % length) for i in range(length)])]
    another operation x27 -> x0, matrix products: 15.8 us -> none  [the longest x21 13.8 us: lower_solve(): return lax.linalg.triangular_solve(factor, rhs, left_side=True, lower=True)]
    reduce_scatter x3 -> x0, waiting for transfers between devices: 15.3 us -> none  [apply_fn(): return lax.psum_scatter(total, 'narrow', scatter_dimension=0, tiled=True)]
  transfers between devices with their start and end apart: 22 -> 25, of which waited for: 10 -> 18; matrix products, arithmetic and copies ran while one was open for 5% -> 1% of each run, Pallas kernels for 0% -> 4%
where the time goes in v1:
time: 231 us
  waiting for transfers between devices  130 us (56%)
  Pallas kernels  57.1 us (25%)
  starting transfers between devices  25.2 us (11%)
  between operations  13.9 us (6%)
  local copies, waits for them, and re-layouts  3.41 us (1%)
    psum x3, waiting for transfers between devices, total_over_rows(): values = lax.psum(values, 'blk', axis_index_groups=groups)  73.1 us
    pallas_call x10, Pallas kernels, call(): pl.pallas_call(body, out_shape=[jax.ShapeDtypeStruct(shape, dtype) for sh...  57.1 us
    ppermute x19, waiting for transfers between devices, moved(): lax.ppermute(shard, axis, [(i, (i + by) % length) for i in range(length)])  38.3 us
    ppermute x19, starting transfers between devices, moved(): lax.ppermute(shard, axis, [(i, (i + by) % length) for i in range(length)])  20.3 us
    psum x1, waiting for transfers between devices, total_over_rows(): values = lax.psum(values, 'narrow')  17.5 us
  transfers between devices with their start and end apart: 25, of which 18 were waited for; matrix products, arithmetic and copies ran while one was open for 1% of the time, Pallas kernels for 4%

profile of v1, /device:TPU:0, one launch (start us, length us, event | category | flops | bytes accessed | tf_op | source)
XLA Modules:
  0.0 230.5 jit_solution(3507722656771500402)
XLA Ops:
  6.5 0.5 collective-permute-start
  7.0 5.5 %collective-permute-start.1 = (bf16[384,768]{1,0:T(8,128)(2,1)}, bf16[384,768]{1,0:T(8,128)(2,1)S(1)}, u32[]{:S(2)}, u32[]{:S(2)}) collective-permute-start(bf16[384,768]{1,0:T(8,128)(2,1)} %own.5), channel_id=1, source_target_pairs={{0,14},{2,0},{4,2},{6,4},{8,6},{10,8},{12,10},{14,12},{1,15},{3,1}... | collective-permute-start | bytes 1769480 | tf_op jit(solution)/shard_map/ppermute | solution.py:284
  12.5 0.4 collective-permute-start.2
  13.0 0.9 multiply_bitcast_fusion.seed
  14.0 0.6 fusion
  14.6 1.1 copy-done.1
  15.7 2.7 %shard_map.46 = (bf16[768,384]{1,0:T(8,128)(2,1)S(1)}, bf16[768,384]{1,0:T(8,128)(2,1)S(1)}, f32[16,384]{1,0:T(8,128)S(1)}, f32[8,384]{1,0:T(8,128)}) custom-call(s32[1]{0:T(128)} %constant.3.clone.1.keep, bf16[384,768]{1,0:T(8,128)(2,1)S(1)} %copy-done.1, bf16[384,768]{1,0:T(8,128)(2,1)S(1)} %collective-permute-done.other, bf16[384,768]{1,0:T(8,128)(2,1)S(1)} %copy-done.1), custom_call_target="tpu_custom_call" | custom-call | flops 452984832 | bytes 2949120 | tf_op jit(solution)/shard_map/pallas_call | solution.py:36
  18.4 8.1 %collective-permute-done.1.col = bf16[384,768]{1,0:T(8,128)(2,1)S(1)} collective-permute-done((bf16[384,768]{1,0:T(8,128)(2,1)}, bf16[384,768]{1,0:T(8,128)(2,1)S(1)}, u32[]{:S(2)}, u32[]{:S(2)}) %collective-permute-start.1) | collective-permute-done | bytes 589856 | tf_op jit(solution)/shard_map/ppermute | solution.py:284
  26.5 2.7 %shard_map.47 = (bf16[768,384]{1,0:T(8,128)(2,1)S(1)}, bf16[768,384]{1,0:T(8,128)(2,1)S(1)}, f32[16,384]{1,0:T(8,128)S(1)}, f32[8,384]{1,0:T(8,128)S(1)}) custom-call(s32[1]{0:T(128)} %bitcast.keep, bf16[384,768]{1,0:T(8,128)(2,1)S(1)} %copy-done.2, bf16[384,768]{1,0:T(8,128)(2,1)S(1)} %collective-permute-done.other, ...), custom_call_target="tpu_custom_call" | custom-call | flops 452984832 | bytes 2949120 | tf_op jit(solution)/shard_map/pallas_call | solution.py:36
  29.2 9.6 %collective-permute-done.2.col = bf16[384,768]{1,0:T(8,128)(2,1)S(1)} collective-permute-done((bf16[384,768]{1,0:T(8,128)(2,1)}, bf16[384,768]{1,0:T(8,128)(2,1)S(1)}, u32[]{:S(2)}, u32[]{:S(2)}) %collective-permute-start.2) | collective-permute-done | bytes 589856 | tf_op jit(solution)/shard_map/ppermute | solution.py:284
  38.7 2.7 %shard_map.48 = (bf16[768,384]{1,0:T(8,128)(2,1)S(1)}, bf16[768,384]{1,0:T(8,128)(2,1)S(1)}, f32[16,384]{1,0:T(8,128)S(1)}, f32[8,384]{1,0:T(8,128)S(1)}) custom-call(s32[1]{0:T(128)} %bitcast.1.keep, bf16[384,768]{1,0:T(8,128)(2,1)S(1)} %copy-done.2, bf16[384,768]{1,0:T(8,128)(2,1)S(1)} %collective-permute-done.other, ...), custom_call_target="tpu_custom_call" | custom-call | flops 452984832 | bytes 2949120 | tf_op jit(solution)/shard_map/pallas_call | solution.py:36
  41.6 1.6 collective-permute-start.6
  43.2 1.6 collective-permute-start.5
  44.8 3.0 %collective-permute-start.7 = (f32[8,384]{1,0:T(8,128)S(1)}, f32[8,384]{1,0:T(8,128)S(1)}, u32[]{:S(2)}, u32[]{:S(2)}) collective-permute-start(f32[8,384]{1,0:T(8,128)S(1)} %get-tuple-element.30), channel_id=1, source_target_pairs={{0,5},{1,4},{2,7},{3,6},{4,9},{5,8},{6,11},{7,10},{8,13},{9,12},{1... | collective-permute-start | bytes 36872 | tf_op jit(solution)/shard_map/ppermute | solution.py:293
  48.0 0.7 collective-permute-done.5.q1
  48.7 1.0 collective-permute-done.7.q3
  49.7 0.5 shard_map.49
  50.3 1.1 collective-permute-start.10
  51.4 1.8 collective-permute-start.9
  53.1 0.3 collective-permute-start.11
  53.4 1.0 collective-permute-start.12
  54.4 1.6 collective-permute-done.10.near2
  56.0 0.5 collective-permute-done.9.near1
  56.4 4.7 %collective-permute-done.11.q1 = f32[64,384]{1,0:T(8,128)S(1)} collective-permute-done((f32[64,384]{1,0:T(8,128)S(1)}, f32[64,384]{1,0:T(8,128)S(1)}, u32[]{:S(2)}, u32[]{:S(2)}) %collective-permute-start.11) | collective-permute-done | bytes 98336 | tf_op jit(solution)/shard_map/ppermute | solution.py:284
  61.1 1.2 shard_map.50.total
  62.4 1.4 collective-permute-done.13.other_total
  63.8 0.5 shard_map.51
  64.3 1.4 collective-permute-start.14
  65.7 0.2 collective-permute-start.15
  66.0 1.5 collective-permute-start.16
  67.5 1.0 collective-permute-start.17
  68.4 0.8 collective-permute-done.14.near1
  69.2 5.3 %collective-permute-done.15.near2 = f32[64,384]{1,0:T(8,128)S(1)} collective-permute-done((f32[64,384]{1,0:T(8,128)S(1)}, f32[64,384]{1,0:T(8,128)S(1)}, u32[]{:S(2)}, u32[]{:S(2)}) %collective-permute-start.15) | collective-permute-done | bytes 98336 | tf_op jit(solution)/shard_map/ppermute | solution.py:284
  74.5 1.2 shard_map.52.total
  75.8 1.4 collective-permute-done.18.other_total
  77.2 1.1 shard_map.53
  78.4 1.9 collective-permute-start.19
  80.3 1.9 collective-permute-start.20
  82.2 1.1 collective-permute-done.19.near1
  83.3 2.9 %collective-permute-done.20.near2 = f32[64,384]{1,0:T(8,128)S(1)} collective-permute-done((f32[64,384]{1,0:T(8,128)S(1)}, f32[64,384]{1,0:T(8,128)S(1)}, u32[]{:S(2)}, u32[]{:S(2)}) %collective-permute-start.20) | collective-permute-done | bytes 98336 | tf_op jit(solution)/shard_map/ppermute | solution.py:284
  86.2 2.6 %shard_map.54 = (f32[192,128]{1,0:T(8,128)}, f32[192,384]{1,0:T(8,128)S(1)}) custom-call(f32[16,384]{1,0:T(8,128)S(1)} %get-tuple-element.35.degree, f32[128,384]{1,0:T(8,128)S(1)} %get-tuple-element.36.vectors.v0, f32[128,384]{1,0:T(8,128)S(1)} %get-tuple-element.41.vectors.v1, f32[128,384]{1,0:T(8,128)S(1)} %get-tuple-element.44.v2, ...), custom_call_target="tpu_custom_call" | custom-call | flops 452984832 | bytes 2359296 | tf_op jit(solution)/shard_map/pallas_call | solution.py:36
  88.9 17.5 %all-reduce.5.cloned.1.call-done = f32[192,128]{1,0:T(8,128)} async-done(((f32[192,128]{1,0:T(8,128)}), f32[192,128]{1,0:T(8,128)}) %all-reduce.5.cloned.1.call-update) | async-done | bytes 98320 | tf_op jit(solution)/shard_map/psum | solution.py:297
  106.4 24.4 %all-reduce.7.cloned.1.call-done = f32[192,128]{1,0:T(8,128)} async-done(((f32[192,128]{1,0:T(8,128)}), f32[192,128]{1,0:T(8,128)}) %all-reduce.7.cloned.1.call-update) | async-done | bytes 98320 | tf_op jit(solution)/shard_map/psum | solution.py:302
  131.1 23.7 %all-reduce.9.cloned.1.call-done = f32[192,128]{1,0:T(8,128)} async-done(((f32[192,128]{1,0:T(8,128)}), f32[192,128]{1,0:T(8,128)}) %all-reduce.9.cloned.1.call-update) | async-done | bytes 98320 | tf_op jit(solution)/shard_map/psum | solution.py:302
  155.5 24.9 %all-reduce.11.cloned.1.call-done.refs_1_ = f32[192,128]{1,0:T(8,128)} async-done(((f32[192,128]{1,0:T(8,128)}), f32[192,128]{1,0:T(8,128)}) %all-reduce.11.cloned.1.call-update) | async-done | bytes 98320 | tf_op jit(solution)/shard_map/psum | solution.py:302
  180.5 0.9 copy-done.3
  181.4 41.9 %shard_map.55 = f32[384,64]{1,0:T(8,128)S(1)} custom-call(s32[1]{0:T(128)S(6)} %copy.10.refs_0_, f32[192,128]{1,0:T(8,128)S(1)} %copy-done.3, f32[192,384]{1,0:T(8,128)S(1)} %get-tuple-element.46.refs_2_), custom_call_target="tpu_custom_call" | custom-call | flops 1000000000 | bytes 1000000 | tf_op jit(solution)/shard_map/pallas_call | solution.py:36
  223.2 0.8 copy.5
  (32 shorter events, 1.0 us)
Async XLA Ops:
  6.5 7.4 %copy-start = (s32[8,2]{0,1:T(2,128)S(1)}, s32[8,2]{0,1:T(2,128)}, u32[]{:S(2)}) copy-start(s32[8,2]{0,1:T(2,128)} %param.5) | copy-start | bytes 196
  6.5 99.8 %all-reduce.5.cloned.1.call-start = ((), (), s32[]{:S(2)}) async-start(), calls=%async_computation | async-start | bytes 196608 | tf_op jit(solution)/shard_map/psum | solution.py:297
  6.5 8.1 %collective-permute-start = (bf16[384,768]{1,0:T(8,128)(2,1)}, bf16[384,768]{1,0:T(8,128)(2,1)S(1)}, u32[]{:S(2)}, u32[]{:S(2)}) collective-permute-start(bf16[384,768]{1,0:T(8,128)(2,1)} %own.5), channel_id=1, source_target_pairs={{0,1},{1,0},{2,3},{3,2},{4,5},{5,4},{6,7},{7,6},{8,9},{9,8},{10,11... | collective-permute-start | bytes 1769480 | tf_op jit(solution)/shard_map/ppermute | solution.py:284
  7.0 19.5 %collective-permute-start.1 = (bf16[384,768]{1,0:T(8,128)(2,1)}, bf16[384,768]{1,0:T(8,128)(2,1)S(1)}, u32[]{:S(2)}, u32[]{:S(2)}) collective-permute-start(bf16[384,768]{1,0:T(8,128)(2,1)} %own.5), channel_id=1, source_target_pairs={{0,14},{2,0},{4,2},{6,4},{8,6},{10,8},{12,10},{14,12},{1,15},{3,1}... | collective-permute-start | bytes 1769480 | tf_op jit(solution)/shard_map/ppermute | solution.py:284
  12.5 26.2 %collective-permute-start.2 = (bf16[384,768]{1,0:T(8,128)(2,1)}, bf16[384,768]{1,0:T(8,128)(2,1)S(1)}, u32[]{:S(2)}, u32[]{:S(2)}) collective-permute-start(bf16[384,768]{1,0:T(8,128)(2,1)} %own.5), channel_id=1, source_target_pairs={{0,12},{2,14},{4,0},{6,2},{8,4},{10,6},{12,8},{14,10},{1,13},{3,15... | collective-permute-start | bytes 1769480 | tf_op jit(solution)/shard_map/ppermute | solution.py:284
  13.9 30.9 %collective-permute-start.8 = (f32[64,384]{1,0:T(8,128)S(1)}, f32[64,384]{1,0:T(8,128)S(1)}, u32[]{:S(2)}, u32[]{:S(2)}) collective-permute-start(f32[64,384]{1,0:T(8,128)S(1)} %multiply_bitcast_fusion.seed), channel_id=1, source_target_pairs={{0,1},{1,0},{2,3},{3,2},{4,5},{5,4},{6,7},{7,6},{8,9},{9,8},{10,11... | collective-permute-start | bytes 294920 | tf_op jit(solution)/shard_map/ppermute | solution.py:284
  14.6 1.1 copy-start.1
  15.7 10.8 %copy-start.2 = (bf16[384,768]{1,0:T(8,128)(2,1)S(1)}, bf16[384,768]{1,0:T(8,128)(2,1)}, u32[]{:S(2)}) copy-start(bf16[384,768]{1,0:T(8,128)(2,1)} %own.5) | copy-start | bytes 1769476
  41.5 8.2 %collective-permute-start.3 = (f32[16,384]{1,0:T(8,128)S(1)}, f32[16,384]{1,0:T(8,128)S(1)}, u32[]{:S(2)}, u32[]{:S(2)}) collective-permute-start(f32[16,384]{1,0:T(8,128)S(1)} %add_add_fusion), channel_id=1, source_target_pairs={{0,1},{1,0},{2,3},{3,2},{4,5},{5,4},{6,7},{7,6},{8,9},{9,8},{10,11... | collective-permute-start | bytes 73736 | tf_op jit(solution)/shard_map/ppermute | solution.py:284
  41.6 6.4 %collective-permute-start.4 = (f32[8,384]{1,0:T(8,128)S(1)}, f32[8,384]{1,0:T(8,128)S(1)}, u32[]{:S(2)}, u32[]{:S(2)}) collective-permute-start(f32[8,384]{1,0:T(8,128)S(1)} %get-tuple-element.29), channel_id=1, source_target_pairs={{0,2},{2,4},{4,6},{6,8},{8,10},{10,12},{12,14},{14,0},{1,3},{3,5},... | collective-permute-start | bytes 36872 | tf_op jit(solution)/shard_map/ppermute | solution.py:284
  41.6 7.1 %collective-permute-start.6 = (f32[8,384]{1,0:T(8,128)S(1)}, f32[8,384]{1,0:T(8,128)S(1)}, u32[]{:S(2)}, u32[]{:S(2)}) collective-permute-start(f32[8,384]{1,0:T(8,128)S(1)} %get-tuple-element.29), channel_id=1, source_target_pairs={{0,3},{1,2},{2,5},{3,4},{4,7},{5,6},{6,9},{7,8},{8,11},{9,10},{10,... | collective-permute-start | bytes 36872 | tf_op jit(solution)/shard_map/ppermute | solution.py:293
  43.2 5.5 %collective-permute-start.5 = (f32[8,384]{1,0:T(8,128)S(1)}, f32[8,384]{1,0:T(8,128)S(1)}, u32[]{:S(2)}, u32[]{:S(2)}) collective-permute-start(f32[8,384]{1,0:T(8,128)S(1)} %get-tuple-element.30), channel_id=1, source_target_pairs={{0,4},{2,6},{4,8},{6,10},{8,12},{10,14},{12,0},{14,2},{1,5},{3,7},... | collective-permute-start | bytes 36872 | tf_op jit(solution)/shard_map/ppermute | solution.py:284
  44.8 4.9 %collective-permute-start.7 = (f32[8,384]{1,0:T(8,128)S(1)}, f32[8,384]{1,0:T(8,128)S(1)}, u32[]{:S(2)}, u32[]{:S(2)}) collective-permute-start(f32[8,384]{1,0:T(8,128)S(1)} %get-tuple-element.30), channel_id=1, source_target_pairs={{0,5},{1,4},{2,7},{3,6},{4,9},{5,8},{6,11},{7,10},{8,13},{9,12},{1... | collective-permute-start | bytes 36872 | tf_op jit(solution)/shard_map/ppermute | solution.py:293
  50.3 5.7 %collective-permute-start.10 = (f32[64,384]{1,0:T(8,128)S(1)}, f32[64,384]{1,0:T(8,128)S(1)}, u32[]{:S(2)}, u32[]{:S(2)}) collective-permute-start(f32[64,384]{1,0:T(8,128)S(1)} %slice.28), channel_id=1, source_target_pairs={{0,12},{2,14},{4,0},{6,2},{8,4},{10,6},{12,8},{14,10},{1,13},{3,15... | collective-permute-start | bytes 294920 | tf_op jit(solution)/shard_map/ppermute | solution.py:284
  51.4 5.1 %collective-permute-start.9 = (f32[64,384]{1,0:T(8,128)S(1)}, f32[64,384]{1,0:T(8,128)S(1)}, u32[]{:S(2)}, u32[]{:S(2)}) collective-permute-start(f32[64,384]{1,0:T(8,128)S(1)} %slice.28), channel_id=1, source_target_pairs={{0,14},{2,0},{4,2},{6,4},{8,6},{10,8},{12,10},{14,12},{1,15},{3,1}... | collective-permute-start | bytes 294920 | tf_op jit(solution)/shard_map/ppermute | solution.py:284
  53.1 8.0 %collective-permute-start.11 = (f32[64,384]{1,0:T(8,128)S(1)}, f32[64,384]{1,0:T(8,128)S(1)}, u32[]{:S(2)}, u32[]{:S(2)}) collective-permute-start(f32[64,384]{1,0:T(8,128)S(1)} %get-tuple-element.37), channel_id=1, source_target_pairs={{0,2},{2,4},{4,6},{6,8},{8,10},{10,12},{12,14},{14,0},{1,3},{3,5},... | collective-permute-start | bytes 294920 | tf_op jit(solution)/shard_map/ppermute | solution.py:284
  53.4 7.7 %collective-permute-start.12 = (f32[64,384]{1,0:T(8,128)S(1)}, f32[64,384]{1,0:T(8,128)S(1)}, u32[]{:S(2)}, u32[]{:S(2)}) collective-permute-start(f32[64,384]{1,0:T(8,128)S(1)} %get-tuple-element.38), channel_id=1, source_target_pairs={{0,4},{2,6},{4,8},{6,10},{8,12},{10,14},{12,0},{14,2},{1,5},{3,7},... | collective-permute-start | bytes 294920 | tf_op jit(solution)/shard_map/ppermute | solution.py:284
  62.3 1.5 collective-permute-start.13
  64.3 4.9 %collective-permute-start.14 = (f32[64,384]{1,0:T(8,128)S(1)}, f32[64,384]{1,0:T(8,128)S(1)}, u32[]{:S(2)}, u32[]{:S(2)}) collective-permute-start(f32[64,384]{1,0:T(8,128)S(1)} %slice.29), channel_id=1, source_target_pairs={{0,14},{2,0},{4,2},{6,4},{8,6},{10,8},{12,10},{14,12},{1,15},{3,1}... | collective-permute-start | bytes 294920 | tf_op jit(solution)/shard_map/ppermute | solution.py:284
  65.7 8.8 %collective-permute-start.15 = (f32[64,384]{1,0:T(8,128)S(1)}, f32[64,384]{1,0:T(8,128)S(1)}, u32[]{:S(2)}, u32[]{:S(2)}) collective-permute-start(f32[64,384]{1,0:T(8,128)S(1)} %slice.29), channel_id=1, source_target_pairs={{0,12},{2,14},{4,0},{6,2},{8,4},{10,6},{12,8},{14,10},{1,13},{3,15... | collective-permute-start | bytes 294920 | tf_op jit(solution)/shard_map/ppermute | solution.py:284
  66.0 8.6 %collective-permute-start.16 = (f32[64,384]{1,0:T(8,128)S(1)}, f32[64,384]{1,0:T(8,128)S(1)}, u32[]{:S(2)}, u32[]{:S(2)}) collective-permute-start(f32[64,384]{1,0:T(8,128)S(1)} %get-tuple-element.42), channel_id=1, source_target_pairs={{0,2},{2,4},{4,6},{6,8},{8,10},{10,12},{12,14},{14,0},{1,3},{3,5},... | collective-permute-start | bytes 294920 | tf_op jit(solution)/shard_map/ppermute | solution.py:284
  67.5 7.1 %collective-permute-start.17 = (f32[64,384]{1,0:T(8,128)S(1)}, f32[64,384]{1,0:T(8,128)S(1)}, u32[]{:S(2)}, u32[]{:S(2)}) collective-permute-start(f32[64,384]{1,0:T(8,128)S(1)} %get-tuple-element.43), channel_id=1, source_target_pairs={{0,4},{2,6},{4,8},{6,10},{8,12},{10,14},{12,0},{14,2},{1,5},{3,7},... | collective-permute-start | bytes 294920 | tf_op jit(solution)/shard_map/ppermute | solution.py:284
  75.7 1.5 collective-permute-start.18
  78.4 4.9 %collective-permute-start.19 = (f32[64,384]{1,0:T(8,128)S(1)}, f32[64,384]{1,0:T(8,128)S(1)}, u32[]{:S(2)}, u32[]{:S(2)}) collective-permute-start(f32[64,384]{1,0:T(8,128)S(1)} %slice.30), channel_id=1, source_target_pairs={{0,14},{2,0},{4,2},{6,4},{8,6},{10,8},{12,10},{14,12},{1,15},{3,1}... | collective-permute-start | bytes 294920 | tf_op jit(solution)/shard_map/ppermute | solution.py:284
  80.3 5.9 %collective-permute-start.20 = (f32[64,384]{1,0:T(8,128)S(1)}, f32[64,384]{1,0:T(8,128)S(1)}, u32[]{:S(2)}, u32[]{:S(2)}) collective-permute-start(f32[64,384]{1,0:T(8,128)S(1)} %slice.30), channel_id=1, source_target_pairs={{0,12},{2,14},{4,0},{6,2},{8,4},{10,6},{12,8},{14,10},{1,13},{3,15... | collective-permute-start | bytes 294920 | tf_op jit(solution)/shard_map/ppermute | solution.py:284
  88.9 42.0 %all-reduce.7.cloned.1.call-start = ((), (), s32[]{:S(2)}) async-start(), calls=%async_computation.1 | async-start | bytes 196608 | tf_op jit(solution)/shard_map/psum | solution.py:302
  106.4 48.4 %all-reduce.9.cloned.1.call-start = ((), (), s32[]{:S(2)}) async-start(), calls=%async_computation.2 | async-start | bytes 196608 | tf_op jit(solution)/shard_map/psum | solution.py:302
  130.9 49.6 %all-reduce.11.cloned.1.call-start = ((), (), s32[]{:S(2)}) async-start(), calls=%async_computation.3 | async-start | bytes 196608 | tf_op jit(solution)/shard_map/psum | solution.py:302
  180.5 0.9 copy-start.3
Sparse Core Ops, SparseCore 0:
  89.0 17.3 all-reduce.4
  108.6 22.2 all-reduce.6
  133.2 21.6 all-reduce.8
  157.0 23.4 all-reduce.10

commit v2 on v1

--- a/solution.py
+++ b/solution.py
@@ -44,22 +44,22 @@
     return out
 
 
-def tile_body(keep, own, other, col, high, low, row_sum, col_sum):
-    weight = keep[0].astype(F32)
-    size = own.shape[0]
-    ones = jnp.ones((8, own.shape[1]), BF16)
+def row_squares(rows):
+    row32 = rows.astype(F32)
+    return jnp.sum(row32 * row32, axis=1, keepdims=True)
+
+
+def fill_tile(weight, row_embs, row_sqs, col_emb, high, low, row_sum, col_sum):
+    size, depth = col_emb.shape
+    ones = jnp.ones((8, depth), BF16)
     ones_rows = jnp.ones((8, size), BF16)
-    col_emb = col[...]
     col32 = col_emb.astype(F32)
     sq_high, sq_low = halves(col32 * col32)
     col_sq = (dot(ones, sq_high, 1, 1) + dot(ones, sq_low, 1, 1))[0:1, :]
     total = jnp.zeros((8, size), F32)
-    for half, rows in enumerate((own, other)):
-        row_emb = rows[...]
-        row32 = row_emb.astype(F32)
-        row_sq = jnp.sum(row32 * row32, axis=1, keepdims=True)
-        inner = dot(row_emb, col_emb, 1, 1)
-        tile = jnp.exp(-KERNEL_GAMMA * (row_sq + col_sq - 2.0 * inner)) * weight
+    for half in range(2):
+        inner = dot(row_embs[half], col_emb, 1, 1)
+        tile = jnp.exp(-KERNEL_GAMMA * (row_sqs[half] + col_sq - 2.0 * inner)) * weight
         tile_high, tile_low = halves(tile)
         high[half * size:(half + 1) * size, :] = tile_high
         low[half * size:(half + 1) * size, :] = tile_low
@@ -68,12 +68,35 @@
     col_sum[...] = total
 
 
-def make_tile(keep, own, other, col):
-    rows, depth = own.shape
+def own_body(own, other, high, low, row_sum, col_sum, row_sq):
+    size = own.shape[0]
+    embs = [own[...], other[...]]
+    sqs = [row_squares(emb) for emb in embs]
+    for half in range(2):
+        row_sq[half * size:(half + 1) * size, :] = jnp.broadcast_to(sqs[half], (size, 128))
+    fill_tile(1.0, embs, sqs, embs[0], high, low, row_sum, col_sum)
+
+
+def near_body(count, keep, own, other, row_sq, *refs):
+    size = own.shape[0]
+    sqs = [row_sq[half * size:(half + 1) * size, 0:1] for half in range(2)]
+    col = jnp.concatenate([ref[...] for ref in refs[:count]], axis=0)
+    fill_tile(keep[0].astype(F32), [own[...], other[...]], sqs, col, *refs[count:])
+
+
+def relayed_body(count, keep, odd, own, other, row_sq, direct, *refs):
+    size = own.shape[0]
+    sqs = [row_sq[half * size:(half + 1) * size, 0:1] for half in range(2)]
+    relayed = jnp.concatenate([ref[...] for ref in refs[:count]], axis=0)
+    col = jnp.where(odd[0] > 0, relayed, direct[...])
+    fill_tile(keep[0].astype(F32), [own[...], other[...]], sqs, col, *refs[count:])
+
+
+def make_tile(body, args, rows, depth, smem=(), extra=()):
     return call(
-        tile_body,
-        [((2 * rows, rows), BF16), ((2 * rows, rows), BF16), ((16, rows), F32), ((8, rows), F32)],
-        [keep, own, other, col], smem=(0,),
+        body,
+        [((2 * rows, rows), BF16), ((2 * rows, rows), BF16), ((16, rows), F32), ((8, rows), F32), *extra],
+        args, smem=smem,
         flops=4 * rows * rows * depth, nbytes=6 * rows * depth + 8 * rows * rows,
     )
 
@@ -83,42 +106,55 @@
     return jnp.concatenate([values[middle:], values[:middle]], axis=0)
 
 
-def per_row(values, width):
-    return jnp.concatenate([
-        jnp.broadcast_to(values[0:1, :], (width, values.shape[1])),
-        jnp.broadcast_to(values[8:9, :], (width, values.shape[1])),
-    ], axis=0)
-
-
-def send_ahead(vectors, tiles, outs):
-    width = vectors.shape[0] // 2
-    whole = jnp.concatenate([vectors[:width], vectors[width:]], axis=1)
-    high, low = halves(whole)
+def send_ahead(own, other, tiles, outs):
+    width = own.shape[0]
+    high, low = halves(jnp.concatenate([own, other], axis=1))
     both = jnp.concatenate([high, low], axis=0)
     for (tile_high, tile_low), out in zip(tiles, outs):
         product = dot(both, tile_high[...])
         out[...] = product[:width] + product[width:] + dot(high, tile_low[...])
 
 
-def first_body(sum0, sum1, sum2, other_sum, q0, q1, q2, q3, seed, other_seed, h1, l1, h2, l2,
-               degree_out, vectors_out, ahead1, ahead2):
-    width = seed.shape[0]
-    own_sum = sum0[...] + sum1[...] + sum2[...]
-    degree = own_sum + swapped(other_sum[...])
-    behind = jnp.concatenate([q0[...] + q1[...], q2[...] + q3[...]], axis=0)
-    degree = degree + behind
+def gram_body(values, out):
+    out[...] = dot(values[...], values[...], 1, 1)
+
+
+def start_body(gram, other_gram, seed, other_seed, own_out, other_out):
+    gram = gram[...] + other_gram[...]
+    factor = inverse_factor(0.5 * (gram + gram.T))
+    own_out[...] = dot(factor, seed[...])
+    other_out[...] = dot(factor, other_seed[...])
+
+
+def first_body(sum0, sum1, sum2, other_sum, q0, q1, q2, q3, start, other_start, h1, l1, h2, l2,
+               degree_out, own_out, other_out, ahead1, ahead2):
+    degree = sum0[...] + sum1[...] + sum2[...] + swapped(other_sum[...])
+    degree = degree + jnp.concatenate([q0[...] + q1[...], q2[...] + q3[...]], axis=0)
     degree_out[...] = degree
     scale = lax.rsqrt(degree)
-    vectors = jnp.concatenate([seed[...], other_seed[...]], axis=0) * per_row(scale, width)
-    vectors_out[...] = vectors
-    send_ahead(vectors, ((h1, l1), (h2, l2)), (ahead1, ahead2))
-
-
-def next_body(total, other_total, degree, h1, l1, h2, l2, vectors_out, ahead1, ahead2):
+    own = start[...] * scale[0:1, :]
+    other = other_start[...] * scale[8:9, :]
+    own_out[...] = own
+    other_out[...] = other
+    send_ahead(own, other, ((h1, l1), (h2, l2)), (ahead1, ahead2))
+
+
+def combined(total, other_total, degree):
     width = total.shape[0] // 2
-    vectors = (total[...] + swapped(other_total[...])) / per_row(degree[...], width)
-    vectors_out[...] = vectors
-    send_ahead(vectors, ((h1, l1), (h2, l2)), (ahead1, ahead2))
+    own = (total[:width, :] + other_total[width:, :]) / degree[0:1, :]
+    other = (total[width:, :] + other_total[:width, :]) / degree[8:9, :]
+    return own, other
+
+
+def next_body(total, other_total, degree, h1, l1, h2, l2, own_out, other_out, ahead1, ahead2):
+    own, other = combined(total, other_total, degree)
+    own_out[...] = own
+    other_out[...] = other
+    send_ahead(own, other, ((h1, l1), (h2, l2)), (ahead1, ahead2))
+
+
+def last_body(total, other_total, degree, own_out, other_out):
+    own_out[...], other_out[...] = combined(total, other_total, degree)
 
 
 def product_rows(vectors, tile_high, tile_low):
@@ -129,29 +165,34 @@
     return product[:width] + product[width:] + dot(high, tile_low[...], 1, 1)
 
 
-def block_body(vectors, near1, near2, q1, q2, h0, l0, h1, l1, h2, l2, total):
+def block_body(own, near1, near2, q1, q2, h0, l0, h1, l1, h2, l2, total):
     width, size = near1.shape
-    product = product_rows(vectors[:width, :], h0, l0)
+    product = product_rows(own[...], h0, l0)
     product = product + product_rows(near1[...], h1, l1)
     product = product + product_rows(near2[...], h2, l2)
     total[:width, :] = product[:, :size] + q1[...] + q2[...]
     total[width:, :] = product[:, size:]
 
 
-def moment_body(degree, v0, v1, v2, near1, near2, h0, l0, h1, l1, h2, l2, moments, scaled):
-    width, size = near1.shape
+def low_body(degree, v0, v1, v2, moments, scaled):
+    width = v0.shape[0]
     root = jnp.sqrt(degree[0:1, :])
-    x0, x1, x2 = v0[:width, :] * root, v1[:width, :] * root, v2[:width, :] * root
+    x0, x1, x2 = v0[...] * root, v1[...] * root, v2[...] * root
     scaled[...] = jnp.concatenate([x0, x1, x2], axis=0)
-    low_order = dot(jnp.concatenate([x0, x1], axis=0), jnp.concatenate([x0, x1], axis=0), 1, 1)
-    high_order = dot(jnp.concatenate([x1, x2], axis=0), x2, 1, 1)
+    left = jnp.concatenate([x0, x1], axis=0)
+    order12 = dot(left, x1, 1, 1)
+    order34 = dot(jnp.concatenate([x1, x2], axis=0), x2, 1, 1)
+    moments[:width, :] = jnp.concatenate([order12[:width], order12[width:]], axis=1)
+    moments[width:, :] = jnp.concatenate([order34[:width], order34[width:]], axis=1)
+
+
+def moment_body(low, own, other, near1, near2, h0, l0, h1, l1, h2, l2, moments):
+    width = own.shape[0]
     last = product_rows(near1[...], h1, l1) + product_rows(near2[...], h2, l2)
-    last = 2.0 * last + product_rows(v2[:width, :], h0, l0)
-    whole = jnp.concatenate([v2[:width, :], v2[width:, :]], axis=1)
-    last = dot(whole, last, 1, 1)
-    moments[0:width, :] = low_order[:width, :]
-    moments[width:2 * width, :] = jnp.concatenate([low_order[width:, width:], high_order[:width]], axis=1)
-    moments[2 * width:, :] = jnp.concatenate([high_order[width:], last], axis=1)
+    last = 2.0 * last + product_rows(own[...], h0, l0)
+    last = dot(jnp.concatenate([own[...], other[...]], axis=1), last, 1, 1)
+    moments[:2 * width, :] = low[...]
+    moments[2 * width:, :] = jnp.concatenate([last[:width // 2], last[width // 2:]], axis=1)
 
 
 def unit(rows, cols):
@@ -204,11 +245,7 @@
     def even(matrix):
         return 0.5 * (matrix + matrix.T)
 
-    base_t = inverse_factor(moments[0])
-    base = base_t.T
-    wide = dot(base_t, jnp.concatenate(moments[1:], axis=1))
-    tall = dot(jnp.concatenate([wide[:, i * n:(i + 1) * n] for i in range(5)], axis=0), base)
-    m = [eye] + [even(tall[i * n:(i + 1) * n]) for i in range(5)]
+    m = [eye] + [even(moment) for moment in moments]
 
     square = dot(m[1], m[1])
     cross = dot(m[1], jnp.concatenate([m[2], square], axis=1))
@@ -266,17 +303,15 @@
     cube = dot(dot(step, step), step)
     power = dot(cube, cube[:, :n])
     norm_t = inverse_factor(even(dot(power, dot(ridged, power), 0, 0)))
-    mixed = dot(basis, dot(power, norm_t, 1, 1)) * math.sqrt(rows)
-    return jnp.concatenate([dot(base, mixed[i * n:(i + 1) * n]) for i in range(3)], axis=0)
-
-
-def dense_body(rows, index, moments, scaled, out):
+    return dot(basis, dot(power, norm_t, 1, 1)) * math.sqrt(rows)
+
+
+def dense_body(rows, index, moments, other_moments, scaled, out):
     n = NVEC
-    packed = moments[...]
-    parts = [packed[i * n:(i + 1) * n, j * n:(j + 1) * n] for i in range(3) for j in range(2)]
-    parts = [0.5 * (part + part.T) for part in parts]
-    coeffs = dense(parts, index[0], rows)
-    out[...] = dot(scaled[...], coeffs, 0, 0)
+    packed = moments[...] + other_moments[...]
+    parts = [packed[i * n:(i + 1) * n, j * n:(j + 1) * n] for i in range(2) for j in range(2)]
+    parts.append(jnp.concatenate([packed[2 * n:, :n], packed[2 * n:, n:]], axis=0))
+    out[...] = dot(dense(parts, index[0], rows), scaled[...], 0, 0)
 
 
 def moved(shard, axis, by):
@@ -293,69 +328,85 @@
     return lax.ppermute(shard, (axis, "narrow"), pairs)
 
 
-def total_over_rows(values):
-    values = lax.psum(values, "narrow")
+def two_terms(values):
     blocks = lax.axis_size("blk")
     span = 1
     while blocks % (2 * span) == 0:
-        groups = [[i, i + span] for i in range(blocks) if i // span % 2 == 0]
-        values = lax.psum(values, "blk", axis_index_groups=groups)
+        other = lax.ppermute(values, "blk", [(i, i ^ span) for i in range(blocks)])
+        values = values + other
         span *= 2
     if span < blocks:
         groups = [list(range(i, blocks, span)) for i in range(span)]
         values = lax.psum(values, "blk", axis_index_groups=groups)
-    return values
+    return values, moved(values, "narrow", 1)
 
 
 def shards(embeddings, pair_mask, shift_index, start_seed):
-    size = embeddings.shape[0]
+    size, depth = embeddings.shape
     blocks = lax.axis_size("blk")
     where = lax.axis_index("blk")
+    chunk = 128 if size % 128 == 0 else size
+    count = size // chunk
     other_emb = moved(embeddings, "narrow", 1)
-    near_emb = [moved(embeddings, "blk", -1), moved(embeddings, "blk", -2)]
+    near2 = [moved(embeddings[i * chunk:(i + 1) * chunk], "blk", -2) for i in range(count)]
     seed = start_seed.astype(F32).T / 1000.0
+    keep = lax.dynamic_slice_in_dim(pair_mask, where, 1, 0)[0]
+    if blocks % 2 == 0:
+        direct = lax.ppermute(embeddings, "blk", [(i, i - 1) for i in range(1, blocks, 2)])
+        relayed = [lax.ppermute(part, "blk", [(i, i + 1) for i in range(0, blocks, 2)]) for part in near2]
+    else:
+        direct, relayed = moved(embeddings, "blk", -1), near2
+    odd = (where % 2 * (blocks % 2 == 0)).astype(jnp.int32).reshape(1)
+
     other_seed = moved(seed, "narrow", 1)
-    keep = lax.dynamic_slice_in_dim(pair_mask, where, 1, 0)[0]
-    flags = [jnp.ones((1,), jnp.int32), keep[0:1], keep[1:2]]
-    tiles, row_sums, col_sums = [], [], []
-    for flag, col in zip(flags, [embeddings] + near_emb):
-        high, low, row_sum, col_sum = make_tile(flag, embeddings, other_emb, col)
-        tiles += [high, low]
-        row_sums.append(row_sum)
-        col_sums.append(col_sum)
-    other_sum = moved(row_sums[0] + row_sums[1] + row_sums[2], "narrow", 1)
-    behind = [moved(col_sums[1], "blk", 1), moved(col_sums[2], "blk", 2),
-              moved_both(col_sums[1], "blk", 1), moved_both(col_sums[2], "blk", 2)]
+    (gram,) = call(gram_body, [((NVEC, NVEC), F32)], [seed], flops=10**7, nbytes=10**5)
+    start, other_start = call(
+        start_body, [((NVEC, size), F32)] * 2, [*two_terms(gram), seed, other_seed], flops=10**9, nbytes=10**6,
+    )
+
+    rows_args = [embeddings, other_emb]
+    h0, l0, rows0, _, row_sq = make_tile(
+        own_body, rows_args, size, depth, extra=(((2 * size, 128), F32),))
+    h2, l2, rows2, cols2 = make_tile(
+        lambda *refs: near_body(count, *refs), [keep[1:2], *rows_args, row_sq, *near2], size, depth, (0,))
+    h1, l1, rows1, cols1 = make_tile(
+        lambda *refs: relayed_body(count, *refs),
+        [keep[0:1], odd, *rows_args, row_sq, direct, *relayed], size, depth, (0, 1))
+    tiles = [h0, l0, h1, l1, h2, l2]
+    other_sum = moved(rows0 + rows1 + rows2, "narrow", 1)
+    behind = [moved(cols1, "blk", 1), moved(cols2, "blk", 2),
+              moved_both(cols1, "blk", 1), moved_both(cols2, "blk", 2)]
     pair_shape = ((2 * NVEC, size), F32)
     half_shape = ((NVEC, size), F32)
     cost = dict(flops=2 * 3 * 128 * 2 * size * 2 * size, nbytes=16 * size * size)
-    degree, vectors, ahead1, ahead2 = call(
-        first_body, [((16, size), F32), pair_shape, half_shape, half_shape],
-        row_sums + [other_sum] + behind + [seed, other_seed] + tiles[2:], **cost,
-    )
-    history = [vectors]
-    for _ in range(2):
-        near1, near2 = moved(vectors[:NVEC], "blk", -1), moved(vectors[:NVEC], "blk", -2)
+    degree, own, other, ahead1, ahead2 = call(
+        first_body, [((16, size), F32)] + [half_shape] * 4,
+        [rows0, rows1, rows2, other_sum] + behind + [start, other_start] + tiles[2:], **cost,
+    )
+    history = [own]
+    for repeat in range(2):
         q1, q2 = moved(ahead1, "blk", 1), moved(ahead2, "blk", 2)
-        (total,) = call(block_body, [pair_shape], [vectors, near1, near2, q1, q2] + tiles, **cost)
+        near = [moved(own, "blk", -1), moved(own, "blk", -2)]
+        (total,) = call(block_body, [pair_shape], [own, *near, q1, q2] + tiles, **cost)
         other_total = moved(total, "narrow", 1)
-        vectors, ahead1, ahead2 = call(
-            next_body, [pair_shape, half_shape, half_shape],
-            [total, other_total, degree] + tiles[2:], **cost,
-        )
-        history.append(vectors)
-    near1, near2 = moved(vectors[:NVEC], "blk", -1), moved(vectors[:NVEC], "blk", -2)
-    moments, scaled = call(
-        moment_body, [((3 * NVEC, 2 * NVEC), F32), ((3 * NVEC, size), F32)],
-        [degree] + history + [near1, near2] + tiles, **cost,
-    )
-    moments = total_over_rows(moments)
+        if repeat == 0:
+            own, other, ahead1, ahead2 = call(
+                next_body, [half_shape] * 4, [total, other_total, degree] + tiles[2:], **cost)
+        else:
+            own, other = call(last_body, [half_shape] * 2, [total, other_total, degree], flops=10**5, nbytes=10**6)
+        history.append(own)
+    near = [moved(own, "blk", -1), moved(own, "blk", -2)]
+    low, scaled = call(
+        low_body, [((2 * NVEC, 2 * NVEC), F32), ((3 * NVEC, size), F32)], [degree] + history,
+        flops=10**8, nbytes=10**6)
+    (moments,) = call(
+        moment_body, [((5 * NVEC // 2, 2 * NVEC), F32)], [low, own, other, *near] + tiles, **cost)
     rows = size * blocks * lax.axis_size("narrow")
     (out,) = call(
-        lambda *refs: dense_body(rows, *refs), [((size, NVEC), F32)],
-        [shift_index, moments, scaled], smem=(0,), flops=10**9, nbytes=10**6,
-    )
-    return out
+        lambda *refs: dense_body(rows, *refs), [half_shape],
+        [shift_index, *two_terms(moments), scaled], smem=(0,), flops=10**9, nbytes=10**6,
+    )
+    return out.T
 
 
 def solution(mesh):

time: 231 us -> 149 us (0.65)
  waiting for transfers between devices: 130 us -> 37.2 us
  starting transfers between devices: 25.2 us -> 51.5 us
  between operations: 13.9 us -> 0.9 us
    psum x4 -> x0, waiting for transfers between devices: 90.6 us -> none  [the longest x3 73.1 us: total_over_rows(): values = lax.psum(values, 'blk', axis_index_groups=groups)]
    ppermute x0 -> x10, starting transfers between devices: none -> 17.9 us  [the longest x6 9.73 us: two_terms(): other = lax.ppermute(values, 'blk', [(i, i ^ span) for i in range(blocks)])]
    ppermute x19 -> x22, waiting for transfers between devices: 38.3 us -> 20.9 us  [moved(): lax.ppermute(shard, axis, [(i, (i + by) % length) for i in range(length)])]
    ppermute x0 -> x10, waiting for transfers between devices: none -> 16.3 us  [the longest x6 15.9 us: two_terms(): other = lax.ppermute(values, 'blk', [(i, i ^ span) for i in range(blocks)])]
    ppermute x19 -> x22, starting transfers between devices: 20.3 us -> 30.4 us  [moved(): lax.ppermute(shard, axis, [(i, (i + by) % length) for i in range(length)])]
    pallas_call x10 -> x13, Pallas kernels: 57.1 us -> 56.8 us  [call(): pl.pallas_call(body, out_shape=[jax.ShapeDtypeStruct(shape, dtype) for sh...]
  transfers between devices with their start and end apart: 25 -> 34, of which waited for: 18 -> 17; matrix products, arithmetic and copies ran while one was open for 1% -> 1% of each run, Pallas kernels for 4% -> 9%
where the time goes in v2:
time: 149 us
  Pallas kernels  56.8 us (38%)
  starting transfers between devices  51.5 us (35%)
  waiting for transfers between devices  37.2 us (25%)
  local copies, waits for them, and re-layouts  1.82 us (1%)
    pallas_call x13, Pallas kernels, call(): pl.pallas_call(body, out_shape=[jax.ShapeDtypeStruct(shape, dtype) for sh...  56.8 us
    ppermute x22, starting transfers between devices, moved(): lax.ppermute(shard, axis, [(i, (i + by) % length) for i in range(length)])  30.4 us
    ppermute x22, waiting for transfers between devices, moved(): lax.ppermute(shard, axis, [(i, (i + by) % length) for i in range(length)])  20.9 us
    ppermute x6, waiting for transfers between devices, two_terms(): other = lax.ppermute(values, 'blk', [(i, i ^ span) for i in range(blocks)])  15.9 us
    ppermute x6, starting transfers between devices, two_terms(): other = lax.ppermute(values, 'blk', [(i, i ^ span) for i in range(blocks)])  9.73 us
    ppermute x3, starting transfers between devices, shards(): lax.ppermute(part, 'blk', [(i, i + 1) for i in range(0, blocks, 2)])  6.93 us
    ppermute x2, starting transfers between devices, moved_both(): return lax.ppermute(shard, (axis, 'narrow'), pairs)  3.2 us
  transfers between devices with their start and end apart: 34, of which 17 were waited for; matrix products, arithmetic and copies ran while one was open for 1% of the time, Pallas kernels for 9%

profile of v2, /device:TPU:0, one launch (start us, length us, event | category | flops | bytes accessed | tf_op | source)
XLA Modules:
  0.0 149.2 jit_solution(14721178586518038580)
XLA Ops:
  0.0 0.9 multiply_bitcast_fusion.values.seed
  1.2 3.0 %collective-permute-start.13 = (f32[64,64]{1,0:T(8,128)S(1)}, f32[64,64]{1,0:T(8,128)S(1)}, u32[]{:S(2)}, u32[]{:S(2)}) collective-permute-start(f32[64,64]{1,0:T(8,128)S(1)} %shard_map.49), channel_id=1, source_target_pairs={{0,2},{2,0},{4,6},{6,4},{8,10},{10,8},{12,14},{14,12},{1,3},{3,1},... | collective-permute-start | bytes 49160 | tf_op jit(solution)/shard_map/ppermute | solution.py:335
  4.2 1.9 %collective-permute-done.13 = f32[64,64]{1,0:T(8,128)S(1)} collective-permute-done((f32[64,64]{1,0:T(8,128)S(1)}, f32[64,64]{1,0:T(8,128)S(1)}, u32[]{:S(2)}, u32[]{:S(2)}) %collective-permute-start.13) | collective-permute-done | bytes 16416 | tf_op jit(solution)/shard_map/ppermute | solution.py:335
  6.1 2.1 %collective-permute-start.14 = (f32[64,64]{1,0:T(8,128)S(1)}, f32[64,64]{1,0:T(8,128)S(1)}, u32[]{:S(2)}, u32[]{:S(2)}) collective-permute-start(f32[64,64]{1,0:T(8,128)S(1)} %add.35), channel_id=1, source_target_pairs={{0,4},{2,6},{4,0},{6,2},{8,12},{10,14},{12,8},{14,10},{1,5},{3,7},... | collective-permute-start | bytes 49160 | tf_op jit(solution)/shard_map/ppermute | solution.py:335
  8.2 1.3 collective-permute-start.1
  9.5 0.6 collective-permute-done.14
  10.1 3.1 %collective-permute-start.15 = (f32[64,64]{1,0:T(8,128)S(1)}, f32[64,64]{1,0:T(8,128)S(1)}, u32[]{:S(2)}, u32[]{:S(2)}) collective-permute-start(f32[64,64]{1,0:T(8,128)S(1)} %add.36), channel_id=1, source_target_pairs={{0,8},{2,10},{4,12},{6,14},{8,0},{10,2},{12,4},{14,6},{1,9},{3,11}... | collective-permute-start | bytes 49160 | tf_op jit(solution)/shard_map/ppermute | solution.py:335
  13.2 1.2 fusion
  14.3 1.4 collective-permute-start.2
  15.9 13.6 %collective-permute-start.6 = (bf16[128,768]{1,0:T(8,128)(2,1)S(1)}, bf16[128,768]{1,0:T(8,128)(2,1)S(1)}, u32[]{:S(2)}, u32[]{:S(2)}) collective-permute-start(bf16[128,768]{1,0:T(8,128)(2,1)S(1)} %get-tuple-element.55), channel_id=1, source_target_pairs={{0,12},{2,14},{4,0},{6,2},{8,4},{10,6},{12,8},{14,10},{1,13},{3,15... | collective-permute-start | bytes 589832 | tf_op jit(solution)/shard_map/ppermute | solution.py:319
  29.5 3.8 %collective-permute-start.3 = (bf16[128,768]{1,0:T(8,128)(2,1)S(1)}, bf16[128,768]{1,0:T(8,128)(2,1)S(1)}, u32[]{:S(2)}, u32[]{:S(2)}) collective-permute-start(bf16[128,768]{1,0:T(8,128)(2,1)S(1)} %collective-permute-done.2.refs_4_), channel_id=1, source_target_pairs={{0,2},{4,6},{8,10},{12,14},{1,3},{5,7},{9,11},{13,15},{16,18},{20,... | collective-permute-start | bytes 589832 | tf_op jit(solution)/shard_map/ppermute | solution.py:356
  33.3 1.3 collective-permute-start.5
  34.6 1.8 %collective-permute-start.7 = (bf16[128,768]{1,0:T(8,128)(2,1)S(1)}, bf16[128,768]{1,0:T(8,128)(2,1)S(1)}, u32[]{:S(2)}, u32[]{:S(2)}) collective-permute-start(bf16[128,768]{1,0:T(8,128)(2,1)S(1)} %collective-permute-done.6.refs_6_), channel_id=1, source_target_pairs={{0,2},{4,6},{8,10},{12,14},{1,3},{5,7},{9,11},{13,15},{16,18},{20,... | collective-permute-start | bytes 589832 | tf_op jit(solution)/shard_map/ppermute | solution.py:356
  37.3 2.6 %shard_map.46 = (bf16[768,384]{1,0:T(8,128)(2,1)S(1)}, bf16[768,384]{1,0:T(8,128)(2,1)S(1)}, f32[16,384]{1,0:T(8,128)S(1)}, f32[8,384]{1,0:T(8,128)}, f32[768,128]{1,0:T(8,128)S(1)}) custom-call(bf16[384,768]{1,0:T(8,128)(2,1)S(1)} %copy-done.1, bf16[384,768]{1,0:T(8,128)(2,1)S(1)} %collective-permute-done.other.refs_3_.refs_2_), custom_call_target="tpu_custom_call" | custom-call | flops 452984832 | bytes 2949120 | tf_op jit(solution)/shard_map/pallas_call | solution.py:36
  40.7 2.6 %shard_map.47 = (bf16[768,384]{1,0:T(8,128)(2,1)S(1)}, bf16[768,384]{1,0:T(8,128)(2,1)S(1)}, f32[16,384]{1,0:T(8,128)S(1)}, f32[8,384]{1,0:T(8,128)S(1)}) custom-call(s32[1]{0:T(128)} %bitcast.refs_0_, s32[1]{0:T(128)} %bitcast.1.refs_1_, bf16[384,768]{1,0:T(8,128)(2,1)S(1)} %copy-done.1, bf16[384,768]{1,0:T(8,128)(2,1)S(1)} %collective-permute-done.other.refs_3_.refs_2_, ...), custom_call_target="tpu_custom_call" | custom-call | flops 452984832 | bytes 2949120 | tf_op jit(solution)/shard_map/pallas_call | solution.py:36
  43.3 2.5 %collective-permute-start.9 = (f32[8,384]{1,0:T(8,128)S(1)}, f32[8,384]{1,0:T(8,128)S(1)}, u32[]{:S(2)}, u32[]{:S(2)}) collective-permute-start(f32[8,384]{1,0:T(8,128)S(1)} %get-tuple-element.34), channel_id=1, source_target_pairs={{0,2},{2,4},{4,6},{6,8},{8,10},{10,12},{12,14},{14,0},{1,3},{3,5},... | collective-permute-start | bytes 36872 | tf_op jit(solution)/shard_map/ppermute | solution.py:319
  45.9 2.7 %shard_map.48 = (bf16[768,384]{1,0:T(8,128)(2,1)S(1)}, bf16[768,384]{1,0:T(8,128)(2,1)S(1)}, f32[16,384]{1,0:T(8,128)S(1)}, f32[8,384]{1,0:T(8,128)S(1)}) custom-call(s32[1]{0:T(128)} %bitcast.2.refs_0_, bf16[384,768]{1,0:T(8,128)(2,1)S(1)} %copy-done.1, bf16[384,768]{1,0:T(8,128)(2,1)S(1)} %collective-permute-done.other.refs_3_.refs_2_, ...), custom_call_target="tpu_custom_call" | custom-call | flops 452984832 | bytes 2949120 | tf_op jit(solution)/shard_map/pallas_call | solution.py:36
  48.6 3.2 %collective-permute-start.12 = (f32[8,384]{1,0:T(8,128)S(1)}, f32[8,384]{1,0:T(8,128)S(1)}, u32[]{:S(2)}, u32[]{:S(2)}) collective-permute-start(f32[8,384]{1,0:T(8,128)S(1)} %get-tuple-element.35), channel_id=1, source_target_pairs={{0,5},{1,4},{2,7},{3,6},{4,9},{5,8},{6,11},{7,10},{8,13},{9,12},{1... | collective-permute-start | bytes 36872 | tf_op jit(solution)/shard_map/ppermute | solution.py:328
  52.4 4.8 %shard_map.50 = (f32[64,384]{1,0:T(8,128)S(1)}, f32[64,384]{1,0:T(8,128)S(1)}) custom-call(f32[64,64]{1,0:T(8,128)S(1)} %add.37.gram, f32[64,64]{1,0:T(8,128)S(1)} %collective-permute-done.16.other_gram, f32[64,384]{1,0:T(8,128)S(1)} %multiply_bitcast_fusion.values.seed, f32[64,384]{1,0:T(8,128)S(1)} %collective-permute-done.17.other_seed), custom_call_target="tpu_custom_call" | custom-call | flops 1000000000 | bytes 1000000 | tf_op jit(solution)/shard_map/pallas_call | solution.py:36
  57.2 1.0 shard_map.51
  58.3 0.9 collective-permute-start.18
  59.1 1.7 %collective-permute-start.19 = (f32[64,384]{1,0:T(8,128)S(1)}, f32[64,384]{1,0:T(8,128)S(1)}, u32[]{:S(2)}, u32[]{:S(2)}) collective-permute-start(f32[64,384]{1,0:T(8,128)S(1)} %get-tuple-element.43.own.v0), channel_id=1, source_target_pairs={{0,12},{2,14},{4,0},{6,2},{8,4},{10,6},{12,8},{14,10},{1,13},{3,15... | collective-permute-start | bytes 294920 | tf_op jit(solution)/shard_map/ppermute | solution.py:319
  60.9 1.4 collective-permute-start.21
  62.3 0.7 collective-permute-done.18.near1
  63.0 5.3 %collective-permute-done.19.near2 = f32[64,384]{1,0:T(8,128)S(1)} collective-permute-done((f32[64,384]{1,0:T(8,128)S(1)}, f32[64,384]{1,0:T(8,128)S(1)}, u32[]{:S(2)}, u32[]{:S(2)}) %collective-permute-start.19) | collective-permute-done | bytes 98336 | tf_op jit(solution)/shard_map/ppermute | solution.py:319
  68.3 0.8 collective-permute-done.20.q1
  69.1 1.2 shard_map.52.total
  70.3 1.4 collective-permute-done.22.other_total
  71.8 1.0 shard_map.53
  72.8 1.7 %collective-permute-start.23 = (f32[64,384]{1,0:T(8,128)S(1)}, f32[64,384]{1,0:T(8,128)S(1)}, u32[]{:S(2)}, u32[]{:S(2)}) collective-permute-start(f32[64,384]{1,0:T(8,128)S(1)} %get-tuple-element.48.own.v1), channel_id=1, source_target_pairs={{0,14},{2,0},{4,2},{6,4},{8,6},{10,8},{12,10},{14,12},{1,15},{3,1}... | collective-permute-start | bytes 294920 | tf_op jit(solution)/shard_map/ppermute | solution.py:319
  74.5 0.7 collective-permute-start.24
  75.2 0.6 collective-permute-start.25
  75.8 1.0 collective-permute-start.26
  76.8 0.8 collective-permute-done.23.near1
  77.7 5.3 %collective-permute-done.24.near2 = f32[64,384]{1,0:T(8,128)S(1)} collective-permute-done((f32[64,384]{1,0:T(8,128)S(1)}, f32[64,384]{1,0:T(8,128)S(1)}, u32[]{:S(2)}, u32[]{:S(2)}) %collective-permute-start.24) | collective-permute-done | bytes 98336 | tf_op jit(solution)/shard_map/ppermute | solution.py:319
  83.3 1.2 shard_map.54.total
  84.5 1.4 collective-permute-done.27.other_total
  86.0 1.8 %collective-permute-start.28 = (f32[64,384]{1,0:T(8,128)S(1)}, f32[64,384]{1,0:T(8,128)S(1)}, u32[]{:S(2)}, u32[]{:S(2)}) collective-permute-start(f32[64,384]{1,0:T(8,128)S(1)} %get-tuple-element.51.v2.own), channel_id=1, source_target_pairs={{0,14},{2,0},{4,2},{6,4},{8,6},{10,8},{12,10},{14,12},{1,15},{3,1}... | collective-permute-start | bytes 294920 | tf_op jit(solution)/shard_map/ppermute | solution.py:319
  87.8 1.4 collective-permute-start.29
  89.8 1.2 collective-permute-done.28.near1
  91.0 3.0 %collective-permute-done.29.near2 = f32[64,384]{1,0:T(8,128)S(1)} collective-permute-done((f32[64,384]{1,0:T(8,128)S(1)}, f32[64,384]{1,0:T(8,128)S(1)}, u32[]{:S(2)}, u32[]{:S(2)}) %collective-permute-start.29) | collective-permute-done | bytes 98336 | tf_op jit(solution)/shard_map/ppermute | solution.py:319
  94.0 1.5 %shard_map.57 = f32[160,128]{1,0:T(8,128)S(1)} custom-call(f32[128,128]{1,0:T(8,128)S(1)} %get-tuple-element.52.low, f32[64,384]{1,0:T(8,128)S(1)} %get-tuple-element.51.v2.own, f32[64,384]{1,0:T(8,128)S(1)} %get-tuple-element.53.other, f32[64,384]{1,0:T(8,128)S(1)} %collective-permute-done.28.near1, f32[64,384]{1,0:T(8,128)S(1)} %collective-permute-done.29.near2, ...), custom_call_target="tpu_custom_call" | custom-call | flops 452984832 | bytes 2359296 | tf_op jit(solution)/shard_map/pallas_call | solution.py:36
  95.8 4.3 %collective-permute-done.30 = f32[160,128]{1,0:T(8,128)S(1)} collective-permute-done((f32[160,128]{1,0:T(8,128)S(1)}, f32[160,128]{1,0:T(8,128)S(1)}, u32[]{:S(2)}, u32[]{:S(2)}) %collective-permute-start.30) | collective-permute-done | bytes 81952 | tf_op jit(solution)/shard_map/ppermute | solution.py:335
  100.1 4.4 %collective-permute-done.31 = f32[160,128]{1,0:T(8,128)S(1)} collective-permute-done((f32[160,128]{1,0:T(8,128)S(1)}, f32[160,128]{1,0:T(8,128)S(1)}, u32[]{:S(2)}, u32[]{:S(2)}) %collective-permute-start.31) | collective-permute-done | bytes 81952 | tf_op jit(solution)/shard_map/ppermute | solution.py:335
  104.6 1.2 collective-permute-start.32
  105.8 4.7 %collective-permute-done.32 = f32[160,128]{1,0:T(8,128)S(1)} collective-permute-done((f32[160,128]{1,0:T(8,128)S(1)}, f32[160,128]{1,0:T(8,128)S(1)}, u32[]{:S(2)}, u32[]{:S(2)}) %collective-permute-start.32) | collective-permute-done | bytes 81952 | tf_op jit(solution)/shard_map/ppermute | solution.py:335
  111.2 0.6 collective-permute-done.33.refs_2_
  111.9 37.4 %shard_map.58 = f32[64,384]{1,0:T(8,128)} custom-call(s32[1]{0:T(128)S(6)} %copy.5.refs_0_, f32[160,128]{1,0:T(8,128)S(1)} %add.40.refs_1_, f32[160,128]{1,0:T(8,128)S(1)} %collective-permute-done.33.refs_2_, f32[192,384]{1,0:T(8,128)S(1)} %get-tuple-element.54.refs_3_), custom_call_target="tpu_custom_call" | custom-call | flops 1000000000 | bytes 1000000 | tf_op jit(solution)/shard_map/pallas_call | solution.py:36
  (48 shorter events, 4.1 us)
Async XLA Ops:
  0.0 36.5 %copy-start = (s32[8,2]{0,1:T(2,128)S(1)}, s32[8,2]{0,1:T(2,128)}, u32[]{:S(2)}) copy-start(s32[8,2]{0,1:T(2,128)} %param.5) | copy-start | bytes 196
  1.2 4.9 %collective-permute-start.13 = (f32[64,64]{1,0:T(8,128)S(1)}, f32[64,64]{1,0:T(8,128)S(1)}, u32[]{:S(2)}, u32[]{:S(2)}) collective-permute-start(f32[64,64]{1,0:T(8,128)S(1)} %shard_map.49), channel_id=1, source_target_pairs={{0,2},{2,0},{4,6},{6,4},{8,10},{10,8},{12,14},{14,12},{1,3},{3,1},... | collective-permute-start | bytes 49160 | tf_op jit(solution)/shard_map/ppermute | solution.py:335
  6.1 4.0 %collective-permute-start.14 = (f32[64,64]{1,0:T(8,128)S(1)}, f32[64,64]{1,0:T(8,128)S(1)}, u32[]{:S(2)}, u32[]{:S(2)}) collective-permute-start(f32[64,64]{1,0:T(8,128)S(1)} %add.35), channel_id=1, source_target_pairs={{0,4},{2,6},{4,0},{6,2},{8,12},{10,14},{12,8},{14,10},{1,5},{3,7},... | collective-permute-start | bytes 49160 | tf_op jit(solution)/shard_map/ppermute | solution.py:335
  8.2 29.0 %collective-permute-start = (bf16[384,768]{1,0:T(8,128)(2,1)}, bf16[384,768]{1,0:T(8,128)(2,1)S(1)}, u32[]{:S(2)}, u32[]{:S(2)}) collective-permute-start(bf16[384,768]{1,0:T(8,128)(2,1)} %refs_1_.1), channel_id=1, source_target_pairs={{0,1},{1,0},{2,3},{3,2},{4,5},{5,4},{6,7},{7,6},{8,9},{9,8},{10,11... | collective-permute-start | bytes 1769480 | tf_op jit(solution)/shard_map/ppermute | solution.py:319
  8.2 32.6 %collective-permute-start.1 = (bf16[384,768]{1,0:T(8,128)(2,1)}, bf16[384,768]{1,0:T(8,128)(2,1)S(1)}, u32[]{:S(2)}, u32[]{:S(2)}) collective-permute-start(bf16[384,768]{1,0:T(8,128)(2,1)} %refs_1_.1), channel_id=1, source_target_pairs={{2,0},{6,4},{10,8},{14,12},{3,1},{7,5},{11,9},{15,13},{18,16},{22,... | collective-permute-start | bytes 1769480 | tf_op jit(solution)/shard_map/ppermute | solution.py:355
  10.1 27.2 %copy-start.1 = (bf16[384,768]{1,0:T(8,128)(2,1)S(1)}, bf16[384,768]{1,0:T(8,128)(2,1)}, u32[]{:S(2)}) copy-start(bf16[384,768]{1,0:T(8,128)(2,1)} %refs_1_.1) | copy-start | bytes 1769476
  10.1 5.8 %collective-permute-start.15 = (f32[64,64]{1,0:T(8,128)S(1)}, f32[64,64]{1,0:T(8,128)S(1)}, u32[]{:S(2)}, u32[]{:S(2)}) collective-permute-start(f32[64,64]{1,0:T(8,128)S(1)} %add.36), channel_id=1, source_target_pairs={{0,8},{2,10},{4,12},{6,14},{8,0},{10,2},{12,4},{14,6},{1,9},{3,11}... | collective-permute-start | bytes 49160 | tf_op jit(solution)/shard_map/ppermute | solution.py:335
  14.3 15.2 %collective-permute-start.2 = (bf16[128,768]{1,0:T(8,128)(2,1)S(1)}, bf16[128,768]{1,0:T(8,128)(2,1)S(1)}, u32[]{:S(2)}, u32[]{:S(2)}) collective-permute-start(bf16[128,768]{1,0:T(8,128)(2,1)S(1)} %get-tuple-element.57), channel_id=1, source_target_pairs={{0,12},{2,14},{4,0},{6,2},{8,4},{10,6},{12,8},{14,10},{1,13},{3,15... | collective-permute-start | bytes 589832 | tf_op jit(solution)/shard_map/ppermute | solution.py:319
  15.7 17.6 %collective-permute-start.4 = (bf16[128,768]{1,0:T(8,128)(2,1)S(1)}, bf16[128,768]{1,0:T(8,128)(2,1)S(1)}, u32[]{:S(2)}, u32[]{:S(2)}) collective-permute-start(bf16[128,768]{1,0:T(8,128)(2,1)S(1)} %get-tuple-element.56), channel_id=1, source_target_pairs={{0,12},{2,14},{4,0},{6,2},{8,4},{10,6},{12,8},{14,10},{1,13},{3,15... | collective-permute-start | bytes 589832 | tf_op jit(solution)/shard_map/ppermute | solution.py:319
  15.9 18.7 %collective-permute-start.6 = (bf16[128,768]{1,0:T(8,128)(2,1)S(1)}, bf16[128,768]{1,0:T(8,128)(2,1)S(1)}, u32[]{:S(2)}, u32[]{:S(2)}) collective-permute-start(bf16[128,768]{1,0:T(8,128)(2,1)S(1)} %get-tuple-element.55), channel_id=1, source_target_pairs={{0,12},{2,14},{4,0},{6,2},{8,4},{10,6},{12,8},{14,10},{1,13},{3,15... | collective-permute-start | bytes 589832 | tf_op jit(solution)/shard_map/ppermute | solution.py:319
  29.5 10.4 %collective-permute-start.3 = (bf16[128,768]{1,0:T(8,128)(2,1)S(1)}, bf16[128,768]{1,0:T(8,128)(2,1)S(1)}, u32[]{:S(2)}, u32[]{:S(2)}) collective-permute-start(bf16[128,768]{1,0:T(8,128)(2,1)S(1)} %collective-permute-done.2.refs_4_), channel_id=1, source_target_pairs={{0,2},{4,6},{8,10},{12,14},{1,3},{5,7},{9,11},{13,15},{16,18},{20,... | collective-permute-start | bytes 589832 | tf_op jit(solution)/shard_map/ppermute | solution.py:356
  33.3 7.1 %collective-permute-start.5 = (bf16[128,768]{1,0:T(8,128)(2,1)S(1)}, bf16[128,768]{1,0:T(8,128)(2,1)S(1)}, u32[]{:S(2)}, u32[]{:S(2)}) collective-permute-start(bf16[128,768]{1,0:T(8,128)(2,1)S(1)} %collective-permute-done.4.refs_5_), channel_id=1, source_target_pairs={{0,2},{4,6},{8,10},{12,14},{1,3},{5,7},{9,11},{13,15},{16,18},{20,... | collective-permute-start | bytes 589832 | tf_op jit(solution)/shard_map/ppermute | solution.py:356
  34.6 6.1 %collective-permute-start.7 = (bf16[128,768]{1,0:T(8,128)(2,1)S(1)}, bf16[128,768]{1,0:T(8,128)(2,1)S(1)}, u32[]{:S(2)}, u32[]{:S(2)}) collective-permute-start(bf16[128,768]{1,0:T(8,128)(2,1)S(1)} %collective-permute-done.6.refs_6_), channel_id=1, source_target_pairs={{0,2},{4,6},{8,10},{12,14},{1,3},{5,7},{9,11},{13,15},{16,18},{20,... | collective-permute-start | bytes 589832 | tf_op jit(solution)/shard_map/ppermute | solution.py:356
  37.2 14.6 %collective-permute-start.17 = (f32[64,384]{1,0:T(8,128)S(1)}, f32[64,384]{1,0:T(8,128)S(1)}, u32[]{:S(2)}, u32[]{:S(2)}) collective-permute-start(f32[64,384]{1,0:T(8,128)S(1)} %multiply_bitcast_fusion.values.seed), channel_id=1, source_target_pairs={{0,1},{1,0},{2,3},{3,2},{4,5},{5,4},{6,7},{7,6},{8,9},{9,8},{10,11... | collective-permute-start | bytes 294920 | tf_op jit(solution)/shard_map/ppermute | solution.py:319
  39.9 8.7 %collective-permute-start.16 = (f32[64,64]{1,0:T(8,128)S(1)}, f32[64,64]{1,0:T(8,128)S(1)}, u32[]{:S(2)}, u32[]{:S(2)}) collective-permute-start(f32[64,64]{1,0:T(8,128)S(1)} %add.37.gram), channel_id=1, source_target_pairs={{0,1},{1,0},{2,3},{3,2},{4,5},{5,4},{6,7},{7,6},{8,9},{9,8},{10,11... | collective-permute-start | bytes 49160 | tf_op jit(solution)/shard_map/ppermute | solution.py:319
  43.3 13.8 %collective-permute-start.11 = (f32[8,384]{1,0:T(8,128)S(1)}, f32[8,384]{1,0:T(8,128)S(1)}, u32[]{:S(2)}, u32[]{:S(2)}) collective-permute-start(f32[8,384]{1,0:T(8,128)S(1)} %get-tuple-element.34), channel_id=1, source_target_pairs={{0,3},{1,2},{2,5},{3,4},{4,7},{5,6},{6,9},{7,8},{8,11},{9,10},{10,... | collective-permute-start | bytes 36872 | tf_op jit(solution)/shard_map/ppermute | solution.py:328
  43.3 13.9 %collective-permute-start.9 = (f32[8,384]{1,0:T(8,128)S(1)}, f32[8,384]{1,0:T(8,128)S(1)}, u32[]{:S(2)}, u32[]{:S(2)}) collective-permute-start(f32[8,384]{1,0:T(8,128)S(1)} %get-tuple-element.34), channel_id=1, source_target_pairs={{0,2},{2,4},{4,6},{6,8},{8,10},{10,12},{12,14},{14,0},{1,3},{3,5},... | collective-permute-start | bytes 36872 | tf_op jit(solution)/shard_map/ppermute | solution.py:319
  48.5 8.7 %collective-permute-start.10 = (f32[8,384]{1,0:T(8,128)S(1)}, f32[8,384]{1,0:T(8,128)S(1)}, u32[]{:S(2)}, u32[]{:S(2)}) collective-permute-start(f32[8,384]{1,0:T(8,128)S(1)} %get-tuple-element.35), channel_id=1, source_target_pairs={{0,4},{2,6},{4,8},{6,10},{8,12},{10,14},{12,0},{14,2},{1,5},{3,7},... | collective-permute-start | bytes 36872 | tf_op jit(solution)/shard_map/ppermute | solution.py:319
  48.6 8.6 %collective-permute-start.12 = (f32[8,384]{1,0:T(8,128)S(1)}, f32[8,384]{1,0:T(8,128)S(1)}, u32[]{:S(2)}, u32[]{:S(2)}) collective-permute-start(f32[8,384]{1,0:T(8,128)S(1)} %get-tuple-element.35), channel_id=1, source_target_pairs={{0,5},{1,4},{2,7},{3,6},{4,9},{5,8},{6,11},{7,10},{8,13},{9,12},{1... | collective-permute-start | bytes 36872 | tf_op jit(solution)/shard_map/ppermute | solution.py:328
  51.8 5.4 %collective-permute-start.8 = (f32[16,384]{1,0:T(8,128)S(1)}, f32[16,384]{1,0:T(8,128)S(1)}, u32[]{:S(2)}, u32[]{:S(2)}) collective-permute-start(f32[16,384]{1,0:T(8,128)S(1)} %add_add_fusion), channel_id=1, source_target_pairs={{0,1},{1,0},{2,3},{3,2},{4,5},{5,4},{6,7},{7,6},{8,9},{9,8},{10,11... | collective-permute-start | bytes 73736 | tf_op jit(solution)/shard_map/ppermute | solution.py:319
  58.3 4.7 %collective-permute-start.18 = (f32[64,384]{1,0:T(8,128)S(1)}, f32[64,384]{1,0:T(8,128)S(1)}, u32[]{:S(2)}, u32[]{:S(2)}) collective-permute-start(f32[64,384]{1,0:T(8,128)S(1)} %get-tuple-element.43.own.v0), channel_id=1, source_target_pairs={{0,14},{2,0},{4,2},{6,4},{8,6},{10,8},{12,10},{14,12},{1,15},{3,1}... | collective-permute-start | bytes 294920 | tf_op jit(solution)/shard_map/ppermute | solution.py:319
  59.1 9.2 %collective-permute-start.19 = (f32[64,384]{1,0:T(8,128)S(1)}, f32[64,384]{1,0:T(8,128)S(1)}, u32[]{:S(2)}, u32[]{:S(2)}) collective-permute-start(f32[64,384]{1,0:T(8,128)S(1)} %get-tuple-element.43.own.v0), channel_id=1, source_target_pairs={{0,12},{2,14},{4,0},{6,2},{8,4},{10,6},{12,8},{14,10},{1,13},{3,15... | collective-permute-start | bytes 294920 | tf_op jit(solution)/shard_map/ppermute | solution.py:319
  60.9 8.2 %collective-permute-start.20 = (f32[64,384]{1,0:T(8,128)S(1)}, f32[64,384]{1,0:T(8,128)S(1)}, u32[]{:S(2)}, u32[]{:S(2)}) collective-permute-start(f32[64,384]{1,0:T(8,128)S(1)} %get-tuple-element.44), channel_id=1, source_target_pairs={{0,2},{2,4},{4,6},{6,8},{8,10},{10,12},{12,14},{14,0},{1,3},{3,5},... | collective-permute-start | bytes 294920 | tf_op jit(solution)/shard_map/ppermute | solution.py:319
  60.9 8.2 %collective-permute-start.21 = (f32[64,384]{1,0:T(8,128)S(1)}, f32[64,384]{1,0:T(8,128)S(1)}, u32[]{:S(2)}, u32[]{:S(2)}) collective-permute-start(f32[64,384]{1,0:T(8,128)S(1)} %get-tuple-element.45), channel_id=1, source_target_pairs={{0,4},{2,6},{4,8},{6,10},{8,12},{10,14},{12,0},{14,2},{1,5},{3,7},... | collective-permute-start | bytes 294920 | tf_op jit(solution)/shard_map/ppermute | solution.py:319
  70.3 1.5 %collective-permute-start.22 = (f32[128,384]{1,0:T(8,128)S(1)}, f32[128,384]{1,0:T(8,128)S(1)}, u32[]{:S(2)}, u32[]{:S(2)}) collective-permute-start(f32[128,384]{1,0:T(8,128)S(1)} %shard_map.52.total), channel_id=1, source_target_pairs={{0,1},{1,0},{2,3},{3,2},{4,5},{5,4},{6,7},{7,6},{8,9},{9,8},{10,11... | collective-permute-start | bytes 589832 | tf_op jit(solution)/shard_map/ppermute | solution.py:319
  72.8 4.9 %collective-permute-start.23 = (f32[64,384]{1,0:T(8,128)S(1)}, f32[64,384]{1,0:T(8,128)S(1)}, u32[]{:S(2)}, u32[]{:S(2)}) collective-permute-start(f32[64,384]{1,0:T(8,128)S(1)} %get-tuple-element.48.own.v1), channel_id=1, source_target_pairs={{0,14},{2,0},{4,2},{6,4},{8,6},{10,8},{12,10},{14,12},{1,15},{3,1}... | collective-permute-start | bytes 294920 | tf_op jit(solution)/shard_map/ppermute | solution.py:319
  74.5 8.4 %collective-permute-start.24 = (f32[64,384]{1,0:T(8,128)S(1)}, f32[64,384]{1,0:T(8,128)S(1)}, u32[]{:S(2)}, u32[]{:S(2)}) collective-permute-start(f32[64,384]{1,0:T(8,128)S(1)} %get-tuple-element.48.own.v1), channel_id=1, source_target_pairs={{0,12},{2,14},{4,0},{6,2},{8,4},{10,6},{12,8},{14,10},{1,13},{3,15... | collective-permute-start | bytes 294920 | tf_op jit(solution)/shard_map/ppermute | solution.py:319
  75.2 8.0 %collective-permute-start.25 = (f32[64,384]{1,0:T(8,128)S(1)}, f32[64,384]{1,0:T(8,128)S(1)}, u32[]{:S(2)}, u32[]{:S(2)}) collective-permute-start(f32[64,384]{1,0:T(8,128)S(1)} %get-tuple-element.49), channel_id=1, source_target_pairs={{0,2},{2,4},{4,6},{6,8},{8,10},{10,12},{12,14},{14,0},{1,3},{3,5},... | collective-permute-start | bytes 294920 | tf_op jit(solution)/shard_map/ppermute | solution.py:319
  75.8 7.4 %collective-permute-start.26 = (f32[64,384]{1,0:T(8,128)S(1)}, f32[64,384]{1,0:T(8,128)S(1)}, u32[]{:S(2)}, u32[]{:S(2)}) collective-permute-start(f32[64,384]{1,0:T(8,128)S(1)} %get-tuple-element.50), channel_id=1, source_target_pairs={{0,4},{2,6},{4,8},{6,10},{8,12},{10,14},{12,0},{14,2},{1,5},{3,7},... | collective-permute-start | bytes 294920 | tf_op jit(solution)/shard_map/ppermute | solution.py:319
  84.4 1.5 %collective-permute-start.27 = (f32[128,384]{1,0:T(8,128)S(1)}, f32[128,384]{1,0:T(8,128)S(1)}, u32[]{:S(2)}, u32[]{:S(2)}) collective-permute-start(f32[128,384]{1,0:T(8,128)S(1)} %shard_map.54.total), channel_id=1, source_target_pairs={{0,1},{1,0},{2,3},{3,2},{4,5},{5,4},{6,7},{7,6},{8,9},{9,8},{10,11... | collective-permute-start | bytes 589832 | tf_op jit(solution)/shard_map/ppermute | solution.py:319
  86.0 5.0 %collective-permute-start.28 = (f32[64,384]{1,0:T(8,128)S(1)}, f32[64,384]{1,0:T(8,128)S(1)}, u32[]{:S(2)}, u32[]{:S(2)}) collective-permute-start(f32[64,384]{1,0:T(8,128)S(1)} %get-tuple-element.51.v2.own), channel_id=1, source_target_pairs={{0,14},{2,0},{4,2},{6,4},{8,6},{10,8},{12,10},{14,12},{1,15},{3,1}... | collective-permute-start | bytes 294920 | tf_op jit(solution)/shard_map/ppermute | solution.py:319
  87.8 6.2 %collective-permute-start.29 = (f32[64,384]{1,0:T(8,128)S(1)}, f32[64,384]{1,0:T(8,128)S(1)}, u32[]{:S(2)}, u32[]{:S(2)}) collective-permute-start(f32[64,384]{1,0:T(8,128)S(1)} %get-tuple-element.51.v2.own), channel_id=1, source_target_pairs={{0,12},{2,14},{4,0},{6,2},{8,4},{10,6},{12,8},{14,10},{1,13},{3,15... | collective-permute-start | bytes 294920 | tf_op jit(solution)/shard_map/ppermute | solution.py:319
  95.5 4.5 %collective-permute-start.30 = (f32[160,128]{1,0:T(8,128)S(1)}, f32[160,128]{1,0:T(8,128)S(1)}, u32[]{:S(2)}, u32[]{:S(2)}) collective-permute-start(f32[160,128]{1,0:T(8,128)S(1)} %shard_map.57), channel_id=1, source_target_pairs={{0,2},{2,0},{4,6},{6,4},{8,10},{10,8},{12,14},{14,12},{1,3},{3,1},... | collective-permute-start | bytes 245768 | tf_op jit(solution)/shard_map/ppermute | solution.py:335
  100.1 4.5 %collective-permute-start.31 = (f32[160,128]{1,0:T(8,128)S(1)}, f32[160,128]{1,0:T(8,128)S(1)}, u32[]{:S(2)}, u32[]{:S(2)}) collective-permute-start(f32[160,128]{1,0:T(8,128)S(1)} %add.38), channel_id=1, source_target_pairs={{0,4},{2,6},{4,0},{6,2},{8,12},{10,14},{12,8},{14,10},{1,5},{3,7},... | collective-permute-start | bytes 245768 | tf_op jit(solution)/shard_map/ppermute | solution.py:335
  104.6 5.9 %collective-permute-start.32 = (f32[160,128]{1,0:T(8,128)S(1)}, f32[160,128]{1,0:T(8,128)S(1)}, u32[]{:S(2)}, u32[]{:S(2)}) collective-permute-start(f32[160,128]{1,0:T(8,128)S(1)} %add.39), channel_id=1, source_target_pairs={{0,8},{2,10},{4,12},{6,14},{8,0},{10,2},{12,4},{14,6},{1,9},{3,11}... | collective-permute-start | bytes 245768 | tf_op jit(solution)/shard_map/ppermute | solution.py:335
  110.5 1.3 collective-permute-start.33

commit v3 on v2

--- a/solution.py
+++ b/solution.py
@@ -115,17 +115,6 @@
         out[...] = product[:width] + product[width:] + dot(high, tile_low[...])
 
 
-def gram_body(values, out):
-    out[...] = dot(values[...], values[...], 1, 1)
-
-
-def start_body(gram, other_gram, seed, other_seed, own_out, other_out):
-    gram = gram[...] + other_gram[...]
-    factor = inverse_factor(0.5 * (gram + gram.T))
-    own_out[...] = dot(factor, seed[...])
-    other_out[...] = dot(factor, other_seed[...])
-
-
 def first_body(sum0, sum1, sum2, other_sum, q0, q1, q2, q3, start, other_start, h1, l1, h2, l2,
                degree_out, own_out, other_out, ahead1, ahead2):
     degree = sum0[...] + sum1[...] + sum2[...] + swapped(other_sum[...])
@@ -180,10 +169,11 @@
     x0, x1, x2 = v0[...] * root, v1[...] * root, v2[...] * root
     scaled[...] = jnp.concatenate([x0, x1, x2], axis=0)
     left = jnp.concatenate([x0, x1], axis=0)
-    order12 = dot(left, x1, 1, 1)
+    order012 = dot(left, left, 1, 1)
     order34 = dot(jnp.concatenate([x1, x2], axis=0), x2, 1, 1)
-    moments[:width, :] = jnp.concatenate([order12[:width], order12[width:]], axis=1)
-    moments[width:, :] = jnp.concatenate([order34[:width], order34[width:]], axis=1)
+    moments[:width, :] = order012[:width]
+    moments[width:2 * width, :] = jnp.concatenate([order012[width:, width:], order34[:width]], axis=1)
+    moments[2 * width:, :] = jnp.concatenate([order34[width:], order34[width:]], axis=1)
 
 
 def moment_body(low, own, other, near1, near2, h0, l0, h1, l1, h2, l2, moments):
@@ -191,13 +181,21 @@
     last = product_rows(near1[...], h1, l1) + product_rows(near2[...], h2, l2)
     last = 2.0 * last + product_rows(own[...], h0, l0)
     last = dot(jnp.concatenate([own[...], other[...]], axis=1), last, 1, 1)
-    moments[:2 * width, :] = low[...]
-    moments[2 * width:, :] = jnp.concatenate([last[:width // 2], last[width // 2:]], axis=1)
+    moments[:2 * width, :] = low[:2 * width, :]
+    moments[2 * width:, :] = jnp.concatenate([low[2 * width:, :width], last], axis=1)
 
 
 def unit(rows, cols):
     return (lax.broadcasted_iota(jnp.int32, (rows, cols), 0)
             == lax.broadcasted_iota(jnp.int32, (rows, cols), 1)).astype(F32)
+
+
+def lane(values, k):
+    return jnp.take_along_axis(values, jnp.full(values.shape, k, jnp.int32), axis=1, mode="promise_in_bounds")
+
+
+def sublane(values, k):
+    return jnp.broadcast_to(values[k:k + 1, :], values.shape)
 
 
 def inverse_factor(matrix):
@@ -205,31 +203,48 @@
     work = jnp.concatenate([matrix, unit(size, size)], axis=1)
     blocks = [work[8 * i:8 * i + 8, :] for i in range(size // 8)]
     place = lax.broadcasted_iota(jnp.int32, (8, 2 * size), 0)
-    shape = (8, 2 * size)
-    for k in range(0, size, 2):
+    done = [None] * (size // 8)
+    for k in range(0, size, 4):
         top, r = divmod(k, 8)
         pivot = blocks[top]
-        row0 = jnp.broadcast_to(pivot[r:r + 1, :], shape)
-        row1 = jnp.broadcast_to(pivot[r + 1:r + 2, :], shape)
-        a = jnp.broadcast_to(row0[:, k:k + 1], shape)
-        b = jnp.broadcast_to(row0[:, k + 1:k + 2], shape)
-        d = jnp.broadcast_to(row1[:, k + 1:k + 2], shape)
-        inv_a = 1.0 / a
-        inv_d = a / (a * d - b * b)
-        ratio = b * inv_a
-        row1 = row1 - ratio * row0
+        cols = [lane(pivot, k + j) for j in range(4)]
+        u0, u1, u2, u3 = (sublane(pivot, r + j) for j in range(4))
+        a00, a10, a20, a30 = (sublane(cols[0], r + j) for j in range(4))
+        a11, a21, a31 = (sublane(cols[1], r + j) for j in range(1, 4))
+        a22, a32 = (sublane(cols[2], r + j) for j in range(2, 4))
+        a33 = sublane(cols[3], r + 3)
+        det_a = a00 * a11 - a10 * a10
+        inv_a = 1.0 / det_a
+        p00, p10, p11 = a11 * inv_a, a10 * inv_a, a00 * inv_a
+        b00, b01 = a20 * p00 - a21 * p10, a21 * p11 - a20 * p10
+        b10, b11 = a30 * p00 - a31 * p10, a31 * p11 - a30 * p10
+        s00 = a22 - b00 * a20 - b01 * a21
+        s10 = a32 - b10 * a20 - b11 * a21
+        s11 = a33 - b10 * a30 - b11 * a31
+        det_s = s00 * s11 - s10 * s10
+        inv_s = 1.0 / det_s
+        u2 = u2 - b00 * u0 - b01 * u1
+        u3 = u3 - b10 * u0 - b11 * u1
+        t2 = (s11 * u2 - s10 * u3) * inv_s
+        t3 = (s00 * u3 - s10 * u2) * inv_s
+        t0 = (p00 * u0 - p10 * u1) - b00 * t2 - b10 * t3
+        t1 = (p11 * u1 - p10 * u0) - b01 * t2 - b11 * t3
         for i in range(top, size // 8):
-            c0 = jnp.broadcast_to(blocks[i][:, k:k + 1], shape)
-            c1 = jnp.broadcast_to(blocks[i][:, k + 1:k + 2], shape)
-            f0 = c0 * inv_a
-            f1 = (c1 - c0 * ratio) * inv_d
             if i == top:
-                f0 = jnp.where(place > r, f0, 0.0)
-                f1 = jnp.where(place > r + 1, f1, 0.0)
-            blocks[i] = blocks[i] - f0 * row0 - f1 * row1
-    work = jnp.concatenate(blocks, axis=0)
-    diagonal = jnp.sum(work[:, :size] * unit(size, size), axis=1, keepdims=True)
-    return work[:, size:] * lax.rsqrt(diagonal)
+                if r:
+                    continue
+                c = cols
+            else:
+                c = [lane(blocks[i], k + j) for j in range(4)]
+            change = (c[0] * t0 + c[1] * t1) + (c[2] * t2 + c[3] * t3)
+            blocks[i] = blocks[i] - (jnp.where(place > 3, change, 0.0) if i == top else change)
+        v0 = u0 * lax.rsqrt(a00)
+        v1 = (a00 * u1 - a10 * u0) * lax.rsqrt(a00 * det_a)
+        v2 = u2 * lax.rsqrt(s00)
+        v3 = (s00 * u3 - s10 * u2) * lax.rsqrt(s00 * det_s)
+        four = jnp.where(place % 4 == 0, v0, jnp.where(place % 4 == 1, v1, jnp.where(place % 4 == 2, v2, v3)))
+        done[top] = jnp.where(place > 3, four, done[top]) if r else four
+    return jnp.concatenate(done, axis=0)[:, size:]
 
 
 def trace(matrix):
@@ -245,7 +260,11 @@
     def even(matrix):
         return 0.5 * (matrix + matrix.T)
 
-    m = [eye] + [even(moment) for moment in moments]
+    base_t = inverse_factor(moments[0])
+    base = base_t.T
+    wide = dot(base_t, jnp.concatenate(moments[1:], axis=1))
+    tall = dot(jnp.concatenate([wide[:, i * n:(i + 1) * n] for i in range(5)], axis=0), base)
+    m = [eye] + [even(tall[i * n:(i + 1) * n]) for i in range(5)]
 
     square = dot(m[1], m[1])
     cross = dot(m[1], jnp.concatenate([m[2], square], axis=1))
@@ -303,14 +322,15 @@
     cube = dot(dot(step, step), step)
     power = dot(cube, cube[:, :n])
     norm_t = inverse_factor(even(dot(power, dot(ridged, power), 0, 0)))
-    return dot(basis, dot(power, norm_t, 1, 1)) * math.sqrt(rows)
+    mixed = dot(basis, dot(power, norm_t, 1, 1)) * math.sqrt(rows)
+    return jnp.concatenate([dot(base, mixed[i * n:(i + 1) * n]) for i in range(3)], axis=0)
 
 
 def dense_body(rows, index, moments, other_moments, scaled, out):
     n = NVEC
     packed = moments[...] + other_moments[...]
-    parts = [packed[i * n:(i + 1) * n, j * n:(j + 1) * n] for i in range(2) for j in range(2)]
-    parts.append(jnp.concatenate([packed[2 * n:, :n], packed[2 * n:, n:]], axis=0))
+    parts = [packed[i * n:(i + 1) * n, j * n:(j + 1) * n] for i in range(3) for j in range(2)]
+    parts = [0.5 * (part + part.T) for part in parts]
     out[...] = dot(dense(parts, index[0], rows), scaled[...], 0, 0)
 
 
@@ -359,11 +379,6 @@
     odd = (where % 2 * (blocks % 2 == 0)).astype(jnp.int32).reshape(1)
 
     other_seed = moved(seed, "narrow", 1)
-    (gram,) = call(gram_body, [((NVEC, NVEC), F32)], [seed], flops=10**7, nbytes=10**5)
-    start, other_start = call(
-        start_body, [((NVEC, size), F32)] * 2, [*two_terms(gram), seed, other_seed], flops=10**9, nbytes=10**6,
-    )
-
     rows_args = [embeddings, other_emb]
     h0, l0, rows0, _, row_sq = make_tile(
         own_body, rows_args, size, depth, extra=(((2 * size, 128), F32),))
@@ -381,7 +396,7 @@
     cost = dict(flops=2 * 3 * 128 * 2 * size * 2 * size, nbytes=16 * size * size)
     degree, own, other, ahead1, ahead2 = call(
         first_body, [((16, size), F32)] + [half_shape] * 4,
-        [rows0, rows1, rows2, other_sum] + behind + [start, other_start] + tiles[2:], **cost,
+        [rows0, rows1, rows2, other_sum] + behind + [seed, other_seed] + tiles[2:], **cost,
     )
     history = [own]
     for repeat in range(2):
@@ -397,10 +412,10 @@
         history.append(own)
     near = [moved(own, "blk", -1), moved(own, "blk", -2)]
     low, scaled = call(
-        low_body, [((2 * NVEC, 2 * NVEC), F32), ((3 * NVEC, size), F32)], [degree] + history,
+        low_body, [((3 * NVEC, 2 * NVEC), F32), ((3 * NVEC, size), F32)], [degree] + history,
         flops=10**8, nbytes=10**6)
     (moments,) = call(
-        moment_body, [((5 * NVEC // 2, 2 * NVEC), F32)], [low, own, other, *near] + tiles, **cost)
+        moment_body, [((3 * NVEC, 2 * NVEC), F32)], [low, own, other, *near] + tiles, **cost)
     rows = size * blocks * lax.axis_size("narrow")
     (out,) = call(
         lambda *refs: dense_body(rows, *refs), [half_shape],

time: 149 us -> 124 us (0.83)
  Pallas kernels: 56.8 us -> 40.1 us
  starting transfers between devices: 51.5 us -> 39 us
  waiting for transfers between devices: 37.2 us -> 42.2 us
    pallas_call x13 -> x11, Pallas kernels: 56.8 us -> 40.1 us  [call(): pl.pallas_call(body, out_shape=[jax.ShapeDtypeStruct(shape, dtype) for sh...]
    ppermute x22 -> x21, starting transfers between devices: 30.4 us -> 20.9 us  [moved(): lax.ppermute(shard, axis, [(i, (i + by) % length) for i in range(length)])]
    ppermute x6 -> x3, starting transfers between devices: 9.73 us -> 1.57 us  [two_terms(): other = lax.ppermute(values, 'blk', [(i, i ^ span) for i in range(blocks)])]
    ppermute x22 -> x21, waiting for transfers between devices: 20.9 us -> 27 us  [moved(): lax.ppermute(shard, axis, [(i, (i + by) % length) for i in range(length)])]
    ppermute x3, starting transfers between devices: 6.93 us -> 12.1 us  [shards(): lax.ppermute(part, 'blk', [(i, i + 1) for i in range(0, blocks, 2)])]
    ppermute x6 -> x3, waiting for transfers between devices: 15.9 us -> 14.1 us  [two_terms(): other = lax.ppermute(values, 'blk', [(i, i ^ span) for i in range(blocks)])]
  transfers between devices with their start and end apart: 34 -> 30, of which waited for: 17 -> 18; matrix products, arithmetic and copies ran while one was open for 1% -> 1% of each run, Pallas kernels for 9% -> 7%
where the time goes in v3:
time: 124 us
  waiting for transfers between devices  42.2 us (34%)
  Pallas kernels  40.1 us (32%)
  starting transfers between devices  39 us (31%)
  local copies, waits for them, and re-layouts  1.83 us (1%)
    pallas_call x11, Pallas kernels, call(): pl.pallas_call(body, out_shape=[jax.ShapeDtypeStruct(shape, dtype) for sh...  40.1 us
    ppermute x21, waiting for transfers between devices, moved(): lax.ppermute(shard, axis, [(i, (i + by) % length) for i in range(length)])  27 us
    ppermute x21, starting transfers between devices, moved(): lax.ppermute(shard, axis, [(i, (i + by) % length) for i in range(length)])  20.9 us
    ppermute x3, waiting for transfers between devices, two_terms(): other = lax.ppermute(values, 'blk', [(i, i ^ span) for i in range(blocks)])  14.1 us
    ppermute x3, starting transfers between devices, shards(): lax.ppermute(part, 'blk', [(i, i + 1) for i in range(0, blocks, 2)])  12.1 us
    ppermute x2, starting transfers between devices, moved_both(): return lax.ppermute(shard, (axis, 'narrow'), pairs)  3.15 us
  transfers between devices with their start and end apart: 30, of which 18 were waited for; matrix products, arithmetic and copies ran while one was open for 1% of the time, Pallas kernels for 7%

profile of v3, /device:TPU:0, one launch (start us, length us, event | category | flops | bytes accessed | tf_op | source)
XLA Modules:
  0.0 124.0 jit_solution(296018754775583526)
XLA Ops:
  0.0 0.5 collective-permute-start
  0.5 1.3 %collective-permute-start.1 = (bf16[384,768]{1,0:T(8,128)(2,1)}, bf16[384,768]{1,0:T(8,128)(2,1)S(1)}, u32[]{:S(2)}, u32[]{:S(2)}) collective-permute-start(bf16[384,768]{1,0:T(8,128)(2,1)} %refs_1_.1), channel_id=1, source_target_pairs={{2,0},{6,4},{10,8},{14,12},{3,1},{7,5},{11,9},{15,13},{18,16},{22,... | collective-permute-start | bytes 1769480 | tf_op jit(solution)/shard_map/ppermute | solution.py:375
  1.8 1.2 fusion
  2.9 4.8 %collective-permute-start.2 = (bf16[128,768]{1,0:T(8,128)(2,1)S(1)}, bf16[128,768]{1,0:T(8,128)(2,1)S(1)}, u32[]{:S(2)}, u32[]{:S(2)}) collective-permute-start(bf16[128,768]{1,0:T(8,128)(2,1)S(1)} %get-tuple-element.53), channel_id=1, source_target_pairs={{0,12},{2,14},{4,0},{6,2},{8,4},{10,6},{12,8},{14,10},{1,13},{3,15... | collective-permute-start | bytes 589832 | tf_op jit(solution)/shard_map/ppermute | solution.py:339
  8.8 4.2 %collective-permute-done.2.refs_4_ = bf16[128,768]{1,0:T(8,128)(2,1)S(1)} collective-permute-done((bf16[128,768]{1,0:T(8,128)(2,1)S(1)}, bf16[128,768]{1,0:T(8,128)(2,1)S(1)}, u32[]{:S(2)}, u32[]{:S(2)}) %collective-permute-start.2) | collective-permute-done | bytes 196640 | tf_op jit(solution)/shard_map/ppermute | solution.py:339
  13.0 4.6 %collective-permute-start.3 = (bf16[128,768]{1,0:T(8,128)(2,1)S(1)}, bf16[128,768]{1,0:T(8,128)(2,1)S(1)}, u32[]{:S(2)}, u32[]{:S(2)}) collective-permute-start(bf16[128,768]{1,0:T(8,128)(2,1)S(1)} %collective-permute-done.2.refs_4_), channel_id=1, source_target_pairs={{0,2},{4,6},{8,10},{12,14},{1,3},{5,7},{9,11},{13,15},{16,18},{20,... | collective-permute-start | bytes 589832 | tf_op jit(solution)/shard_map/ppermute | solution.py:376
  17.6 4.2 %collective-permute-start.5 = (bf16[128,768]{1,0:T(8,128)(2,1)S(1)}, bf16[128,768]{1,0:T(8,128)(2,1)S(1)}, u32[]{:S(2)}, u32[]{:S(2)}) collective-permute-start(bf16[128,768]{1,0:T(8,128)(2,1)S(1)} %collective-permute-done.4.refs_5_), channel_id=1, source_target_pairs={{0,2},{4,6},{8,10},{12,14},{1,3},{5,7},{9,11},{13,15},{16,18},{20,... | collective-permute-start | bytes 589832 | tf_op jit(solution)/shard_map/ppermute | solution.py:376
  21.9 3.3 %collective-permute-start.7 = (bf16[128,768]{1,0:T(8,128)(2,1)S(1)}, bf16[128,768]{1,0:T(8,128)(2,1)S(1)}, u32[]{:S(2)}, u32[]{:S(2)}) collective-permute-start(bf16[128,768]{1,0:T(8,128)(2,1)S(1)} %collective-permute-done.6.refs_6_), channel_id=1, source_target_pairs={{0,2},{4,6},{8,10},{12,14},{1,3},{5,7},{9,11},{13,15},{16,18},{20,... | collective-permute-start | bytes 589832 | tf_op jit(solution)/shard_map/ppermute | solution.py:376
  25.2 0.6 fusion.1
  25.7 2.6 %shard_map.46 = (bf16[768,384]{1,0:T(8,128)(2,1)S(1)}, bf16[768,384]{1,0:T(8,128)(2,1)S(1)}, f32[16,384]{1,0:T(8,128)S(1)}, f32[8,384]{1,0:T(8,128)}, f32[768,128]{1,0:T(8,128)S(1)}) custom-call(bf16[384,768]{1,0:T(8,128)(2,1)S(1)} %copy-done.1, bf16[384,768]{1,0:T(8,128)(2,1)S(1)} %collective-permute-done.other.refs_3_.refs_2_), custom_call_target="tpu_custom_call" | custom-call | flops 452984832 | bytes 2949120 | tf_op jit(solution)/shard_map/pallas_call | solution.py:36
  28.3 2.6 %shard_map.48 = (bf16[768,384]{1,0:T(8,128)(2,1)S(1)}, bf16[768,384]{1,0:T(8,128)(2,1)S(1)}, f32[16,384]{1,0:T(8,128)S(1)}, f32[8,384]{1,0:T(8,128)S(1)}) custom-call(s32[1]{0:T(128)} %bitcast.2.refs_0_, bf16[384,768]{1,0:T(8,128)(2,1)S(1)} %copy-done.1, bf16[384,768]{1,0:T(8,128)(2,1)S(1)} %collective-permute-done.other.refs_3_.refs_2_, ...), custom_call_target="tpu_custom_call" | custom-call | flops 452984832 | bytes 2949120 | tf_op jit(solution)/shard_map/pallas_call | solution.py:36
  31.0 2.6 %shard_map.47 = (bf16[768,384]{1,0:T(8,128)(2,1)S(1)}, bf16[768,384]{1,0:T(8,128)(2,1)S(1)}, f32[16,384]{1,0:T(8,128)S(1)}, f32[8,384]{1,0:T(8,128)S(1)}) custom-call(s32[1]{0:T(128)} %bitcast.refs_0_, s32[1]{0:T(128)} %bitcast.1.refs_1_, bf16[384,768]{1,0:T(8,128)(2,1)S(1)} %copy-done.1, bf16[384,768]{1,0:T(8,128)(2,1)S(1)} %collective-permute-done.other.refs_3_.refs_2_, ...), custom_call_target="tpu_custom_call" | custom-call | flops 452984832 | bytes 2949120 | tf_op jit(solution)/shard_map/pallas_call | solution.py:36
  33.7 0.6 collective-permute-start.8
  34.5 1.3 %collective-permute-start.9 = (f32[8,384]{1,0:T(8,128)S(1)}, f32[8,384]{1,0:T(8,128)S(1)}, u32[]{:S(2)}, u32[]{:S(2)}) collective-permute-start(f32[8,384]{1,0:T(8,128)S(1)} %get-tuple-element.32), channel_id=1, source_target_pairs={{0,2},{2,4},{4,6},{6,8},{8,10},{10,12},{12,14},{14,0},{1,3},{3,5},... | collective-permute-start | bytes 36872 | tf_op jit(solution)/shard_map/ppermute | solution.py:339
  35.8 1.6 %collective-permute-start.10 = (f32[8,384]{1,0:T(8,128)S(1)}, f32[8,384]{1,0:T(8,128)S(1)}, u32[]{:S(2)}, u32[]{:S(2)}) collective-permute-start(f32[8,384]{1,0:T(8,128)S(1)} %get-tuple-element.33), channel_id=1, source_target_pairs={{0,4},{2,6},{4,8},{6,10},{8,12},{10,14},{12,0},{14,2},{1,5},{3,7},... | collective-permute-start | bytes 36872 | tf_op jit(solution)/shard_map/ppermute | solution.py:339
  37.4 2.9 %collective-permute-start.12 = (f32[8,384]{1,0:T(8,128)S(1)}, f32[8,384]{1,0:T(8,128)S(1)}, u32[]{:S(2)}, u32[]{:S(2)}) collective-permute-start(f32[8,384]{1,0:T(8,128)S(1)} %get-tuple-element.33), channel_id=1, source_target_pairs={{0,5},{1,4},{2,7},{3,6},{4,9},{5,8},{6,11},{7,10},{8,13},{9,12},{1... | collective-permute-start | bytes 36872 | tf_op jit(solution)/shard_map/ppermute | solution.py:348
  40.3 0.6 collective-permute-done.9.q0
  41.3 1.1 collective-permute-done.12.q3
  42.4 1.0 shard_map.49
  43.4 1.1 collective-permute-start.14
  44.5 1.9 %collective-permute-start.15 = (f32[64,384]{1,0:T(8,128)S(1)}, f32[64,384]{1,0:T(8,128)S(1)}, u32[]{:S(2)}, u32[]{:S(2)}) collective-permute-start(f32[64,384]{1,0:T(8,128)S(1)} %get-tuple-element.39.own.v0), channel_id=1, source_target_pairs={{0,12},{2,14},{4,0},{6,2},{8,4},{10,6},{12,8},{14,10},{1,13},{3,15... | collective-permute-start | bytes 294920 | tf_op jit(solution)/shard_map/ppermute | solution.py:339
  46.5 1.0 collective-permute-start.17
  47.5 0.8 collective-permute-done.14.near1
  48.2 1.9 %collective-permute-done.15.near2 = f32[64,384]{1,0:T(8,128)S(1)} collective-permute-done((f32[64,384]{1,0:T(8,128)S(1)}, f32[64,384]{1,0:T(8,128)S(1)}, u32[]{:S(2)}, u32[]{:S(2)}) %collective-permute-start.15) | collective-permute-done | bytes 98336 | tf_op jit(solution)/shard_map/ppermute | solution.py:339
  50.2 4.3 %collective-permute-done.16.q1 = f32[64,384]{1,0:T(8,128)S(1)} collective-permute-done((f32[64,384]{1,0:T(8,128)S(1)}, f32[64,384]{1,0:T(8,128)S(1)}, u32[]{:S(2)}, u32[]{:S(2)}) %collective-permute-start.16) | collective-permute-done | bytes 98336 | tf_op jit(solution)/shard_map/ppermute | solution.py:339
  54.4 1.2 shard_map.50.total
  55.7 1.4 %collective-permute-done.18.other_total = f32[128,384]{1,0:T(8,128)S(1)} collective-permute-done((f32[128,384]{1,0:T(8,128)S(1)}, f32[128,384]{1,0:T(8,128)S(1)}, u32[]{:S(2)}, u32[]{:S(2)}) %collective-permute-start.18) | collective-permute-done | bytes 196640 | tf_op jit(solution)/shard_map/ppermute | solution.py:339
  57.1 1.0 shard_map.51
  58.1 2.0 %collective-permute-start.19 = (f32[64,384]{1,0:T(8,128)S(1)}, f32[64,384]{1,0:T(8,128)S(1)}, u32[]{:S(2)}, u32[]{:S(2)}) collective-permute-start(f32[64,384]{1,0:T(8,128)S(1)} %get-tuple-element.44.own.v1), channel_id=1, source_target_pairs={{0,14},{2,0},{4,2},{6,4},{8,6},{10,8},{12,10},{14,12},{1,15},{3,1}... | collective-permute-start | bytes 294920 | tf_op jit(solution)/shard_map/ppermute | solution.py:339
  60.1 0.5 collective-permute-start.20
  61.1 1.1 collective-permute-start.22
  62.2 1.2 collective-permute-done.19.near1
  63.4 4.9 %collective-permute-done.20.near2 = f32[64,384]{1,0:T(8,128)S(1)} collective-permute-done((f32[64,384]{1,0:T(8,128)S(1)}, f32[64,384]{1,0:T(8,128)S(1)}, u32[]{:S(2)}, u32[]{:S(2)}) %collective-permute-start.20) | collective-permute-done | bytes 98336 | tf_op jit(solution)/shard_map/ppermute | solution.py:339
  68.3 0.5 collective-permute-done.21.q1
  68.9 1.2 shard_map.52.total
  70.1 1.4 %collective-permute-done.23.other_total = f32[128,384]{1,0:T(8,128)S(1)} collective-permute-done((f32[128,384]{1,0:T(8,128)S(1)}, f32[128,384]{1,0:T(8,128)S(1)}, u32[]{:S(2)}, u32[]{:S(2)}) %collective-permute-start.23) | collective-permute-done | bytes 196640 | tf_op jit(solution)/shard_map/ppermute | solution.py:339
  71.6 1.9 %collective-permute-start.24 = (f32[64,384]{1,0:T(8,128)S(1)}, f32[64,384]{1,0:T(8,128)S(1)}, u32[]{:S(2)}, u32[]{:S(2)}) collective-permute-start(f32[64,384]{1,0:T(8,128)S(1)} %get-tuple-element.47.v2.own), channel_id=1, source_target_pairs={{0,14},{2,0},{4,2},{6,4},{8,6},{10,8},{12,10},{14,12},{1,15},{3,1}... | collective-permute-start | bytes 294920 | tf_op jit(solution)/shard_map/ppermute | solution.py:339
  73.5 1.0 collective-permute-start.25
  74.5 0.6 shard_map.54
  75.1 1.6 %collective-permute-done.24.near1 = f32[64,384]{1,0:T(8,128)S(1)} collective-permute-done((f32[64,384]{1,0:T(8,128)S(1)}, f32[64,384]{1,0:T(8,128)S(1)}, u32[]{:S(2)}, u32[]{:S(2)}) %collective-permute-start.24) | collective-permute-done | bytes 98336 | tf_op jit(solution)/shard_map/ppermute | solution.py:339
  76.7 3.0 %collective-permute-done.25.near2 = f32[64,384]{1,0:T(8,128)S(1)} collective-permute-done((f32[64,384]{1,0:T(8,128)S(1)}, f32[64,384]{1,0:T(8,128)S(1)}, u32[]{:S(2)}, u32[]{:S(2)}) %collective-permute-start.25) | collective-permute-done | bytes 98336 | tf_op jit(solution)/shard_map/ppermute | solution.py:339
  79.6 1.6 %shard_map.55 = f32[192,128]{1,0:T(8,128)S(1)} custom-call(f32[192,128]{1,0:T(8,128)S(1)} %get-tuple-element.48.low, f32[64,384]{1,0:T(8,128)S(1)} %get-tuple-element.47.v2.own, f32[64,384]{1,0:T(8,128)S(1)} %get-tuple-element.49.other, f32[64,384]{1,0:T(8,128)S(1)} %collective-permute-done.24.near1, f32[64,384]{1,0:T(8,128)S(1)} %collective-permute-done.25.near2, ...), custom_call_target="tpu_custom_call" | custom-call | flops 452984832 | bytes 2359296 | tf_op jit(solution)/shard_map/pallas_call | solution.py:36
  81.4 4.5 %collective-permute-done.26 = f32[192,128]{1,0:T(8,128)S(1)} collective-permute-done((f32[192,128]{1,0:T(8,128)S(1)}, f32[192,128]{1,0:T(8,128)S(1)}, u32[]{:S(2)}, u32[]{:S(2)}) %collective-permute-start.26) | collective-permute-done | bytes 98336 | tf_op jit(solution)/shard_map/ppermute | solution.py:355
  86.0 4.6 %collective-permute-done.27 = f32[192,128]{1,0:T(8,128)S(1)} collective-permute-done((f32[192,128]{1,0:T(8,128)S(1)}, f32[192,128]{1,0:T(8,128)S(1)}, u32[]{:S(2)}, u32[]{:S(2)}) %collective-permute-start.27) | collective-permute-done | bytes 98336 | tf_op jit(solution)/shard_map/ppermute | solution.py:355
  90.6 1.3 %collective-permute-start.28 = (f32[192,128]{1,0:T(8,128)S(1)}, f32[192,128]{1,0:T(8,128)S(1)}, u32[]{:S(2)}, u32[]{:S(2)}) collective-permute-start(f32[192,128]{1,0:T(8,128)S(1)} %add.27), channel_id=1, source_target_pairs={{0,8},{2,10},{4,12},{6,14},{8,0},{10,2},{12,4},{14,6},{1,9},{3,11}... | collective-permute-start | bytes 294920 | tf_op jit(solution)/shard_map/ppermute | solution.py:355
  91.9 5.1 %collective-permute-done.28 = f32[192,128]{1,0:T(8,128)S(1)} collective-permute-done((f32[192,128]{1,0:T(8,128)S(1)}, f32[192,128]{1,0:T(8,128)S(1)}, u32[]{:S(2)}, u32[]{:S(2)}) %collective-permute-start.28) | collective-permute-done | bytes 98336 | tf_op jit(solution)/shard_map/ppermute | solution.py:355
  97.7 0.6 collective-permute-done.29.refs_2_
  98.3 25.7 %shard_map.56 = f32[64,384]{1,0:T(8,128)} custom-call(s32[1]{0:T(128)S(6)} %copy.5.refs_0_, f32[192,128]{1,0:T(8,128)S(1)} %add.28.refs_1_, f32[192,128]{1,0:T(8,128)S(1)} %collective-permute-done.29.refs_2_, f32[192,384]{1,0:T(8,128)S(1)} %get-tuple-element.50.refs_3_), custom_call_target="tpu_custom_call" | custom-call | flops 1000000000 | bytes 1000000 | tf_op jit(solution)/shard_map/pallas_call | solution.py:36
  (37 shorter events, 2.7 us)
Async XLA Ops:
  0.0 8.7 %copy-start = (s32[8,2]{0,1:T(2,128)S(1)}, s32[8,2]{0,1:T(2,128)}, u32[]{:S(2)}) copy-start(s32[8,2]{0,1:T(2,128)} %param.5) | copy-start | bytes 196
  0.0 25.7 %copy-start.1 = (bf16[384,768]{1,0:T(8,128)(2,1)S(1)}, bf16[384,768]{1,0:T(8,128)(2,1)}, u32[]{:S(2)}) copy-start(bf16[384,768]{1,0:T(8,128)(2,1)} %refs_1_.1) | copy-start | bytes 1769476
  0.0 25.7 %collective-permute-start = (bf16[384,768]{1,0:T(8,128)(2,1)}, bf16[384,768]{1,0:T(8,128)(2,1)S(1)}, u32[]{:S(2)}, u32[]{:S(2)}) collective-permute-start(bf16[384,768]{1,0:T(8,128)(2,1)} %refs_1_.1), channel_id=1, source_target_pairs={{0,1},{1,0},{2,3},{3,2},{4,5},{5,4},{6,7},{7,6},{8,9},{9,8},{10,11... | collective-permute-start | bytes 1769480 | tf_op jit(solution)/shard_map/ppermute | solution.py:339
  0.5 30.6 %collective-permute-start.1 = (bf16[384,768]{1,0:T(8,128)(2,1)}, bf16[384,768]{1,0:T(8,128)(2,1)S(1)}, u32[]{:S(2)}, u32[]{:S(2)}) collective-permute-start(bf16[384,768]{1,0:T(8,128)(2,1)} %refs_1_.1), channel_id=1, source_target_pairs={{2,0},{6,4},{10,8},{14,12},{3,1},{7,5},{11,9},{15,13},{18,16},{22,... | collective-permute-start | bytes 1769480 | tf_op jit(solution)/shard_map/ppermute | solution.py:375
  1.7 7.0 %copy-start.2 = (s32[384,64]{0,1:T(8,128)S(1)}, s32[384,64]{0,1:T(8,128)}, u32[]{:S(2)}) copy-start(s32[384,64]{0,1:T(8,128)} %param.7) | copy-start | bytes 294916
  2.9 10.1 %collective-permute-start.2 = (bf16[128,768]{1,0:T(8,128)(2,1)S(1)}, bf16[128,768]{1,0:T(8,128)(2,1)S(1)}, u32[]{:S(2)}, u32[]{:S(2)}) collective-permute-start(bf16[128,768]{1,0:T(8,128)(2,1)S(1)} %get-tuple-element.53), channel_id=1, source_target_pairs={{0,12},{2,14},{4,0},{6,2},{8,4},{10,6},{12,8},{14,10},{1,13},{3,15... | collective-permute-start | bytes 589832 | tf_op jit(solution)/shard_map/ppermute | solution.py:339
  7.8 9.9 %collective-permute-start.4 = (bf16[128,768]{1,0:T(8,128)(2,1)S(1)}, bf16[128,768]{1,0:T(8,128)(2,1)S(1)}, u32[]{:S(2)}, u32[]{:S(2)}) collective-permute-start(bf16[128,768]{1,0:T(8,128)(2,1)S(1)} %get-tuple-element.52), channel_id=1, source_target_pairs={{0,12},{2,14},{4,0},{6,2},{8,4},{10,6},{12,8},{14,10},{1,13},{3,15... | collective-permute-start | bytes 589832 | tf_op jit(solution)/shard_map/ppermute | solution.py:339
  8.2 13.6 %collective-permute-start.6 = (bf16[128,768]{1,0:T(8,128)(2,1)S(1)}, bf16[128,768]{1,0:T(8,128)(2,1)S(1)}, u32[]{:S(2)}, u32[]{:S(2)}) collective-permute-start(bf16[128,768]{1,0:T(8,128)(2,1)S(1)} %get-tuple-element.51), channel_id=1, source_target_pairs={{0,12},{2,14},{4,0},{6,2},{8,4},{10,6},{12,8},{14,10},{1,13},{3,15... | collective-permute-start | bytes 589832 | tf_op jit(solution)/shard_map/ppermute | solution.py:339
  13.0 18.0 %collective-permute-start.3 = (bf16[128,768]{1,0:T(8,128)(2,1)S(1)}, bf16[128,768]{1,0:T(8,128)(2,1)S(1)}, u32[]{:S(2)}, u32[]{:S(2)}) collective-permute-start(bf16[128,768]{1,0:T(8,128)(2,1)S(1)} %collective-permute-done.2.refs_4_), channel_id=1, source_target_pairs={{0,2},{4,6},{8,10},{12,14},{1,3},{5,7},{9,11},{13,15},{16,18},{20,... | collective-permute-start | bytes 589832 | tf_op jit(solution)/shard_map/ppermute | solution.py:376
  17.6 13.4 %collective-permute-start.5 = (bf16[128,768]{1,0:T(8,128)(2,1)S(1)}, bf16[128,768]{1,0:T(8,128)(2,1)S(1)}, u32[]{:S(2)}, u32[]{:S(2)}) collective-permute-start(bf16[128,768]{1,0:T(8,128)(2,1)S(1)} %collective-permute-done.4.refs_5_), channel_id=1, source_target_pairs={{0,2},{4,6},{8,10},{12,14},{1,3},{5,7},{9,11},{13,15},{16,18},{20,... | collective-permute-start | bytes 589832 | tf_op jit(solution)/shard_map/ppermute | solution.py:376
  21.9 9.2 %collective-permute-start.7 = (bf16[128,768]{1,0:T(8,128)(2,1)S(1)}, bf16[128,768]{1,0:T(8,128)(2,1)S(1)}, u32[]{:S(2)}, u32[]{:S(2)}) collective-permute-start(bf16[128,768]{1,0:T(8,128)(2,1)S(1)} %collective-permute-done.6.refs_6_), channel_id=1, source_target_pairs={{0,2},{4,6},{8,10},{12,14},{1,3},{5,7},{9,11},{13,15},{16,18},{20,... | collective-permute-start | bytes 589832 | tf_op jit(solution)/shard_map/ppermute | solution.py:376
  25.7 11.7 %collective-permute-start.13 = (f32[64,384]{1,0:T(8,128)S(1)}, f32[64,384]{1,0:T(8,128)S(1)}, u32[]{:S(2)}, u32[]{:S(2)}) collective-permute-start(f32[64,384]{1,0:T(8,128)S(1)} %multiply_bitcast_fusion.start), channel_id=1, source_target_pairs={{0,1},{1,0},{2,3},{3,2},{4,5},{5,4},{6,7},{7,6},{8,9},{9,8},{10,11... | collective-permute-start | bytes 294920 | tf_op jit(solution)/shard_map/ppermute | solution.py:339
  33.7 8.7 %collective-permute-start.8 = (f32[16,384]{1,0:T(8,128)S(1)}, f32[16,384]{1,0:T(8,128)S(1)}, u32[]{:S(2)}, u32[]{:S(2)}) collective-permute-start(f32[16,384]{1,0:T(8,128)S(1)} %add_add_fusion), channel_id=1, source_target_pairs={{0,1},{1,0},{2,3},{3,2},{4,5},{5,4},{6,7},{7,6},{8,9},{9,8},{10,11... | collective-permute-start | bytes 73736 | tf_op jit(solution)/shard_map/ppermute | solution.py:339
  34.2 6.0 %collective-permute-start.11 = (f32[8,384]{1,0:T(8,128)S(1)}, f32[8,384]{1,0:T(8,128)S(1)}, u32[]{:S(2)}, u32[]{:S(2)}) collective-permute-start(f32[8,384]{1,0:T(8,128)S(1)} %get-tuple-element.32), channel_id=1, source_target_pairs={{0,3},{1,2},{2,5},{3,4},{4,7},{5,6},{6,9},{7,8},{8,11},{9,10},{10,... | collective-permute-start | bytes 36872 | tf_op jit(solution)/shard_map/ppermute | solution.py:348
  34.5 6.4 %collective-permute-start.9 = (f32[8,384]{1,0:T(8,128)S(1)}, f32[8,384]{1,0:T(8,128)S(1)}, u32[]{:S(2)}, u32[]{:S(2)}) collective-permute-start(f32[8,384]{1,0:T(8,128)S(1)} %get-tuple-element.32), channel_id=1, source_target_pairs={{0,2},{2,4},{4,6},{6,8},{8,10},{10,12},{12,14},{14,0},{1,3},{3,5},... | collective-permute-start | bytes 36872 | tf_op jit(solution)/shard_map/ppermute | solution.py:339
  35.8 5.5 %collective-permute-start.10 = (f32[8,384]{1,0:T(8,128)S(1)}, f32[8,384]{1,0:T(8,128)S(1)}, u32[]{:S(2)}, u32[]{:S(2)}) collective-permute-start(f32[8,384]{1,0:T(8,128)S(1)} %get-tuple-element.33), channel_id=1, source_target_pairs={{0,4},{2,6},{4,8},{6,10},{8,12},{10,14},{12,0},{14,2},{1,5},{3,7},... | collective-permute-start | bytes 36872 | tf_op jit(solution)/shard_map/ppermute | solution.py:339
  37.4 5.0 %collective-permute-start.12 = (f32[8,384]{1,0:T(8,128)S(1)}, f32[8,384]{1,0:T(8,128)S(1)}, u32[]{:S(2)}, u32[]{:S(2)}) collective-permute-start(f32[8,384]{1,0:T(8,128)S(1)} %get-tuple-element.33), channel_id=1, source_target_pairs={{0,5},{1,4},{2,7},{3,6},{4,9},{5,8},{6,11},{7,10},{8,13},{9,12},{1... | collective-permute-start | bytes 36872 | tf_op jit(solution)/shard_map/ppermute | solution.py:348
  43.4 4.8 %collective-permute-start.14 = (f32[64,384]{1,0:T(8,128)S(1)}, f32[64,384]{1,0:T(8,128)S(1)}, u32[]{:S(2)}, u32[]{:S(2)}) collective-permute-start(f32[64,384]{1,0:T(8,128)S(1)} %get-tuple-element.39.own.v0), channel_id=1, source_target_pairs={{0,14},{2,0},{4,2},{6,4},{8,6},{10,8},{12,10},{14,12},{1,15},{3,1}... | collective-permute-start | bytes 294920 | tf_op jit(solution)/shard_map/ppermute | solution.py:339
  44.5 5.6 %collective-permute-start.15 = (f32[64,384]{1,0:T(8,128)S(1)}, f32[64,384]{1,0:T(8,128)S(1)}, u32[]{:S(2)}, u32[]{:S(2)}) collective-permute-start(f32[64,384]{1,0:T(8,128)S(1)} %get-tuple-element.39.own.v0), channel_id=1, source_target_pairs={{0,12},{2,14},{4,0},{6,2},{8,4},{10,6},{12,8},{14,10},{1,13},{3,15... | collective-permute-start | bytes 294920 | tf_op jit(solution)/shard_map/ppermute | solution.py:339
  46.4 8.0 %collective-permute-start.16 = (f32[64,384]{1,0:T(8,128)S(1)}, f32[64,384]{1,0:T(8,128)S(1)}, u32[]{:S(2)}, u32[]{:S(2)}) collective-permute-start(f32[64,384]{1,0:T(8,128)S(1)} %get-tuple-element.40), channel_id=1, source_target_pairs={{0,2},{2,4},{4,6},{6,8},{8,10},{10,12},{12,14},{14,0},{1,3},{3,5},... | collective-permute-start | bytes 294920 | tf_op jit(solution)/shard_map/ppermute | solution.py:339
  46.5 8.0 %collective-permute-start.17 = (f32[64,384]{1,0:T(8,128)S(1)}, f32[64,384]{1,0:T(8,128)S(1)}, u32[]{:S(2)}, u32[]{:S(2)}) collective-permute-start(f32[64,384]{1,0:T(8,128)S(1)} %get-tuple-element.41), channel_id=1, source_target_pairs={{0,4},{2,6},{4,8},{6,10},{8,12},{10,14},{12,0},{14,2},{1,5},{3,7},... | collective-permute-start | bytes 294920 | tf_op jit(solution)/shard_map/ppermute | solution.py:339
  55.6 1.5 %collective-permute-start.18 = (f32[128,384]{1,0:T(8,128)S(1)}, f32[128,384]{1,0:T(8,128)S(1)}, u32[]{:S(2)}, u32[]{:S(2)}) collective-permute-start(f32[128,384]{1,0:T(8,128)S(1)} %shard_map.50.total), channel_id=1, source_target_pairs={{0,1},{1,0},{2,3},{3,2},{4,5},{5,4},{6,7},{7,6},{8,9},{9,8},{10,11... | collective-permute-start | bytes 589832 | tf_op jit(solution)/shard_map/ppermute | solution.py:339
  58.1 5.2 %collective-permute-start.19 = (f32[64,384]{1,0:T(8,128)S(1)}, f32[64,384]{1,0:T(8,128)S(1)}, u32[]{:S(2)}, u32[]{:S(2)}) collective-permute-start(f32[64,384]{1,0:T(8,128)S(1)} %get-tuple-element.44.own.v1), channel_id=1, source_target_pairs={{0,14},{2,0},{4,2},{6,4},{8,6},{10,8},{12,10},{14,12},{1,15},{3,1}... | collective-permute-start | bytes 294920 | tf_op jit(solution)/shard_map/ppermute | solution.py:339
  60.1 8.2 %collective-permute-start.20 = (f32[64,384]{1,0:T(8,128)S(1)}, f32[64,384]{1,0:T(8,128)S(1)}, u32[]{:S(2)}, u32[]{:S(2)}) collective-permute-start(f32[64,384]{1,0:T(8,128)S(1)} %get-tuple-element.44.own.v1), channel_id=1, source_target_pairs={{0,12},{2,14},{4,0},{6,2},{8,4},{10,6},{12,8},{14,10},{1,13},{3,15... | collective-permute-start | bytes 294920 | tf_op jit(solution)/shard_map/ppermute | solution.py:339
  60.7 8.2 %collective-permute-start.21 = (f32[64,384]{1,0:T(8,128)S(1)}, f32[64,384]{1,0:T(8,128)S(1)}, u32[]{:S(2)}, u32[]{:S(2)}) collective-permute-start(f32[64,384]{1,0:T(8,128)S(1)} %get-tuple-element.45), channel_id=1, source_target_pairs={{0,2},{2,4},{4,6},{6,8},{8,10},{10,12},{12,14},{14,0},{1,3},{3,5},... | collective-permute-start | bytes 294920 | tf_op jit(solution)/shard_map/ppermute | solution.py:339
  61.1 7.8 %collective-permute-start.22 = (f32[64,384]{1,0:T(8,128)S(1)}, f32[64,384]{1,0:T(8,128)S(1)}, u32[]{:S(2)}, u32[]{:S(2)}) collective-permute-start(f32[64,384]{1,0:T(8,128)S(1)} %get-tuple-element.46), channel_id=1, source_target_pairs={{0,4},{2,6},{4,8},{6,10},{8,12},{10,14},{12,0},{14,2},{1,5},{3,7},... | collective-permute-start | bytes 294920 | tf_op jit(solution)/shard_map/ppermute | solution.py:339
  70.0 1.5 %collective-permute-start.23 = (f32[128,384]{1,0:T(8,128)S(1)}, f32[128,384]{1,0:T(8,128)S(1)}, u32[]{:S(2)}, u32[]{:S(2)}) collective-permute-start(f32[128,384]{1,0:T(8,128)S(1)} %shard_map.52.total), channel_id=1, source_target_pairs={{0,1},{1,0},{2,3},{3,2},{4,5},{5,4},{6,7},{7,6},{8,9},{9,8},{10,11... | collective-permute-start | bytes 589832 | tf_op jit(solution)/shard_map/ppermute | solution.py:339
  71.6 5.1 %collective-permute-start.24 = (f32[64,384]{1,0:T(8,128)S(1)}, f32[64,384]{1,0:T(8,128)S(1)}, u32[]{:S(2)}, u32[]{:S(2)}) collective-permute-start(f32[64,384]{1,0:T(8,128)S(1)} %get-tuple-element.47.v2.own), channel_id=1, source_target_pairs={{0,14},{2,0},{4,2},{6,4},{8,6},{10,8},{12,10},{14,12},{1,15},{3,1}... | collective-permute-start | bytes 294920 | tf_op jit(solution)/shard_map/ppermute | solution.py:339
  73.5 6.1 %collective-permute-start.25 = (f32[64,384]{1,0:T(8,128)S(1)}, f32[64,384]{1,0:T(8,128)S(1)}, u32[]{:S(2)}, u32[]{:S(2)}) collective-permute-start(f32[64,384]{1,0:T(8,128)S(1)} %get-tuple-element.47.v2.own), channel_id=1, source_target_pairs={{0,12},{2,14},{4,0},{6,2},{8,4},{10,6},{12,8},{14,10},{1,13},{3,15... | collective-permute-start | bytes 294920 | tf_op jit(solution)/shard_map/ppermute | solution.py:339
  81.2 4.7 %collective-permute-start.26 = (f32[192,128]{1,0:T(8,128)S(1)}, f32[192,128]{1,0:T(8,128)S(1)}, u32[]{:S(2)}, u32[]{:S(2)}) collective-permute-start(f32[192,128]{1,0:T(8,128)S(1)} %shard_map.55), channel_id=1, source_target_pairs={{0,2},{2,0},{4,6},{6,4},{8,10},{10,8},{12,14},{14,12},{1,3},{3,1},... | collective-permute-start | bytes 294920 | tf_op jit(solution)/shard_map/ppermute | solution.py:355
  85.9 4.7 %collective-permute-start.27 = (f32[192,128]{1,0:T(8,128)S(1)}, f32[192,128]{1,0:T(8,128)S(1)}, u32[]{:S(2)}, u32[]{:S(2)}) collective-permute-start(f32[192,128]{1,0:T(8,128)S(1)} %add.26), channel_id=1, source_target_pairs={{0,4},{2,6},{4,0},{6,2},{8,12},{10,14},{12,8},{14,10},{1,5},{3,7},... | collective-permute-start | bytes 294920 | tf_op jit(solution)/shard_map/ppermute | solution.py:355
  90.6 6.3 %collective-permute-start.28 = (f32[192,128]{1,0:T(8,128)S(1)}, f32[192,128]{1,0:T(8,128)S(1)}, u32[]{:S(2)}, u32[]{:S(2)}) collective-permute-start(f32[192,128]{1,0:T(8,128)S(1)} %add.27), channel_id=1, source_target_pairs={{0,8},{2,10},{4,12},{6,14},{8,0},{10,2},{12,4},{14,6},{1,9},{3,11}... | collective-permute-start | bytes 294920 | tf_op jit(solution)/shard_map/ppermute | solution.py:355
  97.0 1.4 %collective-permute-start.29 = (f32[192,128]{1,0:T(8,128)S(1)}, f32[192,128]{1,0:T(8,128)S(1)}, u32[]{:S(2)}, u32[]{:S(2)}) collective-permute-start(f32[192,128]{1,0:T(8,128)S(1)} %add.28.refs_1_), channel_id=1, source_target_pairs={{0,1},{1,0},{2,3},{3,2},{4,5},{5,4},{6,7},{7,6},{8,9},{9,8},{10,11... | collective-permute-start | bytes 294920 | tf_op jit(solution)/shard_map/ppermute | solution.py:339

commit v4 on v3

v4 whole, which is shorter than its diff:
```python
import math

import jax
import jax.numpy as jnp
from jax import lax
from jax.experimental import pallas as pl
from jax.experimental.pallas import tpu as pltpu
from jax.sharding import PartitionSpec as P

KERNEL_GAMMA = 2.0
RIDGE_WEIGHT = 1e-05
NVEC = 64
F32 = jnp.float32
BF16 = jnp.bfloat16
VMEM_LIMIT = 48 * 1024 * 1024


def dot(left, right, left_dim=1, right_dim=0):
    precision = lax.Precision.HIGHEST if left.dtype == F32 else None
    return lax.dot_general(
        left, right, (((left_dim,), (right_dim,)), ((), ())),
        precision=precision, preferred_element_type=F32,
    )


def halves(values):
    high = values.astype(BF16)
    return high, (values - high.astype(F32)).astype(BF16)


def call(body, out_shapes, args, smem=(), flops=0, nbytes=0):
    specs = [
        pl.BlockSpec(memory_space=pltpu.SMEM if i in smem else pltpu.VMEM)
        for i in range(len(args))
    ]
    out = pl.pallas_call(
        body,
        out_shape=[jax.ShapeDtypeStruct(shape, dtype) for shape, dtype in out_shapes],
        in_specs=specs,
        out_specs=[pl.BlockSpec(memory_space=pltpu.VMEM) for _ in out_shapes],
        compiler_params=pltpu.CompilerParams(vmem_limit_bytes=VMEM_LIMIT),
        cost_estimate=pl.CostEstimate(flops=flops, bytes_accessed=nbytes, transcendentals=0),
    )(*args)
    return out


LOG2_E = 1.4426950408889634


def sums_along(values):
    rows, depth = values.shape
    folded = values[:, :128]
    for j in range(128, depth, 128):
        folded = folded + values[:, j:j + 128]
    return dot(jnp.ones((8, 128), F32), folded, 1, 1)


def fill_tile(weight, row_embs, row_sqs, col_emb, high, low, row_sum):
    size = col_emb.shape[0]
    col32 = col_emb.astype(F32)
    col_sq = (2.0 * LOG2_E) * sums_along(col32 * col32)[0:1, :]
    total = jnp.zeros((1, size), F32)
    for half in range(2):
        inner = dot(row_embs[half], col_emb, 1, 1)
        tile = jnp.exp2((4.0 * LOG2_E) * inner - (row_sqs[half] + col_sq)) * weight
        tile_high, tile_low = halves(tile)
        high[half * size:(half + 1) * size, :] = tile_high
        low[half * size:(half + 1) * size, :] = tile_low
        row_sum[half * 8:(half + 1) * 8, :] = row_sum[half * 8:(half + 1) * 8, :] + sums_along(tile)
        total = total + jnp.sum(tile, axis=0, keepdims=True)
    return jnp.broadcast_to(total, (8, size))


def own_body(own, other, high, low, row_sum, row_sq, copy):
    size = own.shape[0]
    embs = [own[...], other[...]]
    copy[...] = embs[0]
    sqs = []
    for half in range(2):
        row32 = embs[half].astype(F32)
        sqs.append((2.0 * LOG2_E) * jnp.sum(row32 * row32, axis=1, keepdims=True))
        row_sq[half * size:(half + 1) * size, :] = jnp.broadcast_to(sqs[half], (size, 128))
    row_sum[...] = jnp.zeros(row_sum.shape, F32)
    fill_tile(1.0, embs, sqs, embs[0], high, low, row_sum)


def stored_squares(row_sq, size):
    return [row_sq[half * size:(half + 1) * size, 0:1] for half in range(2)]


def near_body(count, keep, own, other, row_sq, *refs):
    size = own.shape[0]
    col = jnp.concatenate([ref[...] for ref in refs[:count]], axis=0)
    before, high, low, row_sum, col_sum = refs[count:]
    row_sum[...] = before[...]
    col_sum[...] = fill_tile(keep[0].astype(F32), [own[...], other[...]], stored_squares(row_sq, size),
                             col, high, low, row_sum)


def relayed_body(count, keep, odd, own, other, row_sq, direct, *refs):
    size = own.shape[0]
    relayed = jnp.concatenate([ref[...] for ref in refs[:count]], axis=0)
    col = jnp.where(odd[0] > 0, relayed, direct[...])
    before, behind, high, low, row_sum, col_sum = refs[count:]
    row_sum[:8, :] = before[:8, :] + behind[...]
    row_sum[8:, :] = before[8:, :]
    col_sum[...] = fill_tile(keep[0].astype(F32), [own[...], other[...]], stored_squares(row_sq, size),
                             col, high, low, row_sum)


def make_tile(body, args, rows, smem=(), extra=()):
    return call(
        body, [((2 * rows, rows), BF16), ((2 * rows, rows), BF16), ((16, rows), F32), *extra],
        args, smem=smem, flops=2 * 10**9, nbytes=10**6,
    )


def degree_body(sums, behind, other_sums, seed, other_seed, degree_out, scale_out, own_out, other_out):
    top = sums[:8, :] + behind[...] + other_sums[8:, :]
    bottom = sums[8:, :] + other_sums[:8, :]
    degree_out[:8, :] = top
    degree_out[8:, :] = bottom
    scale = lax.rsqrt(top)
    scale_out[...] = scale
    own_out[...] = seed[...] * scale[0:1, :]
    other_out[...] = other_seed[...] * lax.rsqrt(bottom)[0:1, :]


def ahead_body(own, other, h1, l1, h2, l2, ahead1, ahead2):
    width = own.shape[0]
    high, low = halves(jnp.concatenate([own[...], other[...]], axis=1))
    both = jnp.concatenate([high, low], axis=0)
    for tile_high, tile_low, out in ((h1, l1, ahead1), (h2, l2, ahead2)):
        product = dot(both, tile_high[...])
        out[...] = product[:width] + product[width:] + dot(high, tile_low[...])


def combine_body(total, other_total, degree, own_out, other_out):
    width = total.shape[0] // 2
    own_out[...] = (total[:width, :] + other_total[width:, :]) / degree[0:1, :]
    other_out[...] = (total[width:, :] + other_total[:width, :]) / degree[8:9, :]


def product_rows(vectors, tile_high, tile_low):
    width = vectors.shape[0]
    high, low = halves(vectors)
    both = jnp.concatenate([high, low], axis=0)
    product = dot(both, tile_high[...], 1, 1)
    return product[:width] + product[width:] + dot(high, tile_low[...], 1, 1)


def own_product_body(own, h0, l0, out):
    out[...] = product_rows(own[...], h0, l0)


def add_blocks(product, near1, near2, q1, q2, h1, l1, h2, l2, total):
    width, size = near1.shape
    product = product[...] + product_rows(near1, h1, l1) + product_rows(near2, h2, l2)
    total[:width, :] = product[:, :size] + q1[...] + q2[...]
    total[width:, :] = product[:, size:]


def first_block_body(product, seed1, seed2, scale1, scale2, *refs):
    add_blocks(product, seed1[...] * scale1[0:1, :], seed2[...] * scale2[0:1, :], *refs)


def block_body(product, near1, near2, *refs):
    add_blocks(product, near1[...], near2[...], *refs)


def low_body(degree, v0, v1, v2, moments, scaled):
    width = v0.shape[0]
    root = jnp.sqrt(degree[0:1, :])
    x0, x1, x2 = v0[...] * root, v1[...] * root, v2[...] * root
    scaled[...] = jnp.concatenate([x0, x1, x2], axis=0)
    left = jnp.concatenate([x0, x1], axis=0)
    order012 = dot(left, left, 1, 1)
    order34 = dot(jnp.concatenate([x1, x2], axis=0), x2, 1, 1)
    order = [order012[:width, :width], order012[:width, width:], order012[width:, width:],
             order34[:width], order34[width:]]
    for i in range(5):
        moments[i * width:(i + 1) * width, :] = order[i]


def place_of(rows, cols):
    return [lax.broadcasted_iota(jnp.int32, (rows, cols), axis) for axis in range(2)]


def moment_body(core, low, own, other, product, near1, near2, h1, l1, h2, l2, mine, theirs):
    n = own.shape[0]
    last = product_rows(near1[...], h1, l1) + product_rows(near2[...], h2, l2)
    last = 2.0 * last + product[...]
    last = dot(jnp.concatenate([own[...], other[...]], axis=1), last, 1, 1)
    moments = [low[i * n:(i + 1) * n, :] for i in range(5)] + [0.5 * (last + last.T)]
    row, col = place_of(n, n)
    pieces = []
    for i in range(0, 6, 2):
        pair = jnp.where(row >= col, moments[i], moments[i + 1])
        pieces.append(jnp.concatenate([pair[:n // 2], pair[n // 2:]], axis=1))
    d1, d3, d5 = (jnp.sum(moments[i] * unit(n, n), axis=0, keepdims=True) for i in (1, 3, 5))
    row, _ = place_of(8, 2 * n)
    pieces.append(jnp.where(row == 0, jnp.concatenate([d1, d3], axis=1),
                            jnp.where(row == 1, jnp.concatenate([d5, d5], axis=1), 0.0)))
    pieces.append(jnp.zeros((8, 2 * n), F32))
    packed = jnp.concatenate(pieces, axis=0)
    half = packed.shape[0] // 2
    first = core[0] == 0
    mine[...] = jnp.where(first, packed[:half], packed[half:])
    theirs[...] = jnp.where(first, packed[half:], packed[:half])


def unpacked(packed, n):
    row, col = place_of(n, n)
    start = 3 * n // 2
    diagonals = [packed[start:start + 1, :n], packed[start:start + 1, n:], packed[start + 1:start + 2, :n]]
    moments = []
    for i in range(3):
        folded = packed[i * n // 2:(i + 1) * n // 2]
        pair = jnp.concatenate([folded[:, :n], folded[:, n:]], axis=0)
        flipped = pair.T
        moments.append(jnp.where(row >= col, pair, flipped))
        moments.append(jnp.where(row == col, diagonals[i], jnp.where(row < col, pair, flipped)))
    return moments


def unit(rows, cols):
    return (lax.broadcasted_iota(jnp.int32, (rows, cols), 0)
            == lax.broadcasted_iota(jnp.int32, (rows, cols), 1)).astype(F32)


def lane(values, k):
    return jnp.take_along_axis(values, jnp.full(values.shape, k, jnp.int32), axis=1, mode="promise_in_bounds")


def sublane(values, k):
    return jnp.broadcast_to(values[k:k + 1, :], values.shape)


def inverse_factor(matrix):
    size = matrix.shape[0]
    work = jnp.concatenate([matrix, unit(size, size)], axis=1)
    blocks = [work[8 * i:8 * i + 8, :] for i in range(size // 8)]
    place = lax.broadcasted_iota(jnp.int32, (8, 2 * size), 0)
    done = [None] * (size // 8)
    for k in range(0, size, 4):
        top, r = divmod(k, 8)
        pivot = blocks[top]
        cols = [lane(pivot, k + j) for j in range(4)]
        u0, u1, u2, u3 = (sublane(pivot, r + j) for j in range(4))
        a00, a10, a20, a30 = (sublane(cols[0], r + j) for j in range(4))
        a11, a21, a31 = (sublane(cols[1], r + j) for j in range(1, 4))
        a22, a32 = (sublane(cols[2], r + j) for j in range(2, 4))
        a33 = sublane(cols[3], r + 3)
        det_a = a00 * a11 - a10 * a10
        inv_a = 1.0 / det_a
        p00, p10, p11 = a11 * inv_a, a10 * inv_a, a00 * inv_a
        b00, b01 = a20 * p00 - a21 * p10, a21 * p11 - a20 * p10
        b10, b11 = a30 * p00 - a31 * p10, a31 * p11 - a30 * p10
        s00 = a22 - b00 * a20 - b01 * a21
        s10 = a32 - b10 * a20 - b11 * a21
        s11 = a33 - b10 * a30 - b11 * a31
        det_s = s00 * s11 - s10 * s10
        inv_s = 1.0 / det_s
        u2 = u2 - b00 * u0 - b01 * u1
        u3 = u3 - b10 * u0 - b11 * u1
        t2 = (s11 * u2 - s10 * u3) * inv_s
        t3 = (s00 * u3 - s10 * u2) * inv_s
        t0 = (p00 * u0 - p10 * u1) - b00 * t2 - b10 * t3
        t1 = (p11 * u1 - p10 * u0) - b01 * t2 - b11 * t3
        for i in range(top, size // 8):
            if i == top:
                if r:
                    continue
                c = cols
            else:
                c = [lane(blocks[i], k + j) for j in range(4)]
            change = (c[0] * t0 + c[1] * t1) + (c[2] * t2 + c[3] * t3)
            blocks[i] = blocks[i] - (jnp.where(place > 3, change, 0.0) if i == top else change)
        v0 = u0 * lax.rsqrt(a00)
        v1 = (a00 * u1 - a10 * u0) * lax.rsqrt(a00 * det_a)
        v2 = u2 * lax.rsqrt(s00)
        v3 = (s00 * u3 - s10 * u2) * lax.rsqrt(s00 * det_s)
        four = jnp.where(place % 4 == 0, v0, jnp.where(place % 4 == 1, v1, jnp.where(place % 4 == 2, v2, v3)))
        done[top] = jnp.where(place > 3, four, done[top]) if r else four
    return jnp.concatenate(done, axis=0)[:, size:]


def trace(matrix):
    return jnp.sum(matrix * unit(*matrix.shape))


def dense(moments, index, rows, data):
    n = NVEC
    eye = unit(n, n)
    pick = ((lax.broadcasted_iota(jnp.int32, (n, n), 0) == index)
            & (lax.broadcasted_iota(jnp.int32, (n, n), 1) == index)).astype(F32)

    def part(stacked, i):
        return stacked[i * n:(i + 1) * n]

    def below(*parts):
        return jnp.concatenate(parts, axis=0)

    def beside(*parts):
        return jnp.concatenate(parts, axis=1)

    base = inverse_factor(moments[0])
    right = dot(below(*moments[1:]), base, 1, 1)
    m1, m2, m3, m4, m5 = (dot(base, part(right, i)) for i in range(5))
    y0, y1, y2 = (dot(base, part(data, i)) for i in range(3))

    by1 = dot(below(m1, m2, m3, m4), m1)
    square, m21, m31, m41 = (part(by1, i) for i in range(4))
    tri = dot(m1, beside(square, m21, m31))
    gram_r = m2 - square
    image_r = m3 - m21 - m21.T + tri[:, :n]
    mixed_r = m3 - m21
    square_r = m4 - m31 - m31.T + tri[:, n:2 * n]
    cubic_r = m5 - m41 - m41.T + tri[:, 2 * n:]
    shift = 3.0 - jnp.sum(m1 * pick)
    ridge = RIDGE_WEIGHT * (n + trace(gram_r)) / (2 * n)
    ridged = gram_r + ridge * eye
    factor = inverse_factor(ridged)
    inverse = dot(factor, factor, 0, 0)
    keep = 1.0 / (1.0 + ridge)
    step = below(
        beside(m1 * keep + shift * eye, gram_r * keep),
        beside(eye - ridge * inverse, dot(inverse, image_r) + shift * eye),
    )
    twice = dot(step, step)
    power = dot(twice, dot(twice, twice[:, :n]))
    top, bottom = power[:n], power[n:]
    weighted = dot(below(ridged, gram_r, image_r), bottom)
    norm = (1.0 + ridge) * dot(top, top, 0, 0) + dot(bottom, part(weighted, 0), 0, 0)
    factor = inverse_factor(norm)

    middle = m4 - m31
    images = dot(below(
        beside(m1, gram_r), beside(gram_r, image_r),
        beside(m2, mixed_r), beside(mixed_r.T, square_r),
        beside(m3, middle), beside(middle.T, cubic_r),
    ), power)
    whole = dot(power, beside(images[:2 * n], images[2 * n:4 * n], images[4 * n:], power), 0, 0)
    lower = dot(bottom, beside(part(images, 1), part(images, 3), part(weighted, 1), part(weighted, 2)), 0, 0)
    raw = [whole[:, i * n:(i + 1) * n] for i in range(4)] + [lower[:, i * n:(i + 1) * n] for i in range(4)]
    right = dot(below(*raw), factor, 1, 1)
    ritz, image2, image3, excess, p_image, p_image2, p_gram, p_ritz = (dot(factor, part(right, i)) for i in range(8))
    excess = ridge * excess

    shift = 3.0 - jnp.sum(ritz * pick)
    by_ritz = dot(below(ritz, p_gram, excess, p_image, image2), ritz)
    squared, gram_pr, gram_cr = part(by_ritz, 0), p_image - part(by_ritz, 1), part(by_ritz, 2)
    tri = dot(ritz, squared), dot(ritz, gram_cr)
    gram_rr = image2 - squared - tri[1]
    image_cr = image2 - squared
    image_pr = p_image2 - part(by_ritz, 3)
    image_rr = image3 - part(by_ritz, 4) - part(by_ritz, 4).T + tri[0]
    ridge = RIDGE_WEIGHT * (n - trace(excess) + trace(p_gram) + trace(gram_rr)) / (3 * n)
    g_cc = eye - excess + ridge * eye
    g_pp = p_gram + ridge * eye
    g_rr = gram_rr + ridge * eye
    image_gram = below(
        beside(ritz, p_image.T, image_cr), beside(p_image, p_ritz, image_pr), beside(image_cr.T, image_pr.T, image_rr),
    )
    v0 = inverse_factor(g_cc)
    side = dot(below(p_gram, gram_cr.T), v0, 1, 1)
    l10, l20 = side[:n], side[n:]
    outer = dot(side, side, 1, 1)
    v1 = inverse_factor(g_pp - outer[:n, :n])
    l21 = dot(gram_pr.T - outer[n:, :n], v1, 1, 1)
    v2 = inverse_factor(g_rr - outer[n:, n:] - dot(l21, l21, 1, 1))
    zero = jnp.zeros((n, n), F32)
    row0 = beside(v0, zero, zero)
    row1 = dot(v1, beside(-dot(l10, v0), eye, zero))
    row2 = beside(zero, zero, eye) - dot(l20, row0) - dot(l21, row1)
    known = below(row0, row1)
    solved = dot(known, dot(known, image_gram), 0, 0)
    row2 = dot(v2, beside(row2, dot(row2, image_gram)))
    step = solved + dot(row2[:, :3 * n], row2[:, 3 * n:], 0, 0) + shift * unit(3 * n, 3 * n)
    twice = dot(step, step)
    power2 = dot(twice, dot(twice, twice[:, :n]))
    gram = below(
        beside(g_cc, p_gram, gram_cr), beside(p_gram, g_pp, gram_pr), beside(gram_cr.T, gram_pr.T, g_rr),
    )
    norm = dot(power2, dot(gram, power2), 0, 0)

    start = dot(power, below(y0, y1), 0, 0) - dot(dot(m1, bottom), y0, 0, 0)
    image = dot(power, below(y1, y2), 0, 0) - dot(dot(m1, bottom), y1, 0, 0)
    residue = dot(bottom, y1 - dot(m1, y0), 0, 0)
    current = dot(factor, start)
    vectors = below(current, dot(factor, residue), dot(factor, image) - dot(ritz, current))
    return dot(inverse_factor(norm), dot(power2, vectors, 0, 0)) * math.sqrt(rows)


def dense_body(rows, core, index, mine, theirs, scaled, out):
    first = core[0] == 0
    packed = jnp.concatenate([
        jnp.where(first, mine[...], theirs[...]), jnp.where(first, theirs[...], mine[...])], axis=0)
    out[...] = dense(unpacked(packed, NVEC), index[0], rows, scaled[...])


def moved(shard, axis, by):
    length = lax.axis_size(axis)
    return lax.ppermute(shard, axis, [(i, (i + by) % length) for i in range(length)])


def total_over_blocks(values):
    blocks = lax.axis_size("blk")
    span = 1
    while blocks % (2 * span) == 0:
        other = lax.ppermute(values, "blk", [(i, i ^ span) for i in range(blocks)])
        values = values + other
        span *= 2
    if span < blocks:
        groups = [list(range(i, blocks, span)) for i in range(span)]
        values = lax.psum(values, "blk", axis_index_groups=groups)
    return values


def shards(embeddings, pair_mask, shift_index, start_seed):
    size = embeddings.shape[0]
    blocks = lax.axis_size("blk")
    where = lax.axis_index("blk")
    core = lax.axis_index("narrow").astype(jnp.int32).reshape(1)
    chunk = 128 if size % 128 == 0 else size
    count = size // chunk
    other_emb = moved(embeddings, "narrow", 1)
    near2 = [moved(embeddings[i * chunk:(i + 1) * chunk], "blk", -2) for i in range(count)]
    keep = lax.dynamic_slice_in_dim(pair_mask, where, 1, 0)[0]
    seed16 = start_seed.astype(jnp.int16).T
    seeds = [seed16, moved(seed16, "narrow", 1), moved(seed16, "blk", -1), moved(seed16, "blk", -2)]
    seed, other_seed, seed1, seed2 = [part.astype(F32) / 1000.0 for part in seeds]

    emb_args = [embeddings, other_emb]
    h0, l0, sums, row_sq, own_copy = make_tile(
        own_body, emb_args, size, extra=(((2 * size, 128), F32), (embeddings.shape, BF16)))
    if blocks % 2 == 0:
        direct = lax.ppermute(own_copy, "blk", [(i, i - 1) for i in range(1, blocks, 2)])
        relayed = [lax.ppermute(part, "blk", [(i, i + 1) for i in range(0, blocks, 2)]) for part in near2]
    else:
        direct, relayed = moved(own_copy, "blk", -1), near2
    odd = (where % 2 * (blocks % 2 == 0)).astype(jnp.int32).reshape(1)
    col_shape = ((8, size), F32)
    h2, l2, sums, cols2 = make_tile(
        lambda *refs: near_body(count, *refs), [keep[1:2], *emb_args, row_sq, *near2, sums], size, (0,), (col_shape,))
    behind2 = moved(cols2, "blk", 2)
    h1, l1, sums, cols1 = make_tile(
        lambda *refs: relayed_body(count, *refs),
        [keep[0:1], odd, *emb_args, row_sq, direct, *relayed, sums, behind2], size, (0, 1), (col_shape,))
    behind1 = moved(cols1, "blk", 1)
    other_sums = moved(sums + jnp.pad(behind1, ((0, 8), (0, 0))), "narrow", 1)

    pair_shape, half_shape = ((2 * NVEC, size), F32), ((NVEC, size), F32)
    small = dict(flops=10**6, nbytes=10**5)
    middle = dict(flops=10**9, nbytes=10**6)
    degree, scale, own, other = call(
        degree_body, [((16, size), F32), col_shape, half_shape, half_shape],
        [sums, behind1, other_sums, seed, other_seed], **small)
    far = [h1, l1, h2, l2]
    history = [own]
    for repeat in range(2):
        if repeat == 0:
            body, near = first_block_body, [seed1, seed2, moved(scale, "blk", -1), moved(scale, "blk", -2)]
        else:
            body, near = block_body, [moved(own, "blk", -1), moved(own, "blk", -2)]
        ahead1, ahead2 = call(ahead_body, [half_shape] * 2, [own, other, *far], **middle)
        q1, q2 = moved(ahead1, "blk", 1), moved(ahead2, "blk", 2)
        (product,) = call(own_product_body, [((NVEC, 2 * size), F32)], [own, h0, l0], **middle)
        (total,) = call(body, [pair_shape], [product, *near, q1, q2, *far], **middle)
        other_total = moved(total, "narrow", 1)
        own, other = call(combine_body, [half_shape] * 2, [total, other_total, degree], **small)
        history.append(own)
    near = [moved(own, "blk", -1), moved(own, "blk", -2)]
    low, scaled = call(
        low_body, [((5 * NVEC, NVEC), F32), ((3 * NVEC, size), F32)], [degree] + history, **middle)
    (product,) = call(own_product_body, [((NVEC, 2 * size), F32)], [own, h0, l0], **middle)
    packed_shape = ((3 * NVEC // 4 + 8, 2 * NVEC), F32)
    mine, theirs = call(
        moment_body, [packed_shape] * 2, [core, low, own, other, product, *near, *far], smem=(0,), **middle)
    mine = total_over_blocks(mine + moved(theirs, "narrow", 1))
    rows = size * blocks * lax.axis_size("narrow")
    (out,) = call(
        lambda *refs: dense_body(rows, *refs), [half_shape],
        [core, shift_index, mine, moved(mine, "narrow", 1), scaled], smem=(0, 1), flops=2 * 10**10, nbytes=10**6,
    )
    return out.T


def solution(mesh):
    return jax.shard_map(
        shards,
        mesh=mesh,
        in_specs=(
            P(("groups", "blk", "narrow"), None),
            P("groups", None),
            P("groups"),
            P(("groups", "blk", "narrow"), None),
        ),
        out_specs=P(("groups", "blk", "narrow"), None),
        check_vma=False,
    )
```

time: 124 us -> 120 us (0.968)
  waiting for transfers between devices: 42.2 us -> 27.2 us
  local copies, waits for them, and re-layouts: 1.83 us -> 8.98 us
  starting transfers between devices: 39 us -> 45 us
  Pallas kernels: 40.1 us -> 37.6 us
    ppermute x21 -> x24, starting transfers between devices: 20.9 us -> 29 us  [moved(): lax.ppermute(shard, axis, [(i, (i + by) % length) for i in range(length)])]
    ppermute x21 -> x24, waiting for transfers between devices: 27 us -> 18.9 us  [moved(): lax.ppermute(shard, axis, [(i, (i + by) % length) for i in range(length)])]
    ppermute x6 -> x4, waiting for transfers between devices: 15.2 us -> 8.31 us  [the longest x3 8.31 us: total_over_blocks(): other = lax.ppermute(values, 'blk', [(i, i ^ span) for i in range(blocks)])]
    unnamed x6 -> x34, local copies, waits for them, and re-layouts: 0.01 us -> 6.51 us
    pallas_call x11 -> x16, Pallas kernels: 40.1 us -> 37.6 us  [call(): pl.pallas_call(body, out_shape=[jax.ShapeDtypeStruct(shape, dtype) for sh...]
    ppermute x3, starting transfers between devices: 12.1 us -> 10.5 us  [shards(): lax.ppermute(part, 'blk', [(i, i + 1) for i in range(0, blocks, 2)])]
    ppermute x6 -> x4, starting transfers between devices: 6.01 us -> 5.48 us  [the longest x3 4.2 us: total_over_blocks(): other = lax.ppermute(values, 'blk', [(i, i ^ span) for i in range(blocks)])]
  transfers between devices with their start and end apart: 30 -> 31, of which waited for: 18 -> 16; matrix products, arithmetic and copies ran while one was open for 1% -> 2% of each run, Pallas kernels for 7% -> 9%
where the time goes in v4:
time: 120 us
  starting transfers between devices  45 us (38%)
  Pallas kernels  37.6 us (31%)
  waiting for transfers between devices  27.2 us (23%)
  local copies, waits for them, and re-layouts  8.98 us (7%)
    pallas_call x16, Pallas kernels, call(): pl.pallas_call(body, out_shape=[jax.ShapeDtypeStruct(shape, dtype) for sh...  37.6 us
    ppermute x24, starting transfers between devices, moved(): lax.ppermute(shard, axis, [(i, (i + by) % length) for i in range(length)])  29 us
    ppermute x24, waiting for transfers between devices, moved(): lax.ppermute(shard, axis, [(i, (i + by) % length) for i in range(length)])  18.9 us
    ppermute x3, starting transfers between devices, shards(): lax.ppermute(part, 'blk', [(i, i + 1) for i in range(0, blocks, 2)])  10.5 us
    ppermute x3, waiting for transfers between devices, total_over_blocks(): other = lax.ppermute(values, 'blk', [(i, i ^ span) for i in range(blocks)])  8.31 us
    unnamed x34, local copies, waits for them, and re-layouts  6.51 us
    ppermute x3, starting transfers between devices, total_over_blocks(): other = lax.ppermute(values, 'blk', [(i, i ^ span) for i in range(blocks)])  4.2 us
  transfers between devices with their start and end apart: 31, of which 16 were waited for; matrix products, arithmetic and copies ran while one was open for 2% of the time, Pallas kernels for 9%

profile of v4, /device:TPU:0, one launch (start us, length us, event | category | flops | bytes accessed | tf_op | source)
XLA Modules:
  0.0 119.8 jit_solution(3928299659344804000)
XLA Ops:
  0.5 1.8 %fusion = (bf16[128,768]{1,0:T(8,128)(2,1)}, bf16[128,768]{1,0:T(8,128)(2,1)S(1)}, bf16[128,768]{1,0:T(8,128)(2,1)S(1)}) fusion(bf16[384,768]{1,0:T(8,128)(2,1)} %refs_2_.1), kind=kLoop, calls=%fused_computation.7 | loop fusion | bytes 1179648 | tf_op jit(solution)/shard_map/slice | solution.py:428
  2.3 4.7 %collective-permute-start.2 = (bf16[128,768]{1,0:T(8,128)(2,1)S(1)}, bf16[128,768]{1,0:T(8,128)(2,1)S(1)}, u32[]{:S(2)}, u32[]{:S(2)}) collective-permute-start(bf16[128,768]{1,0:T(8,128)(2,1)S(1)} %get-tuple-element.67), channel_id=1, source_target_pairs={{0,12},{2,14},{4,0},{6,2},{8,4},{10,6},{12,8},{14,10},{1,13},{3,15... | collective-permute-start | bytes 589832 | tf_op jit(solution)/shard_map/ppermute | solution.py:404
  7.9 1.9 %shard_map.46 = (bf16[768,384]{1,0:T(8,128)(2,1)S(1)}, bf16[768,384]{1,0:T(8,128)(2,1)S(1)}, f32[16,384]{1,0:T(8,128)S(1)}, f32[768,128]{1,0:T(8,128)S(1)}, bf16[384,768]{1,0:T(8,128)(2,1)S(1)}) custom-call(bf16[384,768]{1,0:T(8,128)(2,1)S(1)} %copy-done.1, bf16[384,768]{1,0:T(8,128)(2,1)S(1)} %collective-permute-done.other.refs_2_.refs_3_), custom_call_target="tpu_custom_call" | custom-call | flops 2000000000 | bytes 1000000 | tf_op jit(solution)/shard_map/pallas_call | solution.py:36
  9.8 0.9 copy-done.8
  10.6 0.8 copy-done.11
  11.4 1.3 %collective-permute-start.1 = (bf16[384,768]{1,0:T(8,128)(2,1)S(1)}, bf16[384,768]{1,0:T(8,128)(2,1)S(1)}, u32[]{:S(2)}, u32[]{:S(2)}) collective-permute-start(bf16[384,768]{1,0:T(8,128)(2,1)S(1)} %get-tuple-element.35), channel_id=1, source_target_pairs={{2,0},{6,4},{10,8},{14,12},{3,1},{7,5},{11,9},{15,13},{18,16},{22,... | collective-permute-start | bytes 1769480 | tf_op jit(solution)/shard_map/ppermute | solution.py:438
  12.8 0.5 fusion.1
  13.4 4.6 %collective-permute-start.3 = (bf16[128,768]{1,0:T(8,128)(2,1)S(1)}, bf16[128,768]{1,0:T(8,128)(2,1)S(1)}, u32[]{:S(2)}, u32[]{:S(2)}) collective-permute-start(bf16[128,768]{1,0:T(8,128)(2,1)S(1)} %collective-permute-done.2.refs_4_), channel_id=1, source_target_pairs={{0,2},{4,6},{8,10},{12,14},{1,3},{5,7},{9,11},{13,15},{16,18},{20,... | collective-permute-start | bytes 589832 | tf_op jit(solution)/shard_map/ppermute | solution.py:439
  17.9 1.9 %collective-permute-start.5 = (bf16[128,768]{1,0:T(8,128)(2,1)S(1)}, bf16[128,768]{1,0:T(8,128)(2,1)S(1)}, u32[]{:S(2)}, u32[]{:S(2)}) collective-permute-start(bf16[128,768]{1,0:T(8,128)(2,1)S(1)} %collective-permute-done.4.refs_5_), channel_id=1, source_target_pairs={{0,2},{4,6},{8,10},{12,14},{1,3},{5,7},{9,11},{13,15},{16,18},{20,... | collective-permute-start | bytes 589832 | tf_op jit(solution)/shard_map/ppermute | solution.py:439
  20.3 4.1 %collective-permute-start.7 = (bf16[128,768]{1,0:T(8,128)(2,1)S(1)}, bf16[128,768]{1,0:T(8,128)(2,1)}, u32[]{:S(2)}, u32[]{:S(2)}) collective-permute-start(bf16[128,768]{1,0:T(8,128)(2,1)S(1)} %collective-permute-done.6.refs_6_), channel_id=1, source_target_pairs={{0,2},{4,6},{8,10},{12,14},{1,3},{5,7},{9,11},{13,15},{16,18},{20,... | collective-permute-start | bytes 589832 | tf_op jit(solution)/shard_map/ppermute | solution.py:439
  24.4 2.5 %shard_map.47 = (bf16[768,384]{1,0:T(8,128)(2,1)S(1)}, bf16[768,384]{1,0:T(8,128)(2,1)S(1)}, f32[16,384]{1,0:T(8,128)S(1)}, f32[8,384]{1,0:T(8,128)S(1)}) custom-call(s32[1]{0:T(128)} %bitcast.3.refs_0_, bf16[384,768]{1,0:T(8,128)(2,1)S(1)} %copy-done.1, bf16[384,768]{1,0:T(8,128)(2,1)S(1)} %collective-permute-done.other.refs_2_.refs_3_, ...), custom_call_target="tpu_custom_call" | custom-call | flops 2000000000 | bytes 1000000 | tf_op jit(solution)/shard_map/pallas_call | solution.py:36
  26.9 0.9 copy-done.2
  27.8 0.8 copy-done.4
  29.1 3.9 %collective-permute-start.13 = (s16[64,384]{1,0:T(8,128)(2,1)S(1)}, s16[64,384]{1,0:T(8,128)(2,1)S(1)}, u32[]{:S(2)}, u32[]{:S(2)}) collective-permute-start(s16[64,384]{1,0:T(8,128)(2,1)S(1)} %get-tuple-element.64), channel_id=1, source_target_pairs={{0,12},{2,14},{4,0},{6,2},{8,4},{10,6},{12,8},{14,10},{1,13},{3,15... | collective-permute-start | bytes 147464 | tf_op jit(solution)/shard_map/ppermute | solution.py:404
  33.0 0.9 collective-permute-start.12
  33.8 0.7 collective-permute-done.8.refs_10_
  34.5 1.0 copy-done.15
  35.5 3.5 %shard_map.48 = (bf16[768,384]{1,0:T(8,128)(2,1)S(1)}, bf16[768,384]{1,0:T(8,128)(2,1)S(1)}, f32[16,384]{1,0:T(8,128)S(1)}, f32[8,384]{1,0:T(8,128)S(1)}) custom-call(s32[1]{0:T(128)} %bitcast.1.refs_0_, s32[1]{0:T(128)} %bitcast.2.refs_1_, bf16[384,768]{1,0:T(8,128)(2,1)S(1)} %copy-done.1, bf16[384,768]{1,0:T(8,128)(2,1)S(1)} %collective-permute-done.other.refs_2_.refs_3_, ...), custom_call_target="tpu_custom_call" | custom-call | flops 2000000000 | bytes 1000000 | tf_op jit(solution)/shard_map/pallas_call | solution.py:36
  39.6 5.9 %collective-permute-done.9.behind = f32[8,384]{1,0:T(8,128)S(1)} collective-permute-done((f32[8,384]{1,0:T(8,128)S(1)}, f32[8,384]{1,0:T(8,128)S(1)}, u32[]{:S(2)}, u32[]{:S(2)}) %collective-permute-start.9) | collective-permute-done | bytes 12320 | tf_op jit(solution)/shard_map/ppermute | solution.py:404
  45.5 1.2 collective-permute-done.10.other_sums
  47.4 4.7 %collective-permute-start.14 = (f32[8,384]{1,0:T(8,128)S(1)}, f32[8,384]{1,0:T(8,128)S(1)}, u32[]{:S(2)}, u32[]{:S(2)}) collective-permute-start(f32[8,384]{1,0:T(8,128)S(1)} %get-tuple-element.45), channel_id=1, source_target_pairs={{0,14},{2,0},{4,2},{6,4},{8,6},{10,8},{12,10},{14,12},{1,15},{3,1}... | collective-permute-start | bytes 36872 | tf_op jit(solution)/shard_map/ppermute | solution.py:404
  52.1 2.0 %collective-permute-start.15 = (f32[8,384]{1,0:T(8,128)S(1)}, f32[8,384]{1,0:T(8,128)S(1)}, u32[]{:S(2)}, u32[]{:S(2)}) collective-permute-start(f32[8,384]{1,0:T(8,128)S(1)} %get-tuple-element.45), channel_id=1, source_target_pairs={{0,12},{2,14},{4,0},{6,2},{8,4},{10,6},{12,8},{14,10},{1,13},{3,15... | collective-permute-start | bytes 36872 | tf_op jit(solution)/shard_map/ppermute | solution.py:404
  54.6 1.2 collective-permute-done.15.scale2
  55.8 0.8 shard_map.52.total
  56.7 1.4 %collective-permute-done.18.other_total = f32[128,384]{1,0:T(8,128)S(1)} collective-permute-done((f32[128,384]{1,0:T(8,128)S(1)}, f32[128,384]{1,0:T(8,128)S(1)}, u32[]{:S(2)}, u32[]{:S(2)}) %collective-permute-start.18) | collective-permute-done | bytes 196640 | tf_op jit(solution)/shard_map/ppermute | solution.py:404
  58.7 2.0 %collective-permute-start.21 = (f32[64,384]{1,0:T(8,128)S(1)}, f32[64,384]{1,0:T(8,128)S(1)}, u32[]{:S(2)}, u32[]{:S(2)}) collective-permute-start(f32[64,384]{1,0:T(8,128)S(1)} %get-tuple-element.55), channel_id=1, source_target_pairs={{0,2},{2,4},{4,6},{6,8},{8,10},{10,12},{12,14},{14,0},{1,3},{3,5},... | collective-permute-start | bytes 294920 | tf_op jit(solution)/shard_map/ppermute | solution.py:404
  60.7 0.6 collective-permute-start.22
  61.3 2.7 %collective-permute-start.19 = (f32[64,384]{1,0:T(8,128)S(1)}, f32[64,384]{1,0:T(8,128)S(1)}, u32[]{:S(2)}, u32[]{:S(2)}) collective-permute-start(f32[64,384]{1,0:T(8,128)S(1)} %get-tuple-element.53.own.v1), channel_id=1, source_target_pairs={{0,14},{2,0},{4,2},{6,4},{8,6},{10,8},{12,10},{14,12},{1,15},{3,1}... | collective-permute-start | bytes 294920 | tf_op jit(solution)/shard_map/ppermute | solution.py:404
  64.0 1.5 %collective-permute-start.20 = (f32[64,384]{1,0:T(8,128)S(1)}, f32[64,384]{1,0:T(8,128)S(1)}, u32[]{:S(2)}, u32[]{:S(2)}) collective-permute-start(f32[64,384]{1,0:T(8,128)S(1)} %get-tuple-element.53.own.v1), channel_id=1, source_target_pairs={{0,12},{2,14},{4,0},{6,2},{8,4},{10,6},{12,8},{14,10},{1,13},{3,15... | collective-permute-start | bytes 294920 | tf_op jit(solution)/shard_map/ppermute | solution.py:404
  66.0 1.3 %collective-permute-done.21.refs_0_ = f32[64,384]{1,0:T(8,128)S(1)} collective-permute-done((f32[64,384]{1,0:T(8,128)S(1)}, f32[64,384]{1,0:T(8,128)S(1)}, u32[]{:S(2)}, u32[]{:S(2)}) %collective-permute-start.21) | collective-permute-done | bytes 98336 | tf_op jit(solution)/shard_map/ppermute | solution.py:404
  67.2 0.9 collective-permute-done.22.refs_1_
  68.2 1.6 %collective-permute-done.20.near2 = f32[64,384]{1,0:T(8,128)S(1)} collective-permute-done((f32[64,384]{1,0:T(8,128)S(1)}, f32[64,384]{1,0:T(8,128)S(1)}, u32[]{:S(2)}, u32[]{:S(2)}) %collective-permute-start.20) | collective-permute-done | bytes 98336 | tf_op jit(solution)/shard_map/ppermute | solution.py:404
  69.7 0.8 shard_map.56.total
  70.6 1.4 %collective-permute-done.23.other_total = f32[128,384]{1,0:T(8,128)S(1)} collective-permute-done((f32[128,384]{1,0:T(8,128)S(1)}, f32[128,384]{1,0:T(8,128)S(1)}, u32[]{:S(2)}, u32[]{:S(2)}) %collective-permute-start.23) | collective-permute-done | bytes 196640 | tf_op jit(solution)/shard_map/ppermute | solution.py:404
  72.1 2.8 %collective-permute-start.24 = (f32[64,384]{1,0:T(8,128)S(1)}, f32[64,384]{1,0:T(8,128)S(1)}, u32[]{:S(2)}, u32[]{:S(2)}) collective-permute-start(f32[64,384]{1,0:T(8,128)S(1)} %get-tuple-element.57.v2.own), channel_id=1, source_target_pairs={{0,14},{2,0},{4,2},{6,4},{8,6},{10,8},{12,10},{14,12},{1,15},{3,1}... | collective-permute-start | bytes 294920 | tf_op jit(solution)/shard_map/ppermute | solution.py:404
  74.9 0.6 collective-permute-start.25
  75.5 1.1 copy-done.10
  76.6 1.1 copy-done.13
  78.7 1.1 collective-permute-done.25.near2
  79.8 1.4 %shard_map.60 = (f32[56,128]{1,0:T(8,128)S(1)}, f32[56,128]{1,0:T(8,128)S(1)}) custom-call(s32[1]{0:T(128)} %bitcast.core.refs_0_, f32[320,64]{1,0:T(8,128)S(1)} %get-tuple-element.58.low, f32[64,384]{1,0:T(8,128)S(1)} %get-tuple-element.57.v2.own, f32[64,384]{1,0:T(8,128)S(1)} %get-tuple-element.59.other, f32[64,768]{1,0:T(8,128)S(1)} %shard_map.59.product, ...), custom_call_target="tpu_custom_call" | custom-call | flops 1000000000 | bytes 1000000 | tf_op jit(solution)/shard_map/pallas_call | solution.py:36
  81.3 1.2 collective-permute-done.26
  82.5 0.8 collective-permute-start.27
  83.3 3.1 %collective-permute-done.27 = f32[56,128]{1,0:T(8,128)S(1)} collective-permute-done((f32[56,128]{1,0:T(8,128)S(1)}, f32[56,128]{1,0:T(8,128)S(1)}, u32[]{:S(2)}, u32[]{:S(2)}) %collective-permute-start.27) | collective-permute-done | bytes 28704 | tf_op jit(solution)/shard_map/ppermute | solution.py:411
  86.4 1.0 collective-permute-start.28
  87.4 2.9 %collective-permute-done.28 = f32[56,128]{1,0:T(8,128)S(1)} collective-permute-done((f32[56,128]{1,0:T(8,128)S(1)}, f32[56,128]{1,0:T(8,128)S(1)}, u32[]{:S(2)}, u32[]{:S(2)}) %collective-permute-start.28) | collective-permute-done | bytes 28704 | tf_op jit(solution)/shard_map/ppermute | solution.py:411
  90.2 2.4 %collective-permute-start.29 = (f32[56,128]{1,0:T(8,128)S(1)}, f32[56,128]{1,0:T(8,128)S(1)}, u32[]{:S(2)}, u32[]{:S(2)}) collective-permute-start(f32[56,128]{1,0:T(8,128)S(1)} %add.29), channel_id=1, source_target_pairs={{0,8},{2,10},{4,12},{6,14},{8,0},{10,2},{12,4},{14,6},{1,9},{3,11}... | collective-permute-start | bytes 86024 | tf_op jit(solution)/shard_map/ppermute | solution.py:411
  92.6 2.4 %collective-permute-done.29 = f32[56,128]{1,0:T(8,128)S(1)} collective-permute-done((f32[56,128]{1,0:T(8,128)S(1)}, f32[56,128]{1,0:T(8,128)S(1)}, u32[]{:S(2)}, u32[]{:S(2)}) %collective-permute-start.29) | collective-permute-done | bytes 28704 | tf_op jit(solution)/shard_map/ppermute | solution.py:411
  96.2 23.6 %shard_map.61 = f32[64,384]{1,0:T(8,128)} custom-call(s32[1]{0:T(128)} %bitcast.core.refs_0_, s32[1]{0:T(128)S(6)} %copy.5.refs_1_, f32[56,128]{1,0:T(8,128)S(1)} %add.30.refs_2_, f32[56,128]{1,0:T(8,128)S(1)} %collective-permute-done.30.refs_3_, f32[192,384]{1,0:T(8,128)S(1)} %get-tuple-element.62.refs_4_), custom_call_target="tpu_custom_call" | custom-call | flops 20000000000 | bytes 1000000 | tf_op jit(solution)/shard_map/pallas_call | solution.py:36
  (76 shorter events, 7.0 us)
Async XLA Ops:
  0.0 12.7 %copy-start = (s32[8,2]{0,1:T(2,128)S(1)}, s32[8,2]{0,1:T(2,128)}, u32[]{:S(2)}) copy-start(s32[8,2]{0,1:T(2,128)} %param.5) | copy-start | bytes 196
  0.0 7.9 %copy-start.1 = (bf16[384,768]{1,0:T(8,128)(2,1)S(1)}, bf16[384,768]{1,0:T(8,128)(2,1)}, u32[]{:S(2)}) copy-start(bf16[384,768]{1,0:T(8,128)(2,1)} %refs_2_.1) | copy-start | bytes 1769476
  0.0 7.9 %collective-permute-start = (bf16[384,768]{1,0:T(8,128)(2,1)}, bf16[384,768]{1,0:T(8,128)(2,1)S(1)}, u32[]{:S(2)}, u32[]{:S(2)}) collective-permute-start(bf16[384,768]{1,0:T(8,128)(2,1)} %refs_2_.1), channel_id=1, source_target_pairs={{0,1},{1,0},{2,3},{3,2},{4,5},{5,4},{6,7},{7,6},{8,9},{9,8},{10,11... | collective-permute-start | bytes 1769480 | tf_op jit(solution)/shard_map/ppermute | solution.py:404
  2.3 11.0 %collective-permute-start.2 = (bf16[128,768]{1,0:T(8,128)(2,1)S(1)}, bf16[128,768]{1,0:T(8,128)(2,1)S(1)}, u32[]{:S(2)}, u32[]{:S(2)}) collective-permute-start(bf16[128,768]{1,0:T(8,128)(2,1)S(1)} %get-tuple-element.67), channel_id=1, source_target_pairs={{0,12},{2,14},{4,0},{6,2},{8,4},{10,6},{12,8},{14,10},{1,13},{3,15... | collective-permute-start | bytes 589832 | tf_op jit(solution)/shard_map/ppermute | solution.py:404
  7.0 11.0 %collective-permute-start.4 = (bf16[128,768]{1,0:T(8,128)(2,1)S(1)}, bf16[128,768]{1,0:T(8,128)(2,1)S(1)}, u32[]{:S(2)}, u32[]{:S(2)}) collective-permute-start(bf16[128,768]{1,0:T(8,128)(2,1)S(1)} %get-tuple-element.66), channel_id=1, source_target_pairs={{0,12},{2,14},{4,0},{6,2},{8,4},{10,6},{12,8},{14,10},{1,13},{3,15... | collective-permute-start | bytes 589832 | tf_op jit(solution)/shard_map/ppermute | solution.py:404
  7.4 12.8 %collective-permute-start.6 = (bf16[128,768]{1,0:T(8,128)(2,1)}, bf16[128,768]{1,0:T(8,128)(2,1)S(1)}, u32[]{:S(2)}, u32[]{:S(2)}) collective-permute-start(bf16[128,768]{1,0:T(8,128)(2,1)} %get-tuple-element.65), channel_id=1, source_target_pairs={{0,12},{2,14},{4,0},{6,2},{8,4},{10,6},{12,8},{14,10},{1,13},{3,15... | collective-permute-start | bytes 589832 | tf_op jit(solution)/shard_map/ppermute | solution.py:404
  9.7 0.9 copy-start.8
  10.6 0.8 copy-start.11
  11.4 15.5 %copy-start.14 = (f32[768,128]{1,0:T(8,128)}, f32[768,128]{1,0:T(8,128)S(1)}, u32[]{:S(2)}) copy-start(f32[768,128]{1,0:T(8,128)S(1)} %get-tuple-element.34.refs_3_.refs_4_) | copy-start | bytes 1179652
  11.4 23.1 %collective-permute-start.1 = (bf16[384,768]{1,0:T(8,128)(2,1)S(1)}, bf16[384,768]{1,0:T(8,128)(2,1)S(1)}, u32[]{:S(2)}, u32[]{:S(2)}) collective-permute-start(bf16[384,768]{1,0:T(8,128)(2,1)S(1)} %get-tuple-element.35), channel_id=1, source_target_pairs={{2,0},{6,4},{10,8},{14,12},{3,1},{7,5},{11,9},{15,13},{18,16},{22,... | collective-permute-start | bytes 1769480 | tf_op jit(solution)/shard_map/ppermute | solution.py:438
  13.4 15.6 %collective-permute-start.3 = (bf16[128,768]{1,0:T(8,128)(2,1)S(1)}, bf16[128,768]{1,0:T(8,128)(2,1)S(1)}, u32[]{:S(2)}, u32[]{:S(2)}) collective-permute-start(bf16[128,768]{1,0:T(8,128)(2,1)S(1)} %collective-permute-done.2.refs_4_), channel_id=1, source_target_pairs={{0,2},{4,6},{8,10},{12,14},{1,3},{5,7},{9,11},{13,15},{16,18},{20,... | collective-permute-start | bytes 589832 | tf_op jit(solution)/shard_map/ppermute | solution.py:439
  17.9 11.1 %collective-permute-start.5 = (bf16[128,768]{1,0:T(8,128)(2,1)S(1)}, bf16[128,768]{1,0:T(8,128)(2,1)S(1)}, u32[]{:S(2)}, u32[]{:S(2)}) collective-permute-start(bf16[128,768]{1,0:T(8,128)(2,1)S(1)} %collective-permute-done.4.refs_5_), channel_id=1, source_target_pairs={{0,2},{4,6},{8,10},{12,14},{1,3},{5,7},{9,11},{13,15},{16,18},{20,... | collective-permute-start | bytes 589832 | tf_op jit(solution)/shard_map/ppermute | solution.py:439
  20.3 12.7 %collective-permute-start.7 = (bf16[128,768]{1,0:T(8,128)(2,1)S(1)}, bf16[128,768]{1,0:T(8,128)(2,1)}, u32[]{:S(2)}, u32[]{:S(2)}) collective-permute-start(bf16[128,768]{1,0:T(8,128)(2,1)S(1)} %collective-permute-done.6.refs_6_), channel_id=1, source_target_pairs={{0,2},{4,6},{8,10},{12,14},{1,3},{5,7},{9,11},{13,15},{16,18},{20,... | collective-permute-start | bytes 589832 | tf_op jit(solution)/shard_map/ppermute | solution.py:439
  24.4 4.6 %copy-start.16 = (s32[384,64]{0,1:T(8,128)S(1)}, s32[384,64]{0,1:T(8,128)}, u32[]{:S(2)}) copy-start(s32[384,64]{0,1:T(8,128)} %param.7) | copy-start | bytes 294916
  26.9 0.9 copy-start.2
  27.8 0.8 copy-start.4
  28.6 5.9 %collective-permute-start.8 = (f32[8,384]{1,0:T(8,128)S(1)}, f32[8,384]{1,0:T(8,128)S(1)}, u32[]{:S(2)}, u32[]{:S(2)}) collective-permute-start(f32[8,384]{1,0:T(8,128)S(1)} %get-tuple-element.38), channel_id=1, source_target_pairs={{0,4},{2,6},{4,8},{6,10},{8,12},{10,14},{12,0},{14,2},{1,5},{3,7},... | collective-permute-start | bytes 36872 | tf_op jit(solution)/shard_map/ppermute | solution.py:404
  29.0 10.6 %collective-permute-start.11 = (s16[64,384]{1,0:T(8,128)(2,1)S(1)}, s16[64,384]{1,0:T(8,128)(2,1)S(1)}, u32[]{:S(2)}, u32[]{:S(2)}) collective-permute-start(s16[64,384]{1,0:T(8,128)(2,1)S(1)} %get-tuple-element.64), channel_id=1, source_target_pairs={{0,1},{1,0},{2,3},{3,2},{4,5},{5,4},{6,7},{7,6},{8,9},{9,8},{10,11... | collective-permute-start | bytes 147464 | tf_op jit(solution)/shard_map/ppermute | solution.py:404
  29.1 16.4 %collective-permute-start.13 = (s16[64,384]{1,0:T(8,128)(2,1)S(1)}, s16[64,384]{1,0:T(8,128)(2,1)S(1)}, u32[]{:S(2)}, u32[]{:S(2)}) collective-permute-start(s16[64,384]{1,0:T(8,128)(2,1)S(1)} %get-tuple-element.64), channel_id=1, source_target_pairs={{0,12},{2,14},{4,0},{6,2},{8,4},{10,6},{12,8},{14,10},{1,13},{3,15... | collective-permute-start | bytes 147464 | tf_op jit(solution)/shard_map/ppermute | solution.py:404
  33.0 14.4 %collective-permute-start.12 = (s16[64,384]{1,0:T(8,128)(2,1)S(1)}, s16[64,384]{1,0:T(8,128)(2,1)S(1)}, u32[]{:S(2)}, u32[]{:S(2)}) collective-permute-start(s16[64,384]{1,0:T(8,128)(2,1)S(1)} %get-tuple-element.64), channel_id=1, source_target_pairs={{0,14},{2,0},{4,2},{6,4},{8,6},{10,8},{12,10},{14,12},{1,15},{3,1}... | collective-permute-start | bytes 147464 | tf_op jit(solution)/shard_map/ppermute | solution.py:404
  34.5 1.0 copy-start.15
  35.5 11.2 %copy-start.5 = (bf16[768,384]{1,0:T(8,128)(2,1)S(1)}, bf16[768,384]{1,0:T(8,128)(2,1)}, u32[]{:S(2)}) copy-start(bf16[768,384]{1,0:T(8,128)(2,1)} %copy-done.4) | copy-start | bytes 1769476
  39.0 30.7 %copy-start.6 = (bf16[768,384]{1,0:T(8,128)(2,1)}, bf16[768,384]{1,0:T(8,128)(2,1)S(1)}, u32[]{:S(2)}) copy-start(bf16[768,384]{1,0:T(8,128)(2,1)S(1)} %get-tuple-element.48.l1.refs_3_) | copy-start | bytes 1769476
  39.0 7.7 %copy-start.3 = (bf16[768,384]{1,0:T(8,128)(2,1)S(1)}, bf16[768,384]{1,0:T(8,128)(2,1)}, u32[]{:S(2)}) copy-start(bf16[768,384]{1,0:T(8,128)(2,1)} %copy-done.2) | copy-start | bytes 1769476
  39.0 6.4 %collective-permute-start.9 = (f32[8,384]{1,0:T(8,128)S(1)}, f32[8,384]{1,0:T(8,128)S(1)}, u32[]{:S(2)}, u32[]{:S(2)}) collective-permute-start(f32[8,384]{1,0:T(8,128)S(1)} %get-tuple-element.40), channel_id=1, source_target_pairs={{0,2},{2,4},{4,6},{6,8},{8,10},{10,12},{12,14},{14,0},{1,3},{3,5},... | collective-permute-start | bytes 36872 | tf_op jit(solution)/shard_map/ppermute | solution.py:404
  45.5 1.2 collective-permute-start.10
  46.7 7.4 %copy-start.9 = (bf16[768,384]{1,0:T(8,128)(2,1)S(1)}, bf16[768,384]{1,0:T(8,128)(2,1)}, u32[]{:S(2)}) copy-start(bf16[768,384]{1,0:T(8,128)(2,1)} %copy-done.8) | copy-start | bytes 1769476
  46.7 7.4 %copy-start.12 = (bf16[768,384]{1,0:T(8,128)(2,1)S(1)}, bf16[768,384]{1,0:T(8,128)(2,1)}, u32[]{:S(2)}) copy-start(bf16[768,384]{1,0:T(8,128)(2,1)} %copy-done.11) | copy-start | bytes 1769476
  47.2 8.6 %collective-permute-start.16 = (f32[64,384]{1,0:T(8,128)S(1)}, f32[64,384]{1,0:T(8,128)S(1)}, u32[]{:S(2)}, u32[]{:S(2)}) collective-permute-start(f32[64,384]{1,0:T(8,128)S(1)} %get-tuple-element.51), channel_id=1, source_target_pairs={{0,2},{2,4},{4,6},{6,8},{8,10},{10,12},{12,14},{14,0},{1,3},{3,5},... | collective-permute-start | bytes 294920 | tf_op jit(solution)/shard_map/ppermute | solution.py:404
  47.3 8.5 %collective-permute-start.17 = (f32[64,384]{1,0:T(8,128)S(1)}, f32[64,384]{1,0:T(8,128)S(1)}, u32[]{:S(2)}, u32[]{:S(2)}) collective-permute-start(f32[64,384]{1,0:T(8,128)S(1)} %get-tuple-element.52), channel_id=1, source_target_pairs={{0,4},{2,6},{4,8},{6,10},{8,12},{10,14},{12,0},{14,2},{1,5},{3,7},... | collective-permute-start | bytes 294920 | tf_op jit(solution)/shard_map/ppermute | solution.py:404
  47.4 7.2 %collective-permute-start.14 = (f32[8,384]{1,0:T(8,128)S(1)}, f32[8,384]{1,0:T(8,128)S(1)}, u32[]{:S(2)}, u32[]{:S(2)}) collective-permute-start(f32[8,384]{1,0:T(8,128)S(1)} %get-tuple-element.45), channel_id=1, source_target_pairs={{0,14},{2,0},{4,2},{6,4},{8,6},{10,8},{12,10},{14,12},{1,15},{3,1}... | collective-permute-start | bytes 36872 | tf_op jit(solution)/shard_map/ppermute | solution.py:404
  52.1 3.7 %collective-permute-start.15 = (f32[8,384]{1,0:T(8,128)S(1)}, f32[8,384]{1,0:T(8,128)S(1)}, u32[]{:S(2)}, u32[]{:S(2)}) collective-permute-start(f32[8,384]{1,0:T(8,128)S(1)} %get-tuple-element.45), channel_id=1, source_target_pairs={{0,12},{2,14},{4,0},{6,2},{8,4},{10,6},{12,8},{14,10},{1,13},{3,15... | collective-permute-start | bytes 36872 | tf_op jit(solution)/shard_map/ppermute | solution.py:404
  56.6 1.5 %collective-permute-start.18 = (f32[128,384]{1,0:T(8,128)S(1)}, f32[128,384]{1,0:T(8,128)S(1)}, u32[]{:S(2)}, u32[]{:S(2)}) collective-permute-start(f32[128,384]{1,0:T(8,128)S(1)} %shard_map.52.total), channel_id=1, source_target_pairs={{0,1},{1,0},{2,3},{3,2},{4,5},{5,4},{6,7},{7,6},{8,9},{9,8},{10,11... | collective-permute-start | bytes 589832 | tf_op jit(solution)/shard_map/ppermute | solution.py:404
  58.7 8.5 %collective-permute-start.21 = (f32[64,384]{1,0:T(8,128)S(1)}, f32[64,384]{1,0:T(8,128)S(1)}, u32[]{:S(2)}, u32[]{:S(2)}) collective-permute-start(f32[64,384]{1,0:T(8,128)S(1)} %get-tuple-element.55), channel_id=1, source_target_pairs={{0,2},{2,4},{4,6},{6,8},{8,10},{10,12},{12,14},{14,0},{1,3},{3,5},... | collective-permute-start | bytes 294920 | tf_op jit(solution)/shard_map/ppermute | solution.py:404
  60.7 7.5 %collective-permute-start.22 = (f32[64,384]{1,0:T(8,128)S(1)}, f32[64,384]{1,0:T(8,128)S(1)}, u32[]{:S(2)}, u32[]{:S(2)}) collective-permute-start(f32[64,384]{1,0:T(8,128)S(1)} %get-tuple-element.56), channel_id=1, source_target_pairs={{0,4},{2,6},{4,8},{6,10},{8,12},{10,14},{12,0},{14,2},{1,5},{3,7},... | collective-permute-start | bytes 294920 | tf_op jit(solution)/shard_map/ppermute | solution.py:404
  61.3 6.9 %collective-permute-start.19 = (f32[64,384]{1,0:T(8,128)S(1)}, f32[64,384]{1,0:T(8,128)S(1)}, u32[]{:S(2)}, u32[]{:S(2)}) collective-permute-start(f32[64,384]{1,0:T(8,128)S(1)} %get-tuple-element.53.own.v1), channel_id=1, source_target_pairs={{0,14},{2,0},{4,2},{6,4},{8,6},{10,8},{12,10},{14,12},{1,15},{3,1}... | collective-permute-start | bytes 294920 | tf_op jit(solution)/shard_map/ppermute | solution.py:404
  64.0 5.7 %collective-permute-start.20 = (f32[64,384]{1,0:T(8,128)S(1)}, f32[64,384]{1,0:T(8,128)S(1)}, u32[]{:S(2)}, u32[]{:S(2)}) collective-permute-start(f32[64,384]{1,0:T(8,128)S(1)} %get-tuple-element.53.own.v1), channel_id=1, source_target_pairs={{0,12},{2,14},{4,0},{6,2},{8,4},{10,6},{12,8},{14,10},{1,13},{3,15... | collective-permute-start | bytes 294920 | tf_op jit(solution)/shard_map/ppermute | solution.py:404
  70.5 1.5 %collective-permute-start.23 = (f32[128,384]{1,0:T(8,128)S(1)}, f32[128,384]{1,0:T(8,128)S(1)}, u32[]{:S(2)}, u32[]{:S(2)}) collective-permute-start(f32[128,384]{1,0:T(8,128)S(1)} %shard_map.56.total), channel_id=1, source_target_pairs={{0,1},{1,0},{2,3},{3,2},{4,5},{5,4},{6,7},{7,6},{8,9},{9,8},{10,11... | collective-permute-start | bytes 589832 | tf_op jit(solution)/shard_map/ppermute | solution.py:404
  72.1 6.6 %collective-permute-start.24 = (f32[64,384]{1,0:T(8,128)S(1)}, f32[64,384]{1,0:T(8,128)S(1)}, u32[]{:S(2)}, u32[]{:S(2)}) collective-permute-start(f32[64,384]{1,0:T(8,128)S(1)} %get-tuple-element.57.v2.own), channel_id=1, source_target_pairs={{0,14},{2,0},{4,2},{6,4},{8,6},{10,8},{12,10},{14,12},{1,15},{3,1}... | collective-permute-start | bytes 294920 | tf_op jit(solution)/shard_map/ppermute | solution.py:404
  74.9 4.9 %collective-permute-start.25 = (f32[64,384]{1,0:T(8,128)S(1)}, f32[64,384]{1,0:T(8,128)S(1)}, u32[]{:S(2)}, u32[]{:S(2)}) collective-permute-start(f32[64,384]{1,0:T(8,128)S(1)} %get-tuple-element.57.v2.own), channel_id=1, source_target_pairs={{0,12},{2,14},{4,0},{6,2},{8,4},{10,6},{12,8},{14,10},{1,13},{3,15... | collective-permute-start | bytes 294920 | tf_op jit(solution)/shard_map/ppermute | solution.py:404
  75.5 1.1 copy-start.10
  76.6 1.1 copy-start.13
  78.1 1.7 %copy-start.7 = (bf16[768,384]{1,0:T(8,128)(2,1)S(1)}, bf16[768,384]{1,0:T(8,128)(2,1)}, u32[]{:S(2)}) copy-start(bf16[768,384]{1,0:T(8,128)(2,1)} %copy-done.6) | copy-start | bytes 1769476
  81.2 1.3 %collective-permute-start.26 = (f32[56,128]{1,0:T(8,128)S(1)}, f32[56,128]{1,0:T(8,128)S(1)}, u32[]{:S(2)}, u32[]{:S(2)}) collective-permute-start(f32[56,128]{1,0:T(8,128)S(1)} %get-tuple-element.61), channel_id=1, source_target_pairs={{0,1},{1,0},{2,3},{3,2},{4,5},{5,4},{6,7},{7,6},{8,9},{9,8},{10,11... | collective-permute-start | bytes 86024 | tf_op jit(solution)/shard_map/ppermute | solution.py:404
  82.5 3.9 %collective-permute-start.27 = (f32[56,128]{1,0:T(8,128)S(1)}, f32[56,128]{1,0:T(8,128)S(1)}, u32[]{:S(2)}, u32[]{:S(2)}) collective-permute-start(f32[56,128]{1,0:T(8,128)S(1)} %add.27), channel_id=1, source_target_pairs={{0,2},{2,0},{4,6},{6,4},{8,10},{10,8},{12,14},{14,12},{1,3},{3,1},... | collective-permute-start | bytes 86024 | tf_op jit(solution)/shard_map/ppermute | solution.py:411
  86.4 3.9 %collective-permute-start.28 = (f32[56,128]{1,0:T(8,128)S(1)}, f32[56,128]{1,0:T(8,128)S(1)}, u32[]{:S(2)}, u32[]{:S(2)}) collective-permute-start(f32[56,128]{1,0:T(8,128)S(1)} %add.28), channel_id=1, source_target_pairs={{0,4},{2,6},{4,0},{6,2},{8,12},{10,14},{12,8},{14,10},{1,5},{3,7},... | collective-permute-start | bytes 86024 | tf_op jit(solution)/shard_map/ppermute | solution.py:411
  90.2 4.8 %collective-permute-start.29 = (f32[56,128]{1,0:T(8,128)S(1)}, f32[56,128]{1,0:T(8,128)S(1)}, u32[]{:S(2)}, u32[]{:S(2)}) collective-permute-start(f32[56,128]{1,0:T(8,128)S(1)} %add.29), channel_id=1, source_target_pairs={{0,8},{2,10},{4,12},{6,14},{8,0},{10,2},{12,4},{14,6},{1,9},{3,11}... | collective-permute-start | bytes 86024 | tf_op jit(solution)/shard_map/ppermute | solution.py:411
  95.0 1.2 %collective-permute-start.30 = (f32[56,128]{1,0:T(8,128)S(1)}, f32[56,128]{1,0:T(8,128)S(1)}, u32[]{:S(2)}, u32[]{:S(2)}) collective-permute-start(f32[56,128]{1,0:T(8,128)S(1)} %add.30.refs_2_), channel_id=1, source_target_pairs={{0,1},{1,0},{2,3},{3,2},{4,5},{5,4},{6,7},{7,6},{8,9},{9,8},{10,11... | collective-permute-start | bytes 86024 | tf_op jit(solution)/shard_map/ppermute | solution.py:404

commit v5 on v4

--- a/solution.py
+++ b/solution.py
@@ -55,57 +55,49 @@
     return dot(jnp.ones((8, 128), F32), folded, 1, 1)
 
 
-def fill_tile(weight, row_embs, row_sqs, col_emb, high, low, row_sum):
+def fill_tile(weight, row_embs, row_sq, col_emb, high, low, row_sum):
     size = col_emb.shape[0]
     col32 = col_emb.astype(F32)
     col_sq = (2.0 * LOG2_E) * sums_along(col32 * col32)[0:1, :]
     total = jnp.zeros((1, size), F32)
     for half in range(2):
+        rows = slice(half * size, (half + 1) * size)
         inner = dot(row_embs[half], col_emb, 1, 1)
-        tile = jnp.exp2((4.0 * LOG2_E) * inner - (row_sqs[half] + col_sq)) * weight
+        squares = jnp.concatenate([row_sq[rows, :]] * (size // 128), axis=1)
+        tile = jnp.exp2((4.0 * LOG2_E) * inner - (squares + col_sq)) * weight
         tile_high, tile_low = halves(tile)
-        high[half * size:(half + 1) * size, :] = tile_high
-        low[half * size:(half + 1) * size, :] = tile_low
+        high[rows, :] = tile_high
+        low[rows, :] = tile_low
         row_sum[half * 8:(half + 1) * 8, :] = row_sum[half * 8:(half + 1) * 8, :] + sums_along(tile)
         total = total + jnp.sum(tile, axis=0, keepdims=True)
     return jnp.broadcast_to(total, (8, size))
 
 
-def own_body(own, other, high, low, row_sum, row_sq, copy):
+def own_body(own, other, high, low, row_sum, row_sq):
     size = own.shape[0]
     embs = [own[...], other[...]]
-    copy[...] = embs[0]
-    sqs = []
     for half in range(2):
         row32 = embs[half].astype(F32)
-        sqs.append((2.0 * LOG2_E) * jnp.sum(row32 * row32, axis=1, keepdims=True))
-        row_sq[half * size:(half + 1) * size, :] = jnp.broadcast_to(sqs[half], (size, 128))
+        squares = (2.0 * LOG2_E) * jnp.sum(row32 * row32, axis=1, keepdims=True)
+        row_sq[half * size:(half + 1) * size, :] = jnp.broadcast_to(squares, (size, 128))
     row_sum[...] = jnp.zeros(row_sum.shape, F32)
-    fill_tile(1.0, embs, sqs, embs[0], high, low, row_sum)
-
-
-def stored_squares(row_sq, size):
-    return [row_sq[half * size:(half + 1) * size, 0:1] for half in range(2)]
-
-
-def near_body(count, keep, own, other, row_sq, *refs):
-    size = own.shape[0]
-    col = jnp.concatenate([ref[...] for ref in refs[:count]], axis=0)
-    before, high, low, row_sum, col_sum = refs[count:]
+    fill_tile(1.0, embs, row_sq, embs[0], high, low, row_sum)
+
+
+def far_body(keep, own, other, row_sq, col, before, seeds, near_seeds,
+             high, low, row_sum, col_sum, seeds_out, near_seeds_out):
     row_sum[...] = before[...]
-    col_sum[...] = fill_tile(keep[0].astype(F32), [own[...], other[...]], stored_squares(row_sq, size),
-                             col, high, low, row_sum)
-
-
-def relayed_body(count, keep, odd, own, other, row_sq, direct, *refs):
-    size = own.shape[0]
-    relayed = jnp.concatenate([ref[...] for ref in refs[:count]], axis=0)
-    col = jnp.where(odd[0] > 0, relayed, direct[...])
-    before, behind, high, low, row_sum, col_sum = refs[count:]
-    row_sum[:8, :] = before[:8, :] + behind[...]
-    row_sum[8:, :] = before[8:, :]
-    col_sum[...] = fill_tile(keep[0].astype(F32), [own[...], other[...]], stored_squares(row_sq, size),
-                             col, high, low, row_sum)
+    col_sum[...] = fill_tile(keep[0].astype(F32), [own[...], other[...]], row_sq, col[...], high, low, row_sum)
+    seeds_out[...] = seeds[...].astype(jnp.int32).astype(F32) / 1000.0
+    near_seeds_out[...] = near_seeds[...].astype(jnp.int32).astype(F32) / 1000.0
+
+
+def relayed_body(keep, choice, own, other, row_sq, direct, relayed, before, first_cols,
+                 high, low, row_sum, col_sum):
+    row_sum[...] = before[...]
+    col = jnp.where(choice[0] > 0, relayed[...], direct[...])
+    col_sum[:8, :] = first_cols[...]
+    col_sum[8:, :] = fill_tile(keep[0].astype(F32), [own[...], other[...]], row_sq, col, high, low, row_sum)
 
 
 def make_tile(body, args, rows, smem=(), extra=()):
@@ -115,30 +107,36 @@
     )
 
 
-def degree_body(sums, behind, other_sums, seed, other_seed, degree_out, scale_out, own_out, other_out):
-    top = sums[:8, :] + behind[...] + other_sums[8:, :]
-    bottom = sums[8:, :] + other_sums[:8, :]
-    degree_out[:8, :] = top
-    degree_out[8:, :] = bottom
-    scale = lax.rsqrt(top)
+def swapped(values):
+    middle = values.shape[0] // 2
+    return jnp.concatenate([values[middle:], values[:middle]], axis=0)
+
+
+def per_row(values, width):
+    shape = (width, values.shape[1])
+    return jnp.concatenate([jnp.broadcast_to(values[i:i + 1, :], shape) for i in (0, 8)], axis=0)
+
+
+def degree_body(sums, other_sums, seeds, degree_out, scale_out, vectors_out):
+    degree = sums[...] + swapped(other_sums[...])
+    scale = lax.rsqrt(degree)
+    degree_out[...] = degree
     scale_out[...] = scale
-    own_out[...] = seed[...] * scale[0:1, :]
-    other_out[...] = other_seed[...] * lax.rsqrt(bottom)[0:1, :]
-
-
-def ahead_body(own, other, h1, l1, h2, l2, ahead1, ahead2):
-    width = own.shape[0]
-    high, low = halves(jnp.concatenate([own[...], other[...]], axis=1))
+    vectors_out[...] = seeds[...] * per_row(scale, seeds.shape[0] // 2)
+
+
+def ahead_body(vectors, h1, l1, h2, l2, ahead):
+    width = vectors.shape[0] // 2
+    high, low = halves(jnp.concatenate([vectors[:width, :], vectors[width:, :]], axis=1))
     both = jnp.concatenate([high, low], axis=0)
-    for tile_high, tile_low, out in ((h1, l1, ahead1), (h2, l2, ahead2)):
+    for half, (tile_high, tile_low) in enumerate(((h1, l1), (h2, l2))):
         product = dot(both, tile_high[...])
-        out[...] = product[:width] + product[width:] + dot(high, tile_low[...])
-
-
-def combine_body(total, other_total, degree, own_out, other_out):
-    width = total.shape[0] // 2
-    own_out[...] = (total[:width, :] + other_total[width:, :]) / degree[0:1, :]
-    other_out[...] = (total[width:, :] + other_total[:width, :]) / degree[8:9, :]
+        product = product[:width] + product[width:] + dot(high, tile_low[...])
+        ahead[half * width:(half + 1) * width, :] = product
+
+
+def combine_body(total, other_total, degree, vectors_out):
+    vectors_out[...] = (total[...] + swapped(other_total[...])) / per_row(degree[...], total.shape[0] // 2)
 
 
 def product_rows(vectors, tile_high, tile_low):
@@ -149,29 +147,33 @@
     return product[:width] + product[width:] + dot(high, tile_low[...], 1, 1)
 
 
-def own_product_body(own, h0, l0, out):
-    out[...] = product_rows(own[...], h0, l0)
-
-
-def add_blocks(product, near1, near2, q1, q2, h1, l1, h2, l2, total):
-    width, size = near1.shape
-    product = product[...] + product_rows(near1, h1, l1) + product_rows(near2, h2, l2)
-    total[:width, :] = product[:, :size] + q1[...] + q2[...]
-    total[width:, :] = product[:, size:]
-
-
-def first_block_body(product, seed1, seed2, scale1, scale2, *refs):
-    add_blocks(product, seed1[...] * scale1[0:1, :], seed2[...] * scale2[0:1, :], *refs)
-
-
-def block_body(product, near1, near2, *refs):
-    add_blocks(product, near1[...], near2[...], *refs)
+def stacked(product):
+    size = product.shape[1] // 2
+    return jnp.concatenate([product[:, :size], product[:, size:]], axis=0)
+
+
+def own_product_body(vectors, h0, l0, out):
+    out[...] = stacked(product_rows(vectors[:vectors.shape[0] // 2, :], h0, l0))
+
+
+def add_blocks(product, near, behind, h1, l1, h2, l2, total):
+    width = near.shape[0] // 2
+    far = product_rows(near[:width], h1, l1) + product_rows(near[width:], h2, l2)
+    total[...] = product[...] + behind[...] + stacked(far)
+
+
+def first_block_body(product, near_seeds, near_scale, *refs):
+    add_blocks(product, near_seeds[...] * per_row(near_scale[...], near_seeds.shape[0] // 2), *refs)
+
+
+def block_body(product, near, *refs):
+    add_blocks(product, near[...], *refs)
 
 
 def low_body(degree, v0, v1, v2, moments, scaled):
-    width = v0.shape[0]
+    width = v0.shape[0] // 2
     root = jnp.sqrt(degree[0:1, :])
-    x0, x1, x2 = v0[...] * root, v1[...] * root, v2[...] * root
+    x0, x1, x2 = v0[:width, :] * root, v1[:width, :] * root, v2[:width, :] * root
     scaled[...] = jnp.concatenate([x0, x1, x2], axis=0)
     left = jnp.concatenate([x0, x1], axis=0)
     order012 = dot(left, left, 1, 1)
@@ -186,11 +188,11 @@
     return [lax.broadcasted_iota(jnp.int32, (rows, cols), axis) for axis in range(2)]
 
 
-def moment_body(core, low, own, other, product, near1, near2, h1, l1, h2, l2, mine, theirs):
-    n = own.shape[0]
-    last = product_rows(near1[...], h1, l1) + product_rows(near2[...], h2, l2)
-    last = 2.0 * last + product[...]
-    last = dot(jnp.concatenate([own[...], other[...]], axis=1), last, 1, 1)
+def moment_body(core, low, vectors, product, near, h1, l1, h2, l2, mine, theirs):
+    n = vectors.shape[0] // 2
+    last = product_rows(near[:n, :], h1, l1) + product_rows(near[n:, :], h2, l2)
+    last = 2.0 * last + jnp.concatenate([product[:n, :], product[n:, :]], axis=1)
+    last = dot(jnp.concatenate([vectors[:n, :], vectors[n:, :]], axis=1), last, 1, 1)
     moments = [low[i * n:(i + 1) * n, :] for i in range(5)] + [0.5 * (last + last.T)]
     row, col = place_of(n, n)
     pieces = []
@@ -399,9 +401,14 @@
     out[...] = dense(unpacked(packed, NVEC), index[0], rows, scaled[...])
 
 
-def moved(shard, axis, by):
-    length = lax.axis_size(axis)
-    return lax.ppermute(shard, axis, [(i, (i + by) % length) for i in range(length)])
+def between_blocks(shard, sign):
+    blocks, cores = lax.axis_size("blk"), lax.axis_size("narrow")
+    pairs = [(i * cores + j, (i + sign * (1 + j)) % blocks * cores + j) for i in range(blocks) for j in range(cores)]
+    return lax.ppermute(shard, ("blk", "narrow"), pairs)
+
+
+def between_cores(shard):
+    return lax.ppermute(shard, "narrow", [(0, 1), (1, 0)])
 
 
 def total_over_blocks(values):
@@ -422,66 +429,60 @@
     blocks = lax.axis_size("blk")
     where = lax.axis_index("blk")
     core = lax.axis_index("narrow").astype(jnp.int32).reshape(1)
-    chunk = 128 if size % 128 == 0 else size
-    count = size // chunk
-    other_emb = moved(embeddings, "narrow", 1)
-    near2 = [moved(embeddings[i * chunk:(i + 1) * chunk], "blk", -2) for i in range(count)]
-    keep = lax.dynamic_slice_in_dim(pair_mask, where, 1, 0)[0]
+    other_emb = between_cores(embeddings)
+    far_emb = between_blocks(embeddings, -1)
+    pairs = [(2 * i, (i - 2) % blocks * 2 + 1) for i in range(blocks)]
+    pairs += [(2 * i + 1, (i - 1) % blocks * 2) for i in range(blocks) if blocks % 2 or i % 2]
+    direct = lax.ppermute(embeddings, ("blk", "narrow"), pairs)
+    choice = (1 - core) * (where % 2 * (1 - blocks % 2)).astype(jnp.int32)
+    keep = lax.dynamic_slice(pair_mask, (where, core[0]), (1, 1))[0]
     seed16 = start_seed.astype(jnp.int16).T
-    seeds = [seed16, moved(seed16, "narrow", 1), moved(seed16, "blk", -1), moved(seed16, "blk", -2)]
-    seed, other_seed, seed1, seed2 = [part.astype(F32) / 1000.0 for part in seeds]
+    seeds16 = jnp.concatenate([seed16, between_cores(seed16)], axis=0)
+    near_seeds16 = between_blocks(seeds16, -1)
 
     emb_args = [embeddings, other_emb]
-    h0, l0, sums, row_sq, own_copy = make_tile(
-        own_body, emb_args, size, extra=(((2 * size, 128), F32), (embeddings.shape, BF16)))
+    pair_shape, row_shape = ((2 * NVEC, size), F32), ((16, size), F32)
+    h0, l0, sums, row_sq = make_tile(own_body, emb_args, size, extra=(((2 * size, 128), F32),))
+    far_emb, sums, near_seeds16 = lax.optimization_barrier((far_emb, sums, near_seeds16))
+    relayed = direct
     if blocks % 2 == 0:
-        direct = lax.ppermute(own_copy, "blk", [(i, i - 1) for i in range(1, blocks, 2)])
-        relayed = [lax.ppermute(part, "blk", [(i, i + 1) for i in range(0, blocks, 2)]) for part in near2]
-    else:
-        direct, relayed = moved(own_copy, "blk", -1), near2
-    odd = (where % 2 * (blocks % 2 == 0)).astype(jnp.int32).reshape(1)
-    col_shape = ((8, size), F32)
-    h2, l2, sums, cols2 = make_tile(
-        lambda *refs: near_body(count, *refs), [keep[1:2], *emb_args, row_sq, *near2, sums], size, (0,), (col_shape,))
-    behind2 = moved(cols2, "blk", 2)
-    h1, l1, sums, cols1 = make_tile(
-        lambda *refs: relayed_body(count, *refs),
-        [keep[0:1], odd, *emb_args, row_sq, direct, *relayed, sums, behind2], size, (0, 1), (col_shape,))
-    behind1 = moved(cols1, "blk", 1)
-    other_sums = moved(sums + jnp.pad(behind1, ((0, 8), (0, 0))), "narrow", 1)
-
-    pair_shape, half_shape = ((2 * NVEC, size), F32), ((NVEC, size), F32)
+        relayed = lax.ppermute(far_emb, ("blk", "narrow"), [(2 * i + 1, 2 * i + 2) for i in range(0, blocks, 2)])
+    h1, l1, sums, cols, seeds, near_seeds = make_tile(
+        far_body, [keep, *emb_args, row_sq, far_emb, sums, seeds16, near_seeds16], size, (0,),
+        (((8, size), F32), pair_shape, pair_shape))
+    h2, l2, sums, cols = make_tile(
+        relayed_body, [keep, choice, *emb_args, row_sq, direct, relayed, sums, cols], size, (0, 1), (row_shape,))
+    sums = sums + between_blocks(cols, 1)
+
     small = dict(flops=10**6, nbytes=10**5)
     middle = dict(flops=10**9, nbytes=10**6)
-    degree, scale, own, other = call(
-        degree_body, [((16, size), F32), col_shape, half_shape, half_shape],
-        [sums, behind1, other_sums, seed, other_seed], **small)
+    degree, scale, vectors = call(
+        degree_body, [row_shape, row_shape, pair_shape], [sums, between_cores(sums), seeds], **small)
     far = [h1, l1, h2, l2]
-    history = [own]
+    history = [vectors]
     for repeat in range(2):
         if repeat == 0:
-            body, near = first_block_body, [seed1, seed2, moved(scale, "blk", -1), moved(scale, "blk", -2)]
+            body, near = first_block_body, [near_seeds, between_blocks(scale, -1)]
         else:
-            body, near = block_body, [moved(own, "blk", -1), moved(own, "blk", -2)]
-        ahead1, ahead2 = call(ahead_body, [half_shape] * 2, [own, other, *far], **middle)
-        q1, q2 = moved(ahead1, "blk", 1), moved(ahead2, "blk", 2)
-        (product,) = call(own_product_body, [((NVEC, 2 * size), F32)], [own, h0, l0], **middle)
-        (total,) = call(body, [pair_shape], [product, *near, q1, q2, *far], **middle)
-        other_total = moved(total, "narrow", 1)
-        own, other = call(combine_body, [half_shape] * 2, [total, other_total, degree], **small)
-        history.append(own)
-    near = [moved(own, "blk", -1), moved(own, "blk", -2)]
+            body, near = block_body, [between_blocks(vectors, -1)]
+        (ahead,) = call(ahead_body, [pair_shape], [vectors, *far], **middle)
+        behind = between_blocks(ahead, 1)
+        (product,) = call(own_product_body, [pair_shape], [vectors, h0, l0], **middle)
+        (total,) = call(body, [pair_shape], [product, *near, behind, *far], **middle)
+        (vectors,) = call(combine_body, [pair_shape], [total, between_cores(total), degree], **small)
+        history.append(vectors)
+    near = between_blocks(vectors, -1)
     low, scaled = call(
         low_body, [((5 * NVEC, NVEC), F32), ((3 * NVEC, size), F32)], [degree] + history, **middle)
-    (product,) = call(own_product_body, [((NVEC, 2 * size), F32)], [own, h0, l0], **middle)
+    (product,) = call(own_product_body, [pair_shape], [vectors, h0, l0], **middle)
     packed_shape = ((3 * NVEC // 4 + 8, 2 * NVEC), F32)
     mine, theirs = call(
-        moment_body, [packed_shape] * 2, [core, low, own, other, product, *near, *far], smem=(0,), **middle)
-    mine = total_over_blocks(mine + moved(theirs, "narrow", 1))
+        moment_body, [packed_shape] * 2, [core, low, vectors, product, near, *far], smem=(0,), **middle)
+    mine = total_over_blocks(mine + between_cores(theirs))
     rows = size * blocks * lax.axis_size("narrow")
     (out,) = call(
-        lambda *refs: dense_body(rows, *refs), [half_shape],
-        [core, shift_index, mine, moved(mine, "narrow", 1), scaled], smem=(0, 1), flops=2 * 10**10, nbytes=10**6,
+        lambda *refs: dense_body(rows, *refs), [((NVEC, size), F32)],
+        [core, shift_index, mine, between_cores(mine), scaled], smem=(0, 1), flops=2 * 10**10, nbytes=10**6,
     )
     return out.T
 

time: 120 us -> 120 us (level)
  waiting for transfers between devices: 27.2 us -> 44.9 us
  starting transfers between devices: 45 us -> 31 us
  local copies, waits for them, and re-layouts: 8.98 us -> 5.41 us
    ppermute x28 -> x17, waiting for transfers between devices: 18.9 us -> 34.7 us  [the longest x8 28.9 us: between_blocks(): return lax.ppermute(shard, ('blk', 'narrow'), pairs)]
    ppermute x28 -> x17, starting transfers between devices: 40.8 us -> 28.7 us  [the longest x8 24.9 us: between_blocks(): return lax.ppermute(shard, ('blk', 'narrow'), pairs)]
    slice x2 -> x0, local copies, waits for them, and re-layouts: 2.39 us -> none  [the longest x1 1.84 us: shards(): embeddings[i * chunk:(i + 1) * chunk]]
    ppermute x3, starting transfers between devices: 4.2 us -> 2.27 us  [total_over_blocks(): other = lax.ppermute(values, 'blk', [(i, i ^ span) for i in range(blocks)])]
    ppermute x3, waiting for transfers between devices: 8.31 us -> 10.2 us  [total_over_blocks(): other = lax.ppermute(values, 'blk', [(i, i ^ span) for i in range(blocks)])]
    unnamed x34 -> x18, local copies, waits for them, and re-layouts: 6.51 us -> 4.8 us
  transfers between devices with their start and end apart: 31 -> 20, of which waited for: 16 -> 14; matrix products, arithmetic and copies ran while one was open for 2% -> 1% of each run, Pallas kernels for 9% -> 5%
where the time goes in v5:
time: 120 us
  waiting for transfers between devices  44.9 us (37%)
  Pallas kernels  36.7 us (31%)
  starting transfers between devices  31 us (26%)
  local copies, waits for them, and re-layouts  5.41 us (5%)
    pallas_call x16, Pallas kernels, call(): pl.pallas_call(body, out_shape=[jax.ShapeDtypeStruct(shape, dtype) for sh...  36.7 us
    ppermute x8, waiting for transfers between devices, between_blocks(): return lax.ppermute(shard, ('blk', 'narrow'), pairs)  28.9 us
    ppermute x8, starting transfers between devices, between_blocks(): return lax.ppermute(shard, ('blk', 'narrow'), pairs)  24.9 us
    ppermute x3, waiting for transfers between devices, total_over_blocks(): other = lax.ppermute(values, 'blk', [(i, i ^ span) for i in range(blocks)])  10.2 us
    ppermute x7, waiting for transfers between devices, between_cores(): return lax.ppermute(shard, 'narrow', [(0, 1), (1, 0)])  5.79 us
    unnamed x18, local copies, waits for them, and re-layouts  4.8 us
    ppermute x1, starting transfers between devices, shards(): direct = lax.ppermute(embeddings, ('blk', 'narrow'), pairs)  2.45 us
  transfers between devices with their start and end apart: 20, of which 14 were waited for; matrix products, arithmetic and copies ran while one was open for 1% of the time, Pallas kernels for 5%

profile of v5, /device:TPU:0, one launch (start us, length us, event | category | flops | bytes accessed | tf_op | source)
XLA Modules:
  0.0 119.8 jit_solution(16987098880474796119)
XLA Ops:
  0.0 0.5 collective-permute-start
  0.5 5.5 %collective-permute-start.2 = (bf16[384,768]{1,0:T(8,128)(2,1)}, bf16[384,768]{1,0:T(8,128)(2,1)S(1)}, u32[]{:S(2)}, u32[]{:S(2)}) collective-permute-start(bf16[384,768]{1,0:T(8,128)(2,1)} %own.5), channel_id=1, source_target_pairs={{0,14},{1,13},{2,0},{3,15},{4,2},{5,1},{6,4},{7,3},{8,6},{9,5},{10... | collective-permute-start | bytes 1769480 | tf_op jit(solution)/shard_map/ppermute | solution.py:407
  6.0 0.9 convert_bitcast_fusion
  6.9 2.5 %collective-permute-start.1 = (bf16[384,768]{1,0:T(8,128)(2,1)}, bf16[384,768]{1,0:T(8,128)(2,1)S(1)}, u32[]{:S(2)}, u32[]{:S(2)}) collective-permute-start(bf16[384,768]{1,0:T(8,128)(2,1)} %own.5), channel_id=1, source_target_pairs={{0,13},{2,15},{4,1},{6,3},{8,5},{10,7},{12,9},{14,11},{3,0},{7,4},... | collective-permute-start | bytes 1769480 | tf_op jit(solution)/shard_map/ppermute | solution.py:436
  9.4 0.6 collective-permute-start.4
  10.0 1.1 copy-done
  11.1 1.9 %shard_map.46 = (bf16[768,384]{1,0:T(8,128)(2,1)S(1)}, bf16[768,384]{1,0:T(8,128)(2,1)S(1)}, f32[16,384]{1,0:T(8,128)S(1)}, f32[768,128]{1,0:T(8,128)S(1)}) custom-call(bf16[384,768]{1,0:T(8,128)(2,1)S(1)} %copy-done, bf16[384,768]{1,0:T(8,128)(2,1)S(1)} %collective-permute-done.other), custom_call_target="tpu_custom_call" | custom-call | flops 2000000000 | bytes 1000000 | tf_op jit(solution)/shard_map/pallas_call | solution.py:36
  12.9 0.8 copy-done.2
  13.8 0.9 copy-done.4
  14.6 0.6 copy-done.6
  15.2 11.7 %collective-permute-done.4.near_seeds = s16[128,384]{1,0:T(8,128)(2,1)S(1)} collective-permute-done((s16[128,384]{1,0:T(8,128)(2,1)S(1)}, s16[128,384]{1,0:T(8,128)(2,1)S(1)}, u32[]{:S(2)}, u32[]{:S(2)}) %collective-permute-start.4) | collective-permute-done | bytes 98336 | tf_op jit(solution)/shard_map/ppermute | solution.py:407
  27.0 0.7 collective-permute-start.5
  27.7 0.7 copy-done.8
  28.3 0.6 dynamic_slice.3
  29.0 0.7 copy-done.7
  29.7 2.6 %shard_map.47 = (bf16[768,384]{1,0:T(8,128)(2,1)S(1)}, bf16[768,384]{1,0:T(8,128)(2,1)S(1)}, f32[16,384]{1,0:T(8,128)S(1)}, f32[8,384]{1,0:T(8,128)S(1)}, f32[12...) custom-call(s32[1]{0:T(128)} %bitcast.1.keep, bf16[384,768]{1,0:T(8,128)(2,1)S(1)} %copy-done.1, ...), custom_call_target="tpu_custom_call" | custom-call | flops 2000000000 | bytes 1000000 | tf_op jit(solution)/shard_map/pallas_call | solution.py:36
  32.3 2.6 %shard_map.48 = (bf16[768,384]{1,0:T(8,128)(2,1)S(1)}, bf16[768,384]{1,0:T(8,128)(2,1)S(1)}, f32[16,384]{1,0:T(8,128)S(1)}, f32[16,384]{1,0:T(8,128)S(1)}) custom-call(s32[1]{0:T(128)} %bitcast.1.keep, s32[1]{0:T(128)S(6)} %mul.7.choice, bf16[384,768]{1,0:T(8,128)(2,1)S(1)} %copy-done.1, bf16[384,768]{1,0:T(8,128)(2,1)S(1)} %collective-permute-done.other, ...), custom_call_target="tpu_custom_call" | custom-call | flops 2000000000 | bytes 1000000 | tf_op jit(solution)/shard_map/pallas_call | solution.py:36
  34.9 6.1 %collective-permute-start.6 = (f32[16,384]{1,0:T(8,128)S(1)}, f32[16,384]{1,0:T(8,128)S(1)}, u32[]{:S(2)}, u32[]{:S(2)}) collective-permute-start(f32[16,384]{1,0:T(8,128)S(1)} %get-tuple-element.37), channel_id=1, source_target_pairs={{0,2},{1,5},{2,4},{3,7},{4,6},{5,9},{6,8},{7,11},{8,10},{9,13},{10... | collective-permute-start | bytes 73736 | tf_op jit(solution)/shard_map/ppermute | solution.py:407
  40.9 6.8 %collective-permute-done.6 = f32[16,384]{1,0:T(8,128)S(1)} collective-permute-done((f32[16,384]{1,0:T(8,128)S(1)}, f32[16,384]{1,0:T(8,128)S(1)}, u32[]{:S(2)}, u32[]{:S(2)}) %collective-permute-start.6) | collective-permute-done | bytes 24608 | tf_op jit(solution)/shard_map/ppermute | solution.py:407
  47.7 1.2 collective-permute-done.7.other_sums
  49.0 0.5 shard_map.51
  49.6 4.7 %collective-permute-start.8 = (f32[16,384]{1,0:T(8,128)S(1)}, f32[16,384]{1,0:T(8,128)S(1)}, u32[]{:S(2)}, u32[]{:S(2)}) collective-permute-start(f32[16,384]{1,0:T(8,128)S(1)} %get-tuple-element.44), channel_id=1, source_target_pairs={{0,14},{1,13},{2,0},{3,15},{4,2},{5,1},{6,4},{7,3},{8,6},{9,5},{10... | collective-permute-start | bytes 73736 | tf_op jit(solution)/shard_map/ppermute | solution.py:407
  54.3 0.5 shard_map.50.product
  54.8 1.0 collective-permute-done.8.near_scale
  55.8 2.1 %collective-permute-done.9.refs_0_ = f32[128,384]{1,0:T(8,128)S(1)} collective-permute-done((f32[128,384]{1,0:T(8,128)S(1)}, f32[128,384]{1,0:T(8,128)S(1)}, u32[]{:S(2)}, u32[]{:S(2)}) %collective-permute-start.9) | collective-permute-done | bytes 196640 | tf_op jit(solution)/shard_map/ppermute | solution.py:407
  57.9 0.8 shard_map.52.total
  58.8 0.1 collective-permute-start.10
  58.8 1.4 %collective-permute-done.10.other_total = f32[128,384]{1,0:T(8,128)S(1)} collective-permute-done((f32[128,384]{1,0:T(8,128)S(1)}, f32[128,384]{1,0:T(8,128)S(1)}, u32[]{:S(2)}, u32[]{:S(2)}) %collective-permute-start.10) | collective-permute-done | bytes 196640 | tf_op jit(solution)/shard_map/ppermute | solution.py:411
  60.3 0.5 shard_map.55
  60.9 4.7 %collective-permute-start.11 = (f32[128,384]{1,0:T(8,128)S(1)}, f32[128,384]{1,0:T(8,128)S(1)}, u32[]{:S(2)}, u32[]{:S(2)}) collective-permute-start(f32[128,384]{1,0:T(8,128)S(1)} %shard_map.53.vectors.v1), channel_id=1, source_target_pairs={{0,14},{1,13},{2,0},{3,15},{4,2},{5,1},{6,4},{7,3},{8,6},{9,5},{10... | collective-permute-start | bytes 589832 | tf_op jit(solution)/shard_map/ppermute | solution.py:407
  65.6 0.5 shard_map.54.product
  66.1 5.0 %collective-permute-done.12.refs_0_ = f32[128,384]{1,0:T(8,128)S(1)} collective-permute-done((f32[128,384]{1,0:T(8,128)S(1)}, f32[128,384]{1,0:T(8,128)S(1)}, u32[]{:S(2)}, u32[]{:S(2)}) %collective-permute-start.12) | collective-permute-done | bytes 196640 | tf_op jit(solution)/shard_map/ppermute | solution.py:407
  71.1 0.8 shard_map.56.total
  71.9 0.1 collective-permute-start.13
  72.0 1.4 %collective-permute-done.13.other_total = f32[128,384]{1,0:T(8,128)S(1)} collective-permute-done((f32[128,384]{1,0:T(8,128)S(1)}, f32[128,384]{1,0:T(8,128)S(1)}, u32[]{:S(2)}, u32[]{:S(2)}) %collective-permute-start.13) | collective-permute-done | bytes 196640 | tf_op jit(solution)/shard_map/ppermute | solution.py:411
  73.5 3.2 %collective-permute-start.14 = (f32[128,384]{1,0:T(8,128)S(1)}, f32[128,384]{1,0:T(8,128)S(1)}, u32[]{:S(2)}, u32[]{:S(2)}) collective-permute-start(f32[128,384]{1,0:T(8,128)S(1)} %shard_map.57.v2.vectors), channel_id=1, source_target_pairs={{0,14},{1,13},{2,0},{3,15},{4,2},{5,1},{6,4},{7,3},{8,6},{9,5},{10... | collective-permute-start | bytes 589832 | tf_op jit(solution)/shard_map/ppermute | solution.py:407
  76.6 0.5 shard_map.59.product
  77.1 0.5 shard_map.58
  77.7 2.2 %collective-permute-done.14.near = f32[128,384]{1,0:T(8,128)S(1)} collective-permute-done((f32[128,384]{1,0:T(8,128)S(1)}, f32[128,384]{1,0:T(8,128)S(1)}, u32[]{:S(2)}, u32[]{:S(2)}) %collective-permute-start.14) | collective-permute-done | bytes 196640 | tf_op jit(solution)/shard_map/ppermute | solution.py:407
  79.8 1.4 %shard_map.60 = (f32[56,128]{1,0:T(8,128)S(1)}, f32[56,128]{1,0:T(8,128)S(1)}) custom-call(s32[1]{0:T(128)} %bitcast.core.refs_0_, f32[320,64]{1,0:T(8,128)S(1)} %get-tuple-element.49.low, f32[128,384]{1,0:T(8,128)S(1)} %shard_map.57.v2.vectors, f32[128,384]{1,0:T(8,128)S(1)} %shard_map.59.product, f32[128,384]{1,0:T(8,128)S(1)} %collective-permute-done.14.near, ...), custom_call_target="tpu_custom_call" | custom-call | flops 1000000000 | bytes 1000000 | tf_op jit(solution)/shard_map/pallas_call | solution.py:36
  81.2 0.1 collective-permute-start.15
  81.3 1.2 collective-permute-done.15
  82.5 3.9 %collective-permute-done.16 = f32[56,128]{1,0:T(8,128)S(1)} collective-permute-done((f32[56,128]{1,0:T(8,128)S(1)}, f32[56,128]{1,0:T(8,128)S(1)}, u32[]{:S(2)}, u32[]{:S(2)}) %collective-permute-start.16) | collective-permute-done | bytes 28704 | tf_op jit(solution)/shard_map/ppermute | solution.py:418
  86.4 3.9 %collective-permute-done.17 = f32[56,128]{1,0:T(8,128)S(1)} collective-permute-done((f32[56,128]{1,0:T(8,128)S(1)}, f32[56,128]{1,0:T(8,128)S(1)}, u32[]{:S(2)}, u32[]{:S(2)}) %collective-permute-start.17) | collective-permute-done | bytes 28704 | tf_op jit(solution)/shard_map/ppermute | solution.py:418
  90.2 2.3 %collective-permute-start.18 = (f32[56,128]{1,0:T(8,128)S(1)}, f32[56,128]{1,0:T(8,128)S(1)}, u32[]{:S(2)}, u32[]{:S(2)}) collective-permute-start(f32[56,128]{1,0:T(8,128)S(1)} %add.31), channel_id=1, source_target_pairs={{0,8},{2,10},{4,12},{6,14},{8,0},{10,2},{12,4},{14,6},{1,9},{3,11}... | collective-permute-start | bytes 86024 | tf_op jit(solution)/shard_map/ppermute | solution.py:418
  92.5 2.5 %collective-permute-done.18 = f32[56,128]{1,0:T(8,128)S(1)} collective-permute-done((f32[56,128]{1,0:T(8,128)S(1)}, f32[56,128]{1,0:T(8,128)S(1)}, u32[]{:S(2)}, u32[]{:S(2)}) %collective-permute-start.18) | collective-permute-done | bytes 28704 | tf_op jit(solution)/shard_map/ppermute | solution.py:418
  95.7 0.5 collective-permute-done.19.refs_3_
  96.2 23.6 %shard_map.61 = f32[64,384]{1,0:T(8,128)} custom-call(s32[1]{0:T(128)} %bitcast.core.refs_0_, s32[1]{0:T(128)S(6)} %copy.5.refs_1_, f32[56,128]{1,0:T(8,128)S(1)} %add.32.refs_2_, f32[56,128]{1,0:T(8,128)S(1)} %collective-permute-done.19.refs_3_, f32[192,384]{1,0:T(8,128)S(1)} %get-tuple-element.52.refs_4_), custom_call_target="tpu_custom_call" | custom-call | flops 20000000000 | bytes 1000000 | tf_op jit(solution)/shard_map/pallas_call | solution.py:36
  (34 shorter events, 0.3 us)
Async XLA Ops:
  0.0 10.0 %collective-permute-start = (bf16[384,768]{1,0:T(8,128)(2,1)}, bf16[384,768]{1,0:T(8,128)(2,1)S(1)}, u32[]{:S(2)}, u32[]{:S(2)}) collective-permute-start(bf16[384,768]{1,0:T(8,128)(2,1)} %own.5), channel_id=1, source_target_pairs={{0,1},{1,0},{2,3},{3,2},{4,5},{5,4},{6,7},{7,6},{8,9},{9,8},{10,11... | collective-permute-start | bytes 1769480 | tf_op jit(solution)/shard_map/ppermute | solution.py:411
  0.5 26.5 %collective-permute-start.2 = (bf16[384,768]{1,0:T(8,128)(2,1)}, bf16[384,768]{1,0:T(8,128)(2,1)S(1)}, u32[]{:S(2)}, u32[]{:S(2)}) collective-permute-start(bf16[384,768]{1,0:T(8,128)(2,1)} %own.5), channel_id=1, source_target_pairs={{0,14},{1,13},{2,0},{3,15},{4,2},{5,1},{6,4},{7,3},{8,6},{9,5},{10... | collective-permute-start | bytes 1769480 | tf_op jit(solution)/shard_map/ppermute | solution.py:407
  6.9 2.5 %collective-permute-start.3 = (s16[64,384]{1,0:T(8,128)(2,1)S(1)}, s16[64,384]{1,0:T(8,128)(2,1)S(1)}, u32[]{:S(2)}, u32[]{:S(2)}) collective-permute-start(s16[64,384]{1,0:T(8,128)(2,1)S(1)} %convert_bitcast_fusion), channel_id=1, source_target_pairs={{0,1},{1,0},{2,3},{3,2},{4,5},{5,4},{6,7},{7,6},{8,9},{9,8},{10,11... | collective-permute-start | bytes 147464 | tf_op jit(solution)/shard_map/ppermute | solution.py:411
  6.9 25.4 %collective-permute-start.1 = (bf16[384,768]{1,0:T(8,128)(2,1)}, bf16[384,768]{1,0:T(8,128)(2,1)S(1)}, u32[]{:S(2)}, u32[]{:S(2)}) collective-permute-start(bf16[384,768]{1,0:T(8,128)(2,1)} %own.5), channel_id=1, source_target_pairs={{0,13},{2,15},{4,1},{6,3},{8,5},{10,7},{12,9},{14,11},{3,0},{7,4},... | collective-permute-start | bytes 1769480 | tf_op jit(solution)/shard_map/ppermute | solution.py:436
  9.4 17.6 %collective-permute-start.4 = (s16[128,384]{1,0:T(8,128)(2,1)S(1)}, s16[128,384]{1,0:T(8,128)(2,1)S(1)}, u32[]{:S(2)}, u32[]{:S(2)}) collective-permute-start(s16[128,384]{1,0:T(8,128)(2,1)S(1)} %pad_add_fusion.seeds), channel_id=1, source_target_pairs={{0,14},{1,13},{2,0},{3,15},{4,2},{5,1},{6,4},{7,3},{8,6},{9,5},{10... | collective-permute-start | bytes 294920 | tf_op jit(solution)/shard_map/ppermute | solution.py:407
  10.0 1.1 copy-start
  11.1 17.9 %copy-start.1 = (bf16[384,768]{1,0:T(8,128)(2,1)S(1)}, bf16[384,768]{1,0:T(8,128)(2,1)}, u32[]{:S(2)}) copy-start(bf16[384,768]{1,0:T(8,128)(2,1)} %own.5) | copy-start | bytes 1769476
  12.9 0.8 copy-start.2
  13.8 0.9 copy-start.4
  14.6 0.6 copy-start.6
  27.0 5.3 %collective-permute-start.5 = (bf16[384,768]{1,0:T(8,128)(2,1)S(1)}, bf16[384,768]{1,0:T(8,128)(2,1)S(1)}, u32[]{:S(2)}, u32[]{:S(2)}) collective-permute-start(bf16[384,768]{1,0:T(8,128)(2,1)S(1)} %collective-permute-done.2.col), channel_id=1, source_target_pairs={{1,2},{5,6},{9,10},{13,14},{17,18},{21,22},{25,26},{29,30}} | collective-permute-start | bytes 1769480 | tf_op jit(solution)/shard_map/ppermute | solution.py:449
  27.7 0.7 copy-start.8
  29.0 0.7 copy-start.7
  34.9 12.9 %collective-permute-start.6 = (f32[16,384]{1,0:T(8,128)S(1)}, f32[16,384]{1,0:T(8,128)S(1)}, u32[]{:S(2)}, u32[]{:S(2)}) collective-permute-start(f32[16,384]{1,0:T(8,128)S(1)} %get-tuple-element.37), channel_id=1, source_target_pairs={{0,2},{1,5},{2,4},{3,7},{4,6},{5,9},{6,8},{7,11},{8,10},{9,13},{10... | collective-permute-start | bytes 73736 | tf_op jit(solution)/shard_map/ppermute | solution.py:407
  47.7 1.2 collective-permute-start.7
  49.0 5.3 %copy-start.3 = (bf16[768,384]{1,0:T(8,128)(2,1)S(1)}, bf16[768,384]{1,0:T(8,128)(2,1)}, u32[]{:S(2)}) copy-start(bf16[768,384]{1,0:T(8,128)(2,1)} %copy-done.2) | copy-start | bytes 1769476
  49.0 5.3 %copy-start.5 = (bf16[768,384]{1,0:T(8,128)(2,1)S(1)}, bf16[768,384]{1,0:T(8,128)(2,1)}, u32[]{:S(2)}) copy-start(bf16[768,384]{1,0:T(8,128)(2,1)} %copy-done.4) | copy-start | bytes 1769476
  49.5 8.4 %collective-permute-start.9 = (f32[128,384]{1,0:T(8,128)S(1)}, f32[128,384]{1,0:T(8,128)S(1)}, u32[]{:S(2)}, u32[]{:S(2)}) collective-permute-start(f32[128,384]{1,0:T(8,128)S(1)} %shard_map.51), channel_id=1, source_target_pairs={{0,2},{1,5},{2,4},{3,7},{4,6},{5,9},{6,8},{7,11},{8,10},{9,13},{10... | collective-permute-start | bytes 589832 | tf_op jit(solution)/shard_map/ppermute | solution.py:407
  49.6 6.2 %collective-permute-start.8 = (f32[16,384]{1,0:T(8,128)S(1)}, f32[16,384]{1,0:T(8,128)S(1)}, u32[]{:S(2)}, u32[]{:S(2)}) collective-permute-start(f32[16,384]{1,0:T(8,128)S(1)} %get-tuple-element.44), channel_id=1, source_target_pairs={{0,14},{1,13},{2,0},{3,15},{4,2},{5,1},{6,4},{7,3},{8,6},{9,5},{10... | collective-permute-start | bytes 73736 | tf_op jit(solution)/shard_map/ppermute | solution.py:407
  58.8 1.5 %collective-permute-start.10 = (f32[128,384]{1,0:T(8,128)S(1)}, f32[128,384]{1,0:T(8,128)S(1)}, u32[]{:S(2)}, u32[]{:S(2)}) collective-permute-start(f32[128,384]{1,0:T(8,128)S(1)} %shard_map.52.total), channel_id=1, source_target_pairs={{0,1},{1,0},{2,3},{3,2},{4,5},{5,4},{6,7},{7,6},{8,9},{9,8},{10,11... | collective-permute-start | bytes 589832 | tf_op jit(solution)/shard_map/ppermute | solution.py:411
  60.8 10.3 %collective-permute-start.12 = (f32[128,384]{1,0:T(8,128)S(1)}, f32[128,384]{1,0:T(8,128)S(1)}, u32[]{:S(2)}, u32[]{:S(2)}) collective-permute-start(f32[128,384]{1,0:T(8,128)S(1)} %shard_map.55), channel_id=1, source_target_pairs={{0,2},{1,5},{2,4},{3,7},{4,6},{5,9},{6,8},{7,11},{8,10},{9,13},{10... | collective-permute-start | bytes 589832 | tf_op jit(solution)/shard_map/ppermute | solution.py:407
  60.9 10.2 %collective-permute-start.11 = (f32[128,384]{1,0:T(8,128)S(1)}, f32[128,384]{1,0:T(8,128)S(1)}, u32[]{:S(2)}, u32[]{:S(2)}) collective-permute-start(f32[128,384]{1,0:T(8,128)S(1)} %shard_map.53.vectors.v1), channel_id=1, source_target_pairs={{0,14},{1,13},{2,0},{3,15},{4,2},{5,1},{6,4},{7,3},{8,6},{9,5},{10... | collective-permute-start | bytes 589832 | tf_op jit(solution)/shard_map/ppermute | solution.py:407
  71.9 1.5 %collective-permute-start.13 = (f32[128,384]{1,0:T(8,128)S(1)}, f32[128,384]{1,0:T(8,128)S(1)}, u32[]{:S(2)}, u32[]{:S(2)}) collective-permute-start(f32[128,384]{1,0:T(8,128)S(1)} %shard_map.56.total), channel_id=1, source_target_pairs={{0,1},{1,0},{2,3},{3,2},{4,5},{5,4},{6,7},{7,6},{8,9},{9,8},{10,11... | collective-permute-start | bytes 589832 | tf_op jit(solution)/shard_map/ppermute | solution.py:411
  73.5 6.4 %collective-permute-start.14 = (f32[128,384]{1,0:T(8,128)S(1)}, f32[128,384]{1,0:T(8,128)S(1)}, u32[]{:S(2)}, u32[]{:S(2)}) collective-permute-start(f32[128,384]{1,0:T(8,128)S(1)} %shard_map.57.v2.vectors), channel_id=1, source_target_pairs={{0,14},{1,13},{2,0},{3,15},{4,2},{5,1},{6,4},{7,3},{8,6},{9,5},{10... | collective-permute-start | bytes 589832 | tf_op jit(solution)/shard_map/ppermute | solution.py:407
  81.2 1.3 %collective-permute-start.15 = (f32[56,128]{1,0:T(8,128)S(1)}, f32[56,128]{1,0:T(8,128)S(1)}, u32[]{:S(2)}, u32[]{:S(2)}) collective-permute-start(f32[56,128]{1,0:T(8,128)S(1)} %get-tuple-element.51), channel_id=1, source_target_pairs={{0,1},{1,0},{2,3},{3,2},{4,5},{5,4},{6,7},{7,6},{8,9},{9,8},{10,11... | collective-permute-start | bytes 86024 | tf_op jit(solution)/shard_map/ppermute | solution.py:411
  82.5 3.9 %collective-permute-start.16 = (f32[56,128]{1,0:T(8,128)S(1)}, f32[56,128]{1,0:T(8,128)S(1)}, u32[]{:S(2)}, u32[]{:S(2)}) collective-permute-start(f32[56,128]{1,0:T(8,128)S(1)} %add.29), channel_id=1, source_target_pairs={{0,2},{2,0},{4,6},{6,4},{8,10},{10,8},{12,14},{14,12},{1,3},{3,1},... | collective-permute-start | bytes 86024 | tf_op jit(solution)/shard_map/ppermute | solution.py:418
  86.4 3.9 %collective-permute-start.17 = (f32[56,128]{1,0:T(8,128)S(1)}, f32[56,128]{1,0:T(8,128)S(1)}, u32[]{:S(2)}, u32[]{:S(2)}) collective-permute-start(f32[56,128]{1,0:T(8,128)S(1)} %add.30), channel_id=1, source_target_pairs={{0,4},{2,6},{4,0},{6,2},{8,12},{10,14},{12,8},{14,10},{1,5},{3,7},... | collective-permute-start | bytes 86024 | tf_op jit(solution)/shard_map/ppermute | solution.py:418
  90.2 4.8 %collective-permute-start.18 = (f32[56,128]{1,0:T(8,128)S(1)}, f32[56,128]{1,0:T(8,128)S(1)}, u32[]{:S(2)}, u32[]{:S(2)}) collective-permute-start(f32[56,128]{1,0:T(8,128)S(1)} %add.31), channel_id=1, source_target_pairs={{0,8},{2,10},{4,12},{6,14},{8,0},{10,2},{12,4},{14,6},{1,9},{3,11}... | collective-permute-start | bytes 86024 | tf_op jit(solution)/shard_map/ppermute | solution.py:418
  95.0 1.2 %collective-permute-start.19 = (f32[56,128]{1,0:T(8,128)S(1)}, f32[56,128]{1,0:T(8,128)S(1)}, u32[]{:S(2)}, u32[]{:S(2)}) collective-permute-start(f32[56,128]{1,0:T(8,128)S(1)} %add.32.refs_2_), channel_id=1, source_target_pairs={{0,1},{1,0},{2,3},{3,2},{4,5},{5,4},{6,7},{7,6},{8,9},{9,8},{10,11... | collective-permute-start | bytes 86024 | tf_op jit(solution)/shard_map/ppermute | solution.py:411

commit v6 on v5

--- a/solution.py
+++ b/solution.py
@@ -73,6 +73,10 @@
     return jnp.broadcast_to(total, (8, size))
 
 
+def seed_values(seeds):
+    return seeds[...].astype(jnp.int32).astype(F32) / 1000.0
+
+
 def own_body(own, other, high, low, row_sum, row_sq):
     size = own.shape[0]
     embs = [own[...], other[...]]
@@ -84,17 +88,15 @@
     fill_tile(1.0, embs, row_sq, embs[0], high, low, row_sum)
 
 
-def far_body(keep, own, other, row_sq, col, before, seeds, near_seeds,
-             high, low, row_sum, col_sum, seeds_out, near_seeds_out):
+def far_body(keep, own, other, row_sq, col, before, high, low, row_sum, col_sum):
     row_sum[...] = before[...]
     col_sum[...] = fill_tile(keep[0].astype(F32), [own[...], other[...]], row_sq, col[...], high, low, row_sum)
-    seeds_out[...] = seeds[...].astype(jnp.int32).astype(F32) / 1000.0
-    near_seeds_out[...] = near_seeds[...].astype(jnp.int32).astype(F32) / 1000.0
-
-
-def relayed_body(keep, choice, own, other, row_sq, direct, relayed, before, first_cols,
-                 high, low, row_sum, col_sum):
+
+
+def relayed_body(keep, choice, own, other, row_sq, direct, relayed, before, first_cols, near_seeds,
+                 high, low, row_sum, col_sum, near_seeds_out):
     row_sum[...] = before[...]
+    near_seeds_out[...] = seed_values(near_seeds)
     col = jnp.where(choice[0] > 0, relayed[...], direct[...])
     col_sum[:8, :] = first_cols[...]
     col_sum[8:, :] = fill_tile(keep[0].astype(F32), [own[...], other[...]], row_sq, col, high, low, row_sum)
@@ -122,7 +124,7 @@
     scale = lax.rsqrt(degree)
     degree_out[...] = degree
     scale_out[...] = scale
-    vectors_out[...] = seeds[...] * per_row(scale, seeds.shape[0] // 2)
+    vectors_out[...] = seed_values(seeds) * per_row(scale, seeds.shape[0] // 2)
 
 
 def ahead_body(vectors, h1, l1, h2, l2, ahead):
@@ -287,8 +289,22 @@
     return jnp.concatenate(done, axis=0)[:, size:]
 
 
+def total(matrix):
+    return jnp.sum(jnp.sum(matrix, axis=0, keepdims=True), axis=1, keepdims=True)
+
+
 def trace(matrix):
-    return jnp.sum(matrix * unit(*matrix.shape))
+    return total(matrix * unit(*matrix.shape))
+
+
+def inverse_root(matrix):
+    eye = unit(*matrix.shape)
+    rest = matrix - eye
+
+    def series():
+        return eye - 0.5 * rest + 0.375 * dot(rest, rest)
+
+    return lax.cond(jnp.sum(rest * rest) < 1e-4, series, lambda: inverse_factor(matrix))
 
 
 def dense(moments, index, rows, data):
@@ -319,7 +335,7 @@
     mixed_r = m3 - m21
     square_r = m4 - m31 - m31.T + tri[:, n:2 * n]
     cubic_r = m5 - m41 - m41.T + tri[:, 2 * n:]
-    shift = 3.0 - jnp.sum(m1 * pick)
+    shift = 3.0 - total(m1 * pick)
     ridge = RIDGE_WEIGHT * (n + trace(gram_r)) / (2 * n)
     ridged = gram_r + ridge * eye
     factor = inverse_factor(ridged)
@@ -349,7 +365,7 @@
     ritz, image2, image3, excess, p_image, p_image2, p_gram, p_ritz = (dot(factor, part(right, i)) for i in range(8))
     excess = ridge * excess
 
-    shift = 3.0 - jnp.sum(ritz * pick)
+    shift = 3.0 - total(ritz * pick)
     by_ritz = dot(below(ritz, p_gram, excess, p_image, image2), ritz)
     squared, gram_pr, gram_cr = part(by_ritz, 0), p_image - part(by_ritz, 1), part(by_ritz, 2)
     tri = dot(ritz, squared), dot(ritz, gram_cr)
@@ -364,7 +380,7 @@
     image_gram = below(
         beside(ritz, p_image.T, image_cr), beside(p_image, p_ritz, image_pr), beside(image_cr.T, image_pr.T, image_rr),
     )
-    v0 = inverse_factor(g_cc)
+    v0 = inverse_root(g_cc)
     side = dot(below(p_gram, gram_cr.T), v0, 1, 1)
     l10, l20 = side[:n], side[n:]
     outer = dot(side, side, 1, 1)
@@ -413,10 +429,17 @@
 
 def total_over_blocks(values):
     blocks = lax.axis_size("blk")
+
+    def exchanged(distance):
+        return lax.ppermute(values, "blk", [(i, i ^ distance) for i in range(blocks)])
+
     span = 1
-    while blocks % (2 * span) == 0:
-        other = lax.ppermute(values, "blk", [(i, i ^ span) for i in range(blocks)])
-        values = values + other
+    while blocks % (4 * span) == 0:
+        first, second, third = exchanged(span), exchanged(2 * span), exchanged(3 * span)
+        values = (values + first) + (second + third)
+        span *= 4
+    if blocks % (2 * span) == 0:
+        values = values + exchanged(span)
         span *= 2
     if span < blocks:
         groups = [list(range(i, blocks, span)) for i in range(span)]
@@ -431,27 +454,27 @@
     core = lax.axis_index("narrow").astype(jnp.int32).reshape(1)
     other_emb = between_cores(embeddings)
     far_emb = between_blocks(embeddings, -1)
+    emb_args = [embeddings, other_emb]
+    pair_shape, row_shape = ((2 * NVEC, size), F32), ((16, size), F32)
+    h0, l0, sums, row_sq = make_tile(own_body, emb_args, size, extra=(((2 * size, 128), F32),))
+    far_emb, sums = lax.optimization_barrier((far_emb, sums))
     pairs = [(2 * i, (i - 2) % blocks * 2 + 1) for i in range(blocks)]
     pairs += [(2 * i + 1, (i - 1) % blocks * 2) for i in range(blocks) if blocks % 2 or i % 2]
     direct = lax.ppermute(embeddings, ("blk", "narrow"), pairs)
-    choice = (1 - core) * (where % 2 * (1 - blocks % 2)).astype(jnp.int32)
-    keep = lax.dynamic_slice(pair_mask, (where, core[0]), (1, 1))[0]
-    seed16 = start_seed.astype(jnp.int16).T
-    seeds16 = jnp.concatenate([seed16, between_cores(seed16)], axis=0)
-    near_seeds16 = between_blocks(seeds16, -1)
-
-    emb_args = [embeddings, other_emb]
-    pair_shape, row_shape = ((2 * NVEC, size), F32), ((16, size), F32)
-    h0, l0, sums, row_sq = make_tile(own_body, emb_args, size, extra=(((2 * size, 128), F32),))
-    far_emb, sums, near_seeds16 = lax.optimization_barrier((far_emb, sums, near_seeds16))
     relayed = direct
     if blocks % 2 == 0:
         relayed = lax.ppermute(far_emb, ("blk", "narrow"), [(2 * i + 1, 2 * i + 2) for i in range(0, blocks, 2)])
-    h1, l1, sums, cols, seeds, near_seeds = make_tile(
-        far_body, [keep, *emb_args, row_sq, far_emb, sums, seeds16, near_seeds16], size, (0,),
-        (((8, size), F32), pair_shape, pair_shape))
-    h2, l2, sums, cols = make_tile(
-        relayed_body, [keep, choice, *emb_args, row_sq, direct, relayed, sums, cols], size, (0, 1), (row_shape,))
+    choice = (1 - core) * (where % 2 * (1 - blocks % 2)).astype(jnp.int32)
+    keep = lax.dynamic_slice(pair_mask, (where, core[0]), (1, 1))[0]
+    h1, l1, sums, cols = make_tile(
+        far_body, [keep, *emb_args, row_sq, far_emb, sums], size, (0,), (((8, size), F32),))
+    seed16 = start_seed.astype(jnp.int16).T
+    seeds = jnp.concatenate([seed16, between_cores(seed16)], axis=0)
+    near_seeds, sums = lax.optimization_barrier((seeds, sums))
+    near_seeds = between_blocks(near_seeds, -1)
+    h2, l2, sums, cols, near_seeds = make_tile(
+        relayed_body, [keep, choice, *emb_args, row_sq, direct, relayed, sums, cols, near_seeds], size, (0, 1),
+        (row_shape, pair_shape))
     sums = sums + between_blocks(cols, 1)
 
     small = dict(flops=10**6, nbytes=10**5)

time: 120 us -> 117 us (0.975)
  waiting for transfers between devices: 44.9 us -> 37.2 us
  starting transfers between devices: 31 us -> 35.3 us
  local copies, waits for them, and re-layouts: 5.41 us -> 7.08 us
  Pallas kernels: 36.7 us -> 35.2 us
    ppermute x3 -> x4, starting transfers between devices: 2.27 us -> 7.92 us  [exchanged(): lax.ppermute(values, 'blk', [(i, i ^ distance) for i in range(blocks)])]
    ppermute x3 -> x4, waiting for transfers between devices: 10.2 us -> 5.08 us  [exchanged(): lax.ppermute(values, 'blk', [(i, i ^ distance) for i in range(blocks)])]
    ppermute x8, waiting for transfers between devices: 28.9 us -> 26.4 us  [between_blocks(): return lax.ppermute(shard, ('blk', 'narrow'), pairs)]
    ppermute x8, starting transfers between devices: 24.9 us -> 22.6 us  [between_blocks(): return lax.ppermute(shard, ('blk', 'narrow'), pairs)]
    unnamed x18 -> x28, local copies, waits for them, and re-layouts: 4.8 us -> 6.51 us
    ppermute x7, starting transfers between devices: 0.67 us -> 2.16 us  [between_cores(): return lax.ppermute(shard, 'narrow', [(0, 1), (1, 0)])]
    pallas_call x16, Pallas kernels: 36.7 us -> 35.2 us  [call(): pl.pallas_call(body, out_shape=[jax.ShapeDtypeStruct(shape, dtype) for sh...]
  transfers between devices with their start and end apart: 20 -> 21, of which waited for: 14 -> 16; matrix products, arithmetic and copies ran while one was open for 1% -> 1% of each run, Pallas kernels for 5% -> 5%
where the time goes in v6:
time: 117 us
  waiting for transfers between devices  37.2 us (32%)
  starting transfers between devices  35.3 us (30%)
  Pallas kernels  35.2 us (30%)
  local copies, waits for them, and re-layouts  7.08 us (6%)
    pallas_call x16, Pallas kernels, call(): pl.pallas_call(body, out_shape=[jax.ShapeDtypeStruct(shape, dtype) for sh...  35.2 us
    ppermute x8, waiting for transfers between devices, between_blocks(): return lax.ppermute(shard, ('blk', 'narrow'), pairs)  26.4 us
    ppermute x8, starting transfers between devices, between_blocks(): return lax.ppermute(shard, ('blk', 'narrow'), pairs)  22.6 us
    ppermute x4, starting transfers between devices, exchanged(): lax.ppermute(values, 'blk', [(i, i ^ distance) for i in range(blocks)])  7.92 us
    unnamed x28, local copies, waits for them, and re-layouts  6.51 us
    ppermute x7, waiting for transfers between devices, between_cores(): return lax.ppermute(shard, 'narrow', [(0, 1), (1, 0)])  5.79 us
    ppermute x4, waiting for transfers between devices, exchanged(): lax.ppermute(values, 'blk', [(i, i ^ distance) for i in range(blocks)])  5.08 us
  transfers between devices with their start and end apart: 21, of which 16 were waited for; matrix products, arithmetic and copies ran while one was open for 1% of the time, Pallas kernels for 5%

profile of v6, /device:TPU:0, one launch (start us, length us, event | category | flops | bytes accessed | tf_op | source)
XLA Modules:
  0.0 116.5 jit_solution(13875700058504934268)
XLA Ops:
  0.5 5.5 %collective-permute-start.2 = (bf16[384,768]{1,0:T(8,128)(2,1)}, bf16[384,768]{1,0:T(8,128)(2,1)S(1)}, u32[]{:S(2)}, u32[]{:S(2)}) collective-permute-start(bf16[384,768]{1,0:T(8,128)(2,1)} %own.5), channel_id=1, source_target_pairs={{0,14},{1,13},{2,0},{3,15},{4,2},{5,1},{6,4},{7,3},{8,6},{9,5},{10... | collective-permute-start | bytes 1769480 | tf_op jit(solution)/shard_map/ppermute | solution.py:423
  6.0 1.9 %collective-permute-start.1 = (bf16[384,768]{1,0:T(8,128)(2,1)}, bf16[384,768]{1,0:T(8,128)(2,1)S(1)}, u32[]{:S(2)}, u32[]{:S(2)}) collective-permute-start(bf16[384,768]{1,0:T(8,128)(2,1)} %own.5), channel_id=1, source_target_pairs={{0,13},{2,15},{4,1},{6,3},{8,5},{10,7},{12,9},{14,11},{3,0},{7,4},... | collective-permute-start | bytes 1769480 | tf_op jit(solution)/shard_map/ppermute | solution.py:463
  7.9 1.1 copy-done
  9.0 1.9 %shard_map.46 = (bf16[768,384]{1,0:T(8,128)(2,1)S(1)}, bf16[768,384]{1,0:T(8,128)(2,1)S(1)}, f32[16,384]{1,0:T(8,128)S(1)}, f32[768,128]{1,0:T(8,128)S(1)}) custom-call(bf16[384,768]{1,0:T(8,128)(2,1)S(1)} %copy-done, bf16[384,768]{1,0:T(8,128)(2,1)S(1)} %collective-permute-done.other), custom_call_target="tpu_custom_call" | custom-call | flops 2000000000 | bytes 1000000 | tf_op jit(solution)/shard_map/pallas_call | solution.py:36
  10.8 0.9 copy-done.6
  11.7 0.8 copy-done.8
  12.5 6.1 %collective-permute-done.2.col = bf16[384,768]{1,0:T(8,128)(2,1)S(1)} collective-permute-done((bf16[384,768]{1,0:T(8,128)(2,1)}, bf16[384,768]{1,0:T(8,128)(2,1)S(1)}, u32[]{:S(2)}, u32[]{:S(2)}) %collective-permute-start.2) | collective-permute-done | bytes 589856 | tf_op jit(solution)/shard_map/ppermute | solution.py:423
  18.6 0.7 collective-permute-start.3
  19.3 1.5 %collective-permute-start.4 = (s16[64,384]{1,0:T(8,128)(2,1)S(1)}, s16[64,384]{1,0:T(8,128)(2,1)}, u32[]{:S(2)}, u32[]{:S(2)}) collective-permute-start(s16[64,384]{1,0:T(8,128)(2,1)S(1)} %convert_bitcast_fusion), channel_id=1, source_target_pairs={{0,1},{1,0},{2,3},{3,2},{4,5},{5,4},{6,7},{7,6},{8,9},{9,8},{10,11... | collective-permute-start | bytes 147464 | tf_op jit(solution)/shard_map/ppermute | solution.py:427
  20.8 0.7 copy-done.13
  21.5 0.6 dynamic_slice.3
  22.1 0.8 pad_add_fusion.seeds
  22.9 2.5 %shard_map.47 = (bf16[768,384]{1,0:T(8,128)(2,1)S(1)}, bf16[768,384]{1,0:T(8,128)(2,1)S(1)}, f32[16,384]{1,0:T(8,128)S(1)}, f32[8,384]{1,0:T(8,128)S(1)}) custom-call(s32[1]{0:T(128)} %bitcast.1.keep, bf16[384,768]{1,0:T(8,128)(2,1)S(1)} %copy-done.1, bf16[384,768]{1,0:T(8,128)(2,1)S(1)} %collective-permute-done.other, ...), custom_call_target="tpu_custom_call" | custom-call | flops 2000000000 | bytes 1000000 | tf_op jit(solution)/shard_map/pallas_call | solution.py:36
  25.4 0.9 copy-done.2
  26.3 0.8 copy-done.4
  27.1 0.6 copy-done.10
  27.7 4.3 %collective-permute-start.5 = (s16[128,384]{1,0:T(8,128)(2,1)S(1)}, s16[128,384]{1,0:T(8,128)(2,1)S(1)}, u32[]{:S(2)}, u32[]{:S(2)}) collective-permute-start(s16[128,384]{1,0:T(8,128)(2,1)S(1)} %pad_add_fusion.seeds), channel_id=1, source_target_pairs={{0,14},{1,13},{2,0},{3,15},{4,2},{5,1},{6,4},{7,3},{8,6},{9,5},{10... | collective-permute-start | bytes 294920 | tf_op jit(solution)/shard_map/ppermute | solution.py:423
  32.0 2.9 %collective-permute-done.5.near_seeds = s16[128,384]{1,0:T(8,128)(2,1)S(1)} collective-permute-done((s16[128,384]{1,0:T(8,128)(2,1)S(1)}, s16[128,384]{1,0:T(8,128)(2,1)S(1)}, u32[]{:S(2)}, u32[]{:S(2)}) %collective-permute-start.5) | collective-permute-done | bytes 98336 | tf_op jit(solution)/shard_map/ppermute | solution.py:423
  35.0 0.7 copy-done.11
  35.7 2.6 %shard_map.48 = (bf16[768,384]{1,0:T(8,128)(2,1)S(1)}, bf16[768,384]{1,0:T(8,128)(2,1)S(1)}, f32[16,384]{1,0:T(8,128)S(1)}, f32[16,384]{1,0:T(8,128)S(1)}, f32[128,384]{1,0:T(8,128)S(1)}) custom-call(s32[1]{0:T(128)} %bitcast.1.keep, s32[1]{0:T(128)S(6)} %mul.7.choice, bf16[384,768]{1,0:T(8,128)(2,1)S(1)} %copy-done.1, ...), custom_call_target="tpu_custom_call" | custom-call | flops 2000000000 | bytes 1000000 | tf_op jit(solution)/shard_map/pallas_call | solution.py:36
  38.3 7.0 %collective-permute-done.6 = f32[16,384]{1,0:T(8,128)S(1)} collective-permute-done((f32[16,384]{1,0:T(8,128)S(1)}, f32[16,384]{1,0:T(8,128)S(1)}, u32[]{:S(2)}, u32[]{:S(2)}) %collective-permute-start.6) | collective-permute-done | bytes 24608 | tf_op jit(solution)/shard_map/ppermute | solution.py:423
  45.4 1.2 %collective-permute-done.7.other_sums = f32[16,384]{1,0:T(8,128)S(1)} collective-permute-done((f32[16,384]{1,0:T(8,128)S(1)}, f32[16,384]{1,0:T(8,128)S(1)}, u32[]{:S(2)}, u32[]{:S(2)}) %collective-permute-start.7) | collective-permute-done | bytes 24608 | tf_op jit(solution)/shard_map/ppermute | solution.py:427
  46.6 0.5 shard_map.51
  47.2 4.7 %collective-permute-start.8 = (f32[16,384]{1,0:T(8,128)S(1)}, f32[16,384]{1,0:T(8,128)S(1)}, u32[]{:S(2)}, u32[]{:S(2)}) collective-permute-start(f32[16,384]{1,0:T(8,128)S(1)} %get-tuple-element.44), channel_id=1, source_target_pairs={{0,14},{1,13},{2,0},{3,15},{4,2},{5,1},{6,4},{7,3},{8,6},{9,5},{10... | collective-permute-start | bytes 73736 | tf_op jit(solution)/shard_map/ppermute | solution.py:423
  51.9 0.5 shard_map.50.product
  52.4 1.0 collective-permute-done.8.near_scale
  53.4 2.1 %collective-permute-done.9.refs_0_ = f32[128,384]{1,0:T(8,128)S(1)} collective-permute-done((f32[128,384]{1,0:T(8,128)S(1)}, f32[128,384]{1,0:T(8,128)S(1)}, u32[]{:S(2)}, u32[]{:S(2)}) %collective-permute-start.9) | collective-permute-done | bytes 196640 | tf_op jit(solution)/shard_map/ppermute | solution.py:423
  55.6 0.8 shard_map.52.total
  56.4 1.4 %collective-permute-done.10.other_total = f32[128,384]{1,0:T(8,128)S(1)} collective-permute-done((f32[128,384]{1,0:T(8,128)S(1)}, f32[128,384]{1,0:T(8,128)S(1)}, u32[]{:S(2)}, u32[]{:S(2)}) %collective-permute-start.10) | collective-permute-done | bytes 196640 | tf_op jit(solution)/shard_map/ppermute | solution.py:427
  57.9 0.5 shard_map.55
  58.5 4.7 %collective-permute-start.11 = (f32[128,384]{1,0:T(8,128)S(1)}, f32[128,384]{1,0:T(8,128)S(1)}, u32[]{:S(2)}, u32[]{:S(2)}) collective-permute-start(f32[128,384]{1,0:T(8,128)S(1)} %shard_map.53.vectors.v1), channel_id=1, source_target_pairs={{0,14},{1,13},{2,0},{3,15},{4,2},{5,1},{6,4},{7,3},{8,6},{9,5},{10... | collective-permute-start | bytes 589832 | tf_op jit(solution)/shard_map/ppermute | solution.py:423
  63.2 0.5 shard_map.54.product
  63.7 5.0 %collective-permute-done.12.refs_0_ = f32[128,384]{1,0:T(8,128)S(1)} collective-permute-done((f32[128,384]{1,0:T(8,128)S(1)}, f32[128,384]{1,0:T(8,128)S(1)}, u32[]{:S(2)}, u32[]{:S(2)}) %collective-permute-start.12) | collective-permute-done | bytes 196640 | tf_op jit(solution)/shard_map/ppermute | solution.py:423
  68.7 0.8 shard_map.56.total
  69.6 1.4 %collective-permute-done.13.other_total = f32[128,384]{1,0:T(8,128)S(1)} collective-permute-done((f32[128,384]{1,0:T(8,128)S(1)}, f32[128,384]{1,0:T(8,128)S(1)}, u32[]{:S(2)}, u32[]{:S(2)}) %collective-permute-start.13) | collective-permute-done | bytes 196640 | tf_op jit(solution)/shard_map/ppermute | solution.py:427
  71.1 3.2 %collective-permute-start.14 = (f32[128,384]{1,0:T(8,128)S(1)}, f32[128,384]{1,0:T(8,128)S(1)}, u32[]{:S(2)}, u32[]{:S(2)}) collective-permute-start(f32[128,384]{1,0:T(8,128)S(1)} %shard_map.57.v2.vectors), channel_id=1, source_target_pairs={{0,14},{1,13},{2,0},{3,15},{4,2},{5,1},{6,4},{7,3},{8,6},{9,5},{10... | collective-permute-start | bytes 589832 | tf_op jit(solution)/shard_map/ppermute | solution.py:423
  74.2 0.5 shard_map.59.product
  74.7 0.5 shard_map.58
  75.3 2.2 %collective-permute-done.14.near = f32[128,384]{1,0:T(8,128)S(1)} collective-permute-done((f32[128,384]{1,0:T(8,128)S(1)}, f32[128,384]{1,0:T(8,128)S(1)}, u32[]{:S(2)}, u32[]{:S(2)}) %collective-permute-start.14) | collective-permute-done | bytes 196640 | tf_op jit(solution)/shard_map/ppermute | solution.py:423
  77.4 1.4 %shard_map.60 = (f32[56,128]{1,0:T(8,128)S(1)}, f32[56,128]{1,0:T(8,128)S(1)}) custom-call(s32[1]{0:T(128)} %bitcast.core.refs_0_, f32[320,64]{1,0:T(8,128)S(1)} %get-tuple-element.49.low, f32[128,384]{1,0:T(8,128)S(1)} %shard_map.57.v2.vectors, f32[128,384]{1,0:T(8,128)S(1)} %shard_map.59.product, f32[128,384]{1,0:T(8,128)S(1)} %collective-permute-done.14.near, ...), custom_call_target="tpu_custom_call" | custom-call | flops 1000000000 | bytes 1000000 | tf_op jit(solution)/shard_map/pallas_call | solution.py:36
  78.9 1.2 %collective-permute-done.15 = f32[56,128]{1,0:T(8,128)S(1)} collective-permute-done((f32[56,128]{1,0:T(8,128)S(1)}, f32[56,128]{1,0:T(8,128)S(1)}, u32[]{:S(2)}, u32[]{:S(2)}) %collective-permute-start.15) | collective-permute-done | bytes 28704 | tf_op jit(solution)/shard_map/ppermute | solution.py:427
  80.1 1.9 %collective-permute-start.17 = (f32[56,128]{1,0:T(8,128)S(1)}, f32[56,128]{1,0:T(8,128)S(1)}, u32[]{:S(2)}, u32[]{:S(2)}) collective-permute-start(f32[56,128]{1,0:T(8,128)S(1)} %add.32), channel_id=1, source_target_pairs={{0,4},{2,6},{4,0},{6,2},{8,12},{10,14},{12,8},{14,10},{1,5},{3,7},... | collective-permute-start | bytes 86024 | tf_op jit(solution)/shard_map/ppermute | solution.py:434
  82.0 1.5 %collective-permute-start.18 = (f32[56,128]{1,0:T(8,128)S(1)}, f32[56,128]{1,0:T(8,128)S(1)}, u32[]{:S(2)}, u32[]{:S(2)}) collective-permute-start(f32[56,128]{1,0:T(8,128)S(1)} %add.32), channel_id=1, source_target_pairs={{0,6},{2,4},{4,2},{6,0},{8,14},{10,12},{12,10},{14,8},{1,7},{3,5},... | collective-permute-start | bytes 86024 | tf_op jit(solution)/shard_map/ppermute | solution.py:434
  84.0 2.8 %collective-permute-done.18 = f32[56,128]{1,0:T(8,128)S(1)} collective-permute-done((f32[56,128]{1,0:T(8,128)S(1)}, f32[56,128]{1,0:T(8,128)S(1)}, u32[]{:S(2)}, u32[]{:S(2)}) %collective-permute-start.18) | collective-permute-done | bytes 28704 | tf_op jit(solution)/shard_map/ppermute | solution.py:434
  86.8 4.4 %collective-permute-start.19 = (f32[56,128]{1,0:T(8,128)S(1)}, f32[56,128]{1,0:T(8,128)S(1)}, u32[]{:S(2)}, u32[]{:S(2)}) collective-permute-start(f32[56,128]{1,0:T(8,128)S(1)} %add_add_fusion), channel_id=1, source_target_pairs={{0,8},{2,10},{4,12},{6,14},{8,0},{10,2},{12,4},{14,6},{1,9},{3,11}... | collective-permute-start | bytes 86024 | tf_op jit(solution)/shard_map/ppermute | solution.py:434
  91.3 1.9 %collective-permute-done.19 = f32[56,128]{1,0:T(8,128)S(1)} collective-permute-done((f32[56,128]{1,0:T(8,128)S(1)}, f32[56,128]{1,0:T(8,128)S(1)}, u32[]{:S(2)}, u32[]{:S(2)}) %collective-permute-start.19) | collective-permute-done | bytes 28704 | tf_op jit(solution)/shard_map/ppermute | solution.py:434
  93.8 0.5 collective-permute-done.20.refs_3_
  94.3 22.2 %shard_map.61 = f32[64,384]{1,0:T(8,128)} custom-call(s32[1]{0:T(128)} %bitcast.core.refs_0_, s32[1]{0:T(128)S(6)} %copy.5.refs_1_, f32[56,128]{1,0:T(8,128)S(1)} %add.36.refs_2_, f32[56,128]{1,0:T(8,128)S(1)} %collective-permute-done.20.refs_3_, f32[192,384]{1,0:T(8,128)S(1)} %get-tuple-element.52.refs_4_), custom_call_target="tpu_custom_call" | custom-call | flops 20000000000 | bytes 1000000 | tf_op jit(solution)/shard_map/pallas_call | solution.py:36
  (45 shorter events, 1.4 us)
Async XLA Ops:
  0.0 7.9 %collective-permute-start = (bf16[384,768]{1,0:T(8,128)(2,1)}, bf16[384,768]{1,0:T(8,128)(2,1)S(1)}, u32[]{:S(2)}, u32[]{:S(2)}) collective-permute-start(bf16[384,768]{1,0:T(8,128)(2,1)} %own.5), channel_id=1, source_target_pairs={{0,1},{1,0},{2,3},{3,2},{4,5},{5,4},{6,7},{7,6},{8,9},{9,8},{10,11... | collective-permute-start | bytes 1769480 | tf_op jit(solution)/shard_map/ppermute | solution.py:427
  0.5 18.2 %collective-permute-start.2 = (bf16[384,768]{1,0:T(8,128)(2,1)}, bf16[384,768]{1,0:T(8,128)(2,1)S(1)}, u32[]{:S(2)}, u32[]{:S(2)}) collective-permute-start(bf16[384,768]{1,0:T(8,128)(2,1)} %own.5), channel_id=1, source_target_pairs={{0,14},{1,13},{2,0},{3,15},{4,2},{5,1},{6,4},{7,3},{8,6},{9,5},{10... | collective-permute-start | bytes 1769480 | tf_op jit(solution)/shard_map/ppermute | solution.py:423
  6.0 26.1 %collective-permute-start.1 = (bf16[384,768]{1,0:T(8,128)(2,1)}, bf16[384,768]{1,0:T(8,128)(2,1)S(1)}, u32[]{:S(2)}, u32[]{:S(2)}) collective-permute-start(bf16[384,768]{1,0:T(8,128)(2,1)} %own.5), channel_id=1, source_target_pairs={{0,13},{2,15},{4,1},{6,3},{8,5},{10,7},{12,9},{14,11},{3,0},{7,4},... | collective-permute-start | bytes 1769480 | tf_op jit(solution)/shard_map/ppermute | solution.py:463
  7.9 1.1 copy-start
  9.0 10.4 %copy-start.12 = (s32[384,64]{0,1:T(8,128)S(1)}, s32[384,64]{0,1:T(8,128)}, u32[]{:S(2)}) copy-start(s32[384,64]{0,1:T(8,128)} %param.7) | copy-start | bytes 294916
  9.0 13.9 %copy-start.1 = (bf16[384,768]{1,0:T(8,128)(2,1)S(1)}, bf16[384,768]{1,0:T(8,128)(2,1)}, u32[]{:S(2)}) copy-start(bf16[384,768]{1,0:T(8,128)(2,1)} %own.5) | copy-start | bytes 1769476
  10.8 0.9 copy-start.6
  11.7 0.8 copy-start.8
  18.6 16.3 %collective-permute-start.3 = (bf16[384,768]{1,0:T(8,128)(2,1)S(1)}, bf16[384,768]{1,0:T(8,128)(2,1)S(1)}, u32[]{:S(2)}, u32[]{:S(2)}) collective-permute-start(bf16[384,768]{1,0:T(8,128)(2,1)S(1)} %collective-permute-done.2.col), channel_id=1, source_target_pairs={{1,2},{5,6},{9,10},{13,14},{17,18},{21,22},{25,26},{29,30}} | collective-permute-start | bytes 1769480 | tf_op jit(solution)/shard_map/ppermute | solution.py:466
  19.3 2.8 %collective-permute-start.4 = (s16[64,384]{1,0:T(8,128)(2,1)S(1)}, s16[64,384]{1,0:T(8,128)(2,1)}, u32[]{:S(2)}, u32[]{:S(2)}) collective-permute-start(s16[64,384]{1,0:T(8,128)(2,1)S(1)} %convert_bitcast_fusion), channel_id=1, source_target_pairs={{0,1},{1,0},{2,3},{3,2},{4,5},{5,4},{6,7},{7,6},{8,9},{9,8},{10,11... | collective-permute-start | bytes 147464 | tf_op jit(solution)/shard_map/ppermute | solution.py:427
  20.8 0.7 copy-start.13
  25.4 0.9 copy-start.2
  26.3 0.8 copy-start.4
  27.1 0.6 copy-start.10
  27.7 7.3 %collective-permute-start.5 = (s16[128,384]{1,0:T(8,128)(2,1)S(1)}, s16[128,384]{1,0:T(8,128)(2,1)S(1)}, u32[]{:S(2)}, u32[]{:S(2)}) collective-permute-start(s16[128,384]{1,0:T(8,128)(2,1)S(1)} %pad_add_fusion.seeds), channel_id=1, source_target_pairs={{0,14},{1,13},{2,0},{3,15},{4,2},{5,1},{6,4},{7,3},{8,6},{9,5},{10... | collective-permute-start | bytes 294920 | tf_op jit(solution)/shard_map/ppermute | solution.py:423
  35.0 0.7 copy-start.11
  35.7 10.9 %copy-start.3 = (bf16[768,384]{1,0:T(8,128)(2,1)S(1)}, bf16[768,384]{1,0:T(8,128)(2,1)}, u32[]{:S(2)}) copy-start(bf16[768,384]{1,0:T(8,128)(2,1)} %copy-done.2) | copy-start | bytes 1769476
  35.7 10.9 %copy-start.5 = (bf16[768,384]{1,0:T(8,128)(2,1)S(1)}, bf16[768,384]{1,0:T(8,128)(2,1)}, u32[]{:S(2)}) copy-start(bf16[768,384]{1,0:T(8,128)(2,1)} %copy-done.4) | copy-start | bytes 1769476
  38.3 7.0 %collective-permute-start.6 = (f32[16,384]{1,0:T(8,128)S(1)}, f32[16,384]{1,0:T(8,128)S(1)}, u32[]{:S(2)}, u32[]{:S(2)}) collective-permute-start(f32[16,384]{1,0:T(8,128)S(1)} %get-tuple-element.38), channel_id=1, source_target_pairs={{0,2},{1,5},{2,4},{3,7},{4,6},{5,9},{6,8},{7,11},{8,10},{9,13},{10... | collective-permute-start | bytes 73736 | tf_op jit(solution)/shard_map/ppermute | solution.py:423
  45.3 1.2 %collective-permute-start.7 = (f32[16,384]{1,0:T(8,128)S(1)}, f32[16,384]{1,0:T(8,128)S(1)}, u32[]{:S(2)}, u32[]{:S(2)}) collective-permute-start(f32[16,384]{1,0:T(8,128)S(1)} %add.31.sums), channel_id=1, source_target_pairs={{0,1},{1,0},{2,3},{3,2},{4,5},{5,4},{6,7},{7,6},{8,9},{9,8},{10,11... | collective-permute-start | bytes 73736 | tf_op jit(solution)/shard_map/ppermute | solution.py:427
  46.6 5.3 %copy-start.7 = (bf16[768,384]{1,0:T(8,128)(2,1)S(1)}, bf16[768,384]{1,0:T(8,128)(2,1)}, u32[]{:S(2)}) copy-start(bf16[768,384]{1,0:T(8,128)(2,1)} %copy-done.6) | copy-start | bytes 1769476
  46.6 5.3 %copy-start.9 = (bf16[768,384]{1,0:T(8,128)(2,1)S(1)}, bf16[768,384]{1,0:T(8,128)(2,1)}, u32[]{:S(2)}) copy-start(bf16[768,384]{1,0:T(8,128)(2,1)} %copy-done.8) | copy-start | bytes 1769476
  47.1 8.4 %collective-permute-start.9 = (f32[128,384]{1,0:T(8,128)S(1)}, f32[128,384]{1,0:T(8,128)S(1)}, u32[]{:S(2)}, u32[]{:S(2)}) collective-permute-start(f32[128,384]{1,0:T(8,128)S(1)} %shard_map.51), channel_id=1, source_target_pairs={{0,2},{1,5},{2,4},{3,7},{4,6},{5,9},{6,8},{7,11},{8,10},{9,13},{10... | collective-permute-start | bytes 589832 | tf_op jit(solution)/shard_map/ppermute | solution.py:423
  47.2 6.2 %collective-permute-start.8 = (f32[16,384]{1,0:T(8,128)S(1)}, f32[16,384]{1,0:T(8,128)S(1)}, u32[]{:S(2)}, u32[]{:S(2)}) collective-permute-start(f32[16,384]{1,0:T(8,128)S(1)} %get-tuple-element.44), channel_id=1, source_target_pairs={{0,14},{1,13},{2,0},{3,15},{4,2},{5,1},{6,4},{7,3},{8,6},{9,5},{10... | collective-permute-start | bytes 73736 | tf_op jit(solution)/shard_map/ppermute | solution.py:423
  56.4 1.5 %collective-permute-start.10 = (f32[128,384]{1,0:T(8,128)S(1)}, f32[128,384]{1,0:T(8,128)S(1)}, u32[]{:S(2)}, u32[]{:S(2)}) collective-permute-start(f32[128,384]{1,0:T(8,128)S(1)} %shard_map.52.total), channel_id=1, source_target_pairs={{0,1},{1,0},{2,3},{3,2},{4,5},{5,4},{6,7},{7,6},{8,9},{9,8},{10,11... | collective-permute-start | bytes 589832 | tf_op jit(solution)/shard_map/ppermute | solution.py:427
  58.4 10.3 %collective-permute-start.12 = (f32[128,384]{1,0:T(8,128)S(1)}, f32[128,384]{1,0:T(8,128)S(1)}, u32[]{:S(2)}, u32[]{:S(2)}) collective-permute-start(f32[128,384]{1,0:T(8,128)S(1)} %shard_map.55), channel_id=1, source_target_pairs={{0,2},{1,5},{2,4},{3,7},{4,6},{5,9},{6,8},{7,11},{8,10},{9,13},{10... | collective-permute-start | bytes 589832 | tf_op jit(solution)/shard_map/ppermute | solution.py:423
  58.5 10.2 %collective-permute-start.11 = (f32[128,384]{1,0:T(8,128)S(1)}, f32[128,384]{1,0:T(8,128)S(1)}, u32[]{:S(2)}, u32[]{:S(2)}) collective-permute-start(f32[128,384]{1,0:T(8,128)S(1)} %shard_map.53.vectors.v1), channel_id=1, source_target_pairs={{0,14},{1,13},{2,0},{3,15},{4,2},{5,1},{6,4},{7,3},{8,6},{9,5},{10... | collective-permute-start | bytes 589832 | tf_op jit(solution)/shard_map/ppermute | solution.py:423
  69.5 1.5 %collective-permute-start.13 = (f32[128,384]{1,0:T(8,128)S(1)}, f32[128,384]{1,0:T(8,128)S(1)}, u32[]{:S(2)}, u32[]{:S(2)}) collective-permute-start(f32[128,384]{1,0:T(8,128)S(1)} %shard_map.56.total), channel_id=1, source_target_pairs={{0,1},{1,0},{2,3},{3,2},{4,5},{5,4},{6,7},{7,6},{8,9},{9,8},{10,11... | collective-permute-start | bytes 589832 | tf_op jit(solution)/shard_map/ppermute | solution.py:427
  71.1 6.4 %collective-permute-start.14 = (f32[128,384]{1,0:T(8,128)S(1)}, f32[128,384]{1,0:T(8,128)S(1)}, u32[]{:S(2)}, u32[]{:S(2)}) collective-permute-start(f32[128,384]{1,0:T(8,128)S(1)} %shard_map.57.v2.vectors), channel_id=1, source_target_pairs={{0,14},{1,13},{2,0},{3,15},{4,2},{5,1},{6,4},{7,3},{8,6},{9,5},{10... | collective-permute-start | bytes 589832 | tf_op jit(solution)/shard_map/ppermute | solution.py:423
  78.8 1.3 %collective-permute-start.15 = (f32[56,128]{1,0:T(8,128)S(1)}, f32[56,128]{1,0:T(8,128)S(1)}, u32[]{:S(2)}, u32[]{:S(2)}) collective-permute-start(f32[56,128]{1,0:T(8,128)S(1)} %get-tuple-element.51), channel_id=1, source_target_pairs={{0,1},{1,0},{2,3},{3,2},{4,5},{5,4},{6,7},{7,6},{8,9},{9,8},{10,11... | collective-permute-start | bytes 86024 | tf_op jit(solution)/shard_map/ppermute | solution.py:427
  80.1 3.9 %collective-permute-start.16 = (f32[56,128]{1,0:T(8,128)S(1)}, f32[56,128]{1,0:T(8,128)S(1)}, u32[]{:S(2)}, u32[]{:S(2)}) collective-permute-start(f32[56,128]{1,0:T(8,128)S(1)} %add.32), channel_id=1, source_target_pairs={{0,2},{2,0},{4,6},{6,4},{8,10},{10,8},{12,14},{14,12},{1,3},{3,1},... | collective-permute-start | bytes 86024 | tf_op jit(solution)/shard_map/ppermute | solution.py:434
  80.1 3.9 %collective-permute-start.17 = (f32[56,128]{1,0:T(8,128)S(1)}, f32[56,128]{1,0:T(8,128)S(1)}, u32[]{:S(2)}, u32[]{:S(2)}) collective-permute-start(f32[56,128]{1,0:T(8,128)S(1)} %add.32), channel_id=1, source_target_pairs={{0,4},{2,6},{4,0},{6,2},{8,12},{10,14},{12,8},{14,10},{1,5},{3,7},... | collective-permute-start | bytes 86024 | tf_op jit(solution)/shard_map/ppermute | solution.py:434
  82.0 4.8 %collective-permute-start.18 = (f32[56,128]{1,0:T(8,128)S(1)}, f32[56,128]{1,0:T(8,128)S(1)}, u32[]{:S(2)}, u32[]{:S(2)}) collective-permute-start(f32[56,128]{1,0:T(8,128)S(1)} %add.32), channel_id=1, source_target_pairs={{0,6},{2,4},{4,2},{6,0},{8,14},{10,12},{12,10},{14,8},{1,7},{3,5},... | collective-permute-start | bytes 86024 | tf_op jit(solution)/shard_map/ppermute | solution.py:434
  86.8 6.3 %collective-permute-start.19 = (f32[56,128]{1,0:T(8,128)S(1)}, f32[56,128]{1,0:T(8,128)S(1)}, u32[]{:S(2)}, u32[]{:S(2)}) collective-permute-start(f32[56,128]{1,0:T(8,128)S(1)} %add_add_fusion), channel_id=1, source_target_pairs={{0,8},{2,10},{4,12},{6,14},{8,0},{10,2},{12,4},{14,6},{1,9},{3,11}... | collective-permute-start | bytes 86024 | tf_op jit(solution)/shard_map/ppermute | solution.py:434
  93.1 1.2 %collective-permute-start.20 = (f32[56,128]{1,0:T(8,128)S(1)}, f32[56,128]{1,0:T(8,128)S(1)}, u32[]{:S(2)}, u32[]{:S(2)}) collective-permute-start(f32[56,128]{1,0:T(8,128)S(1)} %add.36.refs_2_), channel_id=1, source_target_pairs={{0,1},{1,0},{2,3},{3,2},{4,5},{5,4},{6,7},{7,6},{8,9},{9,8},{10,11... | collective-permute-start | bytes 86024 | tf_op jit(solution)/shard_map/ppermute | solution.py:427

commit v7 on v6

--- a/solution.py
+++ b/solution.py
@@ -12,7 +12,7 @@
 NVEC = 64
 F32 = jnp.float32
 BF16 = jnp.bfloat16
-VMEM_LIMIT = 48 * 1024 * 1024
+VMEM_LIMIT = 16 * 1024 * 1024
 
 
 def dot(left, right, left_dim=1, right_dim=0):
@@ -88,15 +88,15 @@
     fill_tile(1.0, embs, row_sq, embs[0], high, low, row_sum)
 
 
-def far_body(keep, own, other, row_sq, col, before, high, low, row_sum, col_sum):
-    row_sum[...] = before[...]
-    col_sum[...] = fill_tile(keep[0].astype(F32), [own[...], other[...]], row_sq, col[...], high, low, row_sum)
-
-
-def relayed_body(keep, choice, own, other, row_sq, direct, relayed, before, first_cols, near_seeds,
-                 high, low, row_sum, col_sum, near_seeds_out):
+def far_body(keep, own, other, row_sq, col, before, near_seeds, high, low, row_sum, col_sum, near_seeds_out):
     row_sum[...] = before[...]
     near_seeds_out[...] = seed_values(near_seeds)
+    col_sum[...] = fill_tile(keep[0].astype(F32), [own[...], other[...]], row_sq, col[...], high, low, row_sum)
+
+
+def relayed_body(keep, choice, own, other, row_sq, direct, relayed, before, first_cols,
+                 high, low, row_sum, col_sum):
+    row_sum[...] = before[...]
     col = jnp.where(choice[0] > 0, relayed[...], direct[...])
     col_sum[:8, :] = first_cols[...]
     col_sum[8:, :] = fill_tile(keep[0].astype(F32), [own[...], other[...]], row_sq, col, high, low, row_sum)
@@ -429,17 +429,12 @@
 
 def total_over_blocks(values):
     blocks = lax.axis_size("blk")
-
-    def exchanged(distance):
-        return lax.ppermute(values, "blk", [(i, i ^ distance) for i in range(blocks)])
-
+    if blocks <= 8:
+        copies = jnp.broadcast_to(values[None], (blocks, *values.shape))
+        return jnp.sum(lax.all_to_all(copies, "blk", 0, 0), axis=0)
     span = 1
-    while blocks % (4 * span) == 0:
-        first, second, third = exchanged(span), exchanged(2 * span), exchanged(3 * span)
-        values = (values + first) + (second + third)
-        span *= 4
-    if blocks % (2 * span) == 0:
-        values = values + exchanged(span)
+    while blocks % (2 * span) == 0:
+        values = values + lax.ppermute(values, "blk", [(i, i ^ span) for i in range(blocks)])
         span *= 2
     if span < blocks:
         groups = [list(range(i, blocks, span)) for i in range(span)]
@@ -454,27 +449,26 @@
     core = lax.axis_index("narrow").astype(jnp.int32).reshape(1)
     other_emb = between_cores(embeddings)
     far_emb = between_blocks(embeddings, -1)
+    seed16 = start_seed.astype(jnp.int16).T
+    seeds = jnp.concatenate([seed16, between_cores(seed16)], axis=0)
+    near_seeds = between_blocks(seeds, -1)
+    keep = lax.dynamic_slice(pair_mask, (where, core[0]), (1, 1))[0]
     emb_args = [embeddings, other_emb]
     pair_shape, row_shape = ((2 * NVEC, size), F32), ((16, size), F32)
     h0, l0, sums, row_sq = make_tile(own_body, emb_args, size, extra=(((2 * size, 128), F32),))
-    far_emb, sums = lax.optimization_barrier((far_emb, sums))
+    far_emb, sums, near_seeds, keep = lax.optimization_barrier((far_emb, sums, near_seeds, keep))
+    second, sums = lax.optimization_barrier((embeddings, sums))
     pairs = [(2 * i, (i - 2) % blocks * 2 + 1) for i in range(blocks)]
     pairs += [(2 * i + 1, (i - 1) % blocks * 2) for i in range(blocks) if blocks % 2 or i % 2]
-    direct = lax.ppermute(embeddings, ("blk", "narrow"), pairs)
+    direct = lax.ppermute(second, ("blk", "narrow"), pairs)
     relayed = direct
     if blocks % 2 == 0:
         relayed = lax.ppermute(far_emb, ("blk", "narrow"), [(2 * i + 1, 2 * i + 2) for i in range(0, blocks, 2)])
     choice = (1 - core) * (where % 2 * (1 - blocks % 2)).astype(jnp.int32)
-    keep = lax.dynamic_slice(pair_mask, (where, core[0]), (1, 1))[0]
-    h1, l1, sums, cols = make_tile(
-        far_body, [keep, *emb_args, row_sq, far_emb, sums], size, (0,), (((8, size), F32),))
-    seed16 = start_seed.astype(jnp.int16).T
-    seeds = jnp.concatenate([seed16, between_cores(seed16)], axis=0)
-    near_seeds, sums = lax.optimization_barrier((seeds, sums))
-    near_seeds = between_blocks(near_seeds, -1)
-    h2, l2, sums, cols, near_seeds = make_tile(
-        relayed_body, [keep, choice, *emb_args, row_sq, direct, relayed, sums, cols, near_seeds], size, (0, 1),
-        (row_shape, pair_shape))
+    h1, l1, sums, cols, near_seeds = make_tile(
+        far_body, [keep, *emb_args, row_sq, far_emb, sums, near_seeds], size, (0,), (((8, size), F32), pair_shape))
+    h2, l2, sums, cols = make_tile(
+        relayed_body, [keep, choice, *emb_args, row_sq, direct, relayed, sums, cols], size, (0, 1), (row_shape,))
     sums = sums + between_blocks(cols, 1)
 
     small = dict(flops=10**6, nbytes=10**5)

time: 117 us -> 117 us (level)
  blocking collectives: 0 us -> 15 us
  starting transfers between devices: 35.3 us -> 25.2 us
  waiting for transfers between devices: 37.2 us -> 32.8 us
  local copies, waits for them, and re-layouts: 7.08 us -> 3.56 us
  Pallas kernels: 35.2 us -> 38.6 us
    all_to_all x0 -> x1, blocking collectives: none -> 15 us  [total_over_blocks(): return jnp.sum(lax.all_to_all(copies, 'blk', 0, 0), axis=0)]
    ppermute x5 -> x1, starting transfers between devices: 9.83 us -> 4.16 us  [shards(): direct = lax.ppermute(second, ('blk', 'narrow'), pairs)]
    unnamed x28 -> x10, local copies, waits for them, and re-layouts: 6.51 us -> 2.89 us
    pallas_call x16, Pallas kernels: 35.2 us -> 38.6 us  [call(): pl.pallas_call(body, out_shape=[jax.ShapeDtypeStruct(shape, dtype) for sh...]
    ppermute x8, starting transfers between devices: 22.6 us -> 19.6 us  [between_blocks(): return lax.ppermute(shard, ('blk', 'narrow'), pairs)]
    ppermute x5 -> x1, waiting for transfers between devices: 5.09 us -> 2.54 us  [shards(): direct = lax.ppermute(second, ('blk', 'narrow'), pairs)]
    ppermute x8, waiting for transfers between devices: 26.4 us -> 24.4 us  [between_blocks(): return lax.ppermute(shard, ('blk', 'narrow'), pairs)]
    ppermute x7, starting transfers between devices: 2.16 us -> 0.74 us  [between_cores(): return lax.ppermute(shard, 'narrow', [(0, 1), (1, 0)])]
  transfers between devices with their start and end apart: 21 -> 17, of which waited for: 16 -> 12; matrix products, arithmetic and copies ran while one was open for 1% -> 1% of each run, Pallas kernels for 5% -> 7%
where the time goes in v7:
time: 117 us
  Pallas kernels  38.6 us (33%)
  waiting for transfers between devices  32.8 us (28%)
  starting transfers between devices  25.2 us (22%)
  blocking collectives  15 us (13%)
  local copies, waits for them, and re-layouts  3.56 us (3%)
    pallas_call x16, Pallas kernels, call(): pl.pallas_call(body, out_shape=[jax.ShapeDtypeStruct(shape, dtype) for sh...  38.6 us
    ppermute x8, waiting for transfers between devices, between_blocks(): return lax.ppermute(shard, ('blk', 'narrow'), pairs)  24.4 us
    ppermute x8, starting transfers between devices, between_blocks(): return lax.ppermute(shard, ('blk', 'narrow'), pairs)  19.6 us
    all_to_all x1, blocking collectives, total_over_blocks(): return jnp.sum(lax.all_to_all(copies, 'blk', 0, 0), axis=0)  15 us
    ppermute x7, waiting for transfers between devices, between_cores(): return lax.ppermute(shard, 'narrow', [(0, 1), (1, 0)])  5.78 us
    ppermute x1, starting transfers between devices, shards(): direct = lax.ppermute(second, ('blk', 'narrow'), pairs)  4.16 us
    unnamed x10, local copies, waits for them, and re-layouts  2.89 us
    ppermute x1, waiting for transfers between devices, shards(): direct = lax.ppermute(second, ('blk', 'narrow'), pairs)  2.54 us
  transfers between devices with their start and end apart: 17, of which 12 were waited for; matrix products, arithmetic and copies ran while one was open for 1% of the time, Pallas kernels for 7%

profile of v7, /device:TPU:0, one launch (start us, length us, event | category | flops | bytes accessed | tf_op | source)
XLA Modules:
  0.0 117.0 jit_solution(3405271607228712729)
XLA Ops:
  0.0 0.5 collective-permute-start.1
  0.5 5.5 %collective-permute-start = (bf16[384,768]{1,0:T(8,128)(2,1)}, bf16[384,768]{1,0:T(8,128)(2,1)S(1)}, u32[]{:S(2)}, u32[]{:S(2)}) collective-permute-start(bf16[384,768]{1,0:T(8,128)(2,1)} %own.5), channel_id=1, source_target_pairs={{0,14},{1,13},{2,0},{3,15},{4,2},{5,1},{6,4},{7,3},{8,6},{9,5},{10... | collective-permute-start | bytes 1769480 | tf_op jit(solution)/shard_map/ppermute | solution.py:423
  6.0 0.9 convert_bitcast_fusion
  6.9 0.0 copy-start.4
  6.9 0.7 copy-done.4
  7.6 0.7 dynamic_slice.3
  8.3 0.7 collective-permute-start.3
  9.0 2.9 %shard_map.46 = (bf16[768,384]{1,0:T(8,128)(2,1)S(1)}, bf16[768,384]{1,0:T(8,128)(2,1)S(1)}, f32[16,384]{1,0:T(8,128)S(1)}, f32[768,128]{1,0:T(8,128)S(1)}) custom-call(bf16[384,768]{1,0:T(8,128)(2,1)} %own.5, bf16[384,768]{1,0:T(8,128)(2,1)S(1)} %collective-permute-done.1.other), custom_call_target="tpu_custom_call" | custom-call | flops 2000000000 | bytes 1000000 | tf_op jit(solution)/shard_map/pallas_call | solution.py:36
  11.9 0.9 copy-done
  12.8 0.6 copy-done.2
  13.4 7.3 %collective-permute-done.3.near_seeds = s16[128,384]{1,0:T(8,128)(2,1)S(1)} collective-permute-done((s16[128,384]{1,0:T(8,128)(2,1)S(1)}, s16[128,384]{1,0:T(8,128)(2,1)S(1)}, u32[]{:S(2)}, u32[]{:S(2)}) %collective-permute-start.3) | collective-permute-done | bytes 98336 | tf_op jit(solution)/shard_map/ppermute | solution.py:423
  20.6 4.2 %collective-permute-start.4 = (bf16[384,768]{1,0:T(8,128)(2,1)}, bf16[384,768]{1,0:T(8,128)(2,1)S(1)}, u32[]{:S(2)}, u32[]{:S(2)}) collective-permute-start(bf16[384,768]{1,0:T(8,128)(2,1)} %own.5), channel_id=1, source_target_pairs={{0,13},{2,15},{4,1},{6,3},{8,5},{10,7},{12,9},{14,11},{3,0},{7,4},... | collective-permute-start | bytes 1769480 | tf_op jit(solution)/shard_map/ppermute | solution.py:463
  24.8 0.7 collective-permute-start.5
  25.5 0.7 copy-done.3
  26.3 3.7 %shard_map.47 = (bf16[768,384]{1,0:T(8,128)(2,1)S(1)}, bf16[768,384]{1,0:T(8,128)(2,1)S(1)}, f32[16,384]{1,0:T(8,128)S(1)}, f32[8,384]{1,0:T(8,128)S(1)}, f32[128,384]{1,0:T(8,128)S(1)}) custom-call(s32[1]{0:T(128)} %bitcast.2.keep, bf16[384,768]{1,0:T(8,128)(2,1)} %own.5, bf16[384,768]{1,0:T(8,128)(2,1)S(1)} %collective-permute-done.1.other, ...), custom_call_target="tpu_custom_call" | custom-call | flops 2000000000 | bytes 1000000 | tf_op jit(solution)/shard_map/pallas_call | solution.py:36
  30.0 2.5 %collective-permute-done.4.direct = bf16[384,768]{1,0:T(8,128)(2,1)S(1)} collective-permute-done((bf16[384,768]{1,0:T(8,128)(2,1)}, bf16[384,768]{1,0:T(8,128)(2,1)S(1)}, u32[]{:S(2)}, u32[]{:S(2)}) %collective-permute-start.4) | collective-permute-done | bytes 589856 | tf_op jit(solution)/shard_map/ppermute | solution.py:463
  32.5 3.7 %shard_map.48 = (bf16[768,384]{1,0:T(8,128)(2,1)S(1)}, bf16[768,384]{1,0:T(8,128)(2,1)S(1)}, f32[16,384]{1,0:T(8,128)S(1)}, f32[16,384]{1,0:T(8,128)S(1)}) custom-call(s32[1]{0:T(128)} %bitcast.2.keep, s32[1]{0:T(128)S(6)} %mul.7.choice, bf16[384,768]{1,0:T(8,128)(2,1)} %own.5, bf16[384,768]{1,0:T(8,128)(2,1)S(1)} %collective-permute-done.1.other, ...), custom_call_target="tpu_custom_call" | custom-call | flops 2000000000 | bytes 1000000 | tf_op jit(solution)/shard_map/pallas_call | solution.py:36
  36.2 0.9 collective-permute-start.6
  37.1 6.8 %collective-permute-done.6 = f32[16,384]{1,0:T(8,128)S(1)} collective-permute-done((f32[16,384]{1,0:T(8,128)S(1)}, f32[16,384]{1,0:T(8,128)S(1)}, u32[]{:S(2)}, u32[]{:S(2)}) %collective-permute-start.6) | collective-permute-done | bytes 24608 | tf_op jit(solution)/shard_map/ppermute | solution.py:423
  43.9 1.2 %collective-permute-done.7.other_sums = f32[16,384]{1,0:T(8,128)S(1)} collective-permute-done((f32[16,384]{1,0:T(8,128)S(1)}, f32[16,384]{1,0:T(8,128)S(1)}, u32[]{:S(2)}, u32[]{:S(2)}) %collective-permute-start.7) | collective-permute-done | bytes 24608 | tf_op jit(solution)/shard_map/ppermute | solution.py:427
  45.1 0.5 shard_map.51
  45.6 0.1 collective-permute-start.9
  45.7 4.7 %collective-permute-start.8 = (f32[16,384]{1,0:T(8,128)S(1)}, f32[16,384]{1,0:T(8,128)S(1)}, u32[]{:S(2)}, u32[]{:S(2)}) collective-permute-start(f32[16,384]{1,0:T(8,128)S(1)} %get-tuple-element.48), channel_id=1, source_target_pairs={{0,14},{1,13},{2,0},{3,15},{4,2},{5,1},{6,4},{7,3},{8,6},{9,5},{10... | collective-permute-start | bytes 73736 | tf_op jit(solution)/shard_map/ppermute | solution.py:423
  50.4 0.5 shard_map.50.product
  50.9 1.0 collective-permute-done.8.near_scale
  51.9 2.1 %collective-permute-done.9.refs_0_ = f32[128,384]{1,0:T(8,128)S(1)} collective-permute-done((f32[128,384]{1,0:T(8,128)S(1)}, f32[128,384]{1,0:T(8,128)S(1)}, u32[]{:S(2)}, u32[]{:S(2)}) %collective-permute-start.9) | collective-permute-done | bytes 196640 | tf_op jit(solution)/shard_map/ppermute | solution.py:423
  54.1 0.8 shard_map.52.total
  54.9 0.1 collective-permute-start.10
  55.0 1.4 %collective-permute-done.10.other_total = f32[128,384]{1,0:T(8,128)S(1)} collective-permute-done((f32[128,384]{1,0:T(8,128)S(1)}, f32[128,384]{1,0:T(8,128)S(1)}, u32[]{:S(2)}, u32[]{:S(2)}) %collective-permute-start.10) | collective-permute-done | bytes 196640 | tf_op jit(solution)/shard_map/ppermute | solution.py:427
  56.4 0.5 shard_map.55
  56.9 0.1 collective-permute-start.12
  57.0 4.7 %collective-permute-start.11 = (f32[128,384]{1,0:T(8,128)S(1)}, f32[128,384]{1,0:T(8,128)S(1)}, u32[]{:S(2)}, u32[]{:S(2)}) collective-permute-start(f32[128,384]{1,0:T(8,128)S(1)} %shard_map.53.vectors.v1), channel_id=1, source_target_pairs={{0,14},{1,13},{2,0},{3,15},{4,2},{5,1},{6,4},{7,3},{8,6},{9,5},{10... | collective-permute-start | bytes 589832 | tf_op jit(solution)/shard_map/ppermute | solution.py:423
  61.7 0.5 shard_map.54.product
  62.2 5.0 %collective-permute-done.12.refs_0_ = f32[128,384]{1,0:T(8,128)S(1)} collective-permute-done((f32[128,384]{1,0:T(8,128)S(1)}, f32[128,384]{1,0:T(8,128)S(1)}, u32[]{:S(2)}, u32[]{:S(2)}) %collective-permute-start.12) | collective-permute-done | bytes 196640 | tf_op jit(solution)/shard_map/ppermute | solution.py:423
  67.2 0.8 shard_map.56.total
  68.0 0.1 collective-permute-start.13
  68.1 1.4 %collective-permute-done.13.other_total = f32[128,384]{1,0:T(8,128)S(1)} collective-permute-done((f32[128,384]{1,0:T(8,128)S(1)}, f32[128,384]{1,0:T(8,128)S(1)}, u32[]{:S(2)}, u32[]{:S(2)}) %collective-permute-start.13) | collective-permute-done | bytes 196640 | tf_op jit(solution)/shard_map/ppermute | solution.py:427
  69.6 3.0 %collective-permute-start.14 = (f32[128,384]{1,0:T(8,128)S(1)}, f32[128,384]{1,0:T(8,128)S(1)}, u32[]{:S(2)}, u32[]{:S(2)}) collective-permute-start(f32[128,384]{1,0:T(8,128)S(1)} %shard_map.57.v2.vectors), channel_id=1, source_target_pairs={{0,14},{1,13},{2,0},{3,15},{4,2},{5,1},{6,4},{7,3},{8,6},{9,5},{10... | collective-permute-start | bytes 589832 | tf_op jit(solution)/shard_map/ppermute | solution.py:423
  72.6 0.5 shard_map.59.product
  73.1 0.5 shard_map.58
  73.6 2.2 %collective-permute-done.14.near = f32[128,384]{1,0:T(8,128)S(1)} collective-permute-done((f32[128,384]{1,0:T(8,128)S(1)}, f32[128,384]{1,0:T(8,128)S(1)}, u32[]{:S(2)}, u32[]{:S(2)}) %collective-permute-start.14) | collective-permute-done | bytes 196640 | tf_op jit(solution)/shard_map/ppermute | solution.py:423
  75.8 1.4 %shard_map.60 = (f32[56,128]{1,0:T(8,128)S(1)}, f32[56,128]{1,0:T(8,128)S(1)}) custom-call(s32[1]{0:T(128)} %bitcast.core.refs_0_, f32[320,64]{1,0:T(8,128)S(1)} %get-tuple-element.53.low, f32[128,384]{1,0:T(8,128)S(1)} %shard_map.57.v2.vectors, f32[128,384]{1,0:T(8,128)S(1)} %shard_map.59.product, f32[128,384]{1,0:T(8,128)S(1)} %collective-permute-done.14.near, ...), custom_call_target="tpu_custom_call" | custom-call | flops 1000000000 | bytes 1000000 | tf_op jit(solution)/shard_map/pallas_call | solution.py:36
  77.2 0.1 collective-permute-start.15
  77.2 1.2 %collective-permute-done.15 = f32[56,128]{1,0:T(8,128)S(1)} collective-permute-done((f32[56,128]{1,0:T(8,128)S(1)}, f32[56,128]{1,0:T(8,128)S(1)}, u32[]{:S(2)}, u32[]{:S(2)}) %collective-permute-start.15) | collective-permute-done | bytes 28704 | tf_op jit(solution)/shard_map/ppermute | solution.py:427
  78.4 15.0 %all_to_all.5 = f32[8,56,128]{2,1,0:T(8,128)S(1)} all-to-all(f32[8,56,128]{2,1,0:T(8,128)S(1)} %broadcast_in_dim.2), channel_id=1, replica_groups=mesh['groups'=2,'blk'=8,'narrow'=2] {'blk'}, dimensions={0} | all-to-all | bytes 458752 | tf_op jit(solution)/shard_map/all_to_all | solution.py:434
  93.5 0.1 collective-permute-start.16
  94.2 0.5 collective-permute-done.16.refs_3_
  94.8 22.2 %shard_map.61 = f32[64,384]{1,0:T(8,128)} custom-call(s32[1]{0:T(128)} %bitcast.core.refs_0_, s32[1]{0:T(128)S(6)} %copy.5.refs_1_, f32[56,128]{1,0:T(8,128)S(1)} %reduce_sum.9.refs_2_, f32[56,128]{1,0:T(8,128)S(1)} %collective-permute-done.16.refs_3_, f32[192,384]{1,0:T(8,128)S(1)} %get-tuple-element.56.refs_4_), custom_call_target="tpu_custom_call" | custom-call | flops 20000000000 | bytes 1000000 | tf_op jit(solution)/shard_map/pallas_call | solution.py:36
  (20 shorter events, 0.2 us)
Async XLA Ops:
  0.0 9.0 %collective-permute-start.1 = (bf16[384,768]{1,0:T(8,128)(2,1)}, bf16[384,768]{1,0:T(8,128)(2,1)S(1)}, u32[]{:S(2)}, u32[]{:S(2)}) collective-permute-start(bf16[384,768]{1,0:T(8,128)(2,1)} %own.5), channel_id=1, source_target_pairs={{0,1},{1,0},{2,3},{3,2},{4,5},{5,4},{6,7},{7,6},{8,9},{9,8},{10,11... | collective-permute-start | bytes 1769480 | tf_op jit(solution)/shard_map/ppermute | solution.py:427
  0.5 20.2 %collective-permute-start = (bf16[384,768]{1,0:T(8,128)(2,1)}, bf16[384,768]{1,0:T(8,128)(2,1)S(1)}, u32[]{:S(2)}, u32[]{:S(2)}) collective-permute-start(bf16[384,768]{1,0:T(8,128)(2,1)} %own.5), channel_id=1, source_target_pairs={{0,14},{1,13},{2,0},{3,15},{4,2},{5,1},{6,4},{7,3},{8,6},{9,5},{10... | collective-permute-start | bytes 1769480 | tf_op jit(solution)/shard_map/ppermute | solution.py:423
  6.9 1.4 %collective-permute-start.2 = (s16[64,384]{1,0:T(8,128)(2,1)S(1)}, s16[64,384]{1,0:T(8,128)(2,1)S(1)}, u32[]{:S(2)}, u32[]{:S(2)}) collective-permute-start(s16[64,384]{1,0:T(8,128)(2,1)S(1)} %convert_bitcast_fusion), channel_id=1, source_target_pairs={{0,1},{1,0},{2,3},{3,2},{4,5},{5,4},{6,7},{7,6},{8,9},{9,8},{10,11... | collective-permute-start | bytes 147464 | tf_op jit(solution)/shard_map/ppermute | solution.py:427
  6.9 0.7 copy-start.4
  8.3 12.4 %collective-permute-start.3 = (s16[128,384]{1,0:T(8,128)(2,1)S(1)}, s16[128,384]{1,0:T(8,128)(2,1)S(1)}, u32[]{:S(2)}, u32[]{:S(2)}) collective-permute-start(s16[128,384]{1,0:T(8,128)(2,1)S(1)} %pad_add_fusion.seeds), channel_id=1, source_target_pairs={{0,14},{1,13},{2,0},{3,15},{4,2},{5,1},{6,4},{7,3},{8,6},{9,5},{10... | collective-permute-start | bytes 294920 | tf_op jit(solution)/shard_map/ppermute | solution.py:423
  11.9 0.9 copy-start
  12.8 0.6 copy-start.2
  20.6 11.9 %collective-permute-start.4 = (bf16[384,768]{1,0:T(8,128)(2,1)}, bf16[384,768]{1,0:T(8,128)(2,1)S(1)}, u32[]{:S(2)}, u32[]{:S(2)}) collective-permute-start(bf16[384,768]{1,0:T(8,128)(2,1)} %own.5), channel_id=1, source_target_pairs={{0,13},{2,15},{4,1},{6,3},{8,5},{10,7},{12,9},{14,11},{3,0},{7,4},... | collective-permute-start | bytes 1769480 | tf_op jit(solution)/shard_map/ppermute | solution.py:463
  24.8 7.7 %collective-permute-start.5 = (bf16[384,768]{1,0:T(8,128)(2,1)S(1)}, bf16[384,768]{1,0:T(8,128)(2,1)S(1)}, u32[]{:S(2)}, u32[]{:S(2)}) collective-permute-start(bf16[384,768]{1,0:T(8,128)(2,1)S(1)} %collective-permute-done.col), channel_id=1, source_target_pairs={{1,2},{5,6},{9,10},{13,14},{17,18},{21,22},{25,26},{29,30}} | collective-permute-start | bytes 1769480 | tf_op jit(solution)/shard_map/ppermute | solution.py:466
  25.5 0.7 copy-start.3
  36.2 7.7 %collective-permute-start.6 = (f32[16,384]{1,0:T(8,128)S(1)}, f32[16,384]{1,0:T(8,128)S(1)}, u32[]{:S(2)}, u32[]{:S(2)}) collective-permute-start(f32[16,384]{1,0:T(8,128)S(1)} %get-tuple-element.42), channel_id=1, source_target_pairs={{0,2},{1,5},{2,4},{3,7},{4,6},{5,9},{6,8},{7,11},{8,10},{9,13},{10... | collective-permute-start | bytes 73736 | tf_op jit(solution)/shard_map/ppermute | solution.py:423
  43.9 1.2 %collective-permute-start.7 = (f32[16,384]{1,0:T(8,128)S(1)}, f32[16,384]{1,0:T(8,128)S(1)}, u32[]{:S(2)}, u32[]{:S(2)}) collective-permute-start(f32[16,384]{1,0:T(8,128)S(1)} %add.19.sums), channel_id=1, source_target_pairs={{0,1},{1,0},{2,3},{3,2},{4,5},{5,4},{6,7},{7,6},{8,9},{9,8},{10,11... | collective-permute-start | bytes 73736 | tf_op jit(solution)/shard_map/ppermute | solution.py:427
  45.1 5.3 %copy-start.1 = (bf16[768,384]{1,0:T(8,128)(2,1)S(1)}, bf16[768,384]{1,0:T(8,128)(2,1)}, u32[]{:S(2)}) copy-start(bf16[768,384]{1,0:T(8,128)(2,1)} %copy-done) | copy-start | bytes 1769476
  45.6 8.4 %collective-permute-start.9 = (f32[128,384]{1,0:T(8,128)S(1)}, f32[128,384]{1,0:T(8,128)S(1)}, u32[]{:S(2)}, u32[]{:S(2)}) collective-permute-start(f32[128,384]{1,0:T(8,128)S(1)} %shard_map.51), channel_id=1, source_target_pairs={{0,2},{1,5},{2,4},{3,7},{4,6},{5,9},{6,8},{7,11},{8,10},{9,13},{10... | collective-permute-start | bytes 589832 | tf_op jit(solution)/shard_map/ppermute | solution.py:423
  45.7 6.2 %collective-permute-start.8 = (f32[16,384]{1,0:T(8,128)S(1)}, f32[16,384]{1,0:T(8,128)S(1)}, u32[]{:S(2)}, u32[]{:S(2)}) collective-permute-start(f32[16,384]{1,0:T(8,128)S(1)} %get-tuple-element.48), channel_id=1, source_target_pairs={{0,14},{1,13},{2,0},{3,15},{4,2},{5,1},{6,4},{7,3},{8,6},{9,5},{10... | collective-permute-start | bytes 73736 | tf_op jit(solution)/shard_map/ppermute | solution.py:423
  54.9 1.5 %collective-permute-start.10 = (f32[128,384]{1,0:T(8,128)S(1)}, f32[128,384]{1,0:T(8,128)S(1)}, u32[]{:S(2)}, u32[]{:S(2)}) collective-permute-start(f32[128,384]{1,0:T(8,128)S(1)} %shard_map.52.total), channel_id=1, source_target_pairs={{0,1},{1,0},{2,3},{3,2},{4,5},{5,4},{6,7},{7,6},{8,9},{9,8},{10,11... | collective-permute-start | bytes 589832 | tf_op jit(solution)/shard_map/ppermute | solution.py:427
  56.9 10.3 %collective-permute-start.12 = (f32[128,384]{1,0:T(8,128)S(1)}, f32[128,384]{1,0:T(8,128)S(1)}, u32[]{:S(2)}, u32[]{:S(2)}) collective-permute-start(f32[128,384]{1,0:T(8,128)S(1)} %shard_map.55), channel_id=1, source_target_pairs={{0,2},{1,5},{2,4},{3,7},{4,6},{5,9},{6,8},{7,11},{8,10},{9,13},{10... | collective-permute-start | bytes 589832 | tf_op jit(solution)/shard_map/ppermute | solution.py:423
  57.0 10.2 %collective-permute-start.11 = (f32[128,384]{1,0:T(8,128)S(1)}, f32[128,384]{1,0:T(8,128)S(1)}, u32[]{:S(2)}, u32[]{:S(2)}) collective-permute-start(f32[128,384]{1,0:T(8,128)S(1)} %shard_map.53.vectors.v1), channel_id=1, source_target_pairs={{0,14},{1,13},{2,0},{3,15},{4,2},{5,1},{6,4},{7,3},{8,6},{9,5},{10... | collective-permute-start | bytes 589832 | tf_op jit(solution)/shard_map/ppermute | solution.py:423
  68.0 1.5 %collective-permute-start.13 = (f32[128,384]{1,0:T(8,128)S(1)}, f32[128,384]{1,0:T(8,128)S(1)}, u32[]{:S(2)}, u32[]{:S(2)}) collective-permute-start(f32[128,384]{1,0:T(8,128)S(1)} %shard_map.56.total), channel_id=1, source_target_pairs={{0,1},{1,0},{2,3},{3,2},{4,5},{5,4},{6,7},{7,6},{8,9},{9,8},{10,11... | collective-permute-start | bytes 589832 | tf_op jit(solution)/shard_map/ppermute | solution.py:427
  69.6 6.2 %collective-permute-start.14 = (f32[128,384]{1,0:T(8,128)S(1)}, f32[128,384]{1,0:T(8,128)S(1)}, u32[]{:S(2)}, u32[]{:S(2)}) collective-permute-start(f32[128,384]{1,0:T(8,128)S(1)} %shard_map.57.v2.vectors), channel_id=1, source_target_pairs={{0,14},{1,13},{2,0},{3,15},{4,2},{5,1},{6,4},{7,3},{8,6},{9,5},{10... | collective-permute-start | bytes 589832 | tf_op jit(solution)/shard_map/ppermute | solution.py:423
  77.2 1.3 %collective-permute-start.15 = (f32[56,128]{1,0:T(8,128)S(1)}, f32[56,128]{1,0:T(8,128)S(1)}, u32[]{:S(2)}, u32[]{:S(2)}) collective-permute-start(f32[56,128]{1,0:T(8,128)S(1)} %get-tuple-element.55), channel_id=1, source_target_pairs={{0,1},{1,0},{2,3},{3,2},{4,5},{5,4},{6,7},{7,6},{8,9},{9,8},{10,11... | collective-permute-start | bytes 86024 | tf_op jit(solution)/shard_map/ppermute | solution.py:427
  93.5 1.3 %collective-permute-start.16 = (f32[56,128]{1,0:T(8,128)S(1)}, f32[56,128]{1,0:T(8,128)S(1)}, u32[]{:S(2)}, u32[]{:S(2)}) collective-permute-start(f32[56,128]{1,0:T(8,128)S(1)} %reduce_sum.9.refs_2_), channel_id=1, source_target_pairs={{0,1},{1,0},{2,3},{3,2},{4,5},{5,4},{6,7},{7,6},{8,9},{9,8},{10,11... | collective-permute-start | bytes 86024 | tf_op jit(solution)/shard_map/ppermute | solution.py:427

commit v8 on v7

--- a/solution.py
+++ b/solution.py
@@ -73,13 +73,10 @@
     return jnp.broadcast_to(total, (8, size))
 
 
-def seed_values(seeds):
-    return seeds[...].astype(jnp.int32).astype(F32) / 1000.0
-
-
-def own_body(own, other, high, low, row_sum, row_sq):
+def own_body(own, other, high, low, row_sum, row_sq, copy):
     size = own.shape[0]
     embs = [own[...], other[...]]
+    copy[...] = embs[0]
     for half in range(2):
         row32 = embs[half].astype(F32)
         squares = (2.0 * LOG2_E) * jnp.sum(row32 * row32, axis=1, keepdims=True)
@@ -88,9 +85,8 @@
     fill_tile(1.0, embs, row_sq, embs[0], high, low, row_sum)
 
 
-def far_body(keep, own, other, row_sq, col, before, near_seeds, high, low, row_sum, col_sum, near_seeds_out):
+def far_body(keep, own, other, row_sq, col, before, high, low, row_sum, col_sum):
     row_sum[...] = before[...]
-    near_seeds_out[...] = seed_values(near_seeds)
     col_sum[...] = fill_tile(keep[0].astype(F32), [own[...], other[...]], row_sq, col[...], high, low, row_sum)
 
 
@@ -119,12 +115,11 @@
     return jnp.concatenate([jnp.broadcast_to(values[i:i + 1, :], shape) for i in (0, 8)], axis=0)
 
 
-def degree_body(sums, other_sums, seeds, degree_out, scale_out, vectors_out):
+def degree_body(sums, other_sums, seeds, degree_out, vectors_out):
     degree = sums[...] + swapped(other_sums[...])
     scale = lax.rsqrt(degree)
     degree_out[...] = degree
-    scale_out[...] = scale
-    vectors_out[...] = seed_values(seeds) * per_row(scale, seeds.shape[0] // 2)
+    vectors_out[...] = seeds[...] * per_row(scale, seeds.shape[0] // 2)
 
 
 def ahead_body(vectors, h1, l1, h2, l2, ahead):
@@ -158,18 +153,10 @@
     out[...] = stacked(product_rows(vectors[:vectors.shape[0] // 2, :], h0, l0))
 
 
-def add_blocks(product, near, behind, h1, l1, h2, l2, total):
+def block_body(product, near, behind, h1, l1, h2, l2, total):
     width = near.shape[0] // 2
-    far = product_rows(near[:width], h1, l1) + product_rows(near[width:], h2, l2)
+    far = product_rows(near[:width, :], h1, l1) + product_rows(near[width:, :], h2, l2)
     total[...] = product[...] + behind[...] + stacked(far)
-
-
-def first_block_body(product, near_seeds, near_scale, *refs):
-    add_blocks(product, near_seeds[...] * per_row(near_scale[...], near_seeds.shape[0] // 2), *refs)
-
-
-def block_body(product, near, *refs):
-    add_blocks(product, near[...], *refs)
 
 
 def low_body(degree, v0, v1, v2, moments, scaled):
@@ -429,9 +416,6 @@
 
 def total_over_blocks(values):
     blocks = lax.axis_size("blk")
-    if blocks <= 8:
-        copies = jnp.broadcast_to(values[None], (blocks, *values.shape))
-        return jnp.sum(lax.all_to_all(copies, "blk", 0, 0), axis=0)
     span = 1
     while blocks % (2 * span) == 0:
         values = values + lax.ppermute(values, "blk", [(i, i ^ span) for i in range(blocks)])
@@ -449,43 +433,40 @@
     core = lax.axis_index("narrow").astype(jnp.int32).reshape(1)
     other_emb = between_cores(embeddings)
     far_emb = between_blocks(embeddings, -1)
-    seed16 = start_seed.astype(jnp.int16).T
-    seeds = jnp.concatenate([seed16, between_cores(seed16)], axis=0)
-    near_seeds = between_blocks(seeds, -1)
+    seed = start_seed.astype(F32).T / 1000.0
+    seeds = jnp.concatenate([seed, between_cores(seed)], axis=0)
     keep = lax.dynamic_slice(pair_mask, (where, core[0]), (1, 1))[0]
     emb_args = [embeddings, other_emb]
     pair_shape, row_shape = ((2 * NVEC, size), F32), ((16, size), F32)
-    h0, l0, sums, row_sq = make_tile(own_body, emb_args, size, extra=(((2 * size, 128), F32),))
-    far_emb, sums, near_seeds, keep = lax.optimization_barrier((far_emb, sums, near_seeds, keep))
-    second, sums = lax.optimization_barrier((embeddings, sums))
+    h0, l0, sums, row_sq, own_copy = make_tile(
+        own_body, emb_args, size, extra=(((2 * size, 128), F32), (embeddings.shape, BF16)))
+    emb_args = [own_copy, other_emb]
+    far_emb, sums, seeds, keep = lax.optimization_barrier((far_emb, sums, seeds, keep))
     pairs = [(2 * i, (i - 2) % blocks * 2 + 1) for i in range(blocks)]
     pairs += [(2 * i + 1, (i - 1) % blocks * 2) for i in range(blocks) if blocks % 2 or i % 2]
-    direct = lax.ppermute(second, ("blk", "narrow"), pairs)
+    direct = lax.ppermute(own_copy, ("blk", "narrow"), pairs)
     relayed = direct
     if blocks % 2 == 0:
         relayed = lax.ppermute(far_emb, ("blk", "narrow"), [(2 * i + 1, 2 * i + 2) for i in range(0, blocks, 2)])
     choice = (1 - core) * (where % 2 * (1 - blocks % 2)).astype(jnp.int32)
-    h1, l1, sums, cols, near_seeds = make_tile(
-        far_body, [keep, *emb_args, row_sq, far_emb, sums, near_seeds], size, (0,), (((8, size), F32), pair_shape))
+    h1, l1, sums, cols = make_tile(
+        far_body, [keep, *emb_args, row_sq, far_emb, sums], size, (0,), (((8, size), F32),))
     h2, l2, sums, cols = make_tile(
         relayed_body, [keep, choice, *emb_args, row_sq, direct, relayed, sums, cols], size, (0, 1), (row_shape,))
     sums = sums + between_blocks(cols, 1)
 
     small = dict(flops=10**6, nbytes=10**5)
     middle = dict(flops=10**9, nbytes=10**6)
-    degree, scale, vectors = call(
-        degree_body, [row_shape, row_shape, pair_shape], [sums, between_cores(sums), seeds], **small)
+    degree, vectors = call(
+        degree_body, [row_shape, pair_shape], [sums, between_cores(sums), seeds], **small)
     far = [h1, l1, h2, l2]
     history = [vectors]
-    for repeat in range(2):
-        if repeat == 0:
-            body, near = first_block_body, [near_seeds, between_blocks(scale, -1)]
-        else:
-            body, near = block_body, [between_blocks(vectors, -1)]
+    for _ in range(2):
+        near = between_blocks(vectors, -1)
         (ahead,) = call(ahead_body, [pair_shape], [vectors, *far], **middle)
         behind = between_blocks(ahead, 1)
         (product,) = call(own_product_body, [pair_shape], [vectors, h0, l0], **middle)
-        (total,) = call(body, [pair_shape], [product, *near, behind, *far], **middle)
+        (total,) = call(block_body, [pair_shape], [product, near, behind, *far], **middle)
         (vectors,) = call(combine_body, [pair_shape], [total, between_cores(total), degree], **small)
         history.append(vectors)
     near = between_blocks(vectors, -1)

time: 117 us -> 115 us (0.983)
  blocking collectives: 15 us -> 0 us
  waiting for transfers between devices: 32.8 us -> 40.8 us
  starting transfers between devices: 25.2 us -> 32.9 us
  Pallas kernels: 38.6 us -> 35.3 us
    all_to_all x1 -> x0, blocking collectives: 15 us -> none  [total_over_blocks(): return jnp.sum(lax.all_to_all(copies, 'blk', 0, 0), axis=0)]
    ppermute x1 -> x4, waiting for transfers between devices: 2.54 us -> 12.1 us  [the longest x3 8.11 us: total_over_blocks(): lax.ppermute(values, 'blk', [(i, i ^ span) for i in range(blocks)])]
    ppermute x1 -> x4, starting transfers between devices: 4.16 us -> 12.9 us  [the longest x1 8.51 us: shards(): direct = lax.ppermute(own_copy, ('blk', 'narrow'), pairs)]
    pallas_call x16, Pallas kernels: 38.6 us -> 35.3 us  [call(): pl.pallas_call(body, out_shape=[jax.ShapeDtypeStruct(shape, dtype) for sh...]
    ppermute x8 -> x7, starting transfers between devices: 19.6 us -> 18.3 us  [between_blocks(): return lax.ppermute(shard, ('blk', 'narrow'), pairs)]
    ppermute x8 -> x7, waiting for transfers between devices: 24.4 us -> 23.2 us  [between_blocks(): return lax.ppermute(shard, ('blk', 'narrow'), pairs)]
    unnamed x10 -> x14, local copies, waits for them, and re-layouts: 2.89 us -> 3.02 us
  transfers between devices with their start and end apart: 17 -> 19, of which waited for: 12 -> 14; matrix products, arithmetic and copies ran while one was open for 1% -> 2% of each run, Pallas kernels for 7% -> 6%
where the time goes in v8:
time: 115 us
  waiting for transfers between devices  40.8 us (35%)
  Pallas kernels  35.3 us (31%)
  starting transfers between devices  32.9 us (29%)
  local copies, waits for them, and re-layouts  4.36 us (4%)
    pallas_call x16, Pallas kernels, call(): pl.pallas_call(body, out_shape=[jax.ShapeDtypeStruct(shape, dtype) for sh...  35.3 us
    ppermute x7, waiting for transfers between devices, between_blocks(): return lax.ppermute(shard, ('blk', 'narrow'), pairs)  23.2 us
    ppermute x7, starting transfers between devices, between_blocks(): return lax.ppermute(shard, ('blk', 'narrow'), pairs)  18.3 us
    ppermute x1, starting transfers between devices, shards(): direct = lax.ppermute(own_copy, ('blk', 'narrow'), pairs)  8.51 us
    ppermute x3, waiting for transfers between devices, total_over_blocks(): lax.ppermute(values, 'blk', [(i, i ^ span) for i in range(blocks)])  8.11 us
    ppermute x7, waiting for transfers between devices, between_cores(): return lax.ppermute(shard, 'narrow', [(0, 1), (1, 0)])  5.51 us
    ppermute x3, starting transfers between devices, total_over_blocks(): lax.ppermute(values, 'blk', [(i, i ^ span) for i in range(blocks)])  4.4 us
    ppermute x1, waiting for transfers between devices, shards(): direct = lax.ppermute(own_copy, ('blk', 'narrow'), pairs)  4.03 us
  transfers between devices with their start and end apart: 19, of which 14 were waited for; matrix products, arithmetic and copies ran while one was open for 2% of the time, Pallas kernels for 6%

profile of v8, /device:TPU:0, one launch (start us, length us, event | category | flops | bytes accessed | tf_op | source)
XLA Modules:
  0.0 115.2 jit_solution(8211915677998897014)
XLA Ops:
  0.0 0.5 collective-permute-start.1
  0.5 5.6 %collective-permute-start = (bf16[384,768]{1,0:T(8,128)(2,1)}, bf16[384,768]{1,0:T(8,128)(2,1)S(1)}, u32[]{:S(2)}, u32[]{:S(2)}) collective-permute-start(bf16[384,768]{1,0:T(8,128)(2,1)} %own.1), channel_id=1, source_target_pairs={{0,14},{1,13},{2,0},{3,15},{4,2},{5,1},{6,4},{7,3},{8,6},{9,5},{10... | collective-permute-start | bytes 1769480 | tf_op jit(solution)/shard_map/ppermute | solution.py:410
  6.0 0.9 multiply_bitcast_fusion
  6.9 0.1 collective-permute-start.2
  7.0 1.3 %dynamic_slice.3 = s32[1,1]{0,1:T(1,128)} dynamic-slice(s32[8,2]{0,1:T(2,128)} %param.5, s32[]{:T(128)S(6)} %select_n.13, s32[]{:T(128)S(6)} %select_n.14), dynamic_slice_sizes={1,1} | dynamic-slice | bytes 12 | tf_op jit(solution)/shard_map/dynamic_slice | solution.py:438
  8.4 1.9 %shard_map.46 = (bf16[768,384]{1,0:T(8,128)(2,1)S(1)}, bf16[768,384]{1,0:T(8,128)(2,1)S(1)}, f32[16,384]{1,0:T(8,128)S(1)}, f32[768,128]{1,0:T(8,128)S(1)}, bf16[384,768]{1,0:T(8,128)(2,1)S(1)}) custom-call(bf16[384,768]{1,0:T(8,128)(2,1)S(1)} %copy-done, bf16[384,768]{1,0:T(8,128)(2,1)S(1)} %collective-permute-done.1.other), custom_call_target="tpu_custom_call" | custom-call | flops 2000000000 | bytes 1000000 | tf_op jit(solution)/shard_map/pallas_call | solution.py:36
  10.3 0.8 copy-done.1
  11.1 0.8 copy-done.3
  11.9 0.6 copy-done.5
  12.5 6.1 %collective-permute-done.col = bf16[384,768]{1,0:T(8,128)(2,1)S(1)} collective-permute-done((bf16[384,768]{1,0:T(8,128)(2,1)}, bf16[384,768]{1,0:T(8,128)(2,1)S(1)}, u32[]{:S(2)}, u32[]{:S(2)}) %collective-permute-start) | collective-permute-done | bytes 589856 | tf_op jit(solution)/shard_map/ppermute | solution.py:410
  18.6 0.7 collective-permute-start.4
  19.3 8.5 %collective-permute-start.3 = (bf16[384,768]{1,0:T(8,128)(2,1)S(1)}, bf16[384,768]{1,0:T(8,128)(2,1)S(1)}, u32[]{:S(2)}, u32[]{:S(2)}) collective-permute-start(bf16[384,768]{1,0:T(8,128)(2,1)S(1)} %get-tuple-element.30.own), channel_id=1, source_target_pairs={{0,13},{2,15},{4,1},{6,3},{8,5},{10,7},{12,9},{14,11},{3,0},{7,4},... | collective-permute-start | bytes 1769480 | tf_op jit(solution)/shard_map/ppermute | solution.py:447
  27.9 0.7 copy-done.6
  28.6 2.6 %shard_map.47 = (bf16[768,384]{1,0:T(8,128)(2,1)S(1)}, bf16[768,384]{1,0:T(8,128)(2,1)S(1)}, f32[16,384]{1,0:T(8,128)S(1)}, f32[8,384]{1,0:T(8,128)S(1)}) custom-call(s32[1]{0:T(128)} %bitcast.2.keep, bf16[384,768]{1,0:T(8,128)(2,1)S(1)} %get-tuple-element.30.own, bf16[384,768]{1,0:T(8,128)(2,1)S(1)} %collective-permute-done.1.other, ...), custom_call_target="tpu_custom_call" | custom-call | flops 2000000000 | bytes 1000000 | tf_op jit(solution)/shard_map/pallas_call | solution.py:36
  31.2 4.0 %collective-permute-done.3.direct = bf16[384,768]{1,0:T(8,128)(2,1)S(1)} collective-permute-done((bf16[384,768]{1,0:T(8,128)(2,1)S(1)}, bf16[384,768]{1,0:T(8,128)(2,1)S(1)}, u32[]{:S(2)}, u32[]{:S(2)}) %collective-permute-start.3) | collective-permute-done | bytes 589856 | tf_op jit(solution)/shard_map/ppermute | solution.py:447
  35.2 2.6 %shard_map.48 = (bf16[768,384]{1,0:T(8,128)(2,1)S(1)}, bf16[768,384]{1,0:T(8,128)(2,1)S(1)}, f32[16,384]{1,0:T(8,128)S(1)}, f32[16,384]{1,0:T(8,128)S(1)}) custom-call(s32[1]{0:T(128)} %bitcast.2.keep, s32[1]{0:T(128)S(6)} %mul.7.choice, bf16[384,768]{1,0:T(8,128)(2,1)S(1)} %get-tuple-element.30.own, bf16[384,768]{1,0:T(8,128)(2,1)S(1)} %collective-permute-done.1.other, ...), custom_call_target="tpu_custom_call" | custom-call | flops 2000000000 | bytes 1000000 | tf_op jit(solution)/shard_map/pallas_call | solution.py:36
  37.8 6.6 %collective-permute-done.5 = f32[16,384]{1,0:T(8,128)S(1)} collective-permute-done((f32[16,384]{1,0:T(8,128)S(1)}, f32[16,384]{1,0:T(8,128)S(1)}, u32[]{:S(2)}, u32[]{:S(2)}) %collective-permute-start.5) | collective-permute-done | bytes 24608 | tf_op jit(solution)/shard_map/ppermute | solution.py:410
  44.4 1.2 %collective-permute-done.6.other_sums = f32[16,384]{1,0:T(8,128)S(1)} collective-permute-done((f32[16,384]{1,0:T(8,128)S(1)}, f32[16,384]{1,0:T(8,128)S(1)}, u32[]{:S(2)}, u32[]{:S(2)}) %collective-permute-start.6) | collective-permute-done | bytes 24608 | tf_op jit(solution)/shard_map/ppermute | solution.py:414
  45.6 0.5 shard_map.51
  46.2 4.7 %collective-permute-start.7 = (f32[128,384]{1,0:T(8,128)S(1)}, f32[128,384]{1,0:T(8,128)S(1)}, u32[]{:S(2)}, u32[]{:S(2)}) collective-permute-start(f32[128,384]{1,0:T(8,128)S(1)} %get-tuple-element.40.vectors.v0), channel_id=1, source_target_pairs={{0,14},{1,13},{2,0},{3,15},{4,2},{5,1},{6,4},{7,3},{8,6},{9,5},{10... | collective-permute-start | bytes 589832 | tf_op jit(solution)/shard_map/ppermute | solution.py:410
  50.9 0.5 shard_map.50.product
  51.4 3.2 %collective-permute-done.8.behind = f32[128,384]{1,0:T(8,128)S(1)} collective-permute-done((f32[128,384]{1,0:T(8,128)S(1)}, f32[128,384]{1,0:T(8,128)S(1)}, u32[]{:S(2)}, u32[]{:S(2)}) %collective-permute-start.8) | collective-permute-done | bytes 196640 | tf_op jit(solution)/shard_map/ppermute | solution.py:410
  54.6 0.8 shard_map.52.total
  55.4 0.2 collective-permute-start.9
  55.6 1.3 %collective-permute-done.9.other_total = f32[128,384]{1,0:T(8,128)S(1)} collective-permute-done((f32[128,384]{1,0:T(8,128)S(1)}, f32[128,384]{1,0:T(8,128)S(1)}, u32[]{:S(2)}, u32[]{:S(2)}) %collective-permute-start.9) | collective-permute-done | bytes 196640 | tf_op jit(solution)/shard_map/ppermute | solution.py:414
  56.9 0.5 shard_map.55
  57.5 0.1 collective-permute-start.11
  57.5 4.9 %collective-permute-start.10 = (f32[128,384]{1,0:T(8,128)S(1)}, f32[128,384]{1,0:T(8,128)S(1)}, u32[]{:S(2)}, u32[]{:S(2)}) collective-permute-start(f32[128,384]{1,0:T(8,128)S(1)} %shard_map.53.vectors.v1), channel_id=1, source_target_pairs={{0,14},{1,13},{2,0},{3,15},{4,2},{5,1},{6,4},{7,3},{8,6},{9,5},{10... | collective-permute-start | bytes 589832 | tf_op jit(solution)/shard_map/ppermute | solution.py:410
  62.4 0.5 shard_map.54.product
  62.9 5.2 %collective-permute-done.11.behind = f32[128,384]{1,0:T(8,128)S(1)} collective-permute-done((f32[128,384]{1,0:T(8,128)S(1)}, f32[128,384]{1,0:T(8,128)S(1)}, u32[]{:S(2)}, u32[]{:S(2)}) %collective-permute-start.11) | collective-permute-done | bytes 196640 | tf_op jit(solution)/shard_map/ppermute | solution.py:410
  68.1 0.8 shard_map.56.total
  68.9 0.1 collective-permute-start.12
  69.0 1.4 %collective-permute-done.12.other_total = f32[128,384]{1,0:T(8,128)S(1)} collective-permute-done((f32[128,384]{1,0:T(8,128)S(1)}, f32[128,384]{1,0:T(8,128)S(1)}, u32[]{:S(2)}, u32[]{:S(2)}) %collective-permute-start.12) | collective-permute-done | bytes 196640 | tf_op jit(solution)/shard_map/ppermute | solution.py:414
  70.4 3.0 %collective-permute-start.13 = (f32[128,384]{1,0:T(8,128)S(1)}, f32[128,384]{1,0:T(8,128)S(1)}, u32[]{:S(2)}, u32[]{:S(2)}) collective-permute-start(f32[128,384]{1,0:T(8,128)S(1)} %shard_map.57.v2.vectors), channel_id=1, source_target_pairs={{0,14},{1,13},{2,0},{3,15},{4,2},{5,1},{6,4},{7,3},{8,6},{9,5},{10... | collective-permute-start | bytes 589832 | tf_op jit(solution)/shard_map/ppermute | solution.py:410
  73.4 0.5 shard_map.59.product
  73.9 0.5 shard_map.58
  74.4 2.2 %collective-permute-done.13.near = f32[128,384]{1,0:T(8,128)S(1)} collective-permute-done((f32[128,384]{1,0:T(8,128)S(1)}, f32[128,384]{1,0:T(8,128)S(1)}, u32[]{:S(2)}, u32[]{:S(2)}) %collective-permute-start.13) | collective-permute-done | bytes 196640 | tf_op jit(solution)/shard_map/ppermute | solution.py:410
  76.6 1.4 %shard_map.60 = (f32[56,128]{1,0:T(8,128)S(1)}, f32[56,128]{1,0:T(8,128)S(1)}) custom-call(s32[1]{0:T(128)} %bitcast.core.refs_0_, f32[320,64]{1,0:T(8,128)S(1)} %get-tuple-element.47.low, f32[128,384]{1,0:T(8,128)S(1)} %shard_map.57.v2.vectors, f32[128,384]{1,0:T(8,128)S(1)} %shard_map.59.product, f32[128,384]{1,0:T(8,128)S(1)} %collective-permute-done.13.near, ...), custom_call_target="tpu_custom_call" | custom-call | flops 1000000000 | bytes 1000000 | tf_op jit(solution)/shard_map/pallas_call | solution.py:36
  78.0 0.2 collective-permute-start.14
  78.2 1.0 collective-permute-done.14
  79.3 1.2 %collective-permute-start.15 = (f32[56,128]{1,0:T(8,128)S(1)}, f32[56,128]{1,0:T(8,128)S(1)}, u32[]{:S(2)}, u32[]{:S(2)}) collective-permute-start(f32[56,128]{1,0:T(8,128)S(1)} %add.29), channel_id=1, source_target_pairs={{0,2},{2,0},{4,6},{6,4},{8,10},{10,8},{12,14},{14,12},{1,3},{3,1},... | collective-permute-start | bytes 86024 | tf_op jit(solution)/shard_map/ppermute | solution.py:421
  80.5 2.6 %collective-permute-done.15 = f32[56,128]{1,0:T(8,128)S(1)} collective-permute-done((f32[56,128]{1,0:T(8,128)S(1)}, f32[56,128]{1,0:T(8,128)S(1)}, u32[]{:S(2)}, u32[]{:S(2)}) %collective-permute-start.15) | collective-permute-done | bytes 28704 | tf_op jit(solution)/shard_map/ppermute | solution.py:421
  83.1 0.9 collective-permute-start.16
  84.0 3.0 %collective-permute-done.16 = f32[56,128]{1,0:T(8,128)S(1)} collective-permute-done((f32[56,128]{1,0:T(8,128)S(1)}, f32[56,128]{1,0:T(8,128)S(1)}, u32[]{:S(2)}, u32[]{:S(2)}) %collective-permute-start.16) | collective-permute-done | bytes 28704 | tf_op jit(solution)/shard_map/ppermute | solution.py:421
  87.0 2.3 %collective-permute-start.17 = (f32[56,128]{1,0:T(8,128)S(1)}, f32[56,128]{1,0:T(8,128)S(1)}, u32[]{:S(2)}, u32[]{:S(2)}) collective-permute-start(f32[56,128]{1,0:T(8,128)S(1)} %add.31), channel_id=1, source_target_pairs={{0,8},{2,10},{4,12},{6,14},{8,0},{10,2},{12,4},{14,6},{1,9},{3,11}... | collective-permute-start | bytes 86024 | tf_op jit(solution)/shard_map/ppermute | solution.py:421
  89.3 2.5 %collective-permute-done.17 = f32[56,128]{1,0:T(8,128)S(1)} collective-permute-done((f32[56,128]{1,0:T(8,128)S(1)}, f32[56,128]{1,0:T(8,128)S(1)}, u32[]{:S(2)}, u32[]{:S(2)}) %collective-permute-start.17) | collective-permute-done | bytes 28704 | tf_op jit(solution)/shard_map/ppermute | solution.py:421
  92.5 0.5 collective-permute-done.18.refs_3_
  93.0 22.2 %shard_map.61 = f32[64,384]{1,0:T(8,128)} custom-call(s32[1]{0:T(128)} %bitcast.core.refs_0_, s32[1]{0:T(128)S(6)} %copy.5.refs_1_, f32[56,128]{1,0:T(8,128)S(1)} %add.32.refs_2_, f32[56,128]{1,0:T(8,128)S(1)} %collective-permute-done.18.refs_3_, f32[192,384]{1,0:T(8,128)S(1)} %get-tuple-element.50.refs_4_), custom_call_target="tpu_custom_call" | custom-call | flops 20000000000 | bytes 1000000 | tf_op jit(solution)/shard_map/pallas_call | solution.py:36
  (28 shorter events, 0.2 us)
Async XLA Ops:
  0.0 8.4 %copy-start = (bf16[384,768]{1,0:T(8,128)(2,1)S(1)}, bf16[384,768]{1,0:T(8,128)(2,1)}, u32[]{:S(2)}) copy-start(bf16[384,768]{1,0:T(8,128)(2,1)} %own.1) | copy-start | bytes 1769476
  0.0 8.4 %collective-permute-start.1 = (bf16[384,768]{1,0:T(8,128)(2,1)}, bf16[384,768]{1,0:T(8,128)(2,1)S(1)}, u32[]{:S(2)}, u32[]{:S(2)}) collective-permute-start(bf16[384,768]{1,0:T(8,128)(2,1)} %own.1), channel_id=1, source_target_pairs={{0,1},{1,0},{2,3},{3,2},{4,5},{5,4},{6,7},{7,6},{8,9},{9,8},{10,11... | collective-permute-start | bytes 1769480 | tf_op jit(solution)/shard_map/ppermute | solution.py:414
  0.5 18.2 %collective-permute-start = (bf16[384,768]{1,0:T(8,128)(2,1)}, bf16[384,768]{1,0:T(8,128)(2,1)S(1)}, u32[]{:S(2)}, u32[]{:S(2)}) collective-permute-start(bf16[384,768]{1,0:T(8,128)(2,1)} %own.1), channel_id=1, source_target_pairs={{0,14},{1,13},{2,0},{3,15},{4,2},{5,1},{6,4},{7,3},{8,6},{9,5},{10... | collective-permute-start | bytes 1769480 | tf_op jit(solution)/shard_map/ppermute | solution.py:410
  6.9 1.4 %collective-permute-start.2 = (f32[64,384]{1,0:T(8,128)S(1)}, f32[64,384]{1,0:T(8,128)S(1)}, u32[]{:S(2)}, u32[]{:S(2)}) collective-permute-start(f32[64,384]{1,0:T(8,128)S(1)} %multiply_bitcast_fusion), channel_id=1, source_target_pairs={{0,1},{1,0},{2,3},{3,2},{4,5},{5,4},{6,7},{7,6},{8,9},{9,8},{10,11... | collective-permute-start | bytes 294920 | tf_op jit(solution)/shard_map/ppermute | solution.py:414
  10.3 0.8 copy-start.1
  11.1 0.8 copy-start.3
  11.9 0.6 copy-start.5
  18.6 12.6 %collective-permute-start.4 = (bf16[384,768]{1,0:T(8,128)(2,1)S(1)}, bf16[384,768]{1,0:T(8,128)(2,1)S(1)}, u32[]{:S(2)}, u32[]{:S(2)}) collective-permute-start(bf16[384,768]{1,0:T(8,128)(2,1)S(1)} %collective-permute-done.col), channel_id=1, source_target_pairs={{1,2},{5,6},{9,10},{13,14},{17,18},{21,22},{25,26},{29,30}} | collective-permute-start | bytes 1769480 | tf_op jit(solution)/shard_map/ppermute | solution.py:450
  19.3 15.9 %collective-permute-start.3 = (bf16[384,768]{1,0:T(8,128)(2,1)S(1)}, bf16[384,768]{1,0:T(8,128)(2,1)S(1)}, u32[]{:S(2)}, u32[]{:S(2)}) collective-permute-start(bf16[384,768]{1,0:T(8,128)(2,1)S(1)} %get-tuple-element.30.own), channel_id=1, source_target_pairs={{0,13},{2,15},{4,1},{6,3},{8,5},{10,7},{12,9},{14,11},{3,0},{7,4},... | collective-permute-start | bytes 1769480 | tf_op jit(solution)/shard_map/ppermute | solution.py:447
  27.9 0.7 copy-start.6
  37.8 6.6 %collective-permute-start.5 = (f32[16,384]{1,0:T(8,128)S(1)}, f32[16,384]{1,0:T(8,128)S(1)}, u32[]{:S(2)}, u32[]{:S(2)}) collective-permute-start(f32[16,384]{1,0:T(8,128)S(1)} %get-tuple-element.37), channel_id=1, source_target_pairs={{0,2},{1,5},{2,4},{3,7},{4,6},{5,9},{6,8},{7,11},{8,10},{9,13},{10... | collective-permute-start | bytes 73736 | tf_op jit(solution)/shard_map/ppermute | solution.py:410
  44.4 1.2 %collective-permute-start.6 = (f32[16,384]{1,0:T(8,128)S(1)}, f32[16,384]{1,0:T(8,128)S(1)}, u32[]{:S(2)}, u32[]{:S(2)}) collective-permute-start(f32[16,384]{1,0:T(8,128)S(1)} %add.28.sums), channel_id=1, source_target_pairs={{0,1},{1,0},{2,3},{3,2},{4,5},{5,4},{6,7},{7,6},{8,9},{9,8},{10,11... | collective-permute-start | bytes 73736 | tf_op jit(solution)/shard_map/ppermute | solution.py:414
  45.6 5.3 %copy-start.2 = (bf16[768,384]{1,0:T(8,128)(2,1)S(1)}, bf16[768,384]{1,0:T(8,128)(2,1)}, u32[]{:S(2)}) copy-start(bf16[768,384]{1,0:T(8,128)(2,1)} %copy-done.1) | copy-start | bytes 1769476
  45.6 5.3 %copy-start.4 = (bf16[768,384]{1,0:T(8,128)(2,1)S(1)}, bf16[768,384]{1,0:T(8,128)(2,1)}, u32[]{:S(2)}) copy-start(bf16[768,384]{1,0:T(8,128)(2,1)} %copy-done.3) | copy-start | bytes 1769476
  46.2 8.4 %collective-permute-start.8 = (f32[128,384]{1,0:T(8,128)S(1)}, f32[128,384]{1,0:T(8,128)S(1)}, u32[]{:S(2)}, u32[]{:S(2)}) collective-permute-start(f32[128,384]{1,0:T(8,128)S(1)} %shard_map.51), channel_id=1, source_target_pairs={{0,2},{1,5},{2,4},{3,7},{4,6},{5,9},{6,8},{7,11},{8,10},{9,13},{10... | collective-permute-start | bytes 589832 | tf_op jit(solution)/shard_map/ppermute | solution.py:410
  46.2 8.4 %collective-permute-start.7 = (f32[128,384]{1,0:T(8,128)S(1)}, f32[128,384]{1,0:T(8,128)S(1)}, u32[]{:S(2)}, u32[]{:S(2)}) collective-permute-start(f32[128,384]{1,0:T(8,128)S(1)} %get-tuple-element.40.vectors.v0), channel_id=1, source_target_pairs={{0,14},{1,13},{2,0},{3,15},{4,2},{5,1},{6,4},{7,3},{8,6},{9,5},{10... | collective-permute-start | bytes 589832 | tf_op jit(solution)/shard_map/ppermute | solution.py:410
  55.4 1.5 %collective-permute-start.9 = (f32[128,384]{1,0:T(8,128)S(1)}, f32[128,384]{1,0:T(8,128)S(1)}, u32[]{:S(2)}, u32[]{:S(2)}) collective-permute-start(f32[128,384]{1,0:T(8,128)S(1)} %shard_map.52.total), channel_id=1, source_target_pairs={{0,1},{1,0},{2,3},{3,2},{4,5},{5,4},{6,7},{7,6},{8,9},{9,8},{10,11... | collective-permute-start | bytes 589832 | tf_op jit(solution)/shard_map/ppermute | solution.py:414
  57.5 10.6 %collective-permute-start.11 = (f32[128,384]{1,0:T(8,128)S(1)}, f32[128,384]{1,0:T(8,128)S(1)}, u32[]{:S(2)}, u32[]{:S(2)}) collective-permute-start(f32[128,384]{1,0:T(8,128)S(1)} %shard_map.55), channel_id=1, source_target_pairs={{0,2},{1,5},{2,4},{3,7},{4,6},{5,9},{6,8},{7,11},{8,10},{9,13},{10... | collective-permute-start | bytes 589832 | tf_op jit(solution)/shard_map/ppermute | solution.py:410
  57.5 10.6 %collective-permute-start.10 = (f32[128,384]{1,0:T(8,128)S(1)}, f32[128,384]{1,0:T(8,128)S(1)}, u32[]{:S(2)}, u32[]{:S(2)}) collective-permute-start(f32[128,384]{1,0:T(8,128)S(1)} %shard_map.53.vectors.v1), channel_id=1, source_target_pairs={{0,14},{1,13},{2,0},{3,15},{4,2},{5,1},{6,4},{7,3},{8,6},{9,5},{10... | collective-permute-start | bytes 589832 | tf_op jit(solution)/shard_map/ppermute | solution.py:410
  68.9 1.5 %collective-permute-start.12 = (f32[128,384]{1,0:T(8,128)S(1)}, f32[128,384]{1,0:T(8,128)S(1)}, u32[]{:S(2)}, u32[]{:S(2)}) collective-permute-start(f32[128,384]{1,0:T(8,128)S(1)} %shard_map.56.total), channel_id=1, source_target_pairs={{0,1},{1,0},{2,3},{3,2},{4,5},{5,4},{6,7},{7,6},{8,9},{9,8},{10,11... | collective-permute-start | bytes 589832 | tf_op jit(solution)/shard_map/ppermute | solution.py:414
  70.4 6.2 %collective-permute-start.13 = (f32[128,384]{1,0:T(8,128)S(1)}, f32[128,384]{1,0:T(8,128)S(1)}, u32[]{:S(2)}, u32[]{:S(2)}) collective-permute-start(f32[128,384]{1,0:T(8,128)S(1)} %shard_map.57.v2.vectors), channel_id=1, source_target_pairs={{0,14},{1,13},{2,0},{3,15},{4,2},{5,1},{6,4},{7,3},{8,6},{9,5},{10... | collective-permute-start | bytes 589832 | tf_op jit(solution)/shard_map/ppermute | solution.py:410
  78.0 1.3 %collective-permute-start.14 = (f32[56,128]{1,0:T(8,128)S(1)}, f32[56,128]{1,0:T(8,128)S(1)}, u32[]{:S(2)}, u32[]{:S(2)}) collective-permute-start(f32[56,128]{1,0:T(8,128)S(1)} %get-tuple-element.49), channel_id=1, source_target_pairs={{0,1},{1,0},{2,3},{3,2},{4,5},{5,4},{6,7},{7,6},{8,9},{9,8},{10,11... | collective-permute-start | bytes 86024 | tf_op jit(solution)/shard_map/ppermute | solution.py:414
  79.3 3.9 %collective-permute-start.15 = (f32[56,128]{1,0:T(8,128)S(1)}, f32[56,128]{1,0:T(8,128)S(1)}, u32[]{:S(2)}, u32[]{:S(2)}) collective-permute-start(f32[56,128]{1,0:T(8,128)S(1)} %add.29), channel_id=1, source_target_pairs={{0,2},{2,0},{4,6},{6,4},{8,10},{10,8},{12,14},{14,12},{1,3},{3,1},... | collective-permute-start | bytes 86024 | tf_op jit(solution)/shard_map/ppermute | solution.py:421
  83.1 3.9 %collective-permute-start.16 = (f32[56,128]{1,0:T(8,128)S(1)}, f32[56,128]{1,0:T(8,128)S(1)}, u32[]{:S(2)}, u32[]{:S(2)}) collective-permute-start(f32[56,128]{1,0:T(8,128)S(1)} %add.30), channel_id=1, source_target_pairs={{0,4},{2,6},{4,0},{6,2},{8,12},{10,14},{12,8},{14,10},{1,5},{3,7},... | collective-permute-start | bytes 86024 | tf_op jit(solution)/shard_map/ppermute | solution.py:421
  87.0 4.8 %collective-permute-start.17 = (f32[56,128]{1,0:T(8,128)S(1)}, f32[56,128]{1,0:T(8,128)S(1)}, u32[]{:S(2)}, u32[]{:S(2)}) collective-permute-start(f32[56,128]{1,0:T(8,128)S(1)} %add.31), channel_id=1, source_target_pairs={{0,8},{2,10},{4,12},{6,14},{8,0},{10,2},{12,4},{14,6},{1,9},{3,11}... | collective-permute-start | bytes 86024 | tf_op jit(solution)/shard_map/ppermute | solution.py:421
  91.8 1.2 %collective-permute-start.18 = (f32[56,128]{1,0:T(8,128)S(1)}, f32[56,128]{1,0:T(8,128)S(1)}, u32[]{:S(2)}, u32[]{:S(2)}) collective-permute-start(f32[56,128]{1,0:T(8,128)S(1)} %add.32.refs_2_), channel_id=1, source_target_pairs={{0,1},{1,0},{2,3},{3,2},{4,5},{5,4},{6,7},{7,6},{8,9},{9,8},{10,11... | collective-permute-start | bytes 86024 | tf_op jit(solution)/shard_map/ppermute | solution.py:414

commit v9 on v8

--- a/solution.py
+++ b/solution.py
@@ -28,20 +28,25 @@
     return high, (values - high.astype(F32)).astype(BF16)
 
 
-def call(body, out_shapes, args, smem=(), flops=0, nbytes=0):
-    specs = [
-        pl.BlockSpec(memory_space=pltpu.SMEM if i in smem else pltpu.VMEM)
-        for i in range(len(args))
-    ]
-    out = pl.pallas_call(
+def call(body, out_shapes, args, flops=0, nbytes=0):
+    return pl.pallas_call(
         body,
         out_shape=[jax.ShapeDtypeStruct(shape, dtype) for shape, dtype in out_shapes],
-        in_specs=specs,
+        in_specs=[pl.BlockSpec(memory_space=pltpu.VMEM) for _ in args],
         out_specs=[pl.BlockSpec(memory_space=pltpu.VMEM) for _ in out_shapes],
         compiler_params=pltpu.CompilerParams(vmem_limit_bytes=VMEM_LIMIT),
         cost_estimate=pl.CostEstimate(flops=flops, bytes_accessed=nbytes, transcendentals=0),
     )(*args)
-    return out
+
+
+def spread(value):
+    return jnp.broadcast_to(value.astype(F32), (8, 128))
+
+
+def chosen(flag, first, second):
+    rows, cols = first.shape
+    wide = jnp.concatenate([flag[0:1, :]] * (cols // 128), axis=1)
+    return jnp.where(jnp.broadcast_to(wide, (rows, cols)) > 0.5, first, second)
 
 
 LOG2_E = 1.4426950408889634
@@ -64,7 +69,9 @@
         rows = slice(half * size, (half + 1) * size)
         inner = dot(row_embs[half], col_emb, 1, 1)
         squares = jnp.concatenate([row_sq[rows, :]] * (size // 128), axis=1)
-        tile = jnp.exp2((4.0 * LOG2_E) * inner - (squares + col_sq)) * weight
+        tile = jnp.exp2((4.0 * LOG2_E) * inner - (squares + col_sq))
+        if weight is not None:
+            tile = tile * weight
         tile_high, tile_low = halves(tile)
         high[rows, :] = tile_high
         low[rows, :] = tile_low
@@ -73,7 +80,7 @@
     return jnp.broadcast_to(total, (8, size))
 
 
-def own_body(own, other, high, low, row_sum, row_sq, copy):
+def own_body(own, other, high, low, row_sum, row_sq, copy, token):
     size = own.shape[0]
     embs = [own[...], other[...]]
     copy[...] = embs[0]
@@ -82,26 +89,22 @@
         squares = (2.0 * LOG2_E) * jnp.sum(row32 * row32, axis=1, keepdims=True)
         row_sq[half * size:(half + 1) * size, :] = jnp.broadcast_to(squares, (size, 128))
     row_sum[...] = jnp.zeros(row_sum.shape, F32)
-    fill_tile(1.0, embs, row_sq, embs[0], high, low, row_sum)
-
-
-def far_body(keep, own, other, row_sq, col, before, high, low, row_sum, col_sum):
+    token[...] = jnp.zeros(token.shape, F32)
+    fill_tile(None, embs, row_sq, embs[0], high, low, row_sum)
+
+
+def far_body(keep, relays, own, other, row_sq, direct, relayed, before, high, low, row_sum, col_sum):
     row_sum[...] = before[...]
-    col_sum[...] = fill_tile(keep[0].astype(F32), [own[...], other[...]], row_sq, col[...], high, low, row_sum)
-
-
-def relayed_body(keep, choice, own, other, row_sq, direct, relayed, before, first_cols,
-                 high, low, row_sum, col_sum):
-    row_sum[...] = before[...]
-    col = jnp.where(choice[0] > 0, relayed[...], direct[...])
-    col_sum[:8, :] = first_cols[...]
-    col_sum[8:, :] = fill_tile(keep[0].astype(F32), [own[...], other[...]], row_sq, col, high, low, row_sum)
-
-
-def make_tile(body, args, rows, smem=(), extra=()):
+    size = own.shape[0]
+    weight = jnp.concatenate([keep[0:1, :]] * (size // 128), axis=1)
+    col = chosen(relays, relayed[...], direct[...])
+    col_sum[...] = fill_tile(weight, [own[...], other[...]], row_sq, col, high, low, row_sum)
+
+
+def make_tile(body, args, rows, extra=()):
     return call(
         body, [((2 * rows, rows), BF16), ((2 * rows, rows), BF16), ((16, rows), F32), *extra],
-        args, smem=smem, flops=2 * 10**9, nbytes=10**6,
+        args, flops=2 * 10**9, nbytes=10**6,
     )
 
 
@@ -122,14 +125,16 @@
     vectors_out[...] = seeds[...] * per_row(scale, seeds.shape[0] // 2)
 
 
-def ahead_body(vectors, h1, l1, h2, l2, ahead):
+def ahead_body(relays, vectors, h1, l1, h2, l2, ahead):
     width = vectors.shape[0] // 2
     high, low = halves(jnp.concatenate([vectors[:width, :], vectors[width:, :]], axis=1))
     both = jnp.concatenate([high, low], axis=0)
-    for half, (tile_high, tile_low) in enumerate(((h1, l1), (h2, l2))):
+    products = []
+    for tile_high, tile_low in ((h1, l1), (h2, l2)):
         product = dot(both, tile_high[...])
-        product = product[:width] + product[width:] + dot(high, tile_low[...])
-        ahead[half * width:(half + 1) * width, :] = product
+        products.append(product[:width] + product[width:] + dot(high, tile_low[...]))
+    ahead[:width, :] = chosen(relays, products[1], products[0])
+    ahead[width:, :] = chosen(relays, products[0], products[1])
 
 
 def combine_body(total, other_total, degree, vectors_out):
@@ -153,10 +158,15 @@
     out[...] = stacked(product_rows(vectors[:vectors.shape[0] // 2, :], h0, l0))
 
 
-def block_body(product, near, behind, h1, l1, h2, l2, total):
+def far_product(relays, near, h1, l1, h2, l2):
     width = near.shape[0] // 2
-    far = product_rows(near[:width, :], h1, l1) + product_rows(near[width:, :], h2, l2)
-    total[...] = product[...] + behind[...] + stacked(far)
+    first = chosen(relays, near[width:, :], near[:width, :])
+    second = chosen(relays, near[:width, :], near[width:, :])
+    return product_rows(first, h1, l1) + product_rows(second, h2, l2)
+
+
+def block_body(relays, product, near, behind, h1, l1, h2, l2, total):
+    total[...] = product[...] + behind[...] + stacked(far_product(relays, near, h1, l1, h2, l2))
 
 
 def low_body(degree, v0, v1, v2, moments, scaled):
@@ -177,9 +187,9 @@
     return [lax.broadcasted_iota(jnp.int32, (rows, cols), axis) for axis in range(2)]
 
 
-def moment_body(core, low, vectors, product, near, h1, l1, h2, l2, mine, theirs):
+def moment_body(core, relays, low, vectors, product, near, h1, l1, h2, l2, mine, theirs):
     n = vectors.shape[0] // 2
-    last = product_rows(near[:n, :], h1, l1) + product_rows(near[n:, :], h2, l2)
+    last = far_product(relays, near, h1, l1, h2, l2)
     last = 2.0 * last + jnp.concatenate([product[:n, :], product[n:, :]], axis=1)
     last = dot(jnp.concatenate([vectors[:n, :], vectors[n:, :]], axis=1), last, 1, 1)
     moments = [low[i * n:(i + 1) * n, :] for i in range(5)] + [0.5 * (last + last.T)]
@@ -195,9 +205,8 @@
     pieces.append(jnp.zeros((8, 2 * n), F32))
     packed = jnp.concatenate(pieces, axis=0)
     half = packed.shape[0] // 2
-    first = core[0] == 0
-    mine[...] = jnp.where(first, packed[:half], packed[half:])
-    theirs[...] = jnp.where(first, packed[half:], packed[:half])
+    mine[...] = chosen(core, packed[half:], packed[:half])
+    theirs[...] = chosen(core, packed[:half], packed[half:])
 
 
 def unpacked(packed, n):
@@ -398,10 +407,10 @@
 
 
 def dense_body(rows, core, index, mine, theirs, scaled, out):
-    first = core[0] == 0
     packed = jnp.concatenate([
-        jnp.where(first, mine[...], theirs[...]), jnp.where(first, theirs[...], mine[...])], axis=0)
-    out[...] = dense(unpacked(packed, NVEC), index[0], rows, scaled[...])
+        chosen(core, theirs[...], mine[...]), chosen(core, mine[...], theirs[...])], axis=0)
+    index = jnp.broadcast_to(index[0:1, :NVEC], (NVEC, NVEC)).astype(jnp.int32)
+    out[...] = dense(unpacked(packed, NVEC), index, rows, scaled[...])
 
 
 def between_blocks(shard, sign):
@@ -430,29 +439,38 @@
     size = embeddings.shape[0]
     blocks = lax.axis_size("blk")
     where = lax.axis_index("blk")
-    core = lax.axis_index("narrow").astype(jnp.int32).reshape(1)
+    core = lax.axis_index("narrow")
     other_emb = between_cores(embeddings)
-    far_emb = between_blocks(embeddings, -1)
+    relaying = blocks % 2 == 0
+    back1 = [(i, (i - 1) % blocks) for i in range(blocks) if i % 2 or not relaying]
+    back2 = [(i, (i - 2) % blocks) for i in range(blocks)]
+    orders = [
+        [(2 * i + j, 2 * k) for i, k in back1] + [(2 * i + 1 - j, 2 * k + 1) for i, k in back2] for j in range(2)]
+
+    def between_shards(shard, pairs):
+        return lax.ppermute(shard, ("blk", "narrow"), pairs)
+
+    def relay(shard):
+        pairs = [(2 * i + 1, 2 * i + 2) for i in range(0, blocks, 2)]
+        return between_shards(shard, pairs) if relaying else shard
+
+    first = between_shards(embeddings, orders[0])
     seed = start_seed.astype(F32).T / 1000.0
     seeds = jnp.concatenate([seed, between_cores(seed)], axis=0)
-    keep = lax.dynamic_slice(pair_mask, (where, core[0]), (1, 1))[0]
-    emb_args = [embeddings, other_emb]
+    keep = spread(lax.dynamic_slice(pair_mask, (where, core), (1, 1)))
+    relays = spread((1 - core) * (where % 2) * int(relaying))
     pair_shape, row_shape = ((2 * NVEC, size), F32), ((16, size), F32)
-    h0, l0, sums, row_sq, own_copy = make_tile(
-        own_body, emb_args, size, extra=(((2 * size, 128), F32), (embeddings.shape, BF16)))
-    emb_args = [own_copy, other_emb]
-    far_emb, sums, seeds, keep = lax.optimization_barrier((far_emb, sums, seeds, keep))
-    pairs = [(2 * i, (i - 2) % blocks * 2 + 1) for i in range(blocks)]
-    pairs += [(2 * i + 1, (i - 1) % blocks * 2) for i in range(blocks) if blocks % 2 or i % 2]
-    direct = lax.ppermute(own_copy, ("blk", "narrow"), pairs)
-    relayed = direct
-    if blocks % 2 == 0:
-        relayed = lax.ppermute(far_emb, ("blk", "narrow"), [(2 * i + 1, 2 * i + 2) for i in range(0, blocks, 2)])
-    choice = (1 - core) * (where % 2 * (1 - blocks % 2)).astype(jnp.int32)
-    h1, l1, sums, cols = make_tile(
-        far_body, [keep, *emb_args, row_sq, far_emb, sums], size, (0,), (((8, size), F32),))
-    h2, l2, sums, cols = make_tile(
-        relayed_body, [keep, choice, *emb_args, row_sq, direct, relayed, sums, cols], size, (0, 1), (row_shape,))
+    h0, l0, sums, row_sq, own_copy, token = make_tile(
+        own_body, [embeddings, other_emb], size,
+        (((2 * size, 128), F32), (embeddings.shape, BF16), ((8, 128), F32)))
+    first, seeds, keep, relays, token = lax.optimization_barrier((first, seeds, keep, relays, token))
+    second = between_shards(own_copy, orders[1])
+    tile_args = [keep, relays, own_copy, other_emb, row_sq]
+    h1, l1, sums, cols1 = make_tile(
+        far_body, [*tile_args, first, relay(first), sums], size, (((8, size), F32),))
+    h2, l2, sums, cols2 = make_tile(
+        far_body, [*tile_args, second, relay(second), sums], size, (((8, size), F32),))
+    cols = jnp.concatenate([jnp.where(relays[0, 0] > 0.5, cols2, cols1), jnp.where(relays[0, 0] > 0.5, cols1, cols2)])
     sums = sums + between_blocks(cols, 1)
 
     small = dict(flops=10**6, nbytes=10**5)
@@ -463,10 +481,10 @@
     history = [vectors]
     for _ in range(2):
         near = between_blocks(vectors, -1)
-        (ahead,) = call(ahead_body, [pair_shape], [vectors, *far], **middle)
+        (ahead,) = call(ahead_body, [pair_shape], [relays, vectors, *far], **middle)
         behind = between_blocks(ahead, 1)
         (product,) = call(own_product_body, [pair_shape], [vectors, h0, l0], **middle)
-        (total,) = call(block_body, [pair_shape], [product, near, behind, *far], **middle)
+        (total,) = call(block_body, [pair_shape], [relays, product, near, behind, *far], **middle)
         (vectors,) = call(combine_body, [pair_shape], [total, between_cores(total), degree], **small)
         history.append(vectors)
     near = between_blocks(vectors, -1)
@@ -475,12 +493,12 @@
     (product,) = call(own_product_body, [pair_shape], [vectors, h0, l0], **middle)
     packed_shape = ((3 * NVEC // 4 + 8, 2 * NVEC), F32)
     mine, theirs = call(
-        moment_body, [packed_shape] * 2, [core, low, vectors, product, near, *far], smem=(0,), **middle)
+        moment_body, [packed_shape] * 2, [spread(core), relays, low, vectors, product, near, *far], **middle)
     mine = total_over_blocks(mine + between_cores(theirs))
     rows = size * blocks * lax.axis_size("narrow")
     (out,) = call(
         lambda *refs: dense_body(rows, *refs), [((NVEC, size), F32)],
-        [core, shift_index, mine, between_cores(mine), scaled], smem=(0, 1), flops=2 * 10**10, nbytes=10**6,
+        [spread(core), spread(shift_index), mine, between_cores(mine), scaled], flops=2 * 10**10, nbytes=10**6,
     )
     return out.T
 

time: 115 us -> 113 us (0.983)
  waiting for transfers between devices: 40.8 us -> 35 us
  starting transfers between devices: 32.9 us -> 36.3 us
  between operations: 0.85 us -> 2.23 us
    ppermute x7 -> x6, waiting for transfers between devices: 23.2 us -> 14.7 us  [between_blocks(): return lax.ppermute(shard, ('blk', 'narrow'), pairs)]
    ppermute x7 -> x6, starting transfers between devices: 18.3 us -> 21.2 us  [between_blocks(): return lax.ppermute(shard, ('blk', 'narrow'), pairs)]
    ppermute x2 -> x4, waiting for transfers between devices: 4.03 us -> 5.78 us  [between_shards(): return lax.ppermute(shard, ('blk', 'narrow'), pairs)]
    unnamed x14 -> x22, local copies, waits for them, and re-layouts: 3.02 us -> 3.43 us
    ppermute x2 -> x4, starting transfers between devices: 9.19 us -> 9.52 us  [between_shards(): return lax.ppermute(shard, ('blk', 'narrow'), pairs)]
  transfers between devices with their start and end apart: 19 -> 20, of which waited for: 14 -> 14; matrix products, arithmetic and copies ran while one was open for 2% -> 1% of each run, Pallas kernels for 6% -> 5%
where the time goes in v9:
time: 113 us
  starting transfers between devices  36.3 us (32%)
  waiting for transfers between devices  35 us (31%)
  Pallas kernels  34.5 us (31%)
  local copies, waits for them, and re-layouts  4.54 us (4%)
  between operations  2.23 us (2%)
    pallas_call x16, Pallas kernels, call(): pl.pallas_call(body, out_shape=[jax.ShapeDtypeStruct(shape, dtype) for sh...  34.5 us
    ppermute x6, starting transfers between devices, between_blocks(): return lax.ppermute(shard, ('blk', 'narrow'), pairs)  21.2 us
    ppermute x6, waiting for transfers between devices, between_blocks(): return lax.ppermute(shard, ('blk', 'narrow'), pairs)  14.7 us
    ppermute x4, starting transfers between devices, between_shards(): return lax.ppermute(shard, ('blk', 'narrow'), pairs)  9.52 us
    ppermute x3, waiting for transfers between devices, total_over_blocks(): lax.ppermute(values, 'blk', [(i, i ^ span) for i in range(blocks)])  8.64 us
    ppermute x7, waiting for transfers between devices, between_cores(): return lax.ppermute(shard, 'narrow', [(0, 1), (1, 0)])  5.89 us
    ppermute x4, waiting for transfers between devices, between_shards(): return lax.ppermute(shard, ('blk', 'narrow'), pairs)  5.78 us
    ppermute x3, starting transfers between devices, total_over_blocks(): lax.ppermute(values, 'blk', [(i, i ^ span) for i in range(blocks)])  4.19 us
  transfers between devices with their start and end apart: 20, of which 14 were waited for; matrix products, arithmetic and copies ran while one was open for 1% of the time, Pallas kernels for 5%

profile of v9, /device:TPU:0, one launch (start us, length us, event | category | flops | bytes accessed | tf_op | source)
XLA Modules:
  0.0 112.7 jit_solution(4544406638312502177)
XLA Ops:
  0.0 0.5 collective-permute-start.2
  0.5 1.3 %collective-permute-start = (bf16[384,768]{1,0:T(8,128)(2,1)}, bf16[384,768]{1,0:T(8,128)(2,1)S(1)}, u32[]{:S(2)}, u32[]{:S(2)}) collective-permute-start(bf16[384,768]{1,0:T(8,128)(2,1)} %own.1), channel_id=1, source_target_pairs={{2,0},{6,4},{10,8},{14,12},{1,13},{3,15},{5,1},{7,3},{9,5},{11,7},... | collective-permute-start | bytes 1769480 | tf_op jit(solution)/shard_map/ppermute | solution.py:451
  1.7 0.6 collective-permute-done.2.other
  2.3 1.1 copy-done
  3.4 2.2 %shard_map.46 = (bf16[768,384]{1,0:T(8,128)(2,1)S(1)}, bf16[768,384]{1,0:T(8,128)(2,1)S(1)}, f32[16,384]{1,0:T(8,128)S(1)}, f32[768,128]{1,0:T(8,128)S(1)}, bf16...) custom-call(bf16[384,768]{1,0:T(8,128)(2,1)S(1)} %copy-done, bf16[384,768]{1,0:T(8,128)(2,1)S(1)} %collective-permute-done.2.other), custom_call_target="tpu_custom_call" | custom-call | flops 2000000000 | bytes 1000000 | tf_op jit(solution)/shard_map/pallas_call | solution.py:32
  5.6 0.8 copy-done.5
  6.4 0.9 copy-done.7
  7.2 6.9 %collective-permute-start.3 = (bf16[384,768]{1,0:T(8,128)(2,1)S(1)}, bf16[384,768]{1,0:T(8,128)(2,1)S(1)}, u32[]{:S(2)}, u32[]{:S(2)}) collective-permute-start(bf16[384,768]{1,0:T(8,128)(2,1)S(1)} %get-tuple-element.30.own), channel_id=1, source_target_pairs={{3,0},{7,4},{11,8},{15,12},{0,13},{2,15},{4,1},{6,3},{8,5},{10,7},... | collective-permute-start | bytes 1769480 | tf_op jit(solution)/shard_map/ppermute | solution.py:451
  14.2 0.7 copy-done.10
  14.9 0.6 dynamic_slice.3
  16.2 0.7 collective-permute-start.5
  16.9 5.8 %collective-permute-done.3.direct = bf16[384,768]{1,0:T(8,128)(2,1)S(1)} collective-permute-done((bf16[384,768]{1,0:T(8,128)(2,1)S(1)}, bf16[384,768]{1,0:T(8,128)(2,1)S(1)}, u32[]{:S(2)}, u32[]{:S(2)}) %collective-permute-start.3) | collective-permute-done | bytes 589856 | tf_op jit(solution)/shard_map/ppermute | solution.py:451
  22.7 0.7 collective-permute-start.4
  23.4 0.5 slice.4
  24.6 2.0 %shard_map.47 = (bf16[768,384]{1,0:T(8,128)(2,1)S(1)}, bf16[768,384]{1,0:T(8,128)(2,1)S(1)}, f32[16,384]{1,0:T(8,128)S(1)}, f32[8,384]{1,0:T(8,128)S(1)}) custom-call(f32[8,128]{1,0:T(8,128)S(1)} %broadcast_in_dim.22.keep, f32[8,128]{1,0:T(8,128)S(1)} %broadcast_in_dim.23.relays, bf16[384,768]{1,0:T(8,128)(2,1)S(1)} %get-tuple-element.30.own, ...), custom_call_target="tpu_custom_call" | custom-call | flops 2000000000 | bytes 1000000 | tf_op jit(solution)/shard_map/pallas_call | solution.py:32
  26.5 2.0 %shard_map.48 = (bf16[768,384]{1,0:T(8,128)(2,1)S(1)}, bf16[768,384]{1,0:T(8,128)(2,1)S(1)}, f32[16,384]{1,0:T(8,128)S(1)}, f32[8,384]{1,0:T(8,128)S(1)}) custom-call(f32[8,128]{1,0:T(8,128)S(1)} %broadcast_in_dim.22.keep, f32[8,128]{1,0:T(8,128)S(1)} %broadcast_in_dim.23.relays, bf16[384,768]{1,0:T(8,128)(2,1)S(1)} %get-tuple-element.30.own, ...), custom_call_target="tpu_custom_call" | custom-call | flops 2000000000 | bytes 1000000 | tf_op jit(solution)/shard_map/pallas_call | solution.py:32
  28.6 8.7 %collective-permute-start.6 = (f32[16,384]{1,0:T(8,128)S(1)}, f32[16,384]{1,0:T(8,128)S(1)}, u32[]{:S(2)}, u32[]{:S(2)}) collective-permute-start(f32[16,384]{1,0:T(8,128)S(1)} %pad_maximum_fusion.1), channel_id=1, source_target_pairs={{0,2},{1,5},{2,4},{3,7},{4,6},{5,9},{6,8},{7,11},{8,10},{9,13},{10... | collective-permute-start | bytes 73736 | tf_op jit(solution)/shard_map/ppermute | solution.py:419
  37.3 2.0 %collective-permute-done.6 = f32[16,384]{1,0:T(8,128)S(1)} collective-permute-done((f32[16,384]{1,0:T(8,128)S(1)}, f32[16,384]{1,0:T(8,128)S(1)}, u32[]{:S(2)}, u32[]{:S(2)}) %collective-permute-start.6) | collective-permute-done | bytes 24608 | tf_op jit(solution)/shard_map/ppermute | solution.py:419
  39.3 0.1 collective-permute-start.7
  39.5 1.1 collective-permute-done.7.other_sums
  40.6 0.5 shard_map.51
  41.1 1.9 %collective-permute-start.9 = (f32[128,384]{1,0:T(8,128)S(1)}, f32[128,384]{1,0:T(8,128)S(1)}, u32[]{:S(2)}, u32[]{:S(2)}) collective-permute-start(f32[128,384]{1,0:T(8,128)S(1)} %shard_map.51), channel_id=1, source_target_pairs={{0,2},{1,5},{2,4},{3,7},{4,6},{5,9},{6,8},{7,11},{8,10},{9,13},{10... | collective-permute-start | bytes 589832 | tf_op jit(solution)/shard_map/ppermute | solution.py:419
  43.0 2.9 %collective-permute-start.8 = (f32[128,384]{1,0:T(8,128)S(1)}, f32[128,384]{1,0:T(8,128)S(1)}, u32[]{:S(2)}, u32[]{:S(2)}) collective-permute-start(f32[128,384]{1,0:T(8,128)S(1)} %get-tuple-element.40.vectors.v0), channel_id=1, source_target_pairs={{0,14},{1,13},{2,0},{3,15},{4,2},{5,1},{6,4},{7,3},{8,6},{9,5},{10... | collective-permute-start | bytes 589832 | tf_op jit(solution)/shard_map/ppermute | solution.py:419
  45.9 0.5 shard_map.50.product
  46.4 5.2 %collective-permute-done.9.behind = f32[128,384]{1,0:T(8,128)S(1)} collective-permute-done((f32[128,384]{1,0:T(8,128)S(1)}, f32[128,384]{1,0:T(8,128)S(1)}, u32[]{:S(2)}, u32[]{:S(2)}) %collective-permute-start.9) | collective-permute-done | bytes 196640 | tf_op jit(solution)/shard_map/ppermute | solution.py:419
  51.6 0.8 shard_map.52.total
  52.5 1.4 %collective-permute-done.10.other_total = f32[128,384]{1,0:T(8,128)S(1)} collective-permute-done((f32[128,384]{1,0:T(8,128)S(1)}, f32[128,384]{1,0:T(8,128)S(1)}, u32[]{:S(2)}, u32[]{:S(2)}) %collective-permute-start.10) | collective-permute-done | bytes 196640 | tf_op jit(solution)/shard_map/ppermute | solution.py:423
  54.0 0.5 shard_map.55
  54.5 1.2 %collective-permute-start.12 = (f32[128,384]{1,0:T(8,128)S(1)}, f32[128,384]{1,0:T(8,128)S(1)}, u32[]{:S(2)}, u32[]{:S(2)}) collective-permute-start(f32[128,384]{1,0:T(8,128)S(1)} %shard_map.55), channel_id=1, source_target_pairs={{0,2},{1,5},{2,4},{3,7},{4,6},{5,9},{6,8},{7,11},{8,10},{9,13},{10... | collective-permute-start | bytes 589832 | tf_op jit(solution)/shard_map/ppermute | solution.py:419
  55.7 3.6 %collective-permute-start.11 = (f32[128,384]{1,0:T(8,128)S(1)}, f32[128,384]{1,0:T(8,128)S(1)}, u32[]{:S(2)}, u32[]{:S(2)}) collective-permute-start(f32[128,384]{1,0:T(8,128)S(1)} %shard_map.53.vectors.v1), channel_id=1, source_target_pairs={{0,14},{1,13},{2,0},{3,15},{4,2},{5,1},{6,4},{7,3},{8,6},{9,5},{10... | collective-permute-start | bytes 589832 | tf_op jit(solution)/shard_map/ppermute | solution.py:419
  59.3 0.5 shard_map.54.product
  59.8 5.3 %collective-permute-done.12.behind = f32[128,384]{1,0:T(8,128)S(1)} collective-permute-done((f32[128,384]{1,0:T(8,128)S(1)}, f32[128,384]{1,0:T(8,128)S(1)}, u32[]{:S(2)}, u32[]{:S(2)}) %collective-permute-start.12) | collective-permute-done | bytes 196640 | tf_op jit(solution)/shard_map/ppermute | solution.py:419
  65.1 0.8 shard_map.56.total
  66.0 1.4 %collective-permute-done.13.other_total = f32[128,384]{1,0:T(8,128)S(1)} collective-permute-done((f32[128,384]{1,0:T(8,128)S(1)}, f32[128,384]{1,0:T(8,128)S(1)}, u32[]{:S(2)}, u32[]{:S(2)}) %collective-permute-start.13) | collective-permute-done | bytes 196640 | tf_op jit(solution)/shard_map/ppermute | solution.py:423
  67.4 2.9 %collective-permute-start.14 = (f32[128,384]{1,0:T(8,128)S(1)}, f32[128,384]{1,0:T(8,128)S(1)}, u32[]{:S(2)}, u32[]{:S(2)}) collective-permute-start(f32[128,384]{1,0:T(8,128)S(1)} %shard_map.57.v2.vectors), channel_id=1, source_target_pairs={{0,14},{1,13},{2,0},{3,15},{4,2},{5,1},{6,4},{7,3},{8,6},{9,5},{10... | collective-permute-start | bytes 589832 | tf_op jit(solution)/shard_map/ppermute | solution.py:419
  70.4 0.5 shard_map.59.product
  70.9 0.5 shard_map.58
  71.4 2.2 %collective-permute-done.14.near = f32[128,384]{1,0:T(8,128)S(1)} collective-permute-done((f32[128,384]{1,0:T(8,128)S(1)}, f32[128,384]{1,0:T(8,128)S(1)}, u32[]{:S(2)}, u32[]{:S(2)}) %collective-permute-start.14) | collective-permute-done | bytes 196640 | tf_op jit(solution)/shard_map/ppermute | solution.py:419
  73.6 1.4 %shard_map.60 = (f32[56,128]{1,0:T(8,128)S(1)}, f32[56,128]{1,0:T(8,128)S(1)}) custom-call(f32[8,128]{1,0:T(8,128)S(1)} %broadcast_in_dim.19.core.refs_0_, f32[8,128]{1,0:T(8,128)S(1)} %broadcast_in_dim.23.relays, f32[320,64]{1,0:T(8,128)S(1)} %get-tuple-element.47.low, f32[128,384]{1,0:T(8,128)S(1)} %shard_map.57.v2.vectors, ...), custom_call_target="tpu_custom_call" | custom-call | flops 1000000000 | bytes 1000000 | tf_op jit(solution)/shard_map/pallas_call | solution.py:32
  74.9 0.6 collective-permute-start.15
  75.5 0.9 collective-permute-done.15
  76.4 2.3 %collective-permute-start.16 = (f32[56,128]{1,0:T(8,128)S(1)}, f32[56,128]{1,0:T(8,128)S(1)}, u32[]{:S(2)}, u32[]{:S(2)}) collective-permute-start(f32[56,128]{1,0:T(8,128)S(1)} %add.29), channel_id=1, source_target_pairs={{0,2},{2,0},{4,6},{6,4},{8,10},{10,8},{12,14},{14,12},{1,3},{3,1},... | collective-permute-start | bytes 86024 | tf_op jit(solution)/shard_map/ppermute | solution.py:430
  78.7 1.8 %collective-permute-done.16 = f32[56,128]{1,0:T(8,128)S(1)} collective-permute-done((f32[56,128]{1,0:T(8,128)S(1)}, f32[56,128]{1,0:T(8,128)S(1)}, u32[]{:S(2)}, u32[]{:S(2)}) %collective-permute-start.16) | collective-permute-done | bytes 28704 | tf_op jit(solution)/shard_map/ppermute | solution.py:430
  80.7 3.8 %collective-permute-done.17 = f32[56,128]{1,0:T(8,128)S(1)} collective-permute-done((f32[56,128]{1,0:T(8,128)S(1)}, f32[56,128]{1,0:T(8,128)S(1)}, u32[]{:S(2)}, u32[]{:S(2)}) %collective-permute-start.17) | collective-permute-done | bytes 28704 | tf_op jit(solution)/shard_map/ppermute | solution.py:430
  84.5 1.8 %collective-permute-start.18 = (f32[56,128]{1,0:T(8,128)S(1)}, f32[56,128]{1,0:T(8,128)S(1)}, u32[]{:S(2)}, u32[]{:S(2)}) collective-permute-start(f32[56,128]{1,0:T(8,128)S(1)} %add.31), channel_id=1, source_target_pairs={{0,8},{2,10},{4,12},{6,14},{8,0},{10,2},{12,4},{14,6},{1,9},{3,11}... | collective-permute-start | bytes 86024 | tf_op jit(solution)/shard_map/ppermute | solution.py:430
  86.2 3.0 %collective-permute-done.18 = f32[56,128]{1,0:T(8,128)S(1)} collective-permute-done((f32[56,128]{1,0:T(8,128)S(1)}, f32[56,128]{1,0:T(8,128)S(1)}, u32[]{:S(2)}, u32[]{:S(2)}) %collective-permute-start.18) | collective-permute-done | bytes 28704 | tf_op jit(solution)/shard_map/ppermute | solution.py:430
  89.9 0.5 collective-permute-done.19.refs_3_
  90.5 22.2 %shard_map.61 = f32[64,384]{1,0:T(8,128)} custom-call(f32[8,128]{1,0:T(8,128)S(1)} %broadcast_in_dim.19.core.refs_0_, f32[8,128]{1,0:T(8,128)S(1)} %broadcast_in_dim.20.refs_1_, f32[56,128]{1,0:T(8,128)S(1)} %add.32.refs_2_, f32[56,128]{1,0:T(8,128)S(1)} %collective-permute-done.19.refs_3_, f32[192,384]{1,0:T(8,128)S(1)} %get-tuple-element.50.refs_4_), custom_call_target="tpu_custom_call" | custom-call | flops 20000000000 | bytes 1000000 | tf_op jit(solution)/shard_map/pallas_call | solution.py:32
  (45 shorter events, 0.6 us)
Async XLA Ops:
  0.0 2.3 %collective-permute-start.2 = (bf16[384,768]{1,0:T(8,128)(2,1)}, bf16[384,768]{1,0:T(8,128)(2,1)S(1)}, u32[]{:S(2)}, u32[]{:S(2)}) collective-permute-start(bf16[384,768]{1,0:T(8,128)(2,1)} %own.1), channel_id=1, source_target_pairs={{0,1},{1,0},{2,3},{3,2},{4,5},{5,4},{6,7},{7,6},{8,9},{9,8},{10,11... | collective-permute-start | bytes 1769480 | tf_op jit(solution)/shard_map/ppermute | solution.py:423
  0.5 15.7 %collective-permute-start = (bf16[384,768]{1,0:T(8,128)(2,1)}, bf16[384,768]{1,0:T(8,128)(2,1)S(1)}, u32[]{:S(2)}, u32[]{:S(2)}) collective-permute-start(bf16[384,768]{1,0:T(8,128)(2,1)} %own.1), channel_id=1, source_target_pairs={{2,0},{6,4},{10,8},{14,12},{1,13},{3,15},{5,1},{7,3},{9,5},{11,7},... | collective-permute-start | bytes 1769480 | tf_op jit(solution)/shard_map/ppermute | solution.py:451
  2.3 1.1 copy-start
  3.4 10.7 %copy-start.9 = (s32[384,64]{0,1:T(8,128)S(1)}, s32[384,64]{0,1:T(8,128)}, u32[]{:S(2)}) copy-start(s32[384,64]{0,1:T(8,128)} %param.7) | copy-start | bytes 294916
  5.6 0.8 copy-start.5
  6.4 0.9 copy-start.7
  7.2 15.5 %collective-permute-start.3 = (bf16[384,768]{1,0:T(8,128)(2,1)S(1)}, bf16[384,768]{1,0:T(8,128)(2,1)S(1)}, u32[]{:S(2)}, u32[]{:S(2)}) collective-permute-start(bf16[384,768]{1,0:T(8,128)(2,1)S(1)} %get-tuple-element.30.own), channel_id=1, source_target_pairs={{3,0},{7,4},{11,8},{15,12},{0,13},{2,15},{4,1},{6,3},{8,5},{10,7},... | collective-permute-start | bytes 1769480 | tf_op jit(solution)/shard_map/ppermute | solution.py:451
  14.1 2.0 %collective-permute-start.1 = (f32[64,384]{1,0:T(8,128)S(1)}, f32[64,384]{1,0:T(8,128)S(1)}, u32[]{:S(2)}, u32[]{:S(2)}) collective-permute-start(f32[64,384]{1,0:T(8,128)S(1)} %multiply_bitcast_fusion), channel_id=1, source_target_pairs={{0,1},{1,0},{2,3},{3,2},{4,5},{5,4},{6,7},{7,6},{8,9},{9,8},{10,11... | collective-permute-start | bytes 294920 | tf_op jit(solution)/shard_map/ppermute | solution.py:423
  14.2 0.7 copy-start.10
  16.2 8.3 %collective-permute-start.5 = (bf16[384,768]{1,0:T(8,128)(2,1)S(1)}, bf16[384,768]{1,0:T(8,128)(2,1)S(1)}, u32[]{:S(2)}, u32[]{:S(2)}) collective-permute-start(bf16[384,768]{1,0:T(8,128)(2,1)S(1)} %collective-permute-done.direct), channel_id=1, source_target_pairs={{1,2},{5,6},{9,10},{13,14},{17,18},{21,22},{25,26},{29,30}} | collective-permute-start | bytes 1769480 | tf_op jit(solution)/shard_map/ppermute | solution.py:451
  22.7 3.8 %collective-permute-start.4 = (bf16[384,768]{1,0:T(8,128)(2,1)S(1)}, bf16[384,768]{1,0:T(8,128)(2,1)S(1)}, u32[]{:S(2)}, u32[]{:S(2)}) collective-permute-start(bf16[384,768]{1,0:T(8,128)(2,1)S(1)} %collective-permute-done.3.direct), channel_id=1, source_target_pairs={{1,2},{5,6},{9,10},{13,14},{17,18},{21,22},{25,26},{29,30}} | collective-permute-start | bytes 1769480 | tf_op jit(solution)/shard_map/ppermute | solution.py:451
  26.5 38.6 %copy-start.1 = (bf16[768,384]{1,0:T(8,128)(2,1)}, bf16[768,384]{1,0:T(8,128)(2,1)S(1)}, u32[]{:S(2)}) copy-start(bf16[768,384]{1,0:T(8,128)(2,1)S(1)} %get-tuple-element.44.l1) | copy-start | bytes 1769476
  28.5 36.6 %copy-start.3 = (bf16[768,384]{1,0:T(8,128)(2,1)}, bf16[768,384]{1,0:T(8,128)(2,1)S(1)}, u32[]{:S(2)}) copy-start(bf16[768,384]{1,0:T(8,128)(2,1)S(1)} %get-tuple-element.46.l2) | copy-start | bytes 1769476
  28.6 10.8 %collective-permute-start.6 = (f32[16,384]{1,0:T(8,128)S(1)}, f32[16,384]{1,0:T(8,128)S(1)}, u32[]{:S(2)}, u32[]{:S(2)}) collective-permute-start(f32[16,384]{1,0:T(8,128)S(1)} %pad_maximum_fusion.1), channel_id=1, source_target_pairs={{0,2},{1,5},{2,4},{3,7},{4,6},{5,9},{6,8},{7,11},{8,10},{9,13},{10... | collective-permute-start | bytes 73736 | tf_op jit(solution)/shard_map/ppermute | solution.py:419
  39.3 1.2 %collective-permute-start.7 = (f32[16,384]{1,0:T(8,128)S(1)}, f32[16,384]{1,0:T(8,128)S(1)}, u32[]{:S(2)}, u32[]{:S(2)}) collective-permute-start(f32[16,384]{1,0:T(8,128)S(1)} %add.28.sums), channel_id=1, source_target_pairs={{0,1},{1,0},{2,3},{3,2},{4,5},{5,4},{6,7},{7,6},{8,9},{9,8},{10,11... | collective-permute-start | bytes 73736 | tf_op jit(solution)/shard_map/ppermute | solution.py:423
  40.6 5.3 %copy-start.6 = (bf16[768,384]{1,0:T(8,128)(2,1)S(1)}, bf16[768,384]{1,0:T(8,128)(2,1)}, u32[]{:S(2)}) copy-start(bf16[768,384]{1,0:T(8,128)(2,1)} %copy-done.5) | copy-start | bytes 1769476
  40.6 5.3 %copy-start.8 = (bf16[768,384]{1,0:T(8,128)(2,1)S(1)}, bf16[768,384]{1,0:T(8,128)(2,1)}, u32[]{:S(2)}) copy-start(bf16[768,384]{1,0:T(8,128)(2,1)} %copy-done.7) | copy-start | bytes 1769476
  41.1 10.5 %collective-permute-start.9 = (f32[128,384]{1,0:T(8,128)S(1)}, f32[128,384]{1,0:T(8,128)S(1)}, u32[]{:S(2)}, u32[]{:S(2)}) collective-permute-start(f32[128,384]{1,0:T(8,128)S(1)} %shard_map.51), channel_id=1, source_target_pairs={{0,2},{1,5},{2,4},{3,7},{4,6},{5,9},{6,8},{7,11},{8,10},{9,13},{10... | collective-permute-start | bytes 589832 | tf_op jit(solution)/shard_map/ppermute | solution.py:419
  43.0 8.7 %collective-permute-start.8 = (f32[128,384]{1,0:T(8,128)S(1)}, f32[128,384]{1,0:T(8,128)S(1)}, u32[]{:S(2)}, u32[]{:S(2)}) collective-permute-start(f32[128,384]{1,0:T(8,128)S(1)} %get-tuple-element.40.vectors.v0), channel_id=1, source_target_pairs={{0,14},{1,13},{2,0},{3,15},{4,2},{5,1},{6,4},{7,3},{8,6},{9,5},{10... | collective-permute-start | bytes 589832 | tf_op jit(solution)/shard_map/ppermute | solution.py:419
  52.4 1.5 %collective-permute-start.10 = (f32[128,384]{1,0:T(8,128)S(1)}, f32[128,384]{1,0:T(8,128)S(1)}, u32[]{:S(2)}, u32[]{:S(2)}) collective-permute-start(f32[128,384]{1,0:T(8,128)S(1)} %shard_map.52.total), channel_id=1, source_target_pairs={{0,1},{1,0},{2,3},{3,2},{4,5},{5,4},{6,7},{7,6},{8,9},{9,8},{10,11... | collective-permute-start | bytes 589832 | tf_op jit(solution)/shard_map/ppermute | solution.py:423
  54.5 10.6 %collective-permute-start.12 = (f32[128,384]{1,0:T(8,128)S(1)}, f32[128,384]{1,0:T(8,128)S(1)}, u32[]{:S(2)}, u32[]{:S(2)}) collective-permute-start(f32[128,384]{1,0:T(8,128)S(1)} %shard_map.55), channel_id=1, source_target_pairs={{0,2},{1,5},{2,4},{3,7},{4,6},{5,9},{6,8},{7,11},{8,10},{9,13},{10... | collective-permute-start | bytes 589832 | tf_op jit(solution)/shard_map/ppermute | solution.py:419
  55.7 9.3 %collective-permute-start.11 = (f32[128,384]{1,0:T(8,128)S(1)}, f32[128,384]{1,0:T(8,128)S(1)}, u32[]{:S(2)}, u32[]{:S(2)}) collective-permute-start(f32[128,384]{1,0:T(8,128)S(1)} %shard_map.53.vectors.v1), channel_id=1, source_target_pairs={{0,14},{1,13},{2,0},{3,15},{4,2},{5,1},{6,4},{7,3},{8,6},{9,5},{10... | collective-permute-start | bytes 589832 | tf_op jit(solution)/shard_map/ppermute | solution.py:419
  65.9 1.5 %collective-permute-start.13 = (f32[128,384]{1,0:T(8,128)S(1)}, f32[128,384]{1,0:T(8,128)S(1)}, u32[]{:S(2)}, u32[]{:S(2)}) collective-permute-start(f32[128,384]{1,0:T(8,128)S(1)} %shard_map.56.total), channel_id=1, source_target_pairs={{0,1},{1,0},{2,3},{3,2},{4,5},{5,4},{6,7},{7,6},{8,9},{9,8},{10,11... | collective-permute-start | bytes 589832 | tf_op jit(solution)/shard_map/ppermute | solution.py:423
  67.4 6.1 %collective-permute-start.14 = (f32[128,384]{1,0:T(8,128)S(1)}, f32[128,384]{1,0:T(8,128)S(1)}, u32[]{:S(2)}, u32[]{:S(2)}) collective-permute-start(f32[128,384]{1,0:T(8,128)S(1)} %shard_map.57.v2.vectors), channel_id=1, source_target_pairs={{0,14},{1,13},{2,0},{3,15},{4,2},{5,1},{6,4},{7,3},{8,6},{9,5},{10... | collective-permute-start | bytes 589832 | tf_op jit(solution)/shard_map/ppermute | solution.py:419
  70.8 2.7 %copy-start.2 = (bf16[768,384]{1,0:T(8,128)(2,1)S(1)}, bf16[768,384]{1,0:T(8,128)(2,1)}, u32[]{:S(2)}) copy-start(bf16[768,384]{1,0:T(8,128)(2,1)} %copy-done.1) | copy-start | bytes 1769476
  70.8 2.7 %copy-start.4 = (bf16[768,384]{1,0:T(8,128)(2,1)S(1)}, bf16[768,384]{1,0:T(8,128)(2,1)}, u32[]{:S(2)}) copy-start(bf16[768,384]{1,0:T(8,128)(2,1)} %copy-done.3) | copy-start | bytes 1769476
  74.9 1.5 %collective-permute-start.15 = (f32[56,128]{1,0:T(8,128)S(1)}, f32[56,128]{1,0:T(8,128)S(1)}, u32[]{:S(2)}, u32[]{:S(2)}) collective-permute-start(f32[56,128]{1,0:T(8,128)S(1)} %get-tuple-element.49), channel_id=1, source_target_pairs={{0,1},{1,0},{2,3},{3,2},{4,5},{5,4},{6,7},{7,6},{8,9},{9,8},{10,11... | collective-permute-start | bytes 86024 | tf_op jit(solution)/shard_map/ppermute | solution.py:423
  76.4 4.2 %collective-permute-start.16 = (f32[56,128]{1,0:T(8,128)S(1)}, f32[56,128]{1,0:T(8,128)S(1)}, u32[]{:S(2)}, u32[]{:S(2)}) collective-permute-start(f32[56,128]{1,0:T(8,128)S(1)} %add.29), channel_id=1, source_target_pairs={{0,2},{2,0},{4,6},{6,4},{8,10},{10,8},{12,14},{14,12},{1,3},{3,1},... | collective-permute-start | bytes 86024 | tf_op jit(solution)/shard_map/ppermute | solution.py:430
  80.6 3.9 %collective-permute-start.17 = (f32[56,128]{1,0:T(8,128)S(1)}, f32[56,128]{1,0:T(8,128)S(1)}, u32[]{:S(2)}, u32[]{:S(2)}) collective-permute-start(f32[56,128]{1,0:T(8,128)S(1)} %add.30), channel_id=1, source_target_pairs={{0,4},{2,6},{4,0},{6,2},{8,12},{10,14},{12,8},{14,10},{1,5},{3,7},... | collective-permute-start | bytes 86024 | tf_op jit(solution)/shard_map/ppermute | solution.py:430
  84.5 4.8 %collective-permute-start.18 = (f32[56,128]{1,0:T(8,128)S(1)}, f32[56,128]{1,0:T(8,128)S(1)}, u32[]{:S(2)}, u32[]{:S(2)}) collective-permute-start(f32[56,128]{1,0:T(8,128)S(1)} %add.31), channel_id=1, source_target_pairs={{0,8},{2,10},{4,12},{6,14},{8,0},{10,2},{12,4},{14,6},{1,9},{3,11}... | collective-permute-start | bytes 86024 | tf_op jit(solution)/shard_map/ppermute | solution.py:430
  89.3 1.2 %collective-permute-start.19 = (f32[56,128]{1,0:T(8,128)S(1)}, f32[56,128]{1,0:T(8,128)S(1)}, u32[]{:S(2)}, u32[]{:S(2)}) collective-permute-start(f32[56,128]{1,0:T(8,128)S(1)} %add.32.refs_2_), channel_id=1, source_target_pairs={{0,1},{1,0},{2,3},{3,2},{4,5},{5,4},{6,7},{7,6},{8,9},{9,8},{10,11... | collective-permute-start | bytes 86024 | tf_op jit(solution)/shard_map/ppermute | solution.py:423

commit v10 on v9

--- a/solution.py
+++ b/solution.py
@@ -93,8 +93,8 @@
     fill_tile(None, embs, row_sq, embs[0], high, low, row_sum)
 
 
-def far_body(keep, relays, own, other, row_sq, direct, relayed, before, high, low, row_sum, col_sum):
-    row_sum[...] = before[...]
+def far_body(keep, relays, token, own, other, row_sq, direct, relayed, before, high, low, row_sum, col_sum):
+    row_sum[...] = before[...] + token[0:1, 0:1]
     size = own.shape[0]
     weight = jnp.concatenate([keep[0:1, :]] * (size // 128), axis=1)
     col = chosen(relays, relayed[...], direct[...])
@@ -242,42 +242,57 @@
     blocks = [work[8 * i:8 * i + 8, :] for i in range(size // 8)]
     place = lax.broadcasted_iota(jnp.int32, (8, 2 * size), 0)
     done = [None] * (size // 8)
+
+    def corner(cols, r):
+        return [[sublane(cols[j], r + i) for j in range(i + 1)] for i in range(4)]
+
+    pivot = corner([lane(blocks[0], j) for j in range(4)], 0)
     for k in range(0, size, 4):
         top, r = divmod(k, 8)
-        pivot = blocks[top]
-        cols = [lane(pivot, k + j) for j in range(4)]
-        u0, u1, u2, u3 = (sublane(pivot, r + j) for j in range(4))
-        a00, a10, a20, a30 = (sublane(cols[0], r + j) for j in range(4))
-        a11, a21, a31 = (sublane(cols[1], r + j) for j in range(1, 4))
-        a22, a32 = (sublane(cols[2], r + j) for j in range(2, 4))
-        a33 = sublane(cols[3], r + 3)
+        (a00,), (a10, a11), (a20, a21, a22), (a30, a31, a32, a33) = pivot
+        u0, u1, u2, u3 = u = [sublane(blocks[top], r + j) for j in range(4)]
         det_a = a00 * a11 - a10 * a10
         inv_a = 1.0 / det_a
         p00, p10, p11 = a11 * inv_a, a10 * inv_a, a00 * inv_a
         b00, b01 = a20 * p00 - a21 * p10, a21 * p11 - a20 * p10
         b10, b11 = a30 * p00 - a31 * p10, a31 * p11 - a30 * p10
-        s00 = a22 - b00 * a20 - b01 * a21
-        s10 = a32 - b10 * a20 - b11 * a21
-        s11 = a33 - b10 * a30 - b11 * a31
+        s00 = a22 - (b00 * a20 + b01 * a21)
+        s10 = a32 - (b10 * a20 + b11 * a21)
+        s11 = a33 - (b10 * a30 + b11 * a31)
         det_s = s00 * s11 - s10 * s10
         inv_s = 1.0 / det_s
-        u2 = u2 - b00 * u0 - b01 * u1
-        u3 = u3 - b10 * u0 - b11 * u1
-        t2 = (s11 * u2 - s10 * u3) * inv_s
-        t3 = (s00 * u3 - s10 * u2) * inv_s
-        t0 = (p00 * u0 - p10 * u1) - b00 * t2 - b10 * t3
-        t1 = (p11 * u1 - p10 * u0) - b01 * t2 - b11 * t3
+        q22, q32, q33 = s11 * inv_s, -s10 * inv_s, s00 * inv_s
+        q20, q21 = -(q22 * b00 + q32 * b10), -(q22 * b01 + q32 * b11)
+        q30, q31 = -(q32 * b00 + q33 * b10), -(q32 * b01 + q33 * b11)
+        q00 = p00 - (b00 * q20 + b10 * q30)
+        q10 = -p10 - (b01 * q20 + b11 * q30)
+        q11 = p11 - (b01 * q21 + b11 * q31)
+        inverse = [[q00, q10, q20, q30], [q10, q11, q21, q31], [q20, q21, q22, q32], [q30, q31, q32, q33]]
+
+        def applied(values):
+            return [(row[0] * values[0] + row[1] * values[1]) + (row[2] * values[2] + row[3] * values[3])
+                    for row in inverse]
+
+        if k + 4 < size:
+            across = [lane(blocks[top], k + 4 + j) for j in range(4)]
+            cross = [[sublane(across[j], r + i) for i in range(4)] for j in range(4)]
+            after = across if r == 0 else [lane(blocks[top + 1], k + 4 + j) for j in range(4)]
+            plain = corner(after, 4 - r)
+            solved = [applied(column) for column in cross]
+            pivot = [[plain[i][j] - ((cross[i][0] * solved[j][0] + cross[i][1] * solved[j][1])
+                                     + (cross[i][2] * solved[j][2] + cross[i][3] * solved[j][3]))
+                      for j in range(i + 1)] for i in range(4)]
+        t = applied(u)
         for i in range(top, size // 8):
-            if i == top:
-                if r:
-                    continue
-                c = cols
-            else:
-                c = [lane(blocks[i], k + j) for j in range(4)]
-            change = (c[0] * t0 + c[1] * t1) + (c[2] * t2 + c[3] * t3)
+            if i == top and r:
+                continue
+            c = [lane(blocks[i], k + j) for j in range(4)]
+            change = (c[0] * t[0] + c[1] * t[1]) + (c[2] * t[2] + c[3] * t[3])
             blocks[i] = blocks[i] - (jnp.where(place > 3, change, 0.0) if i == top else change)
         v0 = u0 * lax.rsqrt(a00)
         v1 = (a00 * u1 - a10 * u0) * lax.rsqrt(a00 * det_a)
+        u2 = u2 - b00 * u0 - b01 * u1
+        u3 = u3 - b10 * u0 - b11 * u1
         v2 = u2 * lax.rsqrt(s00)
         v3 = (s00 * u3 - s10 * u2) * lax.rsqrt(s00 * det_s)
         four = jnp.where(place % 4 == 0, v0, jnp.where(place % 4 == 1, v1, jnp.where(place % 4 == 2, v2, v3)))
@@ -446,13 +461,11 @@
     back2 = [(i, (i - 2) % blocks) for i in range(blocks)]
     orders = [
         [(2 * i + j, 2 * k) for i, k in back1] + [(2 * i + 1 - j, 2 * k + 1) for i, k in back2] for j in range(2)]
+    if relaying:
+        orders[0] += [(2 * i, 2 * i + 2) for i in range(0, blocks, 2)]
 
     def between_shards(shard, pairs):
         return lax.ppermute(shard, ("blk", "narrow"), pairs)
-
-    def relay(shard):
-        pairs = [(2 * i + 1, 2 * i + 2) for i in range(0, blocks, 2)]
-        return between_shards(shard, pairs) if relaying else shard
 
     first = between_shards(embeddings, orders[0])
     seed = start_seed.astype(F32).T / 1000.0
@@ -464,12 +477,17 @@
         own_body, [embeddings, other_emb], size,
         (((2 * size, 128), F32), (embeddings.shape, BF16), ((8, 128), F32)))
     first, seeds, keep, relays, token = lax.optimization_barrier((first, seeds, keep, relays, token))
+    relayed = [first, own_copy]
+    if relaying:
+        relayed[1] = between_shards(first, [(2 * i, (i - 2) % blocks * 2) for i in range(1, blocks, 2)])
     second = between_shards(own_copy, orders[1])
-    tile_args = [keep, relays, own_copy, other_emb, row_sq]
+    if relaying:
+        relayed[0] = between_shards(first, [(2 * i + 1, 2 * i + 2) for i in range(0, blocks, 2)])
+    tile_args = [keep, relays, token, own_copy, other_emb, row_sq]
     h1, l1, sums, cols1 = make_tile(
-        far_body, [*tile_args, first, relay(first), sums], size, (((8, size), F32),))
+        far_body, [*tile_args, first, relayed[0], sums], size, (((8, size), F32),))
     h2, l2, sums, cols2 = make_tile(
-        far_body, [*tile_args, second, relay(second), sums], size, (((8, size), F32),))
+        far_body, [*tile_args, second, relayed[1], sums], size, (((8, size), F32),))
     cols = jnp.concatenate([jnp.where(relays[0, 0] > 0.5, cols2, cols1), jnp.where(relays[0, 0] > 0.5, cols1, cols2)])
     sums = sums + between_blocks(cols, 1)
 

time: 113 us -> 107 us (0.947)
  Pallas kernels: 34.5 us -> 30.4 us
  waiting for transfers between devices: 35 us -> 31.8 us
  starting transfers between devices: 36.3 us -> 37.9 us
    pallas_call x16, Pallas kernels: 34.5 us -> 30.4 us  [call(): pl.pallas_call(body, out_shape=[jax.ShapeDtypeStruct(shape, dtype) for sh...]
    ppermute x6, starting transfers between devices: 21.2 us -> 17.8 us  [between_blocks(): return lax.ppermute(shard, ('blk', 'narrow'), pairs)]
    ppermute x4, starting transfers between devices: 9.52 us -> 12.4 us  [between_shards(): return lax.ppermute(shard, ('blk', 'narrow'), pairs)]
    ppermute x6, waiting for transfers between devices: 14.7 us -> 12.4 us  [between_blocks(): return lax.ppermute(shard, ('blk', 'narrow'), pairs)]
    ppermute x7, starting transfers between devices: 1.39 us -> 3.57 us  [between_cores(): return lax.ppermute(shard, 'narrow', [(0, 1), (1, 0)])]
    unnamed x22 -> x10, local copies, waits for them, and re-layouts: 3.43 us -> 2.14 us
  transfers between devices with their start and end apart: 20 -> 20, of which waited for: 14 -> 15; matrix products, arithmetic and copies ran while one was open for 1% -> 3% of each run, Pallas kernels for 5% -> 5%
where the time goes in v10:
time: 107 us
  starting transfers between devices  37.9 us (35%)
  waiting for transfers between devices  31.8 us (30%)
  Pallas kernels  30.4 us (28%)
  local copies, waits for them, and re-layouts  3.92 us (4%)
  between operations  2.14 us (2%)
    pallas_call x16, Pallas kernels, call(): pl.pallas_call(body, out_shape=[jax.ShapeDtypeStruct(shape, dtype) for sh...  30.4 us
    ppermute x6, starting transfers between devices, between_blocks(): return lax.ppermute(shard, ('blk', 'narrow'), pairs)  17.8 us
    ppermute x6, waiting for transfers between devices, between_blocks(): return lax.ppermute(shard, ('blk', 'narrow'), pairs)  12.4 us
    ppermute x4, starting transfers between devices, between_shards(): return lax.ppermute(shard, ('blk', 'narrow'), pairs)  12.4 us
    ppermute x3, waiting for transfers between devices, total_over_blocks(): lax.ppermute(values, 'blk', [(i, i ^ span) for i in range(blocks)])  8.64 us
    ppermute x7, waiting for transfers between devices, between_cores(): return lax.ppermute(shard, 'narrow', [(0, 1), (1, 0)])  5.45 us
    ppermute x4, waiting for transfers between devices, between_shards(): return lax.ppermute(shard, ('blk', 'narrow'), pairs)  5.23 us
    ppermute x3, starting transfers between devices, total_over_blocks(): lax.ppermute(values, 'blk', [(i, i ^ span) for i in range(blocks)])  4.19 us
  transfers between devices with their start and end apart: 20, of which 15 were waited for; matrix products, arithmetic and copies ran while one was open for 3% of the time, Pallas kernels for 5%

profile of v10, /device:TPU:0, one launch (start us, length us, event | category | flops | bytes accessed | tf_op | source)
XLA Modules:
  0.0 107.1 jit_solution(11675413879842371063)
XLA Ops:
  0.0 0.5 collective-permute-start.2
  0.5 2.5 %collective-permute-start = (bf16[384,768]{1,0:T(8,128)(2,1)}, bf16[384,768]{1,0:T(8,128)(2,1)S(1)}, u32[]{:S(2)}, u32[]{:S(2)}) collective-permute-start(bf16[384,768]{1,0:T(8,128)(2,1)} %own.1), channel_id=1, source_target_pairs={{2,0},{6,4},{10,8},{14,12},{1,13},{3,15},{5,1},{7,3},{9,5},{11,7},... | collective-permute-start | bytes 1769480 | tf_op jit(solution)/shard_map/ppermute | solution.py:468
  3.0 0.9 multiply_bitcast_fusion
  3.9 2.4 %collective-permute-start.1 = (f32[64,384]{1,0:T(8,128)S(1)}, f32[64,384]{1,0:T(8,128)S(1)}, u32[]{:S(2)}, u32[]{:S(2)}) collective-permute-start(f32[64,384]{1,0:T(8,128)S(1)} %multiply_bitcast_fusion), channel_id=1, source_target_pairs={{0,1},{1,0},{2,3},{3,2},{4,5},{5,4},{6,7},{7,6},{8,9},{9,8},{10,11... | collective-permute-start | bytes 294920 | tf_op jit(solution)/shard_map/ppermute | solution.py:438
  6.3 1.3 %dynamic_slice.3 = s32[1,1]{0,1:T(1,128)} dynamic-slice(s32[8,2]{0,1:T(2,128)} %param.5, s32[]{:T(128)S(6)} %select_n.25, s32[]{:T(128)S(6)} %select_n.26), dynamic_slice_sizes={1,1} | dynamic-slice | bytes 12 | tf_op jit(solution)/shard_map/dynamic_slice | solution.py:473
  8.2 1.9 %shard_map.46 = (bf16[768,384]{1,0:T(8,128)(2,1)S(1)}, bf16[768,384]{1,0:T(8,128)(2,1)S(1)}, f32[16,384]{1,0:T(8,128)S(1)}, f32[768,128]{1,0:T(8,128)S(1)}, bf16...) custom-call(bf16[384,768]{1,0:T(8,128)(2,1)S(1)} %copy-done, bf16[384,768]{1,0:T(8,128)(2,1)S(1)} %collective-permute-done.2.other), custom_call_target="tpu_custom_call" | custom-call | flops 2000000000 | bytes 1000000 | tf_op jit(solution)/shard_map/pallas_call | solution.py:32
  10.1 1.0 collective-permute-done.direct
  11.1 0.7 collective-permute-start.5
  11.8 0.7 collective-permute-start.4
  12.5 8.5 %collective-permute-start.3 = (bf16[384,768]{1,0:T(8,128)(2,1)S(1)}, bf16[384,768]{1,0:T(8,128)(2,1)S(1)}, u32[]{:S(2)}, u32[]{:S(2)}) collective-permute-start(bf16[384,768]{1,0:T(8,128)(2,1)S(1)} %get-tuple-element.34.own), channel_id=1, source_target_pairs={{3,0},{7,4},{11,8},{15,12},{0,13},{2,15},{4,1},{6,3},{8,5},{10,7},... | collective-permute-start | bytes 1769480 | tf_op jit(solution)/shard_map/ppermute | solution.py:468
  21.0 0.5 slice.4
  22.1 2.0 %shard_map.47 = (bf16[768,384]{1,0:T(8,128)(2,1)S(1)}, bf16[768,384]{1,0:T(8,128)(2,1)S(1)}, f32[16,384]{1,0:T(8,128)S(1)}, f32[8,384]{1,0:T(8,128)S(1)}) custom-call(f32[8,128]{1,0:T(8,128)S(1)} %broadcast_in_dim.22.keep, f32[8,128]{1,0:T(8,128)S(1)} %broadcast_in_dim.23.relays, f32[8,128]{1,0:T(8,128)S(1)} %get-tuple-element.33.token, ...), custom_call_target="tpu_custom_call" | custom-call | flops 2000000000 | bytes 1000000 | tf_op jit(solution)/shard_map/pallas_call | solution.py:32
  24.1 4.2 %collective-permute-done.3.direct = bf16[384,768]{1,0:T(8,128)(2,1)S(1)} collective-permute-done((bf16[384,768]{1,0:T(8,128)(2,1)S(1)}, bf16[384,768]{1,0:T(8,128)(2,1)S(1)}, u32[]{:S(2)}, u32[]{:S(2)}) %collective-permute-start.3) | collective-permute-done | bytes 589856 | tf_op jit(solution)/shard_map/ppermute | solution.py:468
  28.4 2.0 %shard_map.48 = (bf16[768,384]{1,0:T(8,128)(2,1)S(1)}, bf16[768,384]{1,0:T(8,128)(2,1)S(1)}, f32[16,384]{1,0:T(8,128)S(1)}, f32[8,384]{1,0:T(8,128)S(1)}) custom-call(f32[8,128]{1,0:T(8,128)S(1)} %broadcast_in_dim.22.keep, f32[8,128]{1,0:T(8,128)S(1)} %broadcast_in_dim.23.relays, f32[8,128]{1,0:T(8,128)S(1)} %get-tuple-element.33.token, ...), custom_call_target="tpu_custom_call" | custom-call | flops 2000000000 | bytes 1000000 | tf_op jit(solution)/shard_map/pallas_call | solution.py:32
  30.3 5.3 %collective-permute-start.6 = (f32[16,384]{1,0:T(8,128)S(1)}, f32[16,384]{1,0:T(8,128)S(1)}, u32[]{:S(2)}, u32[]{:S(2)}) collective-permute-start(f32[16,384]{1,0:T(8,128)S(1)} %pad_maximum_fusion.1), channel_id=1, source_target_pairs={{0,2},{1,5},{2,4},{3,7},{4,6},{5,9},{6,8},{7,11},{8,10},{9,13},{10... | collective-permute-start | bytes 73736 | tf_op jit(solution)/shard_map/ppermute | solution.py:434
  35.6 1.7 %collective-permute-done.6 = f32[16,384]{1,0:T(8,128)S(1)} collective-permute-done((f32[16,384]{1,0:T(8,128)S(1)}, f32[16,384]{1,0:T(8,128)S(1)}, u32[]{:S(2)}, u32[]{:S(2)}) %collective-permute-start.6) | collective-permute-done | bytes 24608 | tf_op jit(solution)/shard_map/ppermute | solution.py:434
  37.3 1.2 %collective-permute-done.7.other_sums = f32[16,384]{1,0:T(8,128)S(1)} collective-permute-done((f32[16,384]{1,0:T(8,128)S(1)}, f32[16,384]{1,0:T(8,128)S(1)}, u32[]{:S(2)}, u32[]{:S(2)}) %collective-permute-start.7) | collective-permute-done | bytes 24608 | tf_op jit(solution)/shard_map/ppermute | solution.py:438
  38.6 0.5 shard_map.51
  39.1 3.1 %collective-permute-start.9 = (f32[128,384]{1,0:T(8,128)S(1)}, f32[128,384]{1,0:T(8,128)S(1)}, u32[]{:S(2)}, u32[]{:S(2)}) collective-permute-start(f32[128,384]{1,0:T(8,128)S(1)} %shard_map.51), channel_id=1, source_target_pairs={{0,2},{1,5},{2,4},{3,7},{4,6},{5,9},{6,8},{7,11},{8,10},{9,13},{10... | collective-permute-start | bytes 589832 | tf_op jit(solution)/shard_map/ppermute | solution.py:434
  42.1 1.7 %collective-permute-start.8 = (f32[128,384]{1,0:T(8,128)S(1)}, f32[128,384]{1,0:T(8,128)S(1)}, u32[]{:S(2)}, u32[]{:S(2)}) collective-permute-start(f32[128,384]{1,0:T(8,128)S(1)} %get-tuple-element.44.vectors.v0), channel_id=1, source_target_pairs={{0,14},{1,13},{2,0},{3,15},{4,2},{5,1},{6,4},{7,3},{8,6},{9,5},{10... | collective-permute-start | bytes 589832 | tf_op jit(solution)/shard_map/ppermute | solution.py:434
  43.9 0.5 shard_map.50.product
  44.3 4.5 %collective-permute-done.9.behind = f32[128,384]{1,0:T(8,128)S(1)} collective-permute-done((f32[128,384]{1,0:T(8,128)S(1)}, f32[128,384]{1,0:T(8,128)S(1)}, u32[]{:S(2)}, u32[]{:S(2)}) %collective-permute-start.9) | collective-permute-done | bytes 196640 | tf_op jit(solution)/shard_map/ppermute | solution.py:434
  48.9 0.9 collective-permute-done.8.near
  49.7 0.8 shard_map.52.total
  50.6 1.4 %collective-permute-done.10.other_total = f32[128,384]{1,0:T(8,128)S(1)} collective-permute-done((f32[128,384]{1,0:T(8,128)S(1)}, f32[128,384]{1,0:T(8,128)S(1)}, u32[]{:S(2)}, u32[]{:S(2)}) %collective-permute-start.10) | collective-permute-done | bytes 196640 | tf_op jit(solution)/shard_map/ppermute | solution.py:438
  52.1 0.5 shard_map.55
  52.6 1.3 %collective-permute-start.12 = (f32[128,384]{1,0:T(8,128)S(1)}, f32[128,384]{1,0:T(8,128)S(1)}, u32[]{:S(2)}, u32[]{:S(2)}) collective-permute-start(f32[128,384]{1,0:T(8,128)S(1)} %shard_map.55), channel_id=1, source_target_pairs={{0,2},{1,5},{2,4},{3,7},{4,6},{5,9},{6,8},{7,11},{8,10},{9,13},{10... | collective-permute-start | bytes 589832 | tf_op jit(solution)/shard_map/ppermute | solution.py:434
  53.9 3.5 %collective-permute-start.11 = (f32[128,384]{1,0:T(8,128)S(1)}, f32[128,384]{1,0:T(8,128)S(1)}, u32[]{:S(2)}, u32[]{:S(2)}) collective-permute-start(f32[128,384]{1,0:T(8,128)S(1)} %shard_map.53.vectors.v1), channel_id=1, source_target_pairs={{0,14},{1,13},{2,0},{3,15},{4,2},{5,1},{6,4},{7,3},{8,6},{9,5},{10... | collective-permute-start | bytes 589832 | tf_op jit(solution)/shard_map/ppermute | solution.py:434
  57.4 0.5 shard_map.54.product
  57.9 5.3 %collective-permute-done.12.behind = f32[128,384]{1,0:T(8,128)S(1)} collective-permute-done((f32[128,384]{1,0:T(8,128)S(1)}, f32[128,384]{1,0:T(8,128)S(1)}, u32[]{:S(2)}, u32[]{:S(2)}) %collective-permute-start.12) | collective-permute-done | bytes 196640 | tf_op jit(solution)/shard_map/ppermute | solution.py:434
  63.2 0.8 shard_map.56.total
  64.1 1.4 %collective-permute-done.13.other_total = f32[128,384]{1,0:T(8,128)S(1)} collective-permute-done((f32[128,384]{1,0:T(8,128)S(1)}, f32[128,384]{1,0:T(8,128)S(1)}, u32[]{:S(2)}, u32[]{:S(2)}) %collective-permute-start.13) | collective-permute-done | bytes 196640 | tf_op jit(solution)/shard_map/ppermute | solution.py:438
  65.5 2.9 %collective-permute-start.14 = (f32[128,384]{1,0:T(8,128)S(1)}, f32[128,384]{1,0:T(8,128)S(1)}, u32[]{:S(2)}, u32[]{:S(2)}) collective-permute-start(f32[128,384]{1,0:T(8,128)S(1)} %shard_map.57.v2.vectors), channel_id=1, source_target_pairs={{0,14},{1,13},{2,0},{3,15},{4,2},{5,1},{6,4},{7,3},{8,6},{9,5},{10... | collective-permute-start | bytes 589832 | tf_op jit(solution)/shard_map/ppermute | solution.py:434
  68.4 1.1 copy-done.2
  69.5 1.1 copy-done.4
  70.6 0.5 shard_map.59.product
  71.1 0.5 shard_map.58
  71.6 1.4 %shard_map.60 = (f32[56,128]{1,0:T(8,128)S(1)}, f32[56,128]{1,0:T(8,128)S(1)}) custom-call(f32[8,128]{1,0:T(8,128)S(1)} %broadcast_in_dim.19.core.refs_0_, f32[8,128]{1,0:T(8,128)S(1)} %broadcast_in_dim.23.relays, f32[320,64]{1,0:T(8,128)S(1)} %get-tuple-element.51.low, f32[128,384]{1,0:T(8,128)S(1)} %shard_map.57.v2.vectors, ...), custom_call_target="tpu_custom_call" | custom-call | flops 1000000000 | bytes 1000000 | tf_op jit(solution)/shard_map/pallas_call | solution.py:32
  73.0 0.6 collective-permute-start.15
  73.6 0.9 collective-permute-done.15
  74.5 2.3 %collective-permute-start.16 = (f32[56,128]{1,0:T(8,128)S(1)}, f32[56,128]{1,0:T(8,128)S(1)}, u32[]{:S(2)}, u32[]{:S(2)}) collective-permute-start(f32[56,128]{1,0:T(8,128)S(1)} %add.29), channel_id=1, source_target_pairs={{0,2},{2,0},{4,6},{6,4},{8,10},{10,8},{12,14},{14,12},{1,3},{3,1},... | collective-permute-start | bytes 86024 | tf_op jit(solution)/shard_map/ppermute | solution.py:445
  76.8 1.8 %collective-permute-done.16 = f32[56,128]{1,0:T(8,128)S(1)} collective-permute-done((f32[56,128]{1,0:T(8,128)S(1)}, f32[56,128]{1,0:T(8,128)S(1)}, u32[]{:S(2)}, u32[]{:S(2)}) %collective-permute-start.16) | collective-permute-done | bytes 28704 | tf_op jit(solution)/shard_map/ppermute | solution.py:445
  78.7 0.1 collective-permute-start.17
  78.8 3.8 %collective-permute-done.17 = f32[56,128]{1,0:T(8,128)S(1)} collective-permute-done((f32[56,128]{1,0:T(8,128)S(1)}, f32[56,128]{1,0:T(8,128)S(1)}, u32[]{:S(2)}, u32[]{:S(2)}) %collective-permute-start.17) | collective-permute-done | bytes 28704 | tf_op jit(solution)/shard_map/ppermute | solution.py:445
  82.6 1.8 %collective-permute-start.18 = (f32[56,128]{1,0:T(8,128)S(1)}, f32[56,128]{1,0:T(8,128)S(1)}, u32[]{:S(2)}, u32[]{:S(2)}) collective-permute-start(f32[56,128]{1,0:T(8,128)S(1)} %add.31), channel_id=1, source_target_pairs={{0,8},{2,10},{4,12},{6,14},{8,0},{10,2},{12,4},{14,6},{1,9},{3,11}... | collective-permute-start | bytes 86024 | tf_op jit(solution)/shard_map/ppermute | solution.py:445
  84.3 3.0 %collective-permute-done.18 = f32[56,128]{1,0:T(8,128)S(1)} collective-permute-done((f32[56,128]{1,0:T(8,128)S(1)}, f32[56,128]{1,0:T(8,128)S(1)}, u32[]{:S(2)}, u32[]{:S(2)}) %collective-permute-start.18) | collective-permute-done | bytes 28704 | tf_op jit(solution)/shard_map/ppermute | solution.py:445
  88.0 0.5 collective-permute-done.19.refs_3_
  88.5 18.6 %shard_map.61 = f32[64,384]{1,0:T(8,128)} custom-call(f32[8,128]{1,0:T(8,128)S(1)} %broadcast_in_dim.19.core.refs_0_, f32[8,128]{1,0:T(8,128)S(1)} %broadcast_in_dim.20.refs_1_, f32[56,128]{1,0:T(8,128)S(1)} %add.32.refs_2_, f32[56,128]{1,0:T(8,128)S(1)} %collective-permute-done.19.refs_3_, f32[192,384]{1,0:T(8,128)S(1)} %get-tuple-element.54.refs_4_), custom_call_target="tpu_custom_call" | custom-call | flops 20000000000 | bytes 1000000 | tf_op jit(solution)/shard_map/pallas_call | solution.py:32
  (33 shorter events, 0.4 us)
Async XLA Ops:
  0.0 8.2 %copy-start = (bf16[384,768]{1,0:T(8,128)(2,1)S(1)}, bf16[384,768]{1,0:T(8,128)(2,1)}, u32[]{:S(2)}) copy-start(bf16[384,768]{1,0:T(8,128)(2,1)} %own.1) | copy-start | bytes 1769476
  0.0 8.2 %collective-permute-start.2 = (bf16[384,768]{1,0:T(8,128)(2,1)}, bf16[384,768]{1,0:T(8,128)(2,1)S(1)}, u32[]{:S(2)}, u32[]{:S(2)}) collective-permute-start(bf16[384,768]{1,0:T(8,128)(2,1)} %own.1), channel_id=1, source_target_pairs={{0,1},{1,0},{2,3},{3,2},{4,5},{5,4},{6,7},{7,6},{8,9},{9,8},{10,11... | collective-permute-start | bytes 1769480 | tf_op jit(solution)/shard_map/ppermute | solution.py:438
  0.5 10.6 %collective-permute-start = (bf16[384,768]{1,0:T(8,128)(2,1)}, bf16[384,768]{1,0:T(8,128)(2,1)S(1)}, u32[]{:S(2)}, u32[]{:S(2)}) collective-permute-start(bf16[384,768]{1,0:T(8,128)(2,1)} %own.1), channel_id=1, source_target_pairs={{2,0},{6,4},{10,8},{14,12},{1,13},{3,15},{5,1},{7,3},{9,5},{11,7},... | collective-permute-start | bytes 1769480 | tf_op jit(solution)/shard_map/ppermute | solution.py:468
  3.9 4.3 %collective-permute-start.1 = (f32[64,384]{1,0:T(8,128)S(1)}, f32[64,384]{1,0:T(8,128)S(1)}, u32[]{:S(2)}, u32[]{:S(2)}) collective-permute-start(f32[64,384]{1,0:T(8,128)S(1)} %multiply_bitcast_fusion), channel_id=1, source_target_pairs={{0,1},{1,0},{2,3},{3,2},{4,5},{5,4},{6,7},{7,6},{8,9},{9,8},{10,11... | collective-permute-start | bytes 294920 | tf_op jit(solution)/shard_map/ppermute | solution.py:438
  10.1 47.3 %copy-start.1 = (bf16[768,384]{1,0:T(8,128)(2,1)}, bf16[768,384]{1,0:T(8,128)(2,1)S(1)}, u32[]{:S(2)}) copy-start(bf16[768,384]{1,0:T(8,128)(2,1)S(1)} %get-tuple-element.45.h0) | copy-start | bytes 1769476
  10.1 47.3 %copy-start.3 = (bf16[768,384]{1,0:T(8,128)(2,1)}, bf16[768,384]{1,0:T(8,128)(2,1)S(1)}, u32[]{:S(2)}) copy-start(bf16[768,384]{1,0:T(8,128)(2,1)S(1)} %get-tuple-element.46.l0) | copy-start | bytes 1769476
  11.1 11.1 %collective-permute-start.5 = (bf16[384,768]{1,0:T(8,128)(2,1)S(1)}, bf16[384,768]{1,0:T(8,128)(2,1)S(1)}, u32[]{:S(2)}, u32[]{:S(2)}) collective-permute-start(bf16[384,768]{1,0:T(8,128)(2,1)S(1)} %collective-permute-done.direct), channel_id=1, source_target_pairs={{1,2},{5,6},{9,10},{13,14},{17,18},{21,22},{25,26},{29,30}} | collective-permute-start | bytes 1769480 | tf_op jit(solution)/shard_map/ppermute | solution.py:468
  11.8 12.3 %collective-permute-start.4 = (bf16[384,768]{1,0:T(8,128)(2,1)S(1)}, bf16[384,768]{1,0:T(8,128)(2,1)S(1)}, u32[]{:S(2)}, u32[]{:S(2)}) collective-permute-start(bf16[384,768]{1,0:T(8,128)(2,1)S(1)} %collective-permute-done.direct), channel_id=1, source_target_pairs={{2,14},{6,2},{10,6},{14,10},{18,30},{22,18},{26,22},{30,26}} | collective-permute-start | bytes 1769480 | tf_op jit(solution)/shard_map/ppermute | solution.py:468
  12.5 15.9 %collective-permute-start.3 = (bf16[384,768]{1,0:T(8,128)(2,1)S(1)}, bf16[384,768]{1,0:T(8,128)(2,1)S(1)}, u32[]{:S(2)}, u32[]{:S(2)}) collective-permute-start(bf16[384,768]{1,0:T(8,128)(2,1)S(1)} %get-tuple-element.34.own), channel_id=1, source_target_pairs={{3,0},{7,4},{11,8},{15,12},{0,13},{2,15},{4,1},{6,3},{8,5},{10,7},... | collective-permute-start | bytes 1769480 | tf_op jit(solution)/shard_map/ppermute | solution.py:468
  30.3 7.0 %collective-permute-start.6 = (f32[16,384]{1,0:T(8,128)S(1)}, f32[16,384]{1,0:T(8,128)S(1)}, u32[]{:S(2)}, u32[]{:S(2)}) collective-permute-start(f32[16,384]{1,0:T(8,128)S(1)} %pad_maximum_fusion.1), channel_id=1, source_target_pairs={{0,2},{1,5},{2,4},{3,7},{4,6},{5,9},{6,8},{7,11},{8,10},{9,13},{10... | collective-permute-start | bytes 73736 | tf_op jit(solution)/shard_map/ppermute | solution.py:434
  37.3 1.2 %collective-permute-start.7 = (f32[16,384]{1,0:T(8,128)S(1)}, f32[16,384]{1,0:T(8,128)S(1)}, u32[]{:S(2)}, u32[]{:S(2)}) collective-permute-start(f32[16,384]{1,0:T(8,128)S(1)} %add.28.sums), channel_id=1, source_target_pairs={{0,1},{1,0},{2,3},{3,2},{4,5},{5,4},{6,7},{7,6},{8,9},{9,8},{10,11... | collective-permute-start | bytes 73736 | tf_op jit(solution)/shard_map/ppermute | solution.py:438
  39.1 9.8 %collective-permute-start.9 = (f32[128,384]{1,0:T(8,128)S(1)}, f32[128,384]{1,0:T(8,128)S(1)}, u32[]{:S(2)}, u32[]{:S(2)}) collective-permute-start(f32[128,384]{1,0:T(8,128)S(1)} %shard_map.51), channel_id=1, source_target_pairs={{0,2},{1,5},{2,4},{3,7},{4,6},{5,9},{6,8},{7,11},{8,10},{9,13},{10... | collective-permute-start | bytes 589832 | tf_op jit(solution)/shard_map/ppermute | solution.py:434
  42.1 7.6 %collective-permute-start.8 = (f32[128,384]{1,0:T(8,128)S(1)}, f32[128,384]{1,0:T(8,128)S(1)}, u32[]{:S(2)}, u32[]{:S(2)}) collective-permute-start(f32[128,384]{1,0:T(8,128)S(1)} %get-tuple-element.44.vectors.v0), channel_id=1, source_target_pairs={{0,14},{1,13},{2,0},{3,15},{4,2},{5,1},{6,4},{7,3},{8,6},{9,5},{10... | collective-permute-start | bytes 589832 | tf_op jit(solution)/shard_map/ppermute | solution.py:434
  50.6 1.5 %collective-permute-start.10 = (f32[128,384]{1,0:T(8,128)S(1)}, f32[128,384]{1,0:T(8,128)S(1)}, u32[]{:S(2)}, u32[]{:S(2)}) collective-permute-start(f32[128,384]{1,0:T(8,128)S(1)} %shard_map.52.total), channel_id=1, source_target_pairs={{0,1},{1,0},{2,3},{3,2},{4,5},{5,4},{6,7},{7,6},{8,9},{9,8},{10,11... | collective-permute-start | bytes 589832 | tf_op jit(solution)/shard_map/ppermute | solution.py:438
  52.6 10.6 %collective-permute-start.12 = (f32[128,384]{1,0:T(8,128)S(1)}, f32[128,384]{1,0:T(8,128)S(1)}, u32[]{:S(2)}, u32[]{:S(2)}) collective-permute-start(f32[128,384]{1,0:T(8,128)S(1)} %shard_map.55), channel_id=1, source_target_pairs={{0,2},{1,5},{2,4},{3,7},{4,6},{5,9},{6,8},{7,11},{8,10},{9,13},{10... | collective-permute-start | bytes 589832 | tf_op jit(solution)/shard_map/ppermute | solution.py:434
  53.9 9.3 %collective-permute-start.11 = (f32[128,384]{1,0:T(8,128)S(1)}, f32[128,384]{1,0:T(8,128)S(1)}, u32[]{:S(2)}, u32[]{:S(2)}) collective-permute-start(f32[128,384]{1,0:T(8,128)S(1)} %shard_map.53.vectors.v1), channel_id=1, source_target_pairs={{0,14},{1,13},{2,0},{3,15},{4,2},{5,1},{6,4},{7,3},{8,6},{9,5},{10... | collective-permute-start | bytes 589832 | tf_op jit(solution)/shard_map/ppermute | solution.py:434
  64.0 1.5 %collective-permute-start.13 = (f32[128,384]{1,0:T(8,128)S(1)}, f32[128,384]{1,0:T(8,128)S(1)}, u32[]{:S(2)}, u32[]{:S(2)}) collective-permute-start(f32[128,384]{1,0:T(8,128)S(1)} %shard_map.56.total), channel_id=1, source_target_pairs={{0,1},{1,0},{2,3},{3,2},{4,5},{5,4},{6,7},{7,6},{8,9},{9,8},{10,11... | collective-permute-start | bytes 589832 | tf_op jit(solution)/shard_map/ppermute | solution.py:438
  65.5 6.1 %collective-permute-start.14 = (f32[128,384]{1,0:T(8,128)S(1)}, f32[128,384]{1,0:T(8,128)S(1)}, u32[]{:S(2)}, u32[]{:S(2)}) collective-permute-start(f32[128,384]{1,0:T(8,128)S(1)} %shard_map.57.v2.vectors), channel_id=1, source_target_pairs={{0,14},{1,13},{2,0},{3,15},{4,2},{5,1},{6,4},{7,3},{8,6},{9,5},{10... | collective-permute-start | bytes 589832 | tf_op jit(solution)/shard_map/ppermute | solution.py:434
  68.4 1.1 copy-start.2
  69.5 1.1 copy-start.4
  73.0 1.5 %collective-permute-start.15 = (f32[56,128]{1,0:T(8,128)S(1)}, f32[56,128]{1,0:T(8,128)S(1)}, u32[]{:S(2)}, u32[]{:S(2)}) collective-permute-start(f32[56,128]{1,0:T(8,128)S(1)} %get-tuple-element.53), channel_id=1, source_target_pairs={{0,1},{1,0},{2,3},{3,2},{4,5},{5,4},{6,7},{7,6},{8,9},{9,8},{10,11... | collective-permute-start | bytes 86024 | tf_op jit(solution)/shard_map/ppermute | solution.py:438
  74.5 4.2 %collective-permute-start.16 = (f32[56,128]{1,0:T(8,128)S(1)}, f32[56,128]{1,0:T(8,128)S(1)}, u32[]{:S(2)}, u32[]{:S(2)}) collective-permute-start(f32[56,128]{1,0:T(8,128)S(1)} %add.29), channel_id=1, source_target_pairs={{0,2},{2,0},{4,6},{6,4},{8,10},{10,8},{12,14},{14,12},{1,3},{3,1},... | collective-permute-start | bytes 86024 | tf_op jit(solution)/shard_map/ppermute | solution.py:445
  78.7 3.9 %collective-permute-start.17 = (f32[56,128]{1,0:T(8,128)S(1)}, f32[56,128]{1,0:T(8,128)S(1)}, u32[]{:S(2)}, u32[]{:S(2)}) collective-permute-start(f32[56,128]{1,0:T(8,128)S(1)} %add.30), channel_id=1, source_target_pairs={{0,4},{2,6},{4,0},{6,2},{8,12},{10,14},{12,8},{14,10},{1,5},{3,7},... | collective-permute-start | bytes 86024 | tf_op jit(solution)/shard_map/ppermute | solution.py:445
  82.6 4.8 %collective-permute-start.18 = (f32[56,128]{1,0:T(8,128)S(1)}, f32[56,128]{1,0:T(8,128)S(1)}, u32[]{:S(2)}, u32[]{:S(2)}) collective-permute-start(f32[56,128]{1,0:T(8,128)S(1)} %add.31), channel_id=1, source_target_pairs={{0,8},{2,10},{4,12},{6,14},{8,0},{10,2},{12,4},{14,6},{1,9},{3,11}... | collective-permute-start | bytes 86024 | tf_op jit(solution)/shard_map/ppermute | solution.py:445
  87.3 1.2 %collective-permute-start.19 = (f32[56,128]{1,0:T(8,128)S(1)}, f32[56,128]{1,0:T(8,128)S(1)}, u32[]{:S(2)}, u32[]{:S(2)}) collective-permute-start(f32[56,128]{1,0:T(8,128)S(1)} %add.32.refs_2_), channel_id=1, source_target_pairs={{0,1},{1,0},{2,3},{3,2},{4,5},{5,4},{6,7},{7,6},{8,9},{9,8},{10,11... | collective-permute-start | bytes 86024 | tf_op jit(solution)/shard_map/ppermute | solution.py:438

commit v11 on v10

--- a/solution.py
+++ b/solution.py
@@ -165,8 +165,12 @@
     return product_rows(first, h1, l1) + product_rows(second, h2, l2)
 
 
-def block_body(relays, product, near, behind, h1, l1, h2, l2, total):
-    total[...] = product[...] + behind[...] + stacked(far_product(relays, near, h1, l1, h2, l2))
+def near_product_body(relays, product, near, h1, l1, h2, l2, total):
+    total[...] = product[...] + stacked(far_product(relays, near, h1, l1, h2, l2))
+
+
+def add_body(total, behind, out):
+    out[...] = total[...] + behind[...]
 
 
 def low_body(degree, v0, v1, v2, moments, scaled):
@@ -467,7 +471,7 @@
     def between_shards(shard, pairs):
         return lax.ppermute(shard, ("blk", "narrow"), pairs)
 
-    first = between_shards(embeddings, orders[0])
+    first, second = between_shards(embeddings, orders[0]), between_shards(embeddings, orders[1])
     seed = start_seed.astype(F32).T / 1000.0
     seeds = jnp.concatenate([seed, between_cores(seed)], axis=0)
     keep = spread(lax.dynamic_slice(pair_mask, (where, core), (1, 1)))
@@ -476,11 +480,11 @@
     h0, l0, sums, row_sq, own_copy, token = make_tile(
         own_body, [embeddings, other_emb], size,
         (((2 * size, 128), F32), (embeddings.shape, BF16), ((8, 128), F32)))
-    first, seeds, keep, relays, token = lax.optimization_barrier((first, seeds, keep, relays, token))
+    first, second, seeds, keep, relays, token = lax.optimization_barrier(
+        (first, second, seeds, keep, relays, token))
     relayed = [first, own_copy]
     if relaying:
         relayed[1] = between_shards(first, [(2 * i, (i - 2) % blocks * 2) for i in range(1, blocks, 2)])
-    second = between_shards(own_copy, orders[1])
     if relaying:
         relayed[0] = between_shards(first, [(2 * i + 1, 2 * i + 2) for i in range(0, blocks, 2)])
     tile_args = [keep, relays, token, own_copy, other_emb, row_sq]
@@ -502,7 +506,8 @@
         (ahead,) = call(ahead_body, [pair_shape], [relays, vectors, *far], **middle)
         behind = between_blocks(ahead, 1)
         (product,) = call(own_product_body, [pair_shape], [vectors, h0, l0], **middle)
-        (total,) = call(block_body, [pair_shape], [relays, product, near, behind, *far], **middle)
+        (total,) = call(near_product_body, [pair_shape], [relays, product, near, *far], **middle)
+        (total,) = call(add_body, [pair_shape], [total, behind], **small)
         (vectors,) = call(combine_body, [pair_shape], [total, between_cores(total), degree], **small)
         history.append(vectors)
     near = between_blocks(vectors, -1)

time: 107 us -> 108 us (level)
  waiting for transfers between devices: 31.8 us -> 40.2 us
  starting transfers between devices: 37.9 us -> 30.6 us
    ppermute x6, waiting for transfers between devices: 12.4 us -> 19 us  [between_blocks(): return lax.ppermute(shard, ('blk', 'narrow'), pairs)]
    ppermute x4, starting transfers between devices: 12.4 us -> 8.16 us  [between_shards(): return lax.ppermute(shard, ('blk', 'narrow'), pairs)]
    ppermute x7, starting transfers between devices: 3.57 us -> 1.09 us  [between_cores(): return lax.ppermute(shard, 'narrow', [(0, 1), (1, 0)])]
    ppermute x4, waiting for transfers between devices: 5.23 us -> 6.55 us  [between_shards(): return lax.ppermute(shard, ('blk', 'narrow'), pairs)]
    pallas_call x16 -> x18, Pallas kernels: 30.4 us -> 30.5 us  [call(): pl.pallas_call(body, out_shape=[jax.ShapeDtypeStruct(shape, dtype) for sh...]
  transfers between devices with their start and end apart: 20 -> 20, of which waited for: 15 -> 16; matrix products, arithmetic and copies ran while one was open for 3% -> 3% of each run, Pallas kernels for 5% -> 8%
where the time goes in v11:
time: 108 us; the launch traced here: 107 us
  waiting for transfers between devices  40.2 us (37%)
  starting transfers between devices  30.6 us (28%)
  Pallas kernels  30.5 us (28%)
  local copies, waits for them, and re-layouts  2.87 us (3%)
  between operations  2.2 us (2%)
    pallas_call x18, Pallas kernels, call(): pl.pallas_call(body, out_shape=[jax.ShapeDtypeStruct(shape, dtype) for sh...  30.5 us
    ppermute x6, waiting for transfers between devices, between_blocks(): return lax.ppermute(shard, ('blk', 'narrow'), pairs)  19 us
    ppermute x6, starting transfers between devices, between_blocks(): return lax.ppermute(shard, ('blk', 'narrow'), pairs)  17.1 us
    ppermute x3, waiting for transfers between devices, total_over_blocks(): lax.ppermute(values, 'blk', [(i, i ^ span) for i in range(blocks)])  9.22 us
    ppermute x4, starting transfers between devices, between_shards(): return lax.ppermute(shard, ('blk', 'narrow'), pairs)  8.16 us
    ppermute x4, waiting for transfers between devices, between_shards(): return lax.ppermute(shard, ('blk', 'narrow'), pairs)  6.55 us
    ppermute x7, waiting for transfers between devices, between_cores(): return lax.ppermute(shard, 'narrow', [(0, 1), (1, 0)])  5.45 us
    ppermute x3, starting transfers between devices, total_over_blocks(): lax.ppermute(values, 'blk', [(i, i ^ span) for i in range(blocks)])  4.24 us
  transfers between devices with their start and end apart: 20, of which 16 were waited for; matrix products, arithmetic and copies ran while one was open for 3% of the time, Pallas kernels for 8%

profile of v11, /device:TPU:0, one launch (start us, length us, event | category | flops | bytes accessed | tf_op | source)
XLA Modules:
  0.0 107.4 jit_solution(11494621120607319117)
XLA Ops:
  0.0 0.5 collective-permute-start.3
  0.5 2.5 %collective-permute-start = (bf16[384,768]{1,0:T(8,128)(2,1)}, bf16[384,768]{1,0:T(8,128)(2,1)S(1)}, u32[]{:S(2)}, u32[]{:S(2)}) collective-permute-start(bf16[384,768]{1,0:T(8,128)(2,1)} %own.1), channel_id=1, source_target_pairs={{2,0},{6,4},{10,8},{14,12},{1,13},{3,15},{5,1},{7,3},{9,5},{11,7},... | collective-permute-start | bytes 1769480 | tf_op jit(solution)/shard_map/ppermute | solution.py:472
  3.0 4.2 %collective-permute-start.1 = (bf16[384,768]{1,0:T(8,128)(2,1)}, bf16[384,768]{1,0:T(8,128)(2,1)S(1)}, u32[]{:S(2)}, u32[]{:S(2)}) collective-permute-start(bf16[384,768]{1,0:T(8,128)(2,1)} %own.1), channel_id=1, source_target_pairs={{3,0},{7,4},{11,8},{15,12},{0,13},{2,15},{4,1},{6,3},{8,5},{10,7},... | collective-permute-start | bytes 1769480 | tf_op jit(solution)/shard_map/ppermute | solution.py:472
  7.2 0.9 multiply_bitcast_fusion
  8.1 0.1 collective-permute-start.2
  8.2 1.3 %dynamic_slice.3 = s32[1,1]{0,1:T(1,128)} dynamic-slice(s32[8,2]{0,1:T(2,128)} %param.5, s32[]{:T(128)S(6)} %select_n.25, s32[]{:T(128)S(6)} %select_n.26), dynamic_slice_sizes={1,1} | dynamic-slice | bytes 12 | tf_op jit(solution)/shard_map/dynamic_slice | solution.py:477
  10.2 1.9 %shard_map.46 = (bf16[768,384]{1,0:T(8,128)(2,1)S(1)}, bf16[768,384]{1,0:T(8,128)(2,1)S(1)}, f32[16,384]{1,0:T(8,128)S(1)}, f32[768,128]{1,0:T(8,128)S(1)}, bf16...) custom-call(bf16[384,768]{1,0:T(8,128)(2,1)S(1)} %copy-done, bf16[384,768]{1,0:T(8,128)(2,1)S(1)} %collective-permute-done.3.other), custom_call_target="tpu_custom_call" | custom-call | flops 2000000000 | bytes 1000000 | tf_op jit(solution)/shard_map/pallas_call | solution.py:32
  12.1 0.3 collective-permute-done.direct
  12.4 6.3 %collective-permute-done.1.direct = bf16[384,768]{1,0:T(8,128)(2,1)S(1)} collective-permute-done((bf16[384,768]{1,0:T(8,128)(2,1)}, bf16[384,768]{1,0:T(8,128)(2,1)S(1)}, u32[]{:S(2)}, u32[]{:S(2)}) %collective-permute-start.1) | collective-permute-done | bytes 589856 | tf_op jit(solution)/shard_map/ppermute | solution.py:472
  18.6 0.7 collective-permute-start.5
  19.3 0.7 collective-permute-start.4
  20.0 0.5 slice.4
  21.2 2.0 %shard_map.47 = (bf16[768,384]{1,0:T(8,128)(2,1)S(1)}, bf16[768,384]{1,0:T(8,128)(2,1)S(1)}, f32[16,384]{1,0:T(8,128)S(1)}, f32[8,384]{1,0:T(8,128)S(1)}) custom-call(f32[8,128]{1,0:T(8,128)S(1)} %broadcast_in_dim.22.keep, f32[8,128]{1,0:T(8,128)S(1)} %broadcast_in_dim.23.relays, f32[8,128]{1,0:T(8,128)S(1)} %get-tuple-element.34.token, ...), custom_call_target="tpu_custom_call" | custom-call | flops 2000000000 | bytes 1000000 | tf_op jit(solution)/shard_map/pallas_call | solution.py:32
  23.2 2.0 %shard_map.48 = (bf16[768,384]{1,0:T(8,128)(2,1)S(1)}, bf16[768,384]{1,0:T(8,128)(2,1)S(1)}, f32[16,384]{1,0:T(8,128)S(1)}, f32[8,384]{1,0:T(8,128)S(1)}) custom-call(f32[8,128]{1,0:T(8,128)S(1)} %broadcast_in_dim.22.keep, f32[8,128]{1,0:T(8,128)S(1)} %broadcast_in_dim.23.relays, f32[8,128]{1,0:T(8,128)S(1)} %get-tuple-element.34.token, ...), custom_call_target="tpu_custom_call" | custom-call | flops 2000000000 | bytes 1000000 | tf_op jit(solution)/shard_map/pallas_call | solution.py:32
  25.2 10.3 %collective-permute-start.6 = (f32[16,384]{1,0:T(8,128)S(1)}, f32[16,384]{1,0:T(8,128)S(1)}, u32[]{:S(2)}, u32[]{:S(2)}) collective-permute-start(f32[16,384]{1,0:T(8,128)S(1)} %pad_maximum_fusion.1), channel_id=1, source_target_pairs={{0,2},{1,5},{2,4},{3,7},{4,6},{5,9},{6,8},{7,11},{8,10},{9,13},{10... | collective-permute-start | bytes 73736 | tf_op jit(solution)/shard_map/ppermute | solution.py:438
  35.5 3.6 %collective-permute-done.6 = f32[16,384]{1,0:T(8,128)S(1)} collective-permute-done((f32[16,384]{1,0:T(8,128)S(1)}, f32[16,384]{1,0:T(8,128)S(1)}, u32[]{:S(2)}, u32[]{:S(2)}) %collective-permute-start.6) | collective-permute-done | bytes 24608 | tf_op jit(solution)/shard_map/ppermute | solution.py:438
  39.1 1.2 %collective-permute-done.7.other_sums = f32[16,384]{1,0:T(8,128)S(1)} collective-permute-done((f32[16,384]{1,0:T(8,128)S(1)}, f32[16,384]{1,0:T(8,128)S(1)}, u32[]{:S(2)}, u32[]{:S(2)}) %collective-permute-start.7) | collective-permute-done | bytes 24608 | tf_op jit(solution)/shard_map/ppermute | solution.py:442
  40.4 2.1 %collective-permute-start.8 = (f32[128,384]{1,0:T(8,128)S(1)}, f32[128,384]{1,0:T(8,128)S(1)}, u32[]{:S(2)}, u32[]{:S(2)}) collective-permute-start(f32[128,384]{1,0:T(8,128)S(1)} %get-tuple-element.46.vectors.v0), channel_id=1, source_target_pairs={{0,14},{1,13},{2,0},{3,15},{4,2},{5,1},{6,4},{7,3},{8,6},{9,5},{10... | collective-permute-start | bytes 589832 | tf_op jit(solution)/shard_map/ppermute | solution.py:438
  42.4 0.5 shard_map.52
  43.0 0.5 shard_map.50.product
  43.5 3.8 %collective-permute-done.8.near = f32[128,384]{1,0:T(8,128)S(1)} collective-permute-done((f32[128,384]{1,0:T(8,128)S(1)}, f32[128,384]{1,0:T(8,128)S(1)}, u32[]{:S(2)}, u32[]{:S(2)}) %collective-permute-start.8) | collective-permute-done | bytes 196640 | tf_op jit(solution)/shard_map/ppermute | solution.py:438
  47.3 0.8 shard_map.51.total
  48.1 3.4 %collective-permute-done.9.behind = f32[128,384]{1,0:T(8,128)S(1)} collective-permute-done((f32[128,384]{1,0:T(8,128)S(1)}, f32[128,384]{1,0:T(8,128)S(1)}, u32[]{:S(2)}, u32[]{:S(2)}) %collective-permute-start.9) | collective-permute-done | bytes 196640 | tf_op jit(solution)/shard_map/ppermute | solution.py:438
  51.6 1.4 %collective-permute-done.10.other_total = f32[128,384]{1,0:T(8,128)S(1)} collective-permute-done((f32[128,384]{1,0:T(8,128)S(1)}, f32[128,384]{1,0:T(8,128)S(1)}, u32[]{:S(2)}, u32[]{:S(2)}) %collective-permute-start.10) | collective-permute-done | bytes 196640 | tf_op jit(solution)/shard_map/ppermute | solution.py:442
  53.1 1.9 %collective-permute-start.11 = (f32[128,384]{1,0:T(8,128)S(1)}, f32[128,384]{1,0:T(8,128)S(1)}, u32[]{:S(2)}, u32[]{:S(2)}) collective-permute-start(f32[128,384]{1,0:T(8,128)S(1)} %shard_map.54.vectors.v1), channel_id=1, source_target_pairs={{0,14},{1,13},{2,0},{3,15},{4,2},{5,1},{6,4},{7,3},{8,6},{9,5},{10... | collective-permute-start | bytes 589832 | tf_op jit(solution)/shard_map/ppermute | solution.py:438
  54.9 0.5 shard_map.57
  55.4 0.3 collective-permute-start.12
  55.7 0.5 shard_map.55.product
  56.2 4.1 %collective-permute-done.11.near = f32[128,384]{1,0:T(8,128)S(1)} collective-permute-done((f32[128,384]{1,0:T(8,128)S(1)}, f32[128,384]{1,0:T(8,128)S(1)}, u32[]{:S(2)}, u32[]{:S(2)}) %collective-permute-start.11) | collective-permute-done | bytes 196640 | tf_op jit(solution)/shard_map/ppermute | solution.py:438
  60.3 0.8 shard_map.56.total
  61.1 2.9 %collective-permute-done.12.behind = f32[128,384]{1,0:T(8,128)S(1)} collective-permute-done((f32[128,384]{1,0:T(8,128)S(1)}, f32[128,384]{1,0:T(8,128)S(1)}, u32[]{:S(2)}, u32[]{:S(2)}) %collective-permute-start.12) | collective-permute-done | bytes 196640 | tf_op jit(solution)/shard_map/ppermute | solution.py:438
  64.1 1.4 %collective-permute-done.13.other_total = f32[128,384]{1,0:T(8,128)S(1)} collective-permute-done((f32[128,384]{1,0:T(8,128)S(1)}, f32[128,384]{1,0:T(8,128)S(1)}, u32[]{:S(2)}, u32[]{:S(2)}) %collective-permute-start.13) | collective-permute-done | bytes 196640 | tf_op jit(solution)/shard_map/ppermute | solution.py:442
  65.5 2.6 %collective-permute-start.14 = (f32[128,384]{1,0:T(8,128)S(1)}, f32[128,384]{1,0:T(8,128)S(1)}, u32[]{:S(2)}, u32[]{:S(2)}) collective-permute-start(f32[128,384]{1,0:T(8,128)S(1)} %shard_map.59.v2.vectors), channel_id=1, source_target_pairs={{0,14},{1,13},{2,0},{3,15},{4,2},{5,1},{6,4},{7,3},{8,6},{9,5},{10... | collective-permute-start | bytes 589832 | tf_op jit(solution)/shard_map/ppermute | solution.py:438
  68.1 1.1 copy-done.6
  69.2 0.5 shard_map.61.product
  69.7 0.5 shard_map.60
  70.2 1.2 %collective-permute-done.14.near = f32[128,384]{1,0:T(8,128)S(1)} collective-permute-done((f32[128,384]{1,0:T(8,128)S(1)}, f32[128,384]{1,0:T(8,128)S(1)}, u32[]{:S(2)}, u32[]{:S(2)}) %collective-permute-start.14) | collective-permute-done | bytes 196640 | tf_op jit(solution)/shard_map/ppermute | solution.py:438
  71.4 1.4 %shard_map.62 = (f32[56,128]{1,0:T(8,128)S(1)}, f32[56,128]{1,0:T(8,128)S(1)}) custom-call(f32[8,128]{1,0:T(8,128)S(1)} %broadcast_in_dim.19.core.refs_0_, f32[8,128]{1,0:T(8,128)S(1)} %broadcast_in_dim.23.relays, f32[320,64]{1,0:T(8,128)S(1)} %get-tuple-element.53.low, f32[128,384]{1,0:T(8,128)S(1)} %shard_map.59.v2.vectors, ...), custom_call_target="tpu_custom_call" | custom-call | flops 1000000000 | bytes 1000000 | tf_op jit(solution)/shard_map/pallas_call | solution.py:32
  72.8 0.4 collective-permute-start.15
  73.2 0.9 collective-permute-done.15
  74.1 2.7 %collective-permute-start.16 = (f32[56,128]{1,0:T(8,128)S(1)}, f32[56,128]{1,0:T(8,128)S(1)}, u32[]{:S(2)}, u32[]{:S(2)}) collective-permute-start(f32[56,128]{1,0:T(8,128)S(1)} %add.29), channel_id=1, source_target_pairs={{0,2},{2,0},{4,6},{6,4},{8,10},{10,8},{12,14},{14,12},{1,3},{3,1},... | collective-permute-start | bytes 86024 | tf_op jit(solution)/shard_map/ppermute | solution.py:449
  76.8 1.8 %collective-permute-done.16 = f32[56,128]{1,0:T(8,128)S(1)} collective-permute-done((f32[56,128]{1,0:T(8,128)S(1)}, f32[56,128]{1,0:T(8,128)S(1)}, u32[]{:S(2)}, u32[]{:S(2)}) %collective-permute-start.16) | collective-permute-done | bytes 28704 | tf_op jit(solution)/shard_map/ppermute | solution.py:449
  78.7 0.1 collective-permute-start.17
  78.8 3.8 %collective-permute-done.17 = f32[56,128]{1,0:T(8,128)S(1)} collective-permute-done((f32[56,128]{1,0:T(8,128)S(1)}, f32[56,128]{1,0:T(8,128)S(1)}, u32[]{:S(2)}, u32[]{:S(2)}) %collective-permute-start.17) | collective-permute-done | bytes 28704 | tf_op jit(solution)/shard_map/ppermute | solution.py:449
  82.6 1.4 %collective-permute-start.18 = (f32[56,128]{1,0:T(8,128)S(1)}, f32[56,128]{1,0:T(8,128)S(1)}, u32[]{:S(2)}, u32[]{:S(2)}) collective-permute-start(f32[56,128]{1,0:T(8,128)S(1)} %add.31), channel_id=1, source_target_pairs={{0,8},{2,10},{4,12},{6,14},{8,0},{10,2},{12,4},{14,6},{1,9},{3,11}... | collective-permute-start | bytes 86024 | tf_op jit(solution)/shard_map/ppermute | solution.py:449
  84.0 3.6 %collective-permute-done.18 = f32[56,128]{1,0:T(8,128)S(1)} collective-permute-done((f32[56,128]{1,0:T(8,128)S(1)}, f32[56,128]{1,0:T(8,128)S(1)}, u32[]{:S(2)}, u32[]{:S(2)}) %collective-permute-start.18) | collective-permute-done | bytes 28704 | tf_op jit(solution)/shard_map/ppermute | solution.py:449
  88.2 0.5 collective-permute-done.19.refs_3_
  88.8 18.6 %shard_map.63 = f32[64,384]{1,0:T(8,128)} custom-call(f32[8,128]{1,0:T(8,128)S(1)} %broadcast_in_dim.19.core.refs_0_, f32[8,128]{1,0:T(8,128)S(1)} %broadcast_in_dim.20.refs_1_, f32[56,128]{1,0:T(8,128)S(1)} %add.32.refs_2_, f32[56,128]{1,0:T(8,128)S(1)} %collective-permute-done.19.refs_3_, f32[192,384]{1,0:T(8,128)S(1)} %get-tuple-element.56.refs_4_), custom_call_target="tpu_custom_call" | custom-call | flops 20000000000 | bytes 1000000 | tf_op jit(solution)/shard_map/pallas_call | solution.py:32
  (39 shorter events, 0.4 us)
Async XLA Ops:
  0.0 10.2 %copy-start = (bf16[384,768]{1,0:T(8,128)(2,1)S(1)}, bf16[384,768]{1,0:T(8,128)(2,1)}, u32[]{:S(2)}) copy-start(bf16[384,768]{1,0:T(8,128)(2,1)} %own.1) | copy-start | bytes 1769476
  0.0 10.2 %collective-permute-start.3 = (bf16[384,768]{1,0:T(8,128)(2,1)}, bf16[384,768]{1,0:T(8,128)(2,1)S(1)}, u32[]{:S(2)}, u32[]{:S(2)}) collective-permute-start(bf16[384,768]{1,0:T(8,128)(2,1)} %own.1), channel_id=1, source_target_pairs={{0,1},{1,0},{2,3},{3,2},{4,5},{5,4},{6,7},{7,6},{8,9},{9,8},{10,11... | collective-permute-start | bytes 1769480 | tf_op jit(solution)/shard_map/ppermute | solution.py:442
  0.5 11.9 %collective-permute-start = (bf16[384,768]{1,0:T(8,128)(2,1)}, bf16[384,768]{1,0:T(8,128)(2,1)S(1)}, u32[]{:S(2)}, u32[]{:S(2)}) collective-permute-start(bf16[384,768]{1,0:T(8,128)(2,1)} %own.1), channel_id=1, source_target_pairs={{2,0},{6,4},{10,8},{14,12},{1,13},{3,15},{5,1},{7,3},{9,5},{11,7},... | collective-permute-start | bytes 1769480 | tf_op jit(solution)/shard_map/ppermute | solution.py:472
  3.0 15.6 %collective-permute-start.1 = (bf16[384,768]{1,0:T(8,128)(2,1)}, bf16[384,768]{1,0:T(8,128)(2,1)S(1)}, u32[]{:S(2)}, u32[]{:S(2)}) collective-permute-start(bf16[384,768]{1,0:T(8,128)(2,1)} %own.1), channel_id=1, source_target_pairs={{3,0},{7,4},{11,8},{15,12},{0,13},{2,15},{4,1},{6,3},{8,5},{10,7},... | collective-permute-start | bytes 1769480 | tf_op jit(solution)/shard_map/ppermute | solution.py:472
  8.1 2.0 %collective-permute-start.2 = (f32[64,384]{1,0:T(8,128)S(1)}, f32[64,384]{1,0:T(8,128)S(1)}, u32[]{:S(2)}, u32[]{:S(2)}) collective-permute-start(f32[64,384]{1,0:T(8,128)S(1)} %multiply_bitcast_fusion), channel_id=1, source_target_pairs={{0,1},{1,0},{2,3},{3,2},{4,5},{5,4},{6,7},{7,6},{8,9},{9,8},{10,11... | collective-permute-start | bytes 294920 | tf_op jit(solution)/shard_map/ppermute | solution.py:442
  12.1 43.6 %copy-start.3 = (bf16[768,384]{1,0:T(8,128)(2,1)}, bf16[768,384]{1,0:T(8,128)(2,1)S(1)}, u32[]{:S(2)}) copy-start(bf16[768,384]{1,0:T(8,128)(2,1)S(1)} %get-tuple-element.47.h0) | copy-start | bytes 1769476
  12.1 43.6 %copy-start.5 = (bf16[768,384]{1,0:T(8,128)(2,1)}, bf16[768,384]{1,0:T(8,128)(2,1)S(1)}, u32[]{:S(2)}) copy-start(bf16[768,384]{1,0:T(8,128)(2,1)S(1)} %get-tuple-element.48.l0) | copy-start | bytes 1769476
  18.6 2.6 %collective-permute-start.5 = (bf16[384,768]{1,0:T(8,128)(2,1)S(1)}, bf16[384,768]{1,0:T(8,128)(2,1)S(1)}, u32[]{:S(2)}, u32[]{:S(2)}) collective-permute-start(bf16[384,768]{1,0:T(8,128)(2,1)S(1)} %collective-permute-done.direct), channel_id=1, source_target_pairs={{1,2},{5,6},{9,10},{13,14},{17,18},{21,22},{25,26},{29,30}} | collective-permute-start | bytes 1769480 | tf_op jit(solution)/shard_map/ppermute | solution.py:472
  19.3 3.9 %collective-permute-start.4 = (bf16[384,768]{1,0:T(8,128)(2,1)S(1)}, bf16[384,768]{1,0:T(8,128)(2,1)S(1)}, u32[]{:S(2)}, u32[]{:S(2)}) collective-permute-start(bf16[384,768]{1,0:T(8,128)(2,1)S(1)} %collective-permute-done.direct), channel_id=1, source_target_pairs={{2,14},{6,2},{10,6},{14,10},{18,30},{22,18},{26,22},{30,26}} | collective-permute-start | bytes 1769480 | tf_op jit(solution)/shard_map/ppermute | solution.py:472
  25.2 35.1 %copy-start.1 = (bf16[768,384]{1,0:T(8,128)(2,1)}, bf16[768,384]{1,0:T(8,128)(2,1)S(1)}, u32[]{:S(2)}) copy-start(bf16[768,384]{1,0:T(8,128)(2,1)S(1)} %get-tuple-element.52.l2) | copy-start | bytes 1769476
  25.2 13.9 %collective-permute-start.6 = (f32[16,384]{1,0:T(8,128)S(1)}, f32[16,384]{1,0:T(8,128)S(1)}, u32[]{:S(2)}, u32[]{:S(2)}) collective-permute-start(f32[16,384]{1,0:T(8,128)S(1)} %pad_maximum_fusion.1), channel_id=1, source_target_pairs={{0,2},{1,5},{2,4},{3,7},{4,6},{5,9},{6,8},{7,11},{8,10},{9,13},{10... | collective-permute-start | bytes 73736 | tf_op jit(solution)/shard_map/ppermute | solution.py:438
  39.1 1.2 %collective-permute-start.7 = (f32[16,384]{1,0:T(8,128)S(1)}, f32[16,384]{1,0:T(8,128)S(1)}, u32[]{:S(2)}, u32[]{:S(2)}) collective-permute-start(f32[16,384]{1,0:T(8,128)S(1)} %add.28.sums), channel_id=1, source_target_pairs={{0,1},{1,0},{2,3},{3,2},{4,5},{5,4},{6,7},{7,6},{8,9},{9,8},{10,11... | collective-permute-start | bytes 73736 | tf_op jit(solution)/shard_map/ppermute | solution.py:442
  40.4 6.9 %collective-permute-start.8 = (f32[128,384]{1,0:T(8,128)S(1)}, f32[128,384]{1,0:T(8,128)S(1)}, u32[]{:S(2)}, u32[]{:S(2)}) collective-permute-start(f32[128,384]{1,0:T(8,128)S(1)} %get-tuple-element.46.vectors.v0), channel_id=1, source_target_pairs={{0,14},{1,13},{2,0},{3,15},{4,2},{5,1},{6,4},{7,3},{8,6},{9,5},{10... | collective-permute-start | bytes 589832 | tf_op jit(solution)/shard_map/ppermute | solution.py:438
  43.0 8.5 %collective-permute-start.9 = (f32[128,384]{1,0:T(8,128)S(1)}, f32[128,384]{1,0:T(8,128)S(1)}, u32[]{:S(2)}, u32[]{:S(2)}) collective-permute-start(f32[128,384]{1,0:T(8,128)S(1)} %shard_map.52), channel_id=1, source_target_pairs={{0,2},{1,5},{2,4},{3,7},{4,6},{5,9},{6,8},{7,11},{8,10},{9,13},{10... | collective-permute-start | bytes 589832 | tf_op jit(solution)/shard_map/ppermute | solution.py:438
  51.5 1.5 %collective-permute-start.10 = (f32[128,384]{1,0:T(8,128)S(1)}, f32[128,384]{1,0:T(8,128)S(1)}, u32[]{:S(2)}, u32[]{:S(2)}) collective-permute-start(f32[128,384]{1,0:T(8,128)S(1)} %shard_map.53.total), channel_id=1, source_target_pairs={{0,1},{1,0},{2,3},{3,2},{4,5},{5,4},{6,7},{7,6},{8,9},{9,8},{10,11... | collective-permute-start | bytes 589832 | tf_op jit(solution)/shard_map/ppermute | solution.py:442
  53.1 7.2 %collective-permute-start.11 = (f32[128,384]{1,0:T(8,128)S(1)}, f32[128,384]{1,0:T(8,128)S(1)}, u32[]{:S(2)}, u32[]{:S(2)}) collective-permute-start(f32[128,384]{1,0:T(8,128)S(1)} %shard_map.54.vectors.v1), channel_id=1, source_target_pairs={{0,14},{1,13},{2,0},{3,15},{4,2},{5,1},{6,4},{7,3},{8,6},{9,5},{10... | collective-permute-start | bytes 589832 | tf_op jit(solution)/shard_map/ppermute | solution.py:438
  55.4 8.5 %collective-permute-start.12 = (f32[128,384]{1,0:T(8,128)S(1)}, f32[128,384]{1,0:T(8,128)S(1)}, u32[]{:S(2)}, u32[]{:S(2)}) collective-permute-start(f32[128,384]{1,0:T(8,128)S(1)} %shard_map.57), channel_id=1, source_target_pairs={{0,2},{1,5},{2,4},{3,7},{4,6},{5,9},{6,8},{7,11},{8,10},{9,13},{10... | collective-permute-start | bytes 589832 | tf_op jit(solution)/shard_map/ppermute | solution.py:438
  61.1 7.0 %copy-start.4 = (bf16[768,384]{1,0:T(8,128)(2,1)S(1)}, bf16[768,384]{1,0:T(8,128)(2,1)}, u32[]{:S(2)}) copy-start(bf16[768,384]{1,0:T(8,128)(2,1)} %copy-done.3) | copy-start | bytes 1769476
  64.0 1.5 %collective-permute-start.13 = (f32[128,384]{1,0:T(8,128)S(1)}, f32[128,384]{1,0:T(8,128)S(1)}, u32[]{:S(2)}, u32[]{:S(2)}) collective-permute-start(f32[128,384]{1,0:T(8,128)S(1)} %shard_map.58.total), channel_id=1, source_target_pairs={{0,1},{1,0},{2,3},{3,2},{4,5},{5,4},{6,7},{7,6},{8,9},{9,8},{10,11... | collective-permute-start | bytes 589832 | tf_op jit(solution)/shard_map/ppermute | solution.py:442
  65.5 5.9 %collective-permute-start.14 = (f32[128,384]{1,0:T(8,128)S(1)}, f32[128,384]{1,0:T(8,128)S(1)}, u32[]{:S(2)}, u32[]{:S(2)}) collective-permute-start(f32[128,384]{1,0:T(8,128)S(1)} %shard_map.59.v2.vectors), channel_id=1, source_target_pairs={{0,14},{1,13},{2,0},{3,15},{4,2},{5,1},{6,4},{7,3},{8,6},{9,5},{10... | collective-permute-start | bytes 589832 | tf_op jit(solution)/shard_map/ppermute | solution.py:438
  68.1 1.1 copy-start.6
  69.6 1.8 %copy-start.2 = (bf16[768,384]{1,0:T(8,128)(2,1)S(1)}, bf16[768,384]{1,0:T(8,128)(2,1)}, u32[]{:S(2)}) copy-start(bf16[768,384]{1,0:T(8,128)(2,1)} %copy-done.1) | copy-start | bytes 1769476
  72.8 1.3 %collective-permute-start.15 = (f32[56,128]{1,0:T(8,128)S(1)}, f32[56,128]{1,0:T(8,128)S(1)}, u32[]{:S(2)}, u32[]{:S(2)}) collective-permute-start(f32[56,128]{1,0:T(8,128)S(1)} %get-tuple-element.55), channel_id=1, source_target_pairs={{0,1},{1,0},{2,3},{3,2},{4,5},{5,4},{6,7},{7,6},{8,9},{9,8},{10,11... | collective-permute-start | bytes 86024 | tf_op jit(solution)/shard_map/ppermute | solution.py:442
  74.1 4.6 %collective-permute-start.16 = (f32[56,128]{1,0:T(8,128)S(1)}, f32[56,128]{1,0:T(8,128)S(1)}, u32[]{:S(2)}, u32[]{:S(2)}) collective-permute-start(f32[56,128]{1,0:T(8,128)S(1)} %add.29), channel_id=1, source_target_pairs={{0,2},{2,0},{4,6},{6,4},{8,10},{10,8},{12,14},{14,12},{1,3},{3,1},... | collective-permute-start | bytes 86024 | tf_op jit(solution)/shard_map/ppermute | solution.py:449
  78.7 3.9 %collective-permute-start.17 = (f32[56,128]{1,0:T(8,128)S(1)}, f32[56,128]{1,0:T(8,128)S(1)}, u32[]{:S(2)}, u32[]{:S(2)}) collective-permute-start(f32[56,128]{1,0:T(8,128)S(1)} %add.30), channel_id=1, source_target_pairs={{0,4},{2,6},{4,0},{6,2},{8,12},{10,14},{12,8},{14,10},{1,5},{3,7},... | collective-permute-start | bytes 86024 | tf_op jit(solution)/shard_map/ppermute | solution.py:449
  82.6 5.0 %collective-permute-start.18 = (f32[56,128]{1,0:T(8,128)S(1)}, f32[56,128]{1,0:T(8,128)S(1)}, u32[]{:S(2)}, u32[]{:S(2)}) collective-permute-start(f32[56,128]{1,0:T(8,128)S(1)} %add.31), channel_id=1, source_target_pairs={{0,8},{2,10},{4,12},{6,14},{8,0},{10,2},{12,4},{14,6},{1,9},{3,11}... | collective-permute-start | bytes 86024 | tf_op jit(solution)/shard_map/ppermute | solution.py:449
  87.6 1.2 %collective-permute-start.19 = (f32[56,128]{1,0:T(8,128)S(1)}, f32[56,128]{1,0:T(8,128)S(1)}, u32[]{:S(2)}, u32[]{:S(2)}) collective-permute-start(f32[56,128]{1,0:T(8,128)S(1)} %add.32.refs_2_), channel_id=1, source_target_pairs={{0,1},{1,0},{2,3},{3,2},{4,5},{5,4},{6,7},{7,6},{8,9},{9,8},{10,11... | collective-permute-start | bytes 86024 | tf_op jit(solution)/shard_map/ppermute | solution.py:442

commit v12 on v11

--- a/solution.py
+++ b/solution.py
@@ -480,11 +480,11 @@
     h0, l0, sums, row_sq, own_copy, token = make_tile(
         own_body, [embeddings, other_emb], size,
         (((2 * size, 128), F32), (embeddings.shape, BF16), ((8, 128), F32)))
-    first, second, seeds, keep, relays, token = lax.optimization_barrier(
-        (first, second, seeds, keep, relays, token))
+    first, seeds, keep, relays, token = lax.optimization_barrier((first, seeds, keep, relays, token))
     relayed = [first, own_copy]
     if relaying:
-        relayed[1] = between_shards(first, [(2 * i, (i - 2) % blocks * 2) for i in range(1, blocks, 2)])
+        forward, second = lax.optimization_barrier((first, second))
+        relayed[1] = between_shards(forward, [(2 * i, (i - 2) % blocks * 2) for i in range(1, blocks, 2)])
     if relaying:
         relayed[0] = between_shards(first, [(2 * i + 1, 2 * i + 2) for i in range(0, blocks, 2)])
     tile_args = [keep, relays, token, own_copy, other_emb, row_sq]

time: 108 us -> 106 us (0.981)
    ppermute x7, starting transfers between devices: 1.09 us -> 3.37 us  [between_cores(): return lax.ppermute(shard, 'narrow', [(0, 1), (1, 0)])]
    ppermute x4, waiting for transfers between devices: 6.55 us -> 4.43 us  [between_shards(): return lax.ppermute(shard, ('blk', 'narrow'), pairs)]
    ppermute x6, waiting for transfers between devices: 19 us -> 20.1 us  [between_blocks(): return lax.ppermute(shard, ('blk', 'narrow'), pairs)]
  transfers between devices with their start and end apart: 20 -> 20, of which waited for: 16 -> 15; matrix products, arithmetic and copies ran while one was open for 3% -> 3% of each run, Pallas kernels for 8% -> 8%
where the time goes in v12:
time: 106 us
  waiting for transfers between devices  39.2 us (37%)
  starting transfers between devices  31.3 us (30%)
  Pallas kernels  30.5 us (29%)
  between operations  2.24 us (2%)
  local copies, waits for them, and re-layouts  1.83 us (2%)
    pallas_call x18, Pallas kernels, call(): pl.pallas_call(body, out_shape=[jax.ShapeDtypeStruct(shape, dtype) for sh...  30.5 us
    ppermute x6, waiting for transfers between devices, between_blocks(): return lax.ppermute(shard, ('blk', 'narrow'), pairs)  20.1 us
    ppermute x6, starting transfers between devices, between_blocks(): return lax.ppermute(shard, ('blk', 'narrow'), pairs)  16.5 us
    ppermute x3, waiting for transfers between devices, total_over_blocks(): lax.ppermute(values, 'blk', [(i, i ^ span) for i in range(blocks)])  9.22 us
    ppermute x4, starting transfers between devices, between_shards(): return lax.ppermute(shard, ('blk', 'narrow'), pairs)  7.24 us
    ppermute x7, waiting for transfers between devices, between_cores(): return lax.ppermute(shard, 'narrow', [(0, 1), (1, 0)])  5.45 us
    ppermute x4, waiting for transfers between devices, between_shards(): return lax.ppermute(shard, ('blk', 'narrow'), pairs)  4.43 us
    ppermute x3, starting transfers between devices, total_over_blocks(): lax.ppermute(values, 'blk', [(i, i ^ span) for i in range(blocks)])  4.19 us
  transfers between devices with their start and end apart: 20, of which 15 were waited for; matrix products, arithmetic and copies ran while one was open for 3% of the time, Pallas kernels for 8%

profile of v12, /device:TPU:0, one launch (start us, length us, event | category | flops | bytes accessed | tf_op | source)
XLA Modules:
  0.0 106.0 jit_solution(17347667828556066067)
XLA Ops:
  0.0 0.5 collective-permute-start.2
  0.5 2.5 %collective-permute-start = (bf16[384,768]{1,0:T(8,128)(2,1)}, bf16[384,768]{1,0:T(8,128)(2,1)S(1)}, u32[]{:S(2)}, u32[]{:S(2)}) collective-permute-start(bf16[384,768]{1,0:T(8,128)(2,1)} %own.1), channel_id=1, source_target_pairs={{2,0},{6,4},{10,8},{14,12},{1,13},{3,15},{5,1},{7,3},{9,5},{11,7},... | collective-permute-start | bytes 1769480 | tf_op jit(solution)/shard_map/ppermute | solution.py:472
  3.0 0.9 multiply_bitcast_fusion
  3.9 2.4 %collective-permute-start.1 = (f32[64,384]{1,0:T(8,128)S(1)}, f32[64,384]{1,0:T(8,128)S(1)}, u32[]{:S(2)}, u32[]{:S(2)}) collective-permute-start(f32[64,384]{1,0:T(8,128)S(1)} %multiply_bitcast_fusion), channel_id=1, source_target_pairs={{0,1},{1,0},{2,3},{3,2},{4,5},{5,4},{6,7},{7,6},{8,9},{9,8},{10,11... | collective-permute-start | bytes 294920 | tf_op jit(solution)/shard_map/ppermute | solution.py:442
  6.3 3.3 %collective-permute-start.3 = (bf16[384,768]{1,0:T(8,128)(2,1)}, bf16[384,768]{1,0:T(8,128)(2,1)S(1)}, u32[]{:S(2)}, u32[]{:S(2)}) collective-permute-start(bf16[384,768]{1,0:T(8,128)(2,1)} %own.1), channel_id=1, source_target_pairs={{3,0},{7,4},{11,8},{15,12},{0,13},{2,15},{4,1},{6,3},{8,5},{10,7},... | collective-permute-start | bytes 1769480 | tf_op jit(solution)/shard_map/ppermute | solution.py:472
  9.6 1.3 %dynamic_slice.3 = s32[1,1]{0,1:T(1,128)} dynamic-slice(s32[8,2]{0,1:T(2,128)} %param.5, s32[]{:T(128)S(6)} %select_n.25, s32[]{:T(128)S(6)} %select_n.26), dynamic_slice_sizes={1,1} | dynamic-slice | bytes 12 | tf_op jit(solution)/shard_map/dynamic_slice | solution.py:477
  11.6 1.9 %shard_map.46 = (bf16[768,384]{1,0:T(8,128)(2,1)S(1)}, bf16[768,384]{1,0:T(8,128)(2,1)S(1)}, f32[16,384]{1,0:T(8,128)S(1)}, f32[768,128]{1,0:T(8,128)S(1)}, bf16...) custom-call(bf16[384,768]{1,0:T(8,128)(2,1)S(1)} %copy-done, bf16[384,768]{1,0:T(8,128)(2,1)S(1)} %collective-permute-done.2.other), custom_call_target="tpu_custom_call" | custom-call | flops 2000000000 | bytes 1000000 | tf_op jit(solution)/shard_map/pallas_call | solution.py:32
  13.5 0.7 collective-permute-start.5
  14.2 4.4 %collective-permute-done.3.direct = bf16[384,768]{1,0:T(8,128)(2,1)S(1)} collective-permute-done((bf16[384,768]{1,0:T(8,128)(2,1)}, bf16[384,768]{1,0:T(8,128)(2,1)S(1)}, u32[]{:S(2)}, u32[]{:S(2)}) %collective-permute-start.3) | collective-permute-done | bytes 589856 | tf_op jit(solution)/shard_map/ppermute | solution.py:472
  18.6 0.7 collective-permute-start.4
  19.3 0.5 slice.4
  20.5 2.0 %shard_map.47 = (bf16[768,384]{1,0:T(8,128)(2,1)S(1)}, bf16[768,384]{1,0:T(8,128)(2,1)S(1)}, f32[16,384]{1,0:T(8,128)S(1)}, f32[8,384]{1,0:T(8,128)S(1)}) custom-call(f32[8,128]{1,0:T(8,128)S(1)} %broadcast_in_dim.22.keep, f32[8,128]{1,0:T(8,128)S(1)} %broadcast_in_dim.23.relays, f32[8,128]{1,0:T(8,128)S(1)} %get-tuple-element.35.token, ...), custom_call_target="tpu_custom_call" | custom-call | flops 2000000000 | bytes 1000000 | tf_op jit(solution)/shard_map/pallas_call | solution.py:32
  22.5 2.0 %shard_map.48 = (bf16[768,384]{1,0:T(8,128)(2,1)S(1)}, bf16[768,384]{1,0:T(8,128)(2,1)S(1)}, f32[16,384]{1,0:T(8,128)S(1)}, f32[8,384]{1,0:T(8,128)S(1)}) custom-call(f32[8,128]{1,0:T(8,128)S(1)} %broadcast_in_dim.22.keep, f32[8,128]{1,0:T(8,128)S(1)} %broadcast_in_dim.23.relays, f32[8,128]{1,0:T(8,128)S(1)} %get-tuple-element.35.token, ...), custom_call_target="tpu_custom_call" | custom-call | flops 2000000000 | bytes 1000000 | tf_op jit(solution)/shard_map/pallas_call | solution.py:32
  24.5 9.7 %collective-permute-start.6 = (f32[16,384]{1,0:T(8,128)S(1)}, f32[16,384]{1,0:T(8,128)S(1)}, u32[]{:S(2)}, u32[]{:S(2)}) collective-permute-start(f32[16,384]{1,0:T(8,128)S(1)} %pad_maximum_fusion.1), channel_id=1, source_target_pairs={{0,2},{1,5},{2,4},{3,7},{4,6},{5,9},{6,8},{7,11},{8,10},{9,13},{10... | collective-permute-start | bytes 73736 | tf_op jit(solution)/shard_map/ppermute | solution.py:438
  34.2 3.6 %collective-permute-done.6 = f32[16,384]{1,0:T(8,128)S(1)} collective-permute-done((f32[16,384]{1,0:T(8,128)S(1)}, f32[16,384]{1,0:T(8,128)S(1)}, u32[]{:S(2)}, u32[]{:S(2)}) %collective-permute-start.6) | collective-permute-done | bytes 24608 | tf_op jit(solution)/shard_map/ppermute | solution.py:438
  37.9 1.2 %collective-permute-done.7.other_sums = f32[16,384]{1,0:T(8,128)S(1)} collective-permute-done((f32[16,384]{1,0:T(8,128)S(1)}, f32[16,384]{1,0:T(8,128)S(1)}, u32[]{:S(2)}, u32[]{:S(2)}) %collective-permute-start.7) | collective-permute-done | bytes 24608 | tf_op jit(solution)/shard_map/ppermute | solution.py:442
  39.1 2.1 %collective-permute-start.8 = (f32[128,384]{1,0:T(8,128)S(1)}, f32[128,384]{1,0:T(8,128)S(1)}, u32[]{:S(2)}, u32[]{:S(2)}) collective-permute-start(f32[128,384]{1,0:T(8,128)S(1)} %get-tuple-element.48.vectors.v0), channel_id=1, source_target_pairs={{0,14},{1,13},{2,0},{3,15},{4,2},{5,1},{6,4},{7,3},{8,6},{9,5},{10... | collective-permute-start | bytes 589832 | tf_op jit(solution)/shard_map/ppermute | solution.py:438
  41.1 0.5 shard_map.52
  41.7 0.5 shard_map.50.product
  42.2 3.8 %collective-permute-done.8.near = f32[128,384]{1,0:T(8,128)S(1)} collective-permute-done((f32[128,384]{1,0:T(8,128)S(1)}, f32[128,384]{1,0:T(8,128)S(1)}, u32[]{:S(2)}, u32[]{:S(2)}) %collective-permute-start.8) | collective-permute-done | bytes 196640 | tf_op jit(solution)/shard_map/ppermute | solution.py:438
  46.0 0.8 shard_map.51.total
  46.8 3.4 %collective-permute-done.9.behind = f32[128,384]{1,0:T(8,128)S(1)} collective-permute-done((f32[128,384]{1,0:T(8,128)S(1)}, f32[128,384]{1,0:T(8,128)S(1)}, u32[]{:S(2)}, u32[]{:S(2)}) %collective-permute-start.9) | collective-permute-done | bytes 196640 | tf_op jit(solution)/shard_map/ppermute | solution.py:438
  50.2 0.1 collective-permute-start.10
  50.3 1.4 %collective-permute-done.10.other_total = f32[128,384]{1,0:T(8,128)S(1)} collective-permute-done((f32[128,384]{1,0:T(8,128)S(1)}, f32[128,384]{1,0:T(8,128)S(1)}, u32[]{:S(2)}, u32[]{:S(2)}) %collective-permute-start.10) | collective-permute-done | bytes 196640 | tf_op jit(solution)/shard_map/ppermute | solution.py:442
  51.8 1.8 %collective-permute-start.11 = (f32[128,384]{1,0:T(8,128)S(1)}, f32[128,384]{1,0:T(8,128)S(1)}, u32[]{:S(2)}, u32[]{:S(2)}) collective-permute-start(f32[128,384]{1,0:T(8,128)S(1)} %shard_map.54.vectors.v1), channel_id=1, source_target_pairs={{0,14},{1,13},{2,0},{3,15},{4,2},{5,1},{6,4},{7,3},{8,6},{9,5},{10... | collective-permute-start | bytes 589832 | tf_op jit(solution)/shard_map/ppermute | solution.py:438
  53.6 0.5 shard_map.57
  54.2 0.3 collective-permute-start.12
  54.5 0.5 shard_map.55.product
  54.9 4.0 %collective-permute-done.11.near = f32[128,384]{1,0:T(8,128)S(1)} collective-permute-done((f32[128,384]{1,0:T(8,128)S(1)}, f32[128,384]{1,0:T(8,128)S(1)}, u32[]{:S(2)}, u32[]{:S(2)}) %collective-permute-start.11) | collective-permute-done | bytes 196640 | tf_op jit(solution)/shard_map/ppermute | solution.py:438
  59.0 0.8 shard_map.56.total
  59.8 2.9 %collective-permute-done.12.behind = f32[128,384]{1,0:T(8,128)S(1)} collective-permute-done((f32[128,384]{1,0:T(8,128)S(1)}, f32[128,384]{1,0:T(8,128)S(1)}, u32[]{:S(2)}, u32[]{:S(2)}) %collective-permute-start.12) | collective-permute-done | bytes 196640 | tf_op jit(solution)/shard_map/ppermute | solution.py:438
  62.7 0.1 collective-permute-start.13
  62.8 1.4 %collective-permute-done.13.other_total = f32[128,384]{1,0:T(8,128)S(1)} collective-permute-done((f32[128,384]{1,0:T(8,128)S(1)}, f32[128,384]{1,0:T(8,128)S(1)}, u32[]{:S(2)}, u32[]{:S(2)}) %collective-permute-start.13) | collective-permute-done | bytes 196640 | tf_op jit(solution)/shard_map/ppermute | solution.py:442
  64.3 2.5 %collective-permute-start.14 = (f32[128,384]{1,0:T(8,128)S(1)}, f32[128,384]{1,0:T(8,128)S(1)}, u32[]{:S(2)}, u32[]{:S(2)}) collective-permute-start(f32[128,384]{1,0:T(8,128)S(1)} %shard_map.59.v2.vectors), channel_id=1, source_target_pairs={{0,14},{1,13},{2,0},{3,15},{4,2},{5,1},{6,4},{7,3},{8,6},{9,5},{10... | collective-permute-start | bytes 589832 | tf_op jit(solution)/shard_map/ppermute | solution.py:438
  66.8 0.5 shard_map.61.product
  67.3 0.5 shard_map.60
  67.8 2.3 %collective-permute-done.14.near = f32[128,384]{1,0:T(8,128)S(1)} collective-permute-done((f32[128,384]{1,0:T(8,128)S(1)}, f32[128,384]{1,0:T(8,128)S(1)}, u32[]{:S(2)}, u32[]{:S(2)}) %collective-permute-start.14) | collective-permute-done | bytes 196640 | tf_op jit(solution)/shard_map/ppermute | solution.py:438
  70.2 1.4 %shard_map.62 = (f32[56,128]{1,0:T(8,128)S(1)}, f32[56,128]{1,0:T(8,128)S(1)}) custom-call(f32[8,128]{1,0:T(8,128)S(1)} %broadcast_in_dim.19.core.refs_0_, f32[8,128]{1,0:T(8,128)S(1)} %broadcast_in_dim.23.relays, f32[320,64]{1,0:T(8,128)S(1)} %get-tuple-element.55.low, f32[128,384]{1,0:T(8,128)S(1)} %shard_map.59.v2.vectors, ...), custom_call_target="tpu_custom_call" | custom-call | flops 1000000000 | bytes 1000000 | tf_op jit(solution)/shard_map/pallas_call | solution.py:32
  71.5 0.4 collective-permute-start.15
  72.0 0.9 collective-permute-done.15
  72.8 2.7 %collective-permute-start.16 = (f32[56,128]{1,0:T(8,128)S(1)}, f32[56,128]{1,0:T(8,128)S(1)}, u32[]{:S(2)}, u32[]{:S(2)}) collective-permute-start(f32[56,128]{1,0:T(8,128)S(1)} %add.29), channel_id=1, source_target_pairs={{0,2},{2,0},{4,6},{6,4},{8,10},{10,8},{12,14},{14,12},{1,3},{3,1},... | collective-permute-start | bytes 86024 | tf_op jit(solution)/shard_map/ppermute | solution.py:449
  75.5 1.8 %collective-permute-done.16 = f32[56,128]{1,0:T(8,128)S(1)} collective-permute-done((f32[56,128]{1,0:T(8,128)S(1)}, f32[56,128]{1,0:T(8,128)S(1)}, u32[]{:S(2)}, u32[]{:S(2)}) %collective-permute-start.16) | collective-permute-done | bytes 28704 | tf_op jit(solution)/shard_map/ppermute | solution.py:449
  77.4 0.1 collective-permute-start.17
  77.5 3.8 %collective-permute-done.17 = f32[56,128]{1,0:T(8,128)S(1)} collective-permute-done((f32[56,128]{1,0:T(8,128)S(1)}, f32[56,128]{1,0:T(8,128)S(1)}, u32[]{:S(2)}, u32[]{:S(2)}) %collective-permute-start.17) | collective-permute-done | bytes 28704 | tf_op jit(solution)/shard_map/ppermute | solution.py:449
  81.3 1.4 %collective-permute-start.18 = (f32[56,128]{1,0:T(8,128)S(1)}, f32[56,128]{1,0:T(8,128)S(1)}, u32[]{:S(2)}, u32[]{:S(2)}) collective-permute-start(f32[56,128]{1,0:T(8,128)S(1)} %add.31), channel_id=1, source_target_pairs={{0,8},{2,10},{4,12},{6,14},{8,0},{10,2},{12,4},{14,6},{1,9},{3,11}... | collective-permute-start | bytes 86024 | tf_op jit(solution)/shard_map/ppermute | solution.py:449
  82.6 3.6 %collective-permute-done.18 = f32[56,128]{1,0:T(8,128)S(1)} collective-permute-done((f32[56,128]{1,0:T(8,128)S(1)}, f32[56,128]{1,0:T(8,128)S(1)}, u32[]{:S(2)}, u32[]{:S(2)}) %collective-permute-start.18) | collective-permute-done | bytes 28704 | tf_op jit(solution)/shard_map/ppermute | solution.py:449
  86.9 0.5 collective-permute-done.19.refs_3_
  87.5 18.6 %shard_map.63 = f32[64,384]{1,0:T(8,128)} custom-call(f32[8,128]{1,0:T(8,128)S(1)} %broadcast_in_dim.19.core.refs_0_, f32[8,128]{1,0:T(8,128)S(1)} %broadcast_in_dim.20.refs_1_, f32[56,128]{1,0:T(8,128)S(1)} %add.32.refs_2_, f32[56,128]{1,0:T(8,128)S(1)} %collective-permute-done.19.refs_3_, f32[192,384]{1,0:T(8,128)S(1)} %get-tuple-element.58.refs_4_), custom_call_target="tpu_custom_call" | custom-call | flops 20000000000 | bytes 1000000 | tf_op jit(solution)/shard_map/pallas_call | solution.py:32
  (43 shorter events, 0.3 us)
Async XLA Ops:
  0.0 11.6 %copy-start = (bf16[384,768]{1,0:T(8,128)(2,1)S(1)}, bf16[384,768]{1,0:T(8,128)(2,1)}, u32[]{:S(2)}) copy-start(bf16[384,768]{1,0:T(8,128)(2,1)} %own.1) | copy-start | bytes 1769476
  0.0 11.6 %collective-permute-start.2 = (bf16[384,768]{1,0:T(8,128)(2,1)}, bf16[384,768]{1,0:T(8,128)(2,1)S(1)}, u32[]{:S(2)}, u32[]{:S(2)}) collective-permute-start(bf16[384,768]{1,0:T(8,128)(2,1)} %own.1), channel_id=1, source_target_pairs={{0,1},{1,0},{2,3},{3,2},{4,5},{5,4},{6,7},{7,6},{8,9},{9,8},{10,11... | collective-permute-start | bytes 1769480 | tf_op jit(solution)/shard_map/ppermute | solution.py:442
  0.5 13.0 %collective-permute-start = (bf16[384,768]{1,0:T(8,128)(2,1)}, bf16[384,768]{1,0:T(8,128)(2,1)S(1)}, u32[]{:S(2)}, u32[]{:S(2)}) collective-permute-start(bf16[384,768]{1,0:T(8,128)(2,1)} %own.1), channel_id=1, source_target_pairs={{2,0},{6,4},{10,8},{14,12},{1,13},{3,15},{5,1},{7,3},{9,5},{11,7},... | collective-permute-start | bytes 1769480 | tf_op jit(solution)/shard_map/ppermute | solution.py:472
  3.9 7.6 %collective-permute-start.1 = (f32[64,384]{1,0:T(8,128)S(1)}, f32[64,384]{1,0:T(8,128)S(1)}, u32[]{:S(2)}, u32[]{:S(2)}) collective-permute-start(f32[64,384]{1,0:T(8,128)S(1)} %multiply_bitcast_fusion), channel_id=1, source_target_pairs={{0,1},{1,0},{2,3},{3,2},{4,5},{5,4},{6,7},{7,6},{8,9},{9,8},{10,11... | collective-permute-start | bytes 294920 | tf_op jit(solution)/shard_map/ppermute | solution.py:442
  6.3 12.4 %collective-permute-start.3 = (bf16[384,768]{1,0:T(8,128)(2,1)}, bf16[384,768]{1,0:T(8,128)(2,1)S(1)}, u32[]{:S(2)}, u32[]{:S(2)}) collective-permute-start(bf16[384,768]{1,0:T(8,128)(2,1)} %own.1), channel_id=1, source_target_pairs={{3,0},{7,4},{11,8},{15,12},{0,13},{2,15},{4,1},{6,3},{8,5},{10,7},... | collective-permute-start | bytes 1769480 | tf_op jit(solution)/shard_map/ppermute | solution.py:472
  13.4 41.0 %copy-start.5 = (bf16[768,384]{1,0:T(8,128)(2,1)}, bf16[768,384]{1,0:T(8,128)(2,1)S(1)}, u32[]{:S(2)}) copy-start(bf16[768,384]{1,0:T(8,128)(2,1)S(1)} %get-tuple-element.49.h0) | copy-start | bytes 1769476
  13.4 41.0 %copy-start.7 = (bf16[768,384]{1,0:T(8,128)(2,1)}, bf16[768,384]{1,0:T(8,128)(2,1)S(1)}, u32[]{:S(2)}) copy-start(bf16[768,384]{1,0:T(8,128)(2,1)S(1)} %get-tuple-element.50.l0) | copy-start | bytes 1769476
  13.5 7.0 %collective-permute-start.5 = (bf16[384,768]{1,0:T(8,128)(2,1)S(1)}, bf16[384,768]{1,0:T(8,128)(2,1)S(1)}, u32[]{:S(2)}, u32[]{:S(2)}) collective-permute-start(bf16[384,768]{1,0:T(8,128)(2,1)S(1)} %collective-permute-done.direct), channel_id=1, source_target_pairs={{1,2},{5,6},{9,10},{13,14},{17,18},{21,22},{25,26},{29,30}} | collective-permute-start | bytes 1769480 | tf_op jit(solution)/shard_map/ppermute | solution.py:472
  18.6 3.8 %collective-permute-start.4 = (bf16[384,768]{1,0:T(8,128)(2,1)S(1)}, bf16[384,768]{1,0:T(8,128)(2,1)S(1)}, u32[]{:S(2)}, u32[]{:S(2)}) collective-permute-start(bf16[384,768]{1,0:T(8,128)(2,1)S(1)} %collective-permute-done.direct), channel_id=1, source_target_pairs={{2,14},{6,2},{10,6},{14,10},{18,30},{22,18},{26,22},{30,26}} | collective-permute-start | bytes 1769480 | tf_op jit(solution)/shard_map/ppermute | solution.py:472
  22.5 36.5 %copy-start.1 = (bf16[768,384]{1,0:T(8,128)(2,1)}, bf16[768,384]{1,0:T(8,128)(2,1)S(1)}, u32[]{:S(2)}) copy-start(bf16[768,384]{1,0:T(8,128)(2,1)S(1)} %get-tuple-element.52.l1) | copy-start | bytes 1769476
  24.5 34.5 %copy-start.3 = (bf16[768,384]{1,0:T(8,128)(2,1)}, bf16[768,384]{1,0:T(8,128)(2,1)S(1)}, u32[]{:S(2)}) copy-start(bf16[768,384]{1,0:T(8,128)(2,1)S(1)} %get-tuple-element.54.l2) | copy-start | bytes 1769476
  24.5 13.3 %collective-permute-start.6 = (f32[16,384]{1,0:T(8,128)S(1)}, f32[16,384]{1,0:T(8,128)S(1)}, u32[]{:S(2)}, u32[]{:S(2)}) collective-permute-start(f32[16,384]{1,0:T(8,128)S(1)} %pad_maximum_fusion.1), channel_id=1, source_target_pairs={{0,2},{1,5},{2,4},{3,7},{4,6},{5,9},{6,8},{7,11},{8,10},{9,13},{10... | collective-permute-start | bytes 73736 | tf_op jit(solution)/shard_map/ppermute | solution.py:438
  37.8 1.2 %collective-permute-start.7 = (f32[16,384]{1,0:T(8,128)S(1)}, f32[16,384]{1,0:T(8,128)S(1)}, u32[]{:S(2)}, u32[]{:S(2)}) collective-permute-start(f32[16,384]{1,0:T(8,128)S(1)} %add.28.sums), channel_id=1, source_target_pairs={{0,1},{1,0},{2,3},{3,2},{4,5},{5,4},{6,7},{7,6},{8,9},{9,8},{10,11... | collective-permute-start | bytes 73736 | tf_op jit(solution)/shard_map/ppermute | solution.py:442
  39.1 6.9 %collective-permute-start.8 = (f32[128,384]{1,0:T(8,128)S(1)}, f32[128,384]{1,0:T(8,128)S(1)}, u32[]{:S(2)}, u32[]{:S(2)}) collective-permute-start(f32[128,384]{1,0:T(8,128)S(1)} %get-tuple-element.48.vectors.v0), channel_id=1, source_target_pairs={{0,14},{1,13},{2,0},{3,15},{4,2},{5,1},{6,4},{7,3},{8,6},{9,5},{10... | collective-permute-start | bytes 589832 | tf_op jit(solution)/shard_map/ppermute | solution.py:438
  41.7 8.5 %collective-permute-start.9 = (f32[128,384]{1,0:T(8,128)S(1)}, f32[128,384]{1,0:T(8,128)S(1)}, u32[]{:S(2)}, u32[]{:S(2)}) collective-permute-start(f32[128,384]{1,0:T(8,128)S(1)} %shard_map.52), channel_id=1, source_target_pairs={{0,2},{1,5},{2,4},{3,7},{4,6},{5,9},{6,8},{7,11},{8,10},{9,13},{10... | collective-permute-start | bytes 589832 | tf_op jit(solution)/shard_map/ppermute | solution.py:438
  50.2 1.5 %collective-permute-start.10 = (f32[128,384]{1,0:T(8,128)S(1)}, f32[128,384]{1,0:T(8,128)S(1)}, u32[]{:S(2)}, u32[]{:S(2)}) collective-permute-start(f32[128,384]{1,0:T(8,128)S(1)} %shard_map.53.total), channel_id=1, source_target_pairs={{0,1},{1,0},{2,3},{3,2},{4,5},{5,4},{6,7},{7,6},{8,9},{9,8},{10,11... | collective-permute-start | bytes 589832 | tf_op jit(solution)/shard_map/ppermute | solution.py:442
  51.8 7.2 %collective-permute-start.11 = (f32[128,384]{1,0:T(8,128)S(1)}, f32[128,384]{1,0:T(8,128)S(1)}, u32[]{:S(2)}, u32[]{:S(2)}) collective-permute-start(f32[128,384]{1,0:T(8,128)S(1)} %shard_map.54.vectors.v1), channel_id=1, source_target_pairs={{0,14},{1,13},{2,0},{3,15},{4,2},{5,1},{6,4},{7,3},{8,6},{9,5},{10... | collective-permute-start | bytes 589832 | tf_op jit(solution)/shard_map/ppermute | solution.py:438
  54.2 8.5 %collective-permute-start.12 = (f32[128,384]{1,0:T(8,128)S(1)}, f32[128,384]{1,0:T(8,128)S(1)}, u32[]{:S(2)}, u32[]{:S(2)}) collective-permute-start(f32[128,384]{1,0:T(8,128)S(1)} %shard_map.57), channel_id=1, source_target_pairs={{0,2},{1,5},{2,4},{3,7},{4,6},{5,9},{6,8},{7,11},{8,10},{9,13},{10... | collective-permute-start | bytes 589832 | tf_op jit(solution)/shard_map/ppermute | solution.py:438
  59.8 7.0 %copy-start.6 = (bf16[768,384]{1,0:T(8,128)(2,1)S(1)}, bf16[768,384]{1,0:T(8,128)(2,1)}, u32[]{:S(2)}) copy-start(bf16[768,384]{1,0:T(8,128)(2,1)} %copy-done.5) | copy-start | bytes 1769476
  59.8 7.0 %copy-start.8 = (bf16[768,384]{1,0:T(8,128)(2,1)S(1)}, bf16[768,384]{1,0:T(8,128)(2,1)}, u32[]{:S(2)}) copy-start(bf16[768,384]{1,0:T(8,128)(2,1)} %copy-done.7) | copy-start | bytes 1769476
  62.7 1.5 %collective-permute-start.13 = (f32[128,384]{1,0:T(8,128)S(1)}, f32[128,384]{1,0:T(8,128)S(1)}, u32[]{:S(2)}, u32[]{:S(2)}) collective-permute-start(f32[128,384]{1,0:T(8,128)S(1)} %shard_map.58.total), channel_id=1, source_target_pairs={{0,1},{1,0},{2,3},{3,2},{4,5},{5,4},{6,7},{7,6},{8,9},{9,8},{10,11... | collective-permute-start | bytes 589832 | tf_op jit(solution)/shard_map/ppermute | solution.py:442
  64.3 5.9 %collective-permute-start.14 = (f32[128,384]{1,0:T(8,128)S(1)}, f32[128,384]{1,0:T(8,128)S(1)}, u32[]{:S(2)}, u32[]{:S(2)}) collective-permute-start(f32[128,384]{1,0:T(8,128)S(1)} %shard_map.59.v2.vectors), channel_id=1, source_target_pairs={{0,14},{1,13},{2,0},{3,15},{4,2},{5,1},{6,4},{7,3},{8,6},{9,5},{10... | collective-permute-start | bytes 589832 | tf_op jit(solution)/shard_map/ppermute | solution.py:438
  67.3 2.9 %copy-start.2 = (bf16[768,384]{1,0:T(8,128)(2,1)S(1)}, bf16[768,384]{1,0:T(8,128)(2,1)}, u32[]{:S(2)}) copy-start(bf16[768,384]{1,0:T(8,128)(2,1)} %copy-done.1) | copy-start | bytes 1769476
  67.3 2.9 %copy-start.4 = (bf16[768,384]{1,0:T(8,128)(2,1)S(1)}, bf16[768,384]{1,0:T(8,128)(2,1)}, u32[]{:S(2)}) copy-start(bf16[768,384]{1,0:T(8,128)(2,1)} %copy-done.3) | copy-start | bytes 1769476
  71.5 1.3 %collective-permute-start.15 = (f32[56,128]{1,0:T(8,128)S(1)}, f32[56,128]{1,0:T(8,128)S(1)}, u32[]{:S(2)}, u32[]{:S(2)}) collective-permute-start(f32[56,128]{1,0:T(8,128)S(1)} %get-tuple-element.57), channel_id=1, source_target_pairs={{0,1},{1,0},{2,3},{3,2},{4,5},{5,4},{6,7},{7,6},{8,9},{9,8},{10,11... | collective-permute-start | bytes 86024 | tf_op jit(solution)/shard_map/ppermute | solution.py:442
  72.8 4.6 %collective-permute-start.16 = (f32[56,128]{1,0:T(8,128)S(1)}, f32[56,128]{1,0:T(8,128)S(1)}, u32[]{:S(2)}, u32[]{:S(2)}) collective-permute-start(f32[56,128]{1,0:T(8,128)S(1)} %add.29), channel_id=1, source_target_pairs={{0,2},{2,0},{4,6},{6,4},{8,10},{10,8},{12,14},{14,12},{1,3},{3,1},... | collective-permute-start | bytes 86024 | tf_op jit(solution)/shard_map/ppermute | solution.py:449
  77.4 3.9 %collective-permute-start.17 = (f32[56,128]{1,0:T(8,128)S(1)}, f32[56,128]{1,0:T(8,128)S(1)}, u32[]{:S(2)}, u32[]{:S(2)}) collective-permute-start(f32[56,128]{1,0:T(8,128)S(1)} %add.30), channel_id=1, source_target_pairs={{0,4},{2,6},{4,0},{6,2},{8,12},{10,14},{12,8},{14,10},{1,5},{3,7},... | collective-permute-start | bytes 86024 | tf_op jit(solution)/shard_map/ppermute | solution.py:449
  81.3 5.0 %collective-permute-start.18 = (f32[56,128]{1,0:T(8,128)S(1)}, f32[56,128]{1,0:T(8,128)S(1)}, u32[]{:S(2)}, u32[]{:S(2)}) collective-permute-start(f32[56,128]{1,0:T(8,128)S(1)} %add.31), channel_id=1, source_target_pairs={{0,8},{2,10},{4,12},{6,14},{8,0},{10,2},{12,4},{14,6},{1,9},{3,11}... | collective-permute-start | bytes 86024 | tf_op jit(solution)/shard_map/ppermute | solution.py:449
  86.2 1.2 %collective-permute-start.19 = (f32[56,128]{1,0:T(8,128)S(1)}, f32[56,128]{1,0:T(8,128)S(1)}, u32[]{:S(2)}, u32[]{:S(2)}) collective-permute-start(f32[56,128]{1,0:T(8,128)S(1)} %add.32.refs_2_), channel_id=1, source_target_pairs={{0,1},{1,0},{2,3},{3,2},{4,5},{5,4},{6,7},{7,6},{8,9},{9,8},{10,11... | collective-permute-start | bytes 86024 | tf_op jit(solution)/shard_map/ppermute | solution.py:442

commit v13 on v12

--- a/solution.py
+++ b/solution.py
@@ -118,11 +118,31 @@
     return jnp.concatenate([jnp.broadcast_to(values[i:i + 1, :], shape) for i in (0, 8)], axis=0)
 
 
-def degree_body(sums, other_sums, seeds, degree_out, vectors_out):
+def packed_rows(values):
+    rows, cols = values.shape
+    biggest = jnp.max(jnp.abs(values), axis=1, keepdims=True)
+    power = jnp.floor(jnp.log2(jnp.maximum(biggest, 1e-30)) + 1e-3)
+    whole = jnp.round(values * jnp.exp2(14.0 - power)).astype(jnp.int32).astype(jnp.int16)
+    powers = jnp.broadcast_to(power, (rows, 128)).T[:16, :]
+    powers = jnp.concatenate([powers] * (cols // 128), axis=1)
+    return jnp.concatenate([whole, powers.astype(jnp.int32).astype(jnp.int16)], axis=0)
+
+
+def unpacked_rows(message):
+    rows, cols = message.shape[0] - 16, message.shape[1]
+    whole = message[:rows, :].astype(jnp.int32).astype(F32)
+    powers = message[rows:, :128].astype(jnp.int32).astype(F32)[0:1, :]
+    scale = jnp.exp2(jnp.broadcast_to(powers, (128, 128)).T[:rows, :] - 14.0)
+    return whole * jnp.concatenate([scale] * (cols // 128), axis=1)
+
+
+def degree_body(sums, other_sums, seeds, degree_out, vectors_out, message):
     degree = sums[...] + swapped(other_sums[...])
     scale = lax.rsqrt(degree)
     degree_out[...] = degree
-    vectors_out[...] = seeds[...] * per_row(scale, seeds.shape[0] // 2)
+    vectors = seeds[...] * per_row(scale, seeds.shape[0] // 2)
+    vectors_out[...] = vectors
+    message[...] = packed_rows(vectors)
 
 
 def ahead_body(relays, vectors, h1, l1, h2, l2, ahead):
@@ -133,12 +153,14 @@
     for tile_high, tile_low in ((h1, l1), (h2, l2)):
         product = dot(both, tile_high[...])
         products.append(product[:width] + product[width:] + dot(high, tile_low[...]))
-    ahead[:width, :] = chosen(relays, products[1], products[0])
-    ahead[width:, :] = chosen(relays, products[0], products[1])
-
-
-def combine_body(total, other_total, degree, vectors_out):
-    vectors_out[...] = (total[...] + swapped(other_total[...])) / per_row(degree[...], total.shape[0] // 2)
+    ahead[...] = packed_rows(jnp.concatenate([
+        chosen(relays, products[1], products[0]), chosen(relays, products[0], products[1])], axis=0))
+
+
+def combine_body(total, other_total, degree, vectors_out, message):
+    vectors = (total[...] + swapped(other_total[...])) / per_row(degree[...], total.shape[0] // 2)
+    vectors_out[...] = vectors
+    message[...] = packed_rows(vectors)
 
 
 def product_rows(vectors, tile_high, tile_low):
@@ -158,10 +180,11 @@
     out[...] = stacked(product_rows(vectors[:vectors.shape[0] // 2, :], h0, l0))
 
 
-def far_product(relays, near, h1, l1, h2, l2):
+def far_product(relays, message, h1, l1, h2, l2):
+    near = unpacked_rows(message)
     width = near.shape[0] // 2
-    first = chosen(relays, near[width:, :], near[:width, :])
-    second = chosen(relays, near[:width, :], near[width:, :])
+    first = chosen(relays, near[width:], near[:width])
+    second = chosen(relays, near[:width], near[width:])
     return product_rows(first, h1, l1) + product_rows(second, h2, l2)
 
 
@@ -170,7 +193,7 @@
 
 
 def add_body(total, behind, out):
-    out[...] = total[...] + behind[...]
+    out[...] = total[...] + unpacked_rows(behind)
 
 
 def low_body(degree, v0, v1, v2, moments, scaled):
@@ -497,20 +520,22 @@
 
     small = dict(flops=10**6, nbytes=10**5)
     middle = dict(flops=10**9, nbytes=10**6)
-    degree, vectors = call(
-        degree_body, [row_shape, pair_shape], [sums, between_cores(sums), seeds], **small)
+    message_shape = ((2 * NVEC + 16, size), jnp.int16)
+    degree, vectors, message = call(
+        degree_body, [row_shape, pair_shape, message_shape], [sums, between_cores(sums), seeds], **small)
     far = [h1, l1, h2, l2]
     history = [vectors]
     for _ in range(2):
-        near = between_blocks(vectors, -1)
-        (ahead,) = call(ahead_body, [pair_shape], [relays, vectors, *far], **middle)
+        near = between_blocks(message, -1)
+        (ahead,) = call(ahead_body, [message_shape], [relays, vectors, *far], **middle)
         behind = between_blocks(ahead, 1)
         (product,) = call(own_product_body, [pair_shape], [vectors, h0, l0], **middle)
         (total,) = call(near_product_body, [pair_shape], [relays, product, near, *far], **middle)
         (total,) = call(add_body, [pair_shape], [total, behind], **small)
-        (vectors,) = call(combine_body, [pair_shape], [total, between_cores(total), degree], **small)
+        vectors, message = call(
+            combine_body, [pair_shape, message_shape], [total, between_cores(total), degree], **small)
         history.append(vectors)
-    near = between_blocks(vectors, -1)
+    near = between_blocks(message, -1)
     low, scaled = call(
         low_body, [((5 * NVEC, NVEC), F32), ((3 * NVEC, size), F32)], [degree] + history, **middle)
     (product,) = call(own_product_body, [pair_shape], [vectors, h0, l0], **middle)

time: 106 us -> 102 us (0.962)
  starting transfers between devices: 31.3 us -> 25.8 us
  Pallas kernels: 30.5 us -> 31.7 us
    ppermute x3, starting transfers between devices: 4.19 us -> 0.61 us  [total_over_blocks(): lax.ppermute(values, 'blk', [(i, i ^ span) for i in range(blocks)])]
    ppermute x3, waiting for transfers between devices: 9.22 us -> 11.9 us  [total_over_blocks(): lax.ppermute(values, 'blk', [(i, i ^ span) for i in range(blocks)])]
    ppermute x6, waiting for transfers between devices: 20.1 us -> 17.6 us  [between_blocks(): return lax.ppermute(shard, ('blk', 'narrow'), pairs)]
    ppermute x6, starting transfers between devices: 16.5 us -> 14.9 us  [between_blocks(): return lax.ppermute(shard, ('blk', 'narrow'), pairs)]
    pallas_call x18, Pallas kernels: 30.5 us -> 31.7 us  [call(): pl.pallas_call(body, out_shape=[jax.ShapeDtypeStruct(shape, dtype) for sh...]
  transfers between devices with their start and end apart: 20 -> 20, of which waited for: 15 -> 15; matrix products, arithmetic and copies ran while one was open for 3% -> 3% of each run, Pallas kernels for 8% -> 9%
where the time goes in v13:
time: 102 us
  waiting for transfers between devices  39.7 us (39%)
  Pallas kernels  31.7 us (31%)
  starting transfers between devices  25.8 us (25%)
  between operations  2.25 us (2%)
  local copies, waits for them, and re-layouts  1.83 us (2%)
    pallas_call x18, Pallas kernels, call(): pl.pallas_call(body, out_shape=[jax.ShapeDtypeStruct(shape, dtype) for sh...  31.7 us
    ppermute x6, waiting for transfers between devices, between_blocks(): return lax.ppermute(shard, ('blk', 'narrow'), pairs)  17.6 us
    ppermute x6, starting transfers between devices, between_blocks(): return lax.ppermute(shard, ('blk', 'narrow'), pairs)  14.9 us
    ppermute x3, waiting for transfers between devices, total_over_blocks(): lax.ppermute(values, 'blk', [(i, i ^ span) for i in range(blocks)])  11.9 us
    ppermute x4, starting transfers between devices, between_shards(): return lax.ppermute(shard, ('blk', 'narrow'), pairs)  7.24 us
    ppermute x7, waiting for transfers between devices, between_cores(): return lax.ppermute(shard, 'narrow', [(0, 1), (1, 0)])  5.78 us
    ppermute x4, waiting for transfers between devices, between_shards(): return lax.ppermute(shard, ('blk', 'narrow'), pairs)  4.43 us
    ppermute x7, starting transfers between devices, between_cores(): return lax.ppermute(shard, 'narrow', [(0, 1), (1, 0)])  3.03 us
  transfers between devices with their start and end apart: 20, of which 15 were waited for; matrix products, arithmetic and copies ran while one was open for 3% of the time, Pallas kernels for 9%

profile of v13, /device:TPU:0, one launch (start us, length us, event | category | flops | bytes accessed | tf_op | source)
XLA Modules:
  0.0 102.2 jit_solution(3104641728388104008)
XLA Ops:
  0.0 0.5 collective-permute-start.2
  0.5 2.5 %collective-permute-start = (bf16[384,768]{1,0:T(8,128)(2,1)}, bf16[384,768]{1,0:T(8,128)(2,1)S(1)}, u32[]{:S(2)}, u32[]{:S(2)}) collective-permute-start(bf16[384,768]{1,0:T(8,128)(2,1)} %own.1), channel_id=1, source_target_pairs={{2,0},{6,4},{10,8},{14,12},{1,13},{3,15},{5,1},{7,3},{9,5},{11,7},... | collective-permute-start | bytes 1769480 | tf_op jit(solution)/shard_map/ppermute | solution.py:495
  3.0 0.9 multiply_bitcast_fusion
  3.9 2.4 %collective-permute-start.1 = (f32[64,384]{1,0:T(8,128)S(1)}, f32[64,384]{1,0:T(8,128)S(1)}, u32[]{:S(2)}, u32[]{:S(2)}) collective-permute-start(f32[64,384]{1,0:T(8,128)S(1)} %multiply_bitcast_fusion), channel_id=1, source_target_pairs={{0,1},{1,0},{2,3},{3,2},{4,5},{5,4},{6,7},{7,6},{8,9},{9,8},{10,11... | collective-permute-start | bytes 294920 | tf_op jit(solution)/shard_map/ppermute | solution.py:465
  6.3 3.3 %collective-permute-start.3 = (bf16[384,768]{1,0:T(8,128)(2,1)}, bf16[384,768]{1,0:T(8,128)(2,1)S(1)}, u32[]{:S(2)}, u32[]{:S(2)}) collective-permute-start(bf16[384,768]{1,0:T(8,128)(2,1)} %own.1), channel_id=1, source_target_pairs={{3,0},{7,4},{11,8},{15,12},{0,13},{2,15},{4,1},{6,3},{8,5},{10,7},... | collective-permute-start | bytes 1769480 | tf_op jit(solution)/shard_map/ppermute | solution.py:495
  9.6 1.3 %dynamic_slice.3 = s32[1,1]{0,1:T(1,128)} dynamic-slice(s32[8,2]{0,1:T(2,128)} %param.5, s32[]{:T(128)S(6)} %select_n.25, s32[]{:T(128)S(6)} %select_n.26), dynamic_slice_sizes={1,1} | dynamic-slice | bytes 12 | tf_op jit(solution)/shard_map/dynamic_slice | solution.py:500
  11.6 1.9 %shard_map.46 = (bf16[768,384]{1,0:T(8,128)(2,1)S(1)}, bf16[768,384]{1,0:T(8,128)(2,1)S(1)}, f32[16,384]{1,0:T(8,128)S(1)}, f32[768,128]{1,0:T(8,128)S(1)}, bf16...) custom-call(bf16[384,768]{1,0:T(8,128)(2,1)S(1)} %copy-done, bf16[384,768]{1,0:T(8,128)(2,1)S(1)} %collective-permute-done.2.other), custom_call_target="tpu_custom_call" | custom-call | flops 2000000000 | bytes 1000000 | tf_op jit(solution)/shard_map/pallas_call | solution.py:32
  13.5 0.7 collective-permute-start.5
  14.2 4.4 %collective-permute-done.3.direct = bf16[384,768]{1,0:T(8,128)(2,1)S(1)} collective-permute-done((bf16[384,768]{1,0:T(8,128)(2,1)}, bf16[384,768]{1,0:T(8,128)(2,1)S(1)}, u32[]{:S(2)}, u32[]{:S(2)}) %collective-permute-start.3) | collective-permute-done | bytes 589856 | tf_op jit(solution)/shard_map/ppermute | solution.py:495
  18.6 0.7 collective-permute-start.4
  19.3 0.5 slice.4
  20.5 2.0 %shard_map.47 = (bf16[768,384]{1,0:T(8,128)(2,1)S(1)}, bf16[768,384]{1,0:T(8,128)(2,1)S(1)}, f32[16,384]{1,0:T(8,128)S(1)}, f32[8,384]{1,0:T(8,128)S(1)}) custom-call(f32[8,128]{1,0:T(8,128)S(1)} %broadcast_in_dim.22.keep, f32[8,128]{1,0:T(8,128)S(1)} %broadcast_in_dim.23.relays, f32[8,128]{1,0:T(8,128)S(1)} %get-tuple-element.40.token, ...), custom_call_target="tpu_custom_call" | custom-call | flops 2000000000 | bytes 1000000 | tf_op jit(solution)/shard_map/pallas_call | solution.py:32
  22.5 2.0 %shard_map.48 = (bf16[768,384]{1,0:T(8,128)(2,1)S(1)}, bf16[768,384]{1,0:T(8,128)(2,1)S(1)}, f32[16,384]{1,0:T(8,128)S(1)}, f32[8,384]{1,0:T(8,128)S(1)}) custom-call(f32[8,128]{1,0:T(8,128)S(1)} %broadcast_in_dim.22.keep, f32[8,128]{1,0:T(8,128)S(1)} %broadcast_in_dim.23.relays, f32[8,128]{1,0:T(8,128)S(1)} %get-tuple-element.40.token, ...), custom_call_target="tpu_custom_call" | custom-call | flops 2000000000 | bytes 1000000 | tf_op jit(solution)/shard_map/pallas_call | solution.py:32
  24.5 9.7 %collective-permute-start.6 = (f32[16,384]{1,0:T(8,128)S(1)}, f32[16,384]{1,0:T(8,128)S(1)}, u32[]{:S(2)}, u32[]{:S(2)}) collective-permute-start(f32[16,384]{1,0:T(8,128)S(1)} %pad_maximum_fusion.1), channel_id=1, source_target_pairs={{0,2},{1,5},{2,4},{3,7},{4,6},{5,9},{6,8},{7,11},{8,10},{9,13},{10... | collective-permute-start | bytes 73736 | tf_op jit(solution)/shard_map/ppermute | solution.py:461
  34.2 3.6 %collective-permute-done.6 = f32[16,384]{1,0:T(8,128)S(1)} collective-permute-done((f32[16,384]{1,0:T(8,128)S(1)}, f32[16,384]{1,0:T(8,128)S(1)}, u32[]{:S(2)}, u32[]{:S(2)}) %collective-permute-start.6) | collective-permute-done | bytes 24608 | tf_op jit(solution)/shard_map/ppermute | solution.py:461
  37.9 1.2 %collective-permute-done.7.other_sums = f32[16,384]{1,0:T(8,128)S(1)} collective-permute-done((f32[16,384]{1,0:T(8,128)S(1)}, f32[16,384]{1,0:T(8,128)S(1)}, u32[]{:S(2)}, u32[]{:S(2)}) %collective-permute-start.7) | collective-permute-done | bytes 24608 | tf_op jit(solution)/shard_map/ppermute | solution.py:465
  39.0 0.2 shard_map.49
  39.2 2.0 %collective-permute-start.8 = (s16[144,384]{1,0:T(8,128)(2,1)S(1)}, s16[144,384]{1,0:T(8,128)(2,1)S(1)}, u32[]{:S(2)}, u32[]{:S(2)}) collective-permute-start(s16[144,384]{1,0:T(8,128)(2,1)S(1)} %get-tuple-element.56), channel_id=1, source_target_pairs={{0,14},{1,13},{2,0},{3,15},{4,2},{5,1},{6,4},{7,3},{8,6},{9,5},{10... | collective-permute-start | bytes 331784 | tf_op jit(solution)/shard_map/ppermute | solution.py:461
  41.3 0.7 shard_map.52
  42.0 0.5 shard_map.50.product
  42.5 1.9 %collective-permute-done.8.near = s16[144,384]{1,0:T(8,128)(2,1)S(1)} collective-permute-done((s16[144,384]{1,0:T(8,128)(2,1)S(1)}, s16[144,384]{1,0:T(8,128)(2,1)S(1)}, u32[]{:S(2)}, u32[]{:S(2)}) %collective-permute-start.8) | collective-permute-done | bytes 110624 | tf_op jit(solution)/shard_map/ppermute | solution.py:461
  44.3 0.9 shard_map.51.total
  45.2 4.2 %collective-permute-done.9.behind = s16[144,384]{1,0:T(8,128)(2,1)S(1)} collective-permute-done((s16[144,384]{1,0:T(8,128)(2,1)S(1)}, s16[144,384]{1,0:T(8,128)(2,1)S(1)}, u32[]{:S(2)}, u32[]{:S(2)}) %collective-permute-start.9) | collective-permute-done | bytes 110624 | tf_op jit(solution)/shard_map/ppermute | solution.py:461
  49.4 0.1 shard_map.53.total
  49.6 1.4 %collective-permute-done.10.other_total = f32[128,384]{1,0:T(8,128)S(1)} collective-permute-done((f32[128,384]{1,0:T(8,128)S(1)}, f32[128,384]{1,0:T(8,128)S(1)}, u32[]{:S(2)}, u32[]{:S(2)}) %collective-permute-start.10) | collective-permute-done | bytes 196640 | tf_op jit(solution)/shard_map/ppermute | solution.py:465
  51.0 0.2 shard_map.54
  51.2 1.0 %collective-permute-start.11 = (s16[144,384]{1,0:T(8,128)(2,1)S(1)}, s16[144,384]{1,0:T(8,128)(2,1)S(1)}, u32[]{:S(2)}, u32[]{:S(2)}) collective-permute-start(s16[144,384]{1,0:T(8,128)(2,1)S(1)} %get-tuple-element.62), channel_id=1, source_target_pairs={{0,14},{1,13},{2,0},{3,15},{4,2},{5,1},{6,4},{7,3},{8,6},{9,5},{10... | collective-permute-start | bytes 331784 | tf_op jit(solution)/shard_map/ppermute | solution.py:461
  52.2 0.7 shard_map.57
  52.9 1.1 %collective-permute-start.12 = (s16[144,384]{1,0:T(8,128)(2,1)S(1)}, s16[144,384]{1,0:T(8,128)(2,1)S(1)}, u32[]{:S(2)}, u32[]{:S(2)}) collective-permute-start(s16[144,384]{1,0:T(8,128)(2,1)S(1)} %shard_map.57), channel_id=1, source_target_pairs={{0,2},{1,5},{2,4},{3,7},{4,6},{5,9},{6,8},{7,11},{8,10},{9,13},{10... | collective-permute-start | bytes 331784 | tf_op jit(solution)/shard_map/ppermute | solution.py:461
  54.0 0.5 shard_map.55.product
  54.4 1.5 %collective-permute-done.11.near = s16[144,384]{1,0:T(8,128)(2,1)S(1)} collective-permute-done((s16[144,384]{1,0:T(8,128)(2,1)S(1)}, s16[144,384]{1,0:T(8,128)(2,1)S(1)}, u32[]{:S(2)}, u32[]{:S(2)}) %collective-permute-start.11) | collective-permute-done | bytes 110624 | tf_op jit(solution)/shard_map/ppermute | solution.py:461
  56.0 0.9 shard_map.56.total
  56.9 3.5 %collective-permute-done.12.behind = s16[144,384]{1,0:T(8,128)(2,1)S(1)} collective-permute-done((s16[144,384]{1,0:T(8,128)(2,1)S(1)}, s16[144,384]{1,0:T(8,128)(2,1)S(1)}, u32[]{:S(2)}, u32[]{:S(2)}) %collective-permute-start.12) | collective-permute-done | bytes 110624 | tf_op jit(solution)/shard_map/ppermute | solution.py:461
  60.4 0.1 shard_map.58.total
  60.6 1.4 %collective-permute-done.13.other_total = f32[128,384]{1,0:T(8,128)S(1)} collective-permute-done((f32[128,384]{1,0:T(8,128)S(1)}, f32[128,384]{1,0:T(8,128)S(1)}, u32[]{:S(2)}, u32[]{:S(2)}) %collective-permute-start.13) | collective-permute-done | bytes 196640 | tf_op jit(solution)/shard_map/ppermute | solution.py:465
  62.0 0.2 shard_map.59
  62.2 1.0 %collective-permute-start.14 = (s16[144,384]{1,0:T(8,128)(2,1)S(1)}, s16[144,384]{1,0:T(8,128)(2,1)S(1)}, u32[]{:S(2)}, u32[]{:S(2)}) collective-permute-start(s16[144,384]{1,0:T(8,128)(2,1)S(1)} %get-tuple-element.65), channel_id=1, source_target_pairs={{0,14},{1,13},{2,0},{3,15},{4,2},{5,1},{6,4},{7,3},{8,6},{9,5},{10... | collective-permute-start | bytes 331784 | tf_op jit(solution)/shard_map/ppermute | solution.py:461
  63.2 0.5 shard_map.61.product
  63.7 0.5 shard_map.60
  64.2 2.9 %collective-permute-done.14.near = s16[144,384]{1,0:T(8,128)(2,1)S(1)} collective-permute-done((s16[144,384]{1,0:T(8,128)(2,1)S(1)}, s16[144,384]{1,0:T(8,128)(2,1)S(1)}, u32[]{:S(2)}, u32[]{:S(2)}) %collective-permute-start.14) | collective-permute-done | bytes 110624 | tf_op jit(solution)/shard_map/ppermute | solution.py:461
  67.1 1.5 %shard_map.62 = (f32[56,128]{1,0:T(8,128)S(1)}, f32[56,128]{1,0:T(8,128)S(1)}) custom-call(f32[8,128]{1,0:T(8,128)S(1)} %broadcast_in_dim.19.core.refs_0_, f32[8,128]{1,0:T(8,128)S(1)} %broadcast_in_dim.23.relays, f32[320,64]{1,0:T(8,128)S(1)} %get-tuple-element.64.low, f32[128,384]{1,0:T(8,128)S(1)} %get-tuple-element.63.v2.vectors, ...), custom_call_target="tpu_custom_call" | custom-call | flops 1000000000 | bytes 1000000 | tf_op jit(solution)/shard_map/pallas_call | solution.py:32
  68.7 1.2 %collective-permute-done.15 = f32[56,128]{1,0:T(8,128)S(1)} collective-permute-done((f32[56,128]{1,0:T(8,128)S(1)}, f32[56,128]{1,0:T(8,128)S(1)}, u32[]{:S(2)}, u32[]{:S(2)}) %collective-permute-start.15) | collective-permute-done | bytes 28704 | tf_op jit(solution)/shard_map/ppermute | solution.py:465
  69.9 3.9 %collective-permute-done.16 = f32[56,128]{1,0:T(8,128)S(1)} collective-permute-done((f32[56,128]{1,0:T(8,128)S(1)}, f32[56,128]{1,0:T(8,128)S(1)}, u32[]{:S(2)}, u32[]{:S(2)}) %collective-permute-start.16) | collective-permute-done | bytes 28704 | tf_op jit(solution)/shard_map/ppermute | solution.py:472
  73.8 3.9 %collective-permute-done.17 = f32[56,128]{1,0:T(8,128)S(1)} collective-permute-done((f32[56,128]{1,0:T(8,128)S(1)}, f32[56,128]{1,0:T(8,128)S(1)}, u32[]{:S(2)}, u32[]{:S(2)}) %collective-permute-start.17) | collective-permute-done | bytes 28704 | tf_op jit(solution)/shard_map/ppermute | solution.py:472
  77.7 0.6 collective-permute-start.18
  78.3 4.2 %collective-permute-done.18 = f32[56,128]{1,0:T(8,128)S(1)} collective-permute-done((f32[56,128]{1,0:T(8,128)S(1)}, f32[56,128]{1,0:T(8,128)S(1)}, u32[]{:S(2)}, u32[]{:S(2)}) %collective-permute-start.18) | collective-permute-done | bytes 28704 | tf_op jit(solution)/shard_map/ppermute | solution.py:472
  83.1 0.5 collective-permute-done.19.refs_3_
  83.6 18.6 %shard_map.63 = f32[64,384]{1,0:T(8,128)} custom-call(f32[8,128]{1,0:T(8,128)S(1)} %broadcast_in_dim.19.core.refs_0_, f32[8,128]{1,0:T(8,128)S(1)} %broadcast_in_dim.20.refs_1_, f32[56,128]{1,0:T(8,128)S(1)} %add.32.refs_2_, f32[56,128]{1,0:T(8,128)S(1)} %collective-permute-done.19.refs_3_, f32[192,384]{1,0:T(8,128)S(1)} %get-tuple-element.68.refs_4_), custom_call_target="tpu_custom_call" | custom-call | flops 20000000000 | bytes 1000000 | tf_op jit(solution)/shard_map/pallas_call | solution.py:32
  (43 shorter events, 0.4 us)
Async XLA Ops:
  0.0 11.6 %copy-start = (bf16[384,768]{1,0:T(8,128)(2,1)S(1)}, bf16[384,768]{1,0:T(8,128)(2,1)}, u32[]{:S(2)}) copy-start(bf16[384,768]{1,0:T(8,128)(2,1)} %own.1) | copy-start | bytes 1769476
  0.0 11.6 %collective-permute-start.2 = (bf16[384,768]{1,0:T(8,128)(2,1)}, bf16[384,768]{1,0:T(8,128)(2,1)S(1)}, u32[]{:S(2)}, u32[]{:S(2)}) collective-permute-start(bf16[384,768]{1,0:T(8,128)(2,1)} %own.1), channel_id=1, source_target_pairs={{0,1},{1,0},{2,3},{3,2},{4,5},{5,4},{6,7},{7,6},{8,9},{9,8},{10,11... | collective-permute-start | bytes 1769480 | tf_op jit(solution)/shard_map/ppermute | solution.py:465
  0.5 13.0 %collective-permute-start = (bf16[384,768]{1,0:T(8,128)(2,1)}, bf16[384,768]{1,0:T(8,128)(2,1)S(1)}, u32[]{:S(2)}, u32[]{:S(2)}) collective-permute-start(bf16[384,768]{1,0:T(8,128)(2,1)} %own.1), channel_id=1, source_target_pairs={{2,0},{6,4},{10,8},{14,12},{1,13},{3,15},{5,1},{7,3},{9,5},{11,7},... | collective-permute-start | bytes 1769480 | tf_op jit(solution)/shard_map/ppermute | solution.py:495
  3.9 7.6 %collective-permute-start.1 = (f32[64,384]{1,0:T(8,128)S(1)}, f32[64,384]{1,0:T(8,128)S(1)}, u32[]{:S(2)}, u32[]{:S(2)}) collective-permute-start(f32[64,384]{1,0:T(8,128)S(1)} %multiply_bitcast_fusion), channel_id=1, source_target_pairs={{0,1},{1,0},{2,3},{3,2},{4,5},{5,4},{6,7},{7,6},{8,9},{9,8},{10,11... | collective-permute-start | bytes 294920 | tf_op jit(solution)/shard_map/ppermute | solution.py:465
  6.3 12.4 %collective-permute-start.3 = (bf16[384,768]{1,0:T(8,128)(2,1)}, bf16[384,768]{1,0:T(8,128)(2,1)S(1)}, u32[]{:S(2)}, u32[]{:S(2)}) collective-permute-start(bf16[384,768]{1,0:T(8,128)(2,1)} %own.1), channel_id=1, source_target_pairs={{3,0},{7,4},{11,8},{15,12},{0,13},{2,15},{4,1},{6,3},{8,5},{10,7},... | collective-permute-start | bytes 1769480 | tf_op jit(solution)/shard_map/ppermute | solution.py:495
  13.4 40.5 %copy-start.5 = (bf16[768,384]{1,0:T(8,128)(2,1)}, bf16[768,384]{1,0:T(8,128)(2,1)S(1)}, u32[]{:S(2)}) copy-start(bf16[768,384]{1,0:T(8,128)(2,1)S(1)} %get-tuple-element.54.h0) | copy-start | bytes 1769476
  13.4 40.5 %copy-start.7 = (bf16[768,384]{1,0:T(8,128)(2,1)}, bf16[768,384]{1,0:T(8,128)(2,1)S(1)}, u32[]{:S(2)}) copy-start(bf16[768,384]{1,0:T(8,128)(2,1)S(1)} %get-tuple-element.55.l0) | copy-start | bytes 1769476
  13.5 7.0 %collective-permute-start.5 = (bf16[384,768]{1,0:T(8,128)(2,1)S(1)}, bf16[384,768]{1,0:T(8,128)(2,1)S(1)}, u32[]{:S(2)}, u32[]{:S(2)}) collective-permute-start(bf16[384,768]{1,0:T(8,128)(2,1)S(1)} %collective-permute-done.direct), channel_id=1, source_target_pairs={{1,2},{5,6},{9,10},{13,14},{17,18},{21,22},{25,26},{29,30}} | collective-permute-start | bytes 1769480 | tf_op jit(solution)/shard_map/ppermute | solution.py:495
  18.6 3.8 %collective-permute-start.4 = (bf16[384,768]{1,0:T(8,128)(2,1)S(1)}, bf16[384,768]{1,0:T(8,128)(2,1)S(1)}, u32[]{:S(2)}, u32[]{:S(2)}) collective-permute-start(bf16[384,768]{1,0:T(8,128)(2,1)S(1)} %collective-permute-done.direct), channel_id=1, source_target_pairs={{2,14},{6,2},{10,6},{14,10},{18,30},{22,18},{26,22},{30,26}} | collective-permute-start | bytes 1769480 | tf_op jit(solution)/shard_map/ppermute | solution.py:495
  22.5 33.5 %copy-start.1 = (bf16[768,384]{1,0:T(8,128)(2,1)}, bf16[768,384]{1,0:T(8,128)(2,1)S(1)}, u32[]{:S(2)}) copy-start(bf16[768,384]{1,0:T(8,128)(2,1)S(1)} %get-tuple-element.58.l1) | copy-start | bytes 1769476
  24.5 31.5 %copy-start.3 = (bf16[768,384]{1,0:T(8,128)(2,1)}, bf16[768,384]{1,0:T(8,128)(2,1)S(1)}, u32[]{:S(2)}) copy-start(bf16[768,384]{1,0:T(8,128)(2,1)S(1)} %get-tuple-element.60.l2) | copy-start | bytes 1769476
  24.5 13.3 %collective-permute-start.6 = (f32[16,384]{1,0:T(8,128)S(1)}, f32[16,384]{1,0:T(8,128)S(1)}, u32[]{:S(2)}, u32[]{:S(2)}) collective-permute-start(f32[16,384]{1,0:T(8,128)S(1)} %pad_maximum_fusion.1), channel_id=1, source_target_pairs={{0,2},{1,5},{2,4},{3,7},{4,6},{5,9},{6,8},{7,11},{8,10},{9,13},{10... | collective-permute-start | bytes 73736 | tf_op jit(solution)/shard_map/ppermute | solution.py:461
  37.8 1.2 %collective-permute-start.7 = (f32[16,384]{1,0:T(8,128)S(1)}, f32[16,384]{1,0:T(8,128)S(1)}, u32[]{:S(2)}, u32[]{:S(2)}) collective-permute-start(f32[16,384]{1,0:T(8,128)S(1)} %add.28.sums), channel_id=1, source_target_pairs={{0,1},{1,0},{2,3},{3,2},{4,5},{5,4},{6,7},{7,6},{8,9},{9,8},{10,11... | collective-permute-start | bytes 73736 | tf_op jit(solution)/shard_map/ppermute | solution.py:465
  39.2 5.1 %collective-permute-start.8 = (s16[144,384]{1,0:T(8,128)(2,1)S(1)}, s16[144,384]{1,0:T(8,128)(2,1)S(1)}, u32[]{:S(2)}, u32[]{:S(2)}) collective-permute-start(s16[144,384]{1,0:T(8,128)(2,1)S(1)} %get-tuple-element.56), channel_id=1, source_target_pairs={{0,14},{1,13},{2,0},{3,15},{4,2},{5,1},{6,4},{7,3},{8,6},{9,5},{10... | collective-permute-start | bytes 331784 | tf_op jit(solution)/shard_map/ppermute | solution.py:461
  41.9 7.5 %collective-permute-start.9 = (s16[144,384]{1,0:T(8,128)(2,1)S(1)}, s16[144,384]{1,0:T(8,128)(2,1)S(1)}, u32[]{:S(2)}, u32[]{:S(2)}) collective-permute-start(s16[144,384]{1,0:T(8,128)(2,1)S(1)} %shard_map.52), channel_id=1, source_target_pairs={{0,2},{1,5},{2,4},{3,7},{4,6},{5,9},{6,8},{7,11},{8,10},{9,13},{10... | collective-permute-start | bytes 331784 | tf_op jit(solution)/shard_map/ppermute | solution.py:461
  49.5 1.5 %collective-permute-start.10 = (f32[128,384]{1,0:T(8,128)S(1)}, f32[128,384]{1,0:T(8,128)S(1)}, u32[]{:S(2)}, u32[]{:S(2)}) collective-permute-start(f32[128,384]{1,0:T(8,128)S(1)} %shard_map.53.total), channel_id=1, source_target_pairs={{0,1},{1,0},{2,3},{3,2},{4,5},{5,4},{6,7},{7,6},{8,9},{9,8},{10,11... | collective-permute-start | bytes 589832 | tf_op jit(solution)/shard_map/ppermute | solution.py:465
  51.2 4.8 %collective-permute-start.11 = (s16[144,384]{1,0:T(8,128)(2,1)S(1)}, s16[144,384]{1,0:T(8,128)(2,1)S(1)}, u32[]{:S(2)}, u32[]{:S(2)}) collective-permute-start(s16[144,384]{1,0:T(8,128)(2,1)S(1)} %get-tuple-element.62), channel_id=1, source_target_pairs={{0,14},{1,13},{2,0},{3,15},{4,2},{5,1},{6,4},{7,3},{8,6},{9,5},{10... | collective-permute-start | bytes 331784 | tf_op jit(solution)/shard_map/ppermute | solution.py:461
  52.9 7.5 %collective-permute-start.12 = (s16[144,384]{1,0:T(8,128)(2,1)S(1)}, s16[144,384]{1,0:T(8,128)(2,1)S(1)}, u32[]{:S(2)}, u32[]{:S(2)}) collective-permute-start(s16[144,384]{1,0:T(8,128)(2,1)S(1)} %shard_map.57), channel_id=1, source_target_pairs={{0,2},{1,5},{2,4},{3,7},{4,6},{5,9},{6,8},{7,11},{8,10},{9,13},{10... | collective-permute-start | bytes 331784 | tf_op jit(solution)/shard_map/ppermute | solution.py:461
  56.0 7.2 %copy-start.8 = (bf16[768,384]{1,0:T(8,128)(2,1)S(1)}, bf16[768,384]{1,0:T(8,128)(2,1)}, u32[]{:S(2)}) copy-start(bf16[768,384]{1,0:T(8,128)(2,1)} %copy-done.7) | copy-start | bytes 1769476
  56.9 6.3 %copy-start.6 = (bf16[768,384]{1,0:T(8,128)(2,1)S(1)}, bf16[768,384]{1,0:T(8,128)(2,1)}, u32[]{:S(2)}) copy-start(bf16[768,384]{1,0:T(8,128)(2,1)} %copy-done.5) | copy-start | bytes 1769476
  60.5 1.5 %collective-permute-start.13 = (f32[128,384]{1,0:T(8,128)S(1)}, f32[128,384]{1,0:T(8,128)S(1)}, u32[]{:S(2)}, u32[]{:S(2)}) collective-permute-start(f32[128,384]{1,0:T(8,128)S(1)} %shard_map.58.total), channel_id=1, source_target_pairs={{0,1},{1,0},{2,3},{3,2},{4,5},{5,4},{6,7},{7,6},{8,9},{9,8},{10,11... | collective-permute-start | bytes 589832 | tf_op jit(solution)/shard_map/ppermute | solution.py:465
  62.2 5.0 %collective-permute-start.14 = (s16[144,384]{1,0:T(8,128)(2,1)S(1)}, s16[144,384]{1,0:T(8,128)(2,1)S(1)}, u32[]{:S(2)}, u32[]{:S(2)}) collective-permute-start(s16[144,384]{1,0:T(8,128)(2,1)S(1)} %get-tuple-element.65), channel_id=1, source_target_pairs={{0,14},{1,13},{2,0},{3,15},{4,2},{5,1},{6,4},{7,3},{8,6},{9,5},{10... | collective-permute-start | bytes 331784 | tf_op jit(solution)/shard_map/ppermute | solution.py:461
  63.7 3.4 %copy-start.2 = (bf16[768,384]{1,0:T(8,128)(2,1)S(1)}, bf16[768,384]{1,0:T(8,128)(2,1)}, u32[]{:S(2)}) copy-start(bf16[768,384]{1,0:T(8,128)(2,1)} %copy-done.1) | copy-start | bytes 1769476
  63.7 3.4 %copy-start.4 = (bf16[768,384]{1,0:T(8,128)(2,1)S(1)}, bf16[768,384]{1,0:T(8,128)(2,1)}, u32[]{:S(2)}) copy-start(bf16[768,384]{1,0:T(8,128)(2,1)} %copy-done.3) | copy-start | bytes 1769476
  68.6 1.3 %collective-permute-start.15 = (f32[56,128]{1,0:T(8,128)S(1)}, f32[56,128]{1,0:T(8,128)S(1)}, u32[]{:S(2)}, u32[]{:S(2)}) collective-permute-start(f32[56,128]{1,0:T(8,128)S(1)} %get-tuple-element.67), channel_id=1, source_target_pairs={{0,1},{1,0},{2,3},{3,2},{4,5},{5,4},{6,7},{7,6},{8,9},{9,8},{10,11... | collective-permute-start | bytes 86024 | tf_op jit(solution)/shard_map/ppermute | solution.py:465
  69.9 3.9 %collective-permute-start.16 = (f32[56,128]{1,0:T(8,128)S(1)}, f32[56,128]{1,0:T(8,128)S(1)}, u32[]{:S(2)}, u32[]{:S(2)}) collective-permute-start(f32[56,128]{1,0:T(8,128)S(1)} %add.29), channel_id=1, source_target_pairs={{0,2},{2,0},{4,6},{6,4},{8,10},{10,8},{12,14},{14,12},{1,3},{3,1},... | collective-permute-start | bytes 86024 | tf_op jit(solution)/shard_map/ppermute | solution.py:472
  73.8 3.9 %collective-permute-start.17 = (f32[56,128]{1,0:T(8,128)S(1)}, f32[56,128]{1,0:T(8,128)S(1)}, u32[]{:S(2)}, u32[]{:S(2)}) collective-permute-start(f32[56,128]{1,0:T(8,128)S(1)} %add.30), channel_id=1, source_target_pairs={{0,4},{2,6},{4,0},{6,2},{8,12},{10,14},{12,8},{14,10},{1,5},{3,7},... | collective-permute-start | bytes 86024 | tf_op jit(solution)/shard_map/ppermute | solution.py:472
  77.7 4.8 %collective-permute-start.18 = (f32[56,128]{1,0:T(8,128)S(1)}, f32[56,128]{1,0:T(8,128)S(1)}, u32[]{:S(2)}, u32[]{:S(2)}) collective-permute-start(f32[56,128]{1,0:T(8,128)S(1)} %add.31), channel_id=1, source_target_pairs={{0,8},{2,10},{4,12},{6,14},{8,0},{10,2},{12,4},{14,6},{1,9},{3,11}... | collective-permute-start | bytes 86024 | tf_op jit(solution)/shard_map/ppermute | solution.py:472
  82.4 1.2 %collective-permute-start.19 = (f32[56,128]{1,0:T(8,128)S(1)}, f32[56,128]{1,0:T(8,128)S(1)}, u32[]{:S(2)}, u32[]{:S(2)}) collective-permute-start(f32[56,128]{1,0:T(8,128)S(1)} %add.32.refs_2_), channel_id=1, source_target_pairs={{0,1},{1,0},{2,3},{3,2},{4,5},{5,4},{6,7},{7,6},{8,9},{9,8},{10,11... | collective-permute-start | bytes 86024 | tf_op jit(solution)/shard_map/ppermute | solution.py:465

commit v14 on v13

--- a/solution.py
+++ b/solution.py
@@ -145,7 +145,7 @@
     message[...] = packed_rows(vectors)
 
 
-def ahead_body(relays, vectors, h1, l1, h2, l2, ahead):
+def ahead_body(vectors, h1, l1, h2, l2, ahead):
     width = vectors.shape[0] // 2
     high, low = halves(jnp.concatenate([vectors[:width, :], vectors[width:, :]], axis=1))
     both = jnp.concatenate([high, low], axis=0)
@@ -153,8 +153,7 @@
     for tile_high, tile_low in ((h1, l1), (h2, l2)):
         product = dot(both, tile_high[...])
         products.append(product[:width] + product[width:] + dot(high, tile_low[...]))
-    ahead[...] = packed_rows(jnp.concatenate([
-        chosen(relays, products[1], products[0]), chosen(relays, products[0], products[1])], axis=0))
+    ahead[...] = packed_rows(jnp.concatenate(products, axis=0))
 
 
 def combine_body(total, other_total, degree, vectors_out, message):
@@ -180,16 +179,14 @@
     out[...] = stacked(product_rows(vectors[:vectors.shape[0] // 2, :], h0, l0))
 
 
-def far_product(relays, message, h1, l1, h2, l2):
+def far_product(message, h1, l1, h2, l2):
     near = unpacked_rows(message)
     width = near.shape[0] // 2
-    first = chosen(relays, near[width:], near[:width])
-    second = chosen(relays, near[:width], near[width:])
-    return product_rows(first, h1, l1) + product_rows(second, h2, l2)
-
-
-def near_product_body(relays, product, near, h1, l1, h2, l2, total):
-    total[...] = product[...] + stacked(far_product(relays, near, h1, l1, h2, l2))
+    return product_rows(near[:width], h1, l1) + product_rows(near[width:], h2, l2)
+
+
+def near_product_body(product, near, h1, l1, h2, l2, total):
+    total[...] = product[...] + stacked(far_product(near, h1, l1, h2, l2))
 
 
 def add_body(total, behind, out):
@@ -214,9 +211,9 @@
     return [lax.broadcasted_iota(jnp.int32, (rows, cols), axis) for axis in range(2)]
 
 
-def moment_body(core, relays, low, vectors, product, near, h1, l1, h2, l2, mine, theirs):
+def moment_body(core, low, vectors, product, near, h1, l1, h2, l2, mine, theirs):
     n = vectors.shape[0] // 2
-    last = far_product(relays, near, h1, l1, h2, l2)
+    last = far_product(near, h1, l1, h2, l2)
     last = 2.0 * last + jnp.concatenate([product[:n, :], product[n:, :]], axis=1)
     last = dot(jnp.concatenate([vectors[:n, :], vectors[n:, :]], axis=1), last, 1, 1)
     moments = [low[i * n:(i + 1) * n, :] for i in range(5)] + [0.5 * (last + last.T)]
@@ -506,16 +503,15 @@
     first, seeds, keep, relays, token = lax.optimization_barrier((first, seeds, keep, relays, token))
     relayed = [first, own_copy]
     if relaying:
+        relayed[0] = between_shards(first, [(2 * i, (i - 2) % blocks * 2) for i in range(1, blocks, 2)])
         forward, second = lax.optimization_barrier((first, second))
-        relayed[1] = between_shards(forward, [(2 * i, (i - 2) % blocks * 2) for i in range(1, blocks, 2)])
-    if relaying:
-        relayed[0] = between_shards(first, [(2 * i + 1, 2 * i + 2) for i in range(0, blocks, 2)])
+        relayed[1] = between_shards(forward, [(2 * i + 1, 2 * i + 2) for i in range(0, blocks, 2)])
     tile_args = [keep, relays, token, own_copy, other_emb, row_sq]
     h1, l1, sums, cols1 = make_tile(
         far_body, [*tile_args, first, relayed[0], sums], size, (((8, size), F32),))
     h2, l2, sums, cols2 = make_tile(
         far_body, [*tile_args, second, relayed[1], sums], size, (((8, size), F32),))
-    cols = jnp.concatenate([jnp.where(relays[0, 0] > 0.5, cols2, cols1), jnp.where(relays[0, 0] > 0.5, cols1, cols2)])
+    cols = jnp.concatenate([cols1, cols2], axis=0)
     sums = sums + between_blocks(cols, 1)
 
     small = dict(flops=10**6, nbytes=10**5)
@@ -527,10 +523,10 @@
     history = [vectors]
     for _ in range(2):
         near = between_blocks(message, -1)
-        (ahead,) = call(ahead_body, [message_shape], [relays, vectors, *far], **middle)
+        (ahead,) = call(ahead_body, [message_shape], [vectors, *far], **middle)
         behind = between_blocks(ahead, 1)
         (product,) = call(own_product_body, [pair_shape], [vectors, h0, l0], **middle)
-        (total,) = call(near_product_body, [pair_shape], [relays, product, near, *far], **middle)
+        (total,) = call(near_product_body, [pair_shape], [product, near, *far], **middle)
         (total,) = call(add_body, [pair_shape], [total, behind], **small)
         vectors, message = call(
             combine_body, [pair_shape, message_shape], [total, between_cores(total), degree], **small)
@@ -541,7 +537,7 @@
     (product,) = call(own_product_body, [pair_shape], [vectors, h0, l0], **middle)
     packed_shape = ((3 * NVEC // 4 + 8, 2 * NVEC), F32)
     mine, theirs = call(
-        moment_body, [packed_shape] * 2, [spread(core), relays, low, vectors, product, near, *far], **middle)
+        moment_body, [packed_shape] * 2, [spread(core), low, vectors, product, near, *far], **middle)
     mine = total_over_blocks(mine + between_cores(theirs))
     rows = size * blocks * lax.axis_size("narrow")
     (out,) = call(

time: 102 us -> 101 us (level)
  waiting for transfers between devices: 39.7 us -> 38.1 us
    ppermute x6, waiting for transfers between devices: 17.6 us -> 16 us  [between_blocks(): return lax.ppermute(shard, ('blk', 'narrow'), pairs)]
    unnamed x18 -> x14, local copies, waits for them, and re-layouts: 0.03 us -> 1.09 us
  transfers between devices with their start and end apart: 20 -> 20, of which waited for: 15 -> 15; matrix products, arithmetic and copies ran while one was open for 3% -> 2% of each run, Pallas kernels for 9% -> 9%
where the time goes in v14:
time: 101 us
  waiting for transfers between devices  38.1 us (38%)
  Pallas kernels  31.6 us (31%)
  starting transfers between devices  26.1 us (26%)
  local copies, waits for them, and re-layouts  2.37 us (2%)
  between operations  1.56 us (2%)
    pallas_call x18, Pallas kernels, call(): pl.pallas_call(body, out_shape=[jax.ShapeDtypeStruct(shape, dtype) for sh...  31.6 us
    ppermute x6, waiting for transfers between devices, between_blocks(): return lax.ppermute(shard, ('blk', 'narrow'), pairs)  16 us
    ppermute x6, starting transfers between devices, between_blocks(): return lax.ppermute(shard, ('blk', 'narrow'), pairs)  15.2 us
    ppermute x3, waiting for transfers between devices, total_over_blocks(): lax.ppermute(values, 'blk', [(i, i ^ span) for i in range(blocks)])  11.9 us
    ppermute x4, starting transfers between devices, between_shards(): return lax.ppermute(shard, ('blk', 'narrow'), pairs)  7.24 us
    ppermute x7, waiting for transfers between devices, between_cores(): return lax.ppermute(shard, 'narrow', [(0, 1), (1, 0)])  5.78 us
    ppermute x4, waiting for transfers between devices, between_shards(): return lax.ppermute(shard, ('blk', 'narrow'), pairs)  4.44 us
    ppermute x7, starting transfers between devices, between_cores(): return lax.ppermute(shard, 'narrow', [(0, 1), (1, 0)])  3.03 us
  transfers between devices with their start and end apart: 20, of which 15 were waited for; matrix products, arithmetic and copies ran while one was open for 2% of the time, Pallas kernels for 9%

profile of v14, /device:TPU:0, one launch (start us, length us, event | category | flops | bytes accessed | tf_op | source)
XLA Modules:
  0.0 100.7 jit_solution(15047506370493215671)
XLA Ops:
  0.0 0.5 collective-permute-start.2
  0.5 2.5 %collective-permute-start = (bf16[384,768]{1,0:T(8,128)(2,1)}, bf16[384,768]{1,0:T(8,128)(2,1)S(1)}, u32[]{:S(2)}, u32[]{:S(2)}) collective-permute-start(bf16[384,768]{1,0:T(8,128)(2,1)} %own.1), channel_id=1, source_target_pairs={{2,0},{6,4},{10,8},{14,12},{1,13},{3,15},{5,1},{7,3},{9,5},{11,7},... | collective-permute-start | bytes 1769480 | tf_op jit(solution)/shard_map/ppermute | solution.py:492
  3.0 0.9 multiply_bitcast_fusion
  3.9 2.4 %collective-permute-start.1 = (f32[64,384]{1,0:T(8,128)S(1)}, f32[64,384]{1,0:T(8,128)S(1)}, u32[]{:S(2)}, u32[]{:S(2)}) collective-permute-start(f32[64,384]{1,0:T(8,128)S(1)} %multiply_bitcast_fusion), channel_id=1, source_target_pairs={{0,1},{1,0},{2,3},{3,2},{4,5},{5,4},{6,7},{7,6},{8,9},{9,8},{10,11... | collective-permute-start | bytes 294920 | tf_op jit(solution)/shard_map/ppermute | solution.py:462
  6.3 3.3 %collective-permute-start.3 = (bf16[384,768]{1,0:T(8,128)(2,1)}, bf16[384,768]{1,0:T(8,128)(2,1)S(1)}, u32[]{:S(2)}, u32[]{:S(2)}) collective-permute-start(bf16[384,768]{1,0:T(8,128)(2,1)} %own.1), channel_id=1, source_target_pairs={{3,0},{7,4},{11,8},{15,12},{0,13},{2,15},{4,1},{6,3},{8,5},{10,7},... | collective-permute-start | bytes 1769480 | tf_op jit(solution)/shard_map/ppermute | solution.py:492
  9.6 1.3 %dynamic_slice.3 = s32[1,1]{0,1:T(1,128)} dynamic-slice(s32[8,2]{0,1:T(2,128)} %param.5, s32[]{:T(128)S(6)} %select_n.13, s32[]{:T(128)S(6)} %select_n.14), dynamic_slice_sizes={1,1} | dynamic-slice | bytes 12 | tf_op jit(solution)/shard_map/dynamic_slice | solution.py:497
  11.6 1.9 %shard_map.46 = (bf16[768,384]{1,0:T(8,128)(2,1)S(1)}, bf16[768,384]{1,0:T(8,128)(2,1)S(1)}, f32[16,384]{1,0:T(8,128)S(1)}, f32[768,128]{1,0:T(8,128)S(1)}, bf16...) custom-call(bf16[384,768]{1,0:T(8,128)(2,1)S(1)} %copy-done, bf16[384,768]{1,0:T(8,128)(2,1)S(1)} %collective-permute-done.2.other), custom_call_target="tpu_custom_call" | custom-call | flops 2000000000 | bytes 1000000 | tf_op jit(solution)/shard_map/pallas_call | solution.py:32
  13.5 0.7 collective-permute-start.5
  14.2 4.4 %collective-permute-done.3.direct = bf16[384,768]{1,0:T(8,128)(2,1)S(1)} collective-permute-done((bf16[384,768]{1,0:T(8,128)(2,1)}, bf16[384,768]{1,0:T(8,128)(2,1)S(1)}, u32[]{:S(2)}, u32[]{:S(2)}) %collective-permute-start.3) | collective-permute-done | bytes 589856 | tf_op jit(solution)/shard_map/ppermute | solution.py:492
  18.6 0.7 collective-permute-start.4
  19.3 2.0 %shard_map.47 = (bf16[768,384]{1,0:T(8,128)(2,1)S(1)}, bf16[768,384]{1,0:T(8,128)(2,1)S(1)}, f32[16,384]{1,0:T(8,128)S(1)}, f32[8,384]{1,0:T(8,128)S(1)}) custom-call(f32[8,128]{1,0:T(8,128)S(1)} %broadcast_in_dim.22.keep, f32[8,128]{1,0:T(8,128)S(1)} %broadcast_in_dim.23.relays, f32[8,128]{1,0:T(8,128)S(1)} %get-tuple-element.40.token, ...), custom_call_target="tpu_custom_call" | custom-call | flops 2000000000 | bytes 1000000 | tf_op jit(solution)/shard_map/pallas_call | solution.py:32
  21.3 2.0 %shard_map.48 = (bf16[768,384]{1,0:T(8,128)(2,1)S(1)}, bf16[768,384]{1,0:T(8,128)(2,1)S(1)}, f32[16,384]{1,0:T(8,128)S(1)}, f32[8,384]{1,0:T(8,128)S(1)}) custom-call(f32[8,128]{1,0:T(8,128)S(1)} %broadcast_in_dim.22.keep, f32[8,128]{1,0:T(8,128)S(1)} %broadcast_in_dim.23.relays, f32[8,128]{1,0:T(8,128)S(1)} %get-tuple-element.40.token, ...), custom_call_target="tpu_custom_call" | custom-call | flops 2000000000 | bytes 1000000 | tf_op jit(solution)/shard_map/pallas_call | solution.py:32
  23.3 10.0 %collective-permute-start.6 = (f32[16,384]{1,0:T(8,128)S(1)}, f32[16,384]{1,0:T(8,128)S(1)}, u32[]{:S(2)}, u32[]{:S(2)}) collective-permute-start(f32[16,384]{1,0:T(8,128)S(1)} %pad_maximum_fusion.1), channel_id=1, source_target_pairs={{0,2},{1,5},{2,4},{3,7},{4,6},{5,9},{6,8},{7,11},{8,10},{9,13},{10... | collective-permute-start | bytes 73736 | tf_op jit(solution)/shard_map/ppermute | solution.py:458
  33.3 3.1 %collective-permute-done.6 = f32[16,384]{1,0:T(8,128)S(1)} collective-permute-done((f32[16,384]{1,0:T(8,128)S(1)}, f32[16,384]{1,0:T(8,128)S(1)}, u32[]{:S(2)}, u32[]{:S(2)}) %collective-permute-start.6) | collective-permute-done | bytes 24608 | tf_op jit(solution)/shard_map/ppermute | solution.py:458
  36.4 1.2 %collective-permute-done.7.other_sums = f32[16,384]{1,0:T(8,128)S(1)} collective-permute-done((f32[16,384]{1,0:T(8,128)S(1)}, f32[16,384]{1,0:T(8,128)S(1)}, u32[]{:S(2)}, u32[]{:S(2)}) %collective-permute-start.7) | collective-permute-done | bytes 24608 | tf_op jit(solution)/shard_map/ppermute | solution.py:462
  37.6 0.2 shard_map.49
  37.8 2.0 %collective-permute-start.8 = (s16[144,384]{1,0:T(8,128)(2,1)S(1)}, s16[144,384]{1,0:T(8,128)(2,1)S(1)}, u32[]{:S(2)}, u32[]{:S(2)}) collective-permute-start(s16[144,384]{1,0:T(8,128)(2,1)S(1)} %get-tuple-element.56), channel_id=1, source_target_pairs={{0,14},{1,13},{2,0},{3,15},{4,2},{5,1},{6,4},{7,3},{8,6},{9,5},{10... | collective-permute-start | bytes 331784 | tf_op jit(solution)/shard_map/ppermute | solution.py:458
  39.8 0.6 shard_map.52
  40.5 0.5 shard_map.50.product
  41.0 1.9 %collective-permute-done.8.near = s16[144,384]{1,0:T(8,128)(2,1)S(1)} collective-permute-done((s16[144,384]{1,0:T(8,128)(2,1)S(1)}, s16[144,384]{1,0:T(8,128)(2,1)S(1)}, u32[]{:S(2)}, u32[]{:S(2)}) %collective-permute-start.8) | collective-permute-done | bytes 110624 | tf_op jit(solution)/shard_map/ppermute | solution.py:458
  42.9 0.8 shard_map.51.total
  43.7 4.2 %collective-permute-done.9.behind = s16[144,384]{1,0:T(8,128)(2,1)S(1)} collective-permute-done((s16[144,384]{1,0:T(8,128)(2,1)S(1)}, s16[144,384]{1,0:T(8,128)(2,1)S(1)}, u32[]{:S(2)}, u32[]{:S(2)}) %collective-permute-start.9) | collective-permute-done | bytes 110624 | tf_op jit(solution)/shard_map/ppermute | solution.py:458
  47.9 0.1 shard_map.53.total
  48.1 1.4 %collective-permute-done.10.other_total = f32[128,384]{1,0:T(8,128)S(1)} collective-permute-done((f32[128,384]{1,0:T(8,128)S(1)}, f32[128,384]{1,0:T(8,128)S(1)}, u32[]{:S(2)}, u32[]{:S(2)}) %collective-permute-start.10) | collective-permute-done | bytes 196640 | tf_op jit(solution)/shard_map/ppermute | solution.py:462
  49.6 0.2 shard_map.54
  49.8 1.0 collective-permute-start.11
  50.8 0.6 shard_map.57
  51.4 1.1 %collective-permute-start.12 = (s16[144,384]{1,0:T(8,128)(2,1)S(1)}, s16[144,384]{1,0:T(8,128)(2,1)S(1)}, u32[]{:S(2)}, u32[]{:S(2)}) collective-permute-start(s16[144,384]{1,0:T(8,128)(2,1)S(1)} %shard_map.57), channel_id=1, source_target_pairs={{0,2},{1,5},{2,4},{3,7},{4,6},{5,9},{6,8},{7,11},{8,10},{9,13},{10... | collective-permute-start | bytes 331784 | tf_op jit(solution)/shard_map/ppermute | solution.py:458
  52.5 0.5 shard_map.55.product
  53.0 1.6 %collective-permute-done.11.near = s16[144,384]{1,0:T(8,128)(2,1)S(1)} collective-permute-done((s16[144,384]{1,0:T(8,128)(2,1)S(1)}, s16[144,384]{1,0:T(8,128)(2,1)S(1)}, u32[]{:S(2)}, u32[]{:S(2)}) %collective-permute-start.11) | collective-permute-done | bytes 110624 | tf_op jit(solution)/shard_map/ppermute | solution.py:458
  54.5 0.9 shard_map.56.total
  55.4 3.5 %collective-permute-done.12.behind = s16[144,384]{1,0:T(8,128)(2,1)S(1)} collective-permute-done((s16[144,384]{1,0:T(8,128)(2,1)S(1)}, s16[144,384]{1,0:T(8,128)(2,1)S(1)}, u32[]{:S(2)}, u32[]{:S(2)}) %collective-permute-start.12) | collective-permute-done | bytes 110624 | tf_op jit(solution)/shard_map/ppermute | solution.py:458
  58.9 0.1 shard_map.58.total
  59.1 1.4 %collective-permute-done.13.other_total = f32[128,384]{1,0:T(8,128)S(1)} collective-permute-done((f32[128,384]{1,0:T(8,128)S(1)}, f32[128,384]{1,0:T(8,128)S(1)}, u32[]{:S(2)}, u32[]{:S(2)}) %collective-permute-start.13) | collective-permute-done | bytes 196640 | tf_op jit(solution)/shard_map/ppermute | solution.py:462
  60.5 0.2 shard_map.59
  60.7 1.0 %collective-permute-start.14 = (s16[144,384]{1,0:T(8,128)(2,1)S(1)}, s16[144,384]{1,0:T(8,128)(2,1)S(1)}, u32[]{:S(2)}, u32[]{:S(2)}) collective-permute-start(s16[144,384]{1,0:T(8,128)(2,1)S(1)} %get-tuple-element.65), channel_id=1, source_target_pairs={{0,14},{1,13},{2,0},{3,15},{4,2},{5,1},{6,4},{7,3},{8,6},{9,5},{10... | collective-permute-start | bytes 331784 | tf_op jit(solution)/shard_map/ppermute | solution.py:458
  61.7 1.1 %copy-done.6 = bf16[768,384]{1,0:T(8,128)(2,1)S(1)} copy-done((bf16[768,384]{1,0:T(8,128)(2,1)S(1)}, bf16[768,384]{1,0:T(8,128)(2,1)}, u32[]{:S(2)}) %copy-start.6) | copy-done | bytes 589848
  62.8 0.5 shard_map.61.product
  63.3 0.5 shard_map.60
  63.8 1.8 %collective-permute-done.14.near = s16[144,384]{1,0:T(8,128)(2,1)S(1)} collective-permute-done((s16[144,384]{1,0:T(8,128)(2,1)S(1)}, s16[144,384]{1,0:T(8,128)(2,1)S(1)}, u32[]{:S(2)}, u32[]{:S(2)}) %collective-permute-start.14) | collective-permute-done | bytes 110624 | tf_op jit(solution)/shard_map/ppermute | solution.py:458
  65.6 1.5 %shard_map.62 = (f32[56,128]{1,0:T(8,128)S(1)}, f32[56,128]{1,0:T(8,128)S(1)}) custom-call(f32[8,128]{1,0:T(8,128)S(1)} %broadcast_in_dim.19.core.refs_0_, f32[320,64]{1,0:T(8,128)S(1)} %get-tuple-element.64.low, f32[128,384]{1,0:T(8,128)S(1)} %get-tuple-element.63.v2.vectors, f32[128,384]{1,0:T(8,128)S(1)} %shard_map.61.product, ...), custom_call_target="tpu_custom_call" | custom-call | flops 1000000000 | bytes 1000000 | tf_op jit(solution)/shard_map/pallas_call | solution.py:32
  67.2 1.2 %collective-permute-done.15 = f32[56,128]{1,0:T(8,128)S(1)} collective-permute-done((f32[56,128]{1,0:T(8,128)S(1)}, f32[56,128]{1,0:T(8,128)S(1)}, u32[]{:S(2)}, u32[]{:S(2)}) %collective-permute-start.15) | collective-permute-done | bytes 28704 | tf_op jit(solution)/shard_map/ppermute | solution.py:462
  68.4 3.9 %collective-permute-done.16 = f32[56,128]{1,0:T(8,128)S(1)} collective-permute-done((f32[56,128]{1,0:T(8,128)S(1)}, f32[56,128]{1,0:T(8,128)S(1)}, u32[]{:S(2)}, u32[]{:S(2)}) %collective-permute-start.16) | collective-permute-done | bytes 28704 | tf_op jit(solution)/shard_map/ppermute | solution.py:469
  72.3 3.9 %collective-permute-done.17 = f32[56,128]{1,0:T(8,128)S(1)} collective-permute-done((f32[56,128]{1,0:T(8,128)S(1)}, f32[56,128]{1,0:T(8,128)S(1)}, u32[]{:S(2)}, u32[]{:S(2)}) %collective-permute-start.17) | collective-permute-done | bytes 28704 | tf_op jit(solution)/shard_map/ppermute | solution.py:469
  76.1 0.6 collective-permute-start.18
  76.7 4.2 %collective-permute-done.18 = f32[56,128]{1,0:T(8,128)S(1)} collective-permute-done((f32[56,128]{1,0:T(8,128)S(1)}, f32[56,128]{1,0:T(8,128)S(1)}, u32[]{:S(2)}, u32[]{:S(2)}) %collective-permute-start.18) | collective-permute-done | bytes 28704 | tf_op jit(solution)/shard_map/ppermute | solution.py:469
  81.6 0.5 collective-permute-done.19.refs_3_
  82.1 18.6 %shard_map.63 = f32[64,384]{1,0:T(8,128)} custom-call(f32[8,128]{1,0:T(8,128)S(1)} %broadcast_in_dim.19.core.refs_0_, f32[8,128]{1,0:T(8,128)S(1)} %broadcast_in_dim.20.refs_1_, f32[56,128]{1,0:T(8,128)S(1)} %add.32.refs_2_, f32[56,128]{1,0:T(8,128)S(1)} %collective-permute-done.19.refs_3_, f32[192,384]{1,0:T(8,128)S(1)} %get-tuple-element.68.refs_4_), custom_call_target="tpu_custom_call" | custom-call | flops 20000000000 | bytes 1000000 | tf_op jit(solution)/shard_map/pallas_call | solution.py:32
  (37 shorter events, 0.4 us)
Async XLA Ops:
  0.0 11.6 %copy-start = (bf16[384,768]{1,0:T(8,128)(2,1)S(1)}, bf16[384,768]{1,0:T(8,128)(2,1)}, u32[]{:S(2)}) copy-start(bf16[384,768]{1,0:T(8,128)(2,1)} %own.1) | copy-start | bytes 1769476
  0.0 11.6 %collective-permute-start.2 = (bf16[384,768]{1,0:T(8,128)(2,1)}, bf16[384,768]{1,0:T(8,128)(2,1)S(1)}, u32[]{:S(2)}, u32[]{:S(2)}) collective-permute-start(bf16[384,768]{1,0:T(8,128)(2,1)} %own.1), channel_id=1, source_target_pairs={{0,1},{1,0},{2,3},{3,2},{4,5},{5,4},{6,7},{7,6},{8,9},{9,8},{10,11... | collective-permute-start | bytes 1769480 | tf_op jit(solution)/shard_map/ppermute | solution.py:462
  0.5 13.0 %collective-permute-start = (bf16[384,768]{1,0:T(8,128)(2,1)}, bf16[384,768]{1,0:T(8,128)(2,1)S(1)}, u32[]{:S(2)}, u32[]{:S(2)}) collective-permute-start(bf16[384,768]{1,0:T(8,128)(2,1)} %own.1), channel_id=1, source_target_pairs={{2,0},{6,4},{10,8},{14,12},{1,13},{3,15},{5,1},{7,3},{9,5},{11,7},... | collective-permute-start | bytes 1769480 | tf_op jit(solution)/shard_map/ppermute | solution.py:492
  3.9 7.6 %collective-permute-start.1 = (f32[64,384]{1,0:T(8,128)S(1)}, f32[64,384]{1,0:T(8,128)S(1)}, u32[]{:S(2)}, u32[]{:S(2)}) collective-permute-start(f32[64,384]{1,0:T(8,128)S(1)} %multiply_bitcast_fusion), channel_id=1, source_target_pairs={{0,1},{1,0},{2,3},{3,2},{4,5},{5,4},{6,7},{7,6},{8,9},{9,8},{10,11... | collective-permute-start | bytes 294920 | tf_op jit(solution)/shard_map/ppermute | solution.py:462
  6.3 12.4 %collective-permute-start.3 = (bf16[384,768]{1,0:T(8,128)(2,1)}, bf16[384,768]{1,0:T(8,128)(2,1)S(1)}, u32[]{:S(2)}, u32[]{:S(2)}) collective-permute-start(bf16[384,768]{1,0:T(8,128)(2,1)} %own.1), channel_id=1, source_target_pairs={{3,0},{7,4},{11,8},{15,12},{0,13},{2,15},{4,1},{6,3},{8,5},{10,7},... | collective-permute-start | bytes 1769480 | tf_op jit(solution)/shard_map/ppermute | solution.py:492
  13.4 39.0 %copy-start.3 = (bf16[768,384]{1,0:T(8,128)(2,1)}, bf16[768,384]{1,0:T(8,128)(2,1)S(1)}, u32[]{:S(2)}) copy-start(bf16[768,384]{1,0:T(8,128)(2,1)S(1)} %get-tuple-element.54.h0) | copy-start | bytes 1769476
  13.4 39.0 %copy-start.5 = (bf16[768,384]{1,0:T(8,128)(2,1)}, bf16[768,384]{1,0:T(8,128)(2,1)S(1)}, u32[]{:S(2)}) copy-start(bf16[768,384]{1,0:T(8,128)(2,1)S(1)} %get-tuple-element.55.l0) | copy-start | bytes 1769476
  13.5 5.8 %collective-permute-start.5 = (bf16[384,768]{1,0:T(8,128)(2,1)S(1)}, bf16[384,768]{1,0:T(8,128)(2,1)S(1)}, u32[]{:S(2)}, u32[]{:S(2)}) collective-permute-start(bf16[384,768]{1,0:T(8,128)(2,1)S(1)} %collective-permute-done.direct), channel_id=1, source_target_pairs={{2,14},{6,2},{10,6},{14,10},{18,30},{22,18},{26,22},{30,26}} | collective-permute-start | bytes 1769480 | tf_op jit(solution)/shard_map/ppermute | solution.py:492
  18.6 2.7 %collective-permute-start.4 = (bf16[384,768]{1,0:T(8,128)(2,1)S(1)}, bf16[384,768]{1,0:T(8,128)(2,1)S(1)}, u32[]{:S(2)}, u32[]{:S(2)}) collective-permute-start(bf16[384,768]{1,0:T(8,128)(2,1)S(1)} %collective-permute-done.direct), channel_id=1, source_target_pairs={{1,2},{5,6},{9,10},{13,14},{17,18},{21,22},{25,26},{29,30}} | collective-permute-start | bytes 1769480 | tf_op jit(solution)/shard_map/ppermute | solution.py:492
  23.3 31.2 %copy-start.1 = (bf16[768,384]{1,0:T(8,128)(2,1)}, bf16[768,384]{1,0:T(8,128)(2,1)S(1)}, u32[]{:S(2)}) copy-start(bf16[768,384]{1,0:T(8,128)(2,1)S(1)} %get-tuple-element.60.l2) | copy-start | bytes 1769476
  23.3 13.1 %collective-permute-start.6 = (f32[16,384]{1,0:T(8,128)S(1)}, f32[16,384]{1,0:T(8,128)S(1)}, u32[]{:S(2)}, u32[]{:S(2)}) collective-permute-start(f32[16,384]{1,0:T(8,128)S(1)} %pad_maximum_fusion.1), channel_id=1, source_target_pairs={{0,2},{1,5},{2,4},{3,7},{4,6},{5,9},{6,8},{7,11},{8,10},{9,13},{10... | collective-permute-start | bytes 73736 | tf_op jit(solution)/shard_map/ppermute | solution.py:458
  36.4 1.2 %collective-permute-start.7 = (f32[16,384]{1,0:T(8,128)S(1)}, f32[16,384]{1,0:T(8,128)S(1)}, u32[]{:S(2)}, u32[]{:S(2)}) collective-permute-start(f32[16,384]{1,0:T(8,128)S(1)} %add.28.sums), channel_id=1, source_target_pairs={{0,1},{1,0},{2,3},{3,2},{4,5},{5,4},{6,7},{7,6},{8,9},{9,8},{10,11... | collective-permute-start | bytes 73736 | tf_op jit(solution)/shard_map/ppermute | solution.py:462
  37.8 5.1 %collective-permute-start.8 = (s16[144,384]{1,0:T(8,128)(2,1)S(1)}, s16[144,384]{1,0:T(8,128)(2,1)S(1)}, u32[]{:S(2)}, u32[]{:S(2)}) collective-permute-start(s16[144,384]{1,0:T(8,128)(2,1)S(1)} %get-tuple-element.56), channel_id=1, source_target_pairs={{0,14},{1,13},{2,0},{3,15},{4,2},{5,1},{6,4},{7,3},{8,6},{9,5},{10... | collective-permute-start | bytes 331784 | tf_op jit(solution)/shard_map/ppermute | solution.py:458
  40.5 7.5 %collective-permute-start.9 = (s16[144,384]{1,0:T(8,128)(2,1)S(1)}, s16[144,384]{1,0:T(8,128)(2,1)S(1)}, u32[]{:S(2)}, u32[]{:S(2)}) collective-permute-start(s16[144,384]{1,0:T(8,128)(2,1)S(1)} %shard_map.52), channel_id=1, source_target_pairs={{0,2},{1,5},{2,4},{3,7},{4,6},{5,9},{6,8},{7,11},{8,10},{9,13},{10... | collective-permute-start | bytes 331784 | tf_op jit(solution)/shard_map/ppermute | solution.py:458
  48.1 1.5 %collective-permute-start.10 = (f32[128,384]{1,0:T(8,128)S(1)}, f32[128,384]{1,0:T(8,128)S(1)}, u32[]{:S(2)}, u32[]{:S(2)}) collective-permute-start(f32[128,384]{1,0:T(8,128)S(1)} %shard_map.53.total), channel_id=1, source_target_pairs={{0,1},{1,0},{2,3},{3,2},{4,5},{5,4},{6,7},{7,6},{8,9},{9,8},{10,11... | collective-permute-start | bytes 589832 | tf_op jit(solution)/shard_map/ppermute | solution.py:462
  49.8 4.8 %collective-permute-start.11 = (s16[144,384]{1,0:T(8,128)(2,1)S(1)}, s16[144,384]{1,0:T(8,128)(2,1)S(1)}, u32[]{:S(2)}, u32[]{:S(2)}) collective-permute-start(s16[144,384]{1,0:T(8,128)(2,1)S(1)} %get-tuple-element.62), channel_id=1, source_target_pairs={{0,14},{1,13},{2,0},{3,15},{4,2},{5,1},{6,4},{7,3},{8,6},{9,5},{10... | collective-permute-start | bytes 331784 | tf_op jit(solution)/shard_map/ppermute | solution.py:458
  51.4 7.5 %collective-permute-start.12 = (s16[144,384]{1,0:T(8,128)(2,1)S(1)}, s16[144,384]{1,0:T(8,128)(2,1)S(1)}, u32[]{:S(2)}, u32[]{:S(2)}) collective-permute-start(s16[144,384]{1,0:T(8,128)(2,1)S(1)} %shard_map.57), channel_id=1, source_target_pairs={{0,2},{1,5},{2,4},{3,7},{4,6},{5,9},{6,8},{7,11},{8,10},{9,13},{10... | collective-permute-start | bytes 331784 | tf_op jit(solution)/shard_map/ppermute | solution.py:458
  55.4 6.3 %copy-start.4 = (bf16[768,384]{1,0:T(8,128)(2,1)S(1)}, bf16[768,384]{1,0:T(8,128)(2,1)}, u32[]{:S(2)}) copy-start(bf16[768,384]{1,0:T(8,128)(2,1)} %copy-done.3) | copy-start | bytes 1769476
  59.0 1.5 %collective-permute-start.13 = (f32[128,384]{1,0:T(8,128)S(1)}, f32[128,384]{1,0:T(8,128)S(1)}, u32[]{:S(2)}, u32[]{:S(2)}) collective-permute-start(f32[128,384]{1,0:T(8,128)S(1)} %shard_map.58.total), channel_id=1, source_target_pairs={{0,1},{1,0},{2,3},{3,2},{4,5},{5,4},{6,7},{7,6},{8,9},{9,8},{10,11... | collective-permute-start | bytes 589832 | tf_op jit(solution)/shard_map/ppermute | solution.py:462
  60.7 5.0 %collective-permute-start.14 = (s16[144,384]{1,0:T(8,128)(2,1)S(1)}, s16[144,384]{1,0:T(8,128)(2,1)S(1)}, u32[]{:S(2)}, u32[]{:S(2)}) collective-permute-start(s16[144,384]{1,0:T(8,128)(2,1)S(1)} %get-tuple-element.65), channel_id=1, source_target_pairs={{0,14},{1,13},{2,0},{3,15},{4,2},{5,1},{6,4},{7,3},{8,6},{9,5},{10... | collective-permute-start | bytes 331784 | tf_op jit(solution)/shard_map/ppermute | solution.py:458
  61.7 1.1 %copy-start.6 = (bf16[768,384]{1,0:T(8,128)(2,1)S(1)}, bf16[768,384]{1,0:T(8,128)(2,1)}, u32[]{:S(2)}) copy-start(bf16[768,384]{1,0:T(8,128)(2,1)} %copy-done.5) | copy-start | bytes 1769476
  63.3 2.4 %copy-start.2 = (bf16[768,384]{1,0:T(8,128)(2,1)S(1)}, bf16[768,384]{1,0:T(8,128)(2,1)}, u32[]{:S(2)}) copy-start(bf16[768,384]{1,0:T(8,128)(2,1)} %copy-done.1) | copy-start | bytes 1769476
  67.1 1.3 %collective-permute-start.15 = (f32[56,128]{1,0:T(8,128)S(1)}, f32[56,128]{1,0:T(8,128)S(1)}, u32[]{:S(2)}, u32[]{:S(2)}) collective-permute-start(f32[56,128]{1,0:T(8,128)S(1)} %get-tuple-element.67), channel_id=1, source_target_pairs={{0,1},{1,0},{2,3},{3,2},{4,5},{5,4},{6,7},{7,6},{8,9},{9,8},{10,11... | collective-permute-start | bytes 86024 | tf_op jit(solution)/shard_map/ppermute | solution.py:462
  68.4 3.9 %collective-permute-start.16 = (f32[56,128]{1,0:T(8,128)S(1)}, f32[56,128]{1,0:T(8,128)S(1)}, u32[]{:S(2)}, u32[]{:S(2)}) collective-permute-start(f32[56,128]{1,0:T(8,128)S(1)} %add.29), channel_id=1, source_target_pairs={{0,2},{2,0},{4,6},{6,4},{8,10},{10,8},{12,14},{14,12},{1,3},{3,1},... | collective-permute-start | bytes 86024 | tf_op jit(solution)/shard_map/ppermute | solution.py:469
  72.3 3.9 %collective-permute-start.17 = (f32[56,128]{1,0:T(8,128)S(1)}, f32[56,128]{1,0:T(8,128)S(1)}, u32[]{:S(2)}, u32[]{:S(2)}) collective-permute-start(f32[56,128]{1,0:T(8,128)S(1)} %add.30), channel_id=1, source_target_pairs={{0,4},{2,6},{4,0},{6,2},{8,12},{10,14},{12,8},{14,10},{1,5},{3,7},... | collective-permute-start | bytes 86024 | tf_op jit(solution)/shard_map/ppermute | solution.py:469
  76.1 4.8 %collective-permute-start.18 = (f32[56,128]{1,0:T(8,128)S(1)}, f32[56,128]{1,0:T(8,128)S(1)}, u32[]{:S(2)}, u32[]{:S(2)}) collective-permute-start(f32[56,128]{1,0:T(8,128)S(1)} %add.31), channel_id=1, source_target_pairs={{0,8},{2,10},{4,12},{6,14},{8,0},{10,2},{12,4},{14,6},{1,9},{3,11}... | collective-permute-start | bytes 86024 | tf_op jit(solution)/shard_map/ppermute | solution.py:469
  80.9 1.2 %collective-permute-start.19 = (f32[56,128]{1,0:T(8,128)S(1)}, f32[56,128]{1,0:T(8,128)S(1)}, u32[]{:S(2)}, u32[]{:S(2)}) collective-permute-start(f32[56,128]{1,0:T(8,128)S(1)} %add.32.refs_2_), channel_id=1, source_target_pairs={{0,1},{1,0},{2,3},{3,2},{4,5},{5,4},{6,7},{7,6},{8,9},{9,8},{10,11... | collective-permute-start | bytes 86024 | tf_op jit(solution)/shard_map/ppermute | solution.py:462

commit v15 on v14

--- a/solution.py
+++ b/solution.py
@@ -211,7 +211,7 @@
     return [lax.broadcasted_iota(jnp.int32, (rows, cols), axis) for axis in range(2)]
 
 
-def moment_body(core, low, vectors, product, near, h1, l1, h2, l2, mine, theirs):
+def moment_body(low, vectors, product, near, h1, l1, h2, l2, packed):
     n = vectors.shape[0] // 2
     last = far_product(near, h1, l1, h2, l2)
     last = 2.0 * last + jnp.concatenate([product[:n, :], product[n:, :]], axis=1)
@@ -226,11 +226,7 @@
     row, _ = place_of(8, 2 * n)
     pieces.append(jnp.where(row == 0, jnp.concatenate([d1, d3], axis=1),
                             jnp.where(row == 1, jnp.concatenate([d5, d5], axis=1), 0.0)))
-    pieces.append(jnp.zeros((8, 2 * n), F32))
-    packed = jnp.concatenate(pieces, axis=0)
-    half = packed.shape[0] // 2
-    mine[...] = chosen(core, packed[half:], packed[:half])
-    theirs[...] = chosen(core, packed[:half], packed[half:])
+    packed[...] = jnp.concatenate(pieces, axis=0)
 
 
 def unpacked(packed, n):
@@ -446,8 +442,7 @@
 
 
 def dense_body(rows, core, index, mine, theirs, scaled, out):
-    packed = jnp.concatenate([
-        chosen(core, theirs[...], mine[...]), chosen(core, mine[...], theirs[...])], axis=0)
+    packed = chosen(core, mine[...], theirs[...])
     index = jnp.broadcast_to(index[0:1, :NVEC], (NVEC, NVEC)).astype(jnp.int32)
     out[...] = dense(unpacked(packed, NVEC), index, rows, scaled[...])
 
@@ -462,11 +457,13 @@
     return lax.ppermute(shard, "narrow", [(0, 1), (1, 0)])
 
 
-def total_over_blocks(values):
+def total_on_one(values):
     blocks = lax.axis_size("blk")
+    values = values + lax.ppermute(values, "narrow", [(0, 1)])
     span = 1
     while blocks % (2 * span) == 0:
-        values = values + lax.ppermute(values, "blk", [(i, i ^ span) for i in range(blocks)])
+        pairs = [(2 * i + 1, 2 * (i ^ span) + 1) for i in range(blocks)]
+        values = values + lax.ppermute(values, ("blk", "narrow"), pairs)
         span *= 2
     if span < blocks:
         groups = [list(range(i, blocks, span)) for i in range(span)]
@@ -535,14 +532,14 @@
     low, scaled = call(
         low_body, [((5 * NVEC, NVEC), F32), ((3 * NVEC, size), F32)], [degree] + history, **middle)
     (product,) = call(own_product_body, [pair_shape], [vectors, h0, l0], **middle)
-    packed_shape = ((3 * NVEC // 4 + 8, 2 * NVEC), F32)
-    mine, theirs = call(
-        moment_body, [packed_shape] * 2, [spread(core), low, vectors, product, near, *far], **middle)
-    mine = total_over_blocks(mine + between_cores(theirs))
+    (packed,) = call(
+        moment_body, [((3 * NVEC // 2 + 8, 2 * NVEC), F32)], [low, vectors, product, near, *far], **middle)
+    packed = total_on_one(packed)
+    handed = lax.ppermute(packed, "narrow", [(1, 0)])
     rows = size * blocks * lax.axis_size("narrow")
     (out,) = call(
         lambda *refs: dense_body(rows, *refs), [((NVEC, size), F32)],
-        [spread(core), spread(shift_index), mine, between_cores(mine), scaled], flops=2 * 10**10, nbytes=10**6,
+        [spread(core), spread(shift_index), packed, handed, scaled], flops=2 * 10**10, nbytes=10**6,
     )
     return out.T
 

time: 101 us -> 106 us (1.050)
  starting transfers between devices: 26.1 us -> 30 us
  waiting for transfers between devices: 38.1 us -> 40.5 us
  local copies, waits for them, and re-layouts: 2.37 us -> 1.28 us
    ppermute x3 -> x5, starting transfers between devices: 0.62 us -> 4.74 us  [the longest x3 1.98 us: total_on_one(): values = values + lax.ppermute(values, ('blk', 'narrow'), pairs)]
    ppermute x3 -> x5, waiting for transfers between devices: 11.9 us -> 14.9 us  [the longest x1 14 us: shards(): handed = lax.ppermute(packed, 'narrow', [(1, 0)])]
    ppermute x7 -> x5, waiting for transfers between devices: 5.78 us -> 4.05 us  [between_cores(): return lax.ppermute(shard, 'narrow', [(0, 1), (1, 0)])]
    ppermute x6, waiting for transfers between devices: 16 us -> 17.1 us  [between_blocks(): return lax.ppermute(shard, ('blk', 'narrow'), pairs)]
    unnamed x14 -> x2, local copies, waits for them, and re-layouts: 1.09 us -> 0.01 us
    ppermute x7 -> x5, starting transfers between devices: 3.03 us -> 2.95 us  [between_cores(): return lax.ppermute(shard, 'narrow', [(0, 1), (1, 0)])]
  transfers between devices with their start and end apart: 20 -> 20, of which waited for: 15 -> 12; matrix products, arithmetic and copies ran while one was open for 2% -> 2% of each run, Pallas kernels for 9% -> 8%
where the time goes in v15:
time: 106 us
  waiting for transfers between devices  40.5 us (38%)
  Pallas kernels  31.5 us (30%)
  starting transfers between devices  30 us (28%)
  between operations  1.59 us (2%)
  local copies, waits for them, and re-layouts  1.28 us (1%)
    pallas_call x18, Pallas kernels, call(): pl.pallas_call(body, out_shape=[jax.ShapeDtypeStruct(shape, dtype) for sh...  31.5 us
    ppermute x6, waiting for transfers between devices, between_blocks(): return lax.ppermute(shard, ('blk', 'narrow'), pairs)  17.1 us
    ppermute x6, starting transfers between devices, between_blocks(): return lax.ppermute(shard, ('blk', 'narrow'), pairs)  15 us
    ppermute x1, waiting for transfers between devices, shards(): handed = lax.ppermute(packed, 'narrow', [(1, 0)])  14 us
    ppermute x4, starting transfers between devices, between_shards(): return lax.ppermute(shard, ('blk', 'narrow'), pairs)  7.24 us
    ppermute x4, waiting for transfers between devices, between_shards(): return lax.ppermute(shard, ('blk', 'narrow'), pairs)  4.46 us
    ppermute x5, waiting for transfers between devices, between_cores(): return lax.ppermute(shard, 'narrow', [(0, 1), (1, 0)])  4.05 us
    ppermute x5, starting transfers between devices, between_cores(): return lax.ppermute(shard, 'narrow', [(0, 1), (1, 0)])  2.95 us
  transfers between devices with their start and end apart: 20, of which 12 were waited for; matrix products, arithmetic and copies ran while one was open for 2% of the time, Pallas kernels for 8%

profile of v15, /device:TPU:0, one launch (start us, length us, event | category | flops | bytes accessed | tf_op | source)
XLA Modules:
  0.0 105.9 jit_solution(12012564744827347146)
XLA Ops:
  0.0 0.5 collective-permute-start.2
  0.5 2.5 %collective-permute-start = (bf16[384,768]{1,0:T(8,128)(2,1)}, bf16[384,768]{1,0:T(8,128)(2,1)S(1)}, u32[]{:S(2)}, u32[]{:S(2)}) collective-permute-start(bf16[384,768]{1,0:T(8,128)(2,1)} %own.1), channel_id=1, source_target_pairs={{2,0},{6,4},{10,8},{14,12},{1,13},{3,15},{5,1},{7,3},{9,5},{11,7},... | collective-permute-start | bytes 1769480 | tf_op jit(solution)/shard_map/ppermute | solution.py:489
  3.0 0.9 multiply_bitcast_fusion
  3.9 2.4 %collective-permute-start.1 = (f32[64,384]{1,0:T(8,128)S(1)}, f32[64,384]{1,0:T(8,128)S(1)}, u32[]{:S(2)}, u32[]{:S(2)}) collective-permute-start(f32[64,384]{1,0:T(8,128)S(1)} %multiply_bitcast_fusion), channel_id=1, source_target_pairs={{0,1},{1,0},{2,3},{3,2},{4,5},{5,4},{6,7},{7,6},{8,9},{9,8},{10,11... | collective-permute-start | bytes 294920 | tf_op jit(solution)/shard_map/ppermute | solution.py:457
  6.3 3.3 %collective-permute-start.3 = (bf16[384,768]{1,0:T(8,128)(2,1)}, bf16[384,768]{1,0:T(8,128)(2,1)S(1)}, u32[]{:S(2)}, u32[]{:S(2)}) collective-permute-start(bf16[384,768]{1,0:T(8,128)(2,1)} %own.1), channel_id=1, source_target_pairs={{3,0},{7,4},{11,8},{15,12},{0,13},{2,15},{4,1},{6,3},{8,5},{10,7},... | collective-permute-start | bytes 1769480 | tf_op jit(solution)/shard_map/ppermute | solution.py:489
  9.6 1.3 %dynamic_slice.3 = s32[1,1]{0,1:T(1,128)} dynamic-slice(s32[8,2]{0,1:T(2,128)} %param.5, s32[]{:T(128)S(6)} %select_n.13, s32[]{:T(128)S(6)} %select_n.14), dynamic_slice_sizes={1,1} | dynamic-slice | bytes 12 | tf_op jit(solution)/shard_map/dynamic_slice | solution.py:494
  11.6 1.9 %shard_map.46 = (bf16[768,384]{1,0:T(8,128)(2,1)S(1)}, bf16[768,384]{1,0:T(8,128)(2,1)S(1)}, f32[16,384]{1,0:T(8,128)S(1)}, f32[768,128]{1,0:T(8,128)S(1)}, bf16...) custom-call(bf16[384,768]{1,0:T(8,128)(2,1)S(1)} %copy-done, bf16[384,768]{1,0:T(8,128)(2,1)S(1)} %collective-permute-done.2.other), custom_call_target="tpu_custom_call" | custom-call | flops 2000000000 | bytes 1000000 | tf_op jit(solution)/shard_map/pallas_call | solution.py:32
  13.5 0.7 collective-permute-start.5
  14.2 4.5 %collective-permute-done.3.direct = bf16[384,768]{1,0:T(8,128)(2,1)S(1)} collective-permute-done((bf16[384,768]{1,0:T(8,128)(2,1)}, bf16[384,768]{1,0:T(8,128)(2,1)S(1)}, u32[]{:S(2)}, u32[]{:S(2)}) %collective-permute-start.3) | collective-permute-done | bytes 589856 | tf_op jit(solution)/shard_map/ppermute | solution.py:489
  18.6 0.7 collective-permute-start.4
  19.3 2.0 %shard_map.47 = (bf16[768,384]{1,0:T(8,128)(2,1)S(1)}, bf16[768,384]{1,0:T(8,128)(2,1)S(1)}, f32[16,384]{1,0:T(8,128)S(1)}, f32[8,384]{1,0:T(8,128)S(1)}) custom-call(f32[8,128]{1,0:T(8,128)S(1)} %broadcast_in_dim.21.keep, f32[8,128]{1,0:T(8,128)S(1)} %broadcast_in_dim.22.relays, f32[8,128]{1,0:T(8,128)S(1)} %get-tuple-element.38.token, ...), custom_call_target="tpu_custom_call" | custom-call | flops 2000000000 | bytes 1000000 | tf_op jit(solution)/shard_map/pallas_call | solution.py:32
  21.3 2.0 %shard_map.48 = (bf16[768,384]{1,0:T(8,128)(2,1)S(1)}, bf16[768,384]{1,0:T(8,128)(2,1)S(1)}, f32[16,384]{1,0:T(8,128)S(1)}, f32[8,384]{1,0:T(8,128)S(1)}) custom-call(f32[8,128]{1,0:T(8,128)S(1)} %broadcast_in_dim.21.keep, f32[8,128]{1,0:T(8,128)S(1)} %broadcast_in_dim.22.relays, f32[8,128]{1,0:T(8,128)S(1)} %get-tuple-element.38.token, ...), custom_call_target="tpu_custom_call" | custom-call | flops 2000000000 | bytes 1000000 | tf_op jit(solution)/shard_map/pallas_call | solution.py:32
  23.3 10.0 %collective-permute-start.6 = (f32[16,384]{1,0:T(8,128)S(1)}, f32[16,384]{1,0:T(8,128)S(1)}, u32[]{:S(2)}, u32[]{:S(2)}) collective-permute-start(f32[16,384]{1,0:T(8,128)S(1)} %pad_maximum_fusion.1), channel_id=1, source_target_pairs={{0,2},{1,5},{2,4},{3,7},{4,6},{5,9},{6,8},{7,11},{8,10},{9,13},{10... | collective-permute-start | bytes 73736 | tf_op jit(solution)/shard_map/ppermute | solution.py:453
  33.3 3.1 %collective-permute-done.6 = f32[16,384]{1,0:T(8,128)S(1)} collective-permute-done((f32[16,384]{1,0:T(8,128)S(1)}, f32[16,384]{1,0:T(8,128)S(1)}, u32[]{:S(2)}, u32[]{:S(2)}) %collective-permute-start.6) | collective-permute-done | bytes 24608 | tf_op jit(solution)/shard_map/ppermute | solution.py:453
  36.4 1.2 %collective-permute-done.7.other_sums = f32[16,384]{1,0:T(8,128)S(1)} collective-permute-done((f32[16,384]{1,0:T(8,128)S(1)}, f32[16,384]{1,0:T(8,128)S(1)}, u32[]{:S(2)}, u32[]{:S(2)}) %collective-permute-start.7) | collective-permute-done | bytes 24608 | tf_op jit(solution)/shard_map/ppermute | solution.py:457
  37.6 0.2 shard_map.49
  37.8 2.0 %collective-permute-start.8 = (s16[144,384]{1,0:T(8,128)(2,1)S(1)}, s16[144,384]{1,0:T(8,128)(2,1)S(1)}, u32[]{:S(2)}, u32[]{:S(2)}) collective-permute-start(s16[144,384]{1,0:T(8,128)(2,1)S(1)} %get-tuple-element.54), channel_id=1, source_target_pairs={{0,14},{1,13},{2,0},{3,15},{4,2},{5,1},{6,4},{7,3},{8,6},{9,5},{10... | collective-permute-start | bytes 331784 | tf_op jit(solution)/shard_map/ppermute | solution.py:453
  39.8 0.6 shard_map.52
  40.5 0.5 shard_map.50.product
  41.0 1.9 %collective-permute-done.8.near = s16[144,384]{1,0:T(8,128)(2,1)S(1)} collective-permute-done((s16[144,384]{1,0:T(8,128)(2,1)S(1)}, s16[144,384]{1,0:T(8,128)(2,1)S(1)}, u32[]{:S(2)}, u32[]{:S(2)}) %collective-permute-start.8) | collective-permute-done | bytes 110624 | tf_op jit(solution)/shard_map/ppermute | solution.py:453
  42.9 0.8 shard_map.51.total
  43.7 4.2 %collective-permute-done.9.behind = s16[144,384]{1,0:T(8,128)(2,1)S(1)} collective-permute-done((s16[144,384]{1,0:T(8,128)(2,1)S(1)}, s16[144,384]{1,0:T(8,128)(2,1)S(1)}, u32[]{:S(2)}, u32[]{:S(2)}) %collective-permute-start.9) | collective-permute-done | bytes 110624 | tf_op jit(solution)/shard_map/ppermute | solution.py:453
  47.9 0.1 shard_map.53.total
  48.1 1.4 %collective-permute-done.10.other_total = f32[128,384]{1,0:T(8,128)S(1)} collective-permute-done((f32[128,384]{1,0:T(8,128)S(1)}, f32[128,384]{1,0:T(8,128)S(1)}, u32[]{:S(2)}, u32[]{:S(2)}) %collective-permute-start.10) | collective-permute-done | bytes 196640 | tf_op jit(solution)/shard_map/ppermute | solution.py:457
  49.6 0.2 shard_map.54
  49.7 1.0 collective-permute-start.11
  50.7 0.6 shard_map.57
  51.4 1.1 %collective-permute-start.12 = (s16[144,384]{1,0:T(8,128)(2,1)S(1)}, s16[144,384]{1,0:T(8,128)(2,1)S(1)}, u32[]{:S(2)}, u32[]{:S(2)}) collective-permute-start(s16[144,384]{1,0:T(8,128)(2,1)S(1)} %shard_map.57), channel_id=1, source_target_pairs={{0,2},{1,5},{2,4},{3,7},{4,6},{5,9},{6,8},{7,11},{8,10},{9,13},{10... | collective-permute-start | bytes 331784 | tf_op jit(solution)/shard_map/ppermute | solution.py:453
  52.5 0.5 shard_map.55.product
  53.0 1.6 %collective-permute-done.11.near = s16[144,384]{1,0:T(8,128)(2,1)S(1)} collective-permute-done((s16[144,384]{1,0:T(8,128)(2,1)S(1)}, s16[144,384]{1,0:T(8,128)(2,1)S(1)}, u32[]{:S(2)}, u32[]{:S(2)}) %collective-permute-start.11) | collective-permute-done | bytes 110624 | tf_op jit(solution)/shard_map/ppermute | solution.py:453
  54.5 0.9 shard_map.56.total
  55.4 3.5 %collective-permute-done.12.behind = s16[144,384]{1,0:T(8,128)(2,1)S(1)} collective-permute-done((s16[144,384]{1,0:T(8,128)(2,1)S(1)}, s16[144,384]{1,0:T(8,128)(2,1)S(1)}, u32[]{:S(2)}, u32[]{:S(2)}) %collective-permute-start.12) | collective-permute-done | bytes 110624 | tf_op jit(solution)/shard_map/ppermute | solution.py:453
  58.9 0.1 shard_map.58.total
  59.0 1.4 %collective-permute-done.13.other_total = f32[128,384]{1,0:T(8,128)S(1)} collective-permute-done((f32[128,384]{1,0:T(8,128)S(1)}, f32[128,384]{1,0:T(8,128)S(1)}, u32[]{:S(2)}, u32[]{:S(2)}) %collective-permute-start.13) | collective-permute-done | bytes 196640 | tf_op jit(solution)/shard_map/ppermute | solution.py:457
  60.5 0.2 shard_map.59
  60.7 0.9 collective-permute-start.14
  61.5 0.5 shard_map.61.product
  62.0 0.5 shard_map.60
  62.5 2.9 %collective-permute-done.14.near = s16[144,384]{1,0:T(8,128)(2,1)S(1)} collective-permute-done((s16[144,384]{1,0:T(8,128)(2,1)S(1)}, s16[144,384]{1,0:T(8,128)(2,1)S(1)}, u32[]{:S(2)}, u32[]{:S(2)}) %collective-permute-start.14) | collective-permute-done | bytes 110624 | tf_op jit(solution)/shard_map/ppermute | solution.py:453
  65.4 1.5 %shard_map.62 = f32[104,128]{1,0:T(8,128)S(1)} custom-call(f32[320,64]{1,0:T(8,128)S(1)} %get-tuple-element.62.low, f32[128,384]{1,0:T(8,128)S(1)} %get-tuple-element.61.v2.vectors, f32[128,384]{1,0:T(8,128)S(1)} %shard_map.61.product, s16[144,384]{1,0:T(8,128)(2,1)S(1)} %collective-permute-done.14.near, bf16[768,384]{1,0:T(8,128)(2,1)S(1)} %get-tuple-element.55.h1, ...), custom_call_target="tpu_custom_call" | custom-call | flops 1000000000 | bytes 1000000 | tf_op jit(solution)/shard_map/pallas_call | solution.py:32
  66.9 1.3 %collective-permute-start.15 = (f32[104,128]{1,0:T(8,128)S(1)}, f32[104,128]{1,0:T(8,128)S(1)}, u32[]{:S(2)}, u32[]{:S(2)}) collective-permute-start(f32[104,128]{1,0:T(8,128)S(1)} %shard_map.62), channel_id=1, source_target_pairs={{0,1},{2,3},{4,5},{6,7},{8,9},{10,11},{12,13},{14,15},{16,17},{18,... | collective-permute-start | bytes 159752 | tf_op jit(solution)/shard_map/ppermute | solution.py:462
  68.2 0.9 collective-permute-done.15
  69.1 0.7 collective-permute-start.16
  69.8 0.7 collective-permute-start.17
  70.5 0.7 collective-permute-start.18
  71.2 1.5 %collective-permute-start.19 = (f32[104,128]{1,0:T(8,128)S(1)}, f32[104,128]{1,0:T(8,128)S(1)}, u32[]{:S(2)}, u32[]{:S(2)}) collective-permute-start(f32[104,128]{1,0:T(8,128)S(1)} %add.32.refs_2_), channel_id=1, source_target_pairs={{1,0},{3,2},{5,4},{7,6},{9,8},{11,10},{13,12},{15,14},{17,16},{19,... | collective-permute-start | bytes 159752 | tf_op jit(solution)/shard_map/ppermute | solution.py:538
  73.3 14.0 %collective-permute-done.19.refs_3_ = f32[104,128]{1,0:T(8,128)S(1)} collective-permute-done((f32[104,128]{1,0:T(8,128)S(1)}, f32[104,128]{1,0:T(8,128)S(1)}, u32[]{:S(2)}, u32[]{:S(2)}) %collective-permute-start.19) | collective-permute-done | bytes 53280 | tf_op jit(solution)/shard_map/ppermute | solution.py:538
  87.3 18.6 %shard_map.63 = f32[64,384]{1,0:T(8,128)} custom-call(f32[8,128]{1,0:T(8,128)S(1)} %broadcast_in_dim.18.refs_0_, f32[8,128]{1,0:T(8,128)S(1)} %broadcast_in_dim.19.refs_1_, f32[104,128]{1,0:T(8,128)S(1)} %add.32.refs_2_, f32[104,128]{1,0:T(8,128)S(1)} %collective-permute-done.19.refs_3_, f32[192,384]{1,0:T(8,128)S(1)} %get-tuple-element.64.refs_4_), custom_call_target="tpu_custom_call" | custom-call | flops 20000000000 | bytes 1000000 | tf_op jit(solution)/shard_map/pallas_call | solution.py:32
  (25 shorter events, 0.3 us)
Async XLA Ops:
  0.0 11.6 %copy-start = (bf16[384,768]{1,0:T(8,128)(2,1)S(1)}, bf16[384,768]{1,0:T(8,128)(2,1)}, u32[]{:S(2)}) copy-start(bf16[384,768]{1,0:T(8,128)(2,1)} %own.1) | copy-start | bytes 1769476
  0.0 11.6 %collective-permute-start.2 = (bf16[384,768]{1,0:T(8,128)(2,1)}, bf16[384,768]{1,0:T(8,128)(2,1)S(1)}, u32[]{:S(2)}, u32[]{:S(2)}) collective-permute-start(bf16[384,768]{1,0:T(8,128)(2,1)} %own.1), channel_id=1, source_target_pairs={{0,1},{1,0},{2,3},{3,2},{4,5},{5,4},{6,7},{7,6},{8,9},{9,8},{10,11... | collective-permute-start | bytes 1769480 | tf_op jit(solution)/shard_map/ppermute | solution.py:457
  0.5 13.0 %collective-permute-start = (bf16[384,768]{1,0:T(8,128)(2,1)}, bf16[384,768]{1,0:T(8,128)(2,1)S(1)}, u32[]{:S(2)}, u32[]{:S(2)}) collective-permute-start(bf16[384,768]{1,0:T(8,128)(2,1)} %own.1), channel_id=1, source_target_pairs={{2,0},{6,4},{10,8},{14,12},{1,13},{3,15},{5,1},{7,3},{9,5},{11,7},... | collective-permute-start | bytes 1769480 | tf_op jit(solution)/shard_map/ppermute | solution.py:489
  3.9 7.6 %collective-permute-start.1 = (f32[64,384]{1,0:T(8,128)S(1)}, f32[64,384]{1,0:T(8,128)S(1)}, u32[]{:S(2)}, u32[]{:S(2)}) collective-permute-start(f32[64,384]{1,0:T(8,128)S(1)} %multiply_bitcast_fusion), channel_id=1, source_target_pairs={{0,1},{1,0},{2,3},{3,2},{4,5},{5,4},{6,7},{7,6},{8,9},{9,8},{10,11... | collective-permute-start | bytes 294920 | tf_op jit(solution)/shard_map/ppermute | solution.py:457
  6.3 12.4 %collective-permute-start.3 = (bf16[384,768]{1,0:T(8,128)(2,1)}, bf16[384,768]{1,0:T(8,128)(2,1)S(1)}, u32[]{:S(2)}, u32[]{:S(2)}) collective-permute-start(bf16[384,768]{1,0:T(8,128)(2,1)} %own.1), channel_id=1, source_target_pairs={{3,0},{7,4},{11,8},{15,12},{0,13},{2,15},{4,1},{6,3},{8,5},{10,7},... | collective-permute-start | bytes 1769480 | tf_op jit(solution)/shard_map/ppermute | solution.py:489
  13.5 5.9 %collective-permute-start.5 = (bf16[384,768]{1,0:T(8,128)(2,1)S(1)}, bf16[384,768]{1,0:T(8,128)(2,1)S(1)}, u32[]{:S(2)}, u32[]{:S(2)}) collective-permute-start(bf16[384,768]{1,0:T(8,128)(2,1)S(1)} %collective-permute-done.direct), channel_id=1, source_target_pairs={{2,14},{6,2},{10,6},{14,10},{18,30},{22,18},{26,22},{30,26}} | collective-permute-start | bytes 1769480 | tf_op jit(solution)/shard_map/ppermute | solution.py:489
  18.6 2.7 %collective-permute-start.4 = (bf16[384,768]{1,0:T(8,128)(2,1)S(1)}, bf16[384,768]{1,0:T(8,128)(2,1)S(1)}, u32[]{:S(2)}, u32[]{:S(2)}) collective-permute-start(bf16[384,768]{1,0:T(8,128)(2,1)S(1)} %collective-permute-done.direct), channel_id=1, source_target_pairs={{1,2},{5,6},{9,10},{13,14},{17,18},{21,22},{25,26},{29,30}} | collective-permute-start | bytes 1769480 | tf_op jit(solution)/shard_map/ppermute | solution.py:489
  23.3 13.1 %collective-permute-start.6 = (f32[16,384]{1,0:T(8,128)S(1)}, f32[16,384]{1,0:T(8,128)S(1)}, u32[]{:S(2)}, u32[]{:S(2)}) collective-permute-start(f32[16,384]{1,0:T(8,128)S(1)} %pad_maximum_fusion.1), channel_id=1, source_target_pairs={{0,2},{1,5},{2,4},{3,7},{4,6},{5,9},{6,8},{7,11},{8,10},{9,13},{10... | collective-permute-start | bytes 73736 | tf_op jit(solution)/shard_map/ppermute | solution.py:453
  36.4 1.2 %collective-permute-start.7 = (f32[16,384]{1,0:T(8,128)S(1)}, f32[16,384]{1,0:T(8,128)S(1)}, u32[]{:S(2)}, u32[]{:S(2)}) collective-permute-start(f32[16,384]{1,0:T(8,128)S(1)} %add.28.sums), channel_id=1, source_target_pairs={{0,1},{1,0},{2,3},{3,2},{4,5},{5,4},{6,7},{7,6},{8,9},{9,8},{10,11... | collective-permute-start | bytes 73736 | tf_op jit(solution)/shard_map/ppermute | solution.py:457
  37.8 5.1 %collective-permute-start.8 = (s16[144,384]{1,0:T(8,128)(2,1)S(1)}, s16[144,384]{1,0:T(8,128)(2,1)S(1)}, u32[]{:S(2)}, u32[]{:S(2)}) collective-permute-start(s16[144,384]{1,0:T(8,128)(2,1)S(1)} %get-tuple-element.54), channel_id=1, source_target_pairs={{0,14},{1,13},{2,0},{3,15},{4,2},{5,1},{6,4},{7,3},{8,6},{9,5},{10... | collective-permute-start | bytes 331784 | tf_op jit(solution)/shard_map/ppermute | solution.py:453
  40.5 7.5 %collective-permute-start.9 = (s16[144,384]{1,0:T(8,128)(2,1)S(1)}, s16[144,384]{1,0:T(8,128)(2,1)S(1)}, u32[]{:S(2)}, u32[]{:S(2)}) collective-permute-start(s16[144,384]{1,0:T(8,128)(2,1)S(1)} %shard_map.52), channel_id=1, source_target_pairs={{0,2},{1,5},{2,4},{3,7},{4,6},{5,9},{6,8},{7,11},{8,10},{9,13},{10... | collective-permute-start | bytes 331784 | tf_op jit(solution)/shard_map/ppermute | solution.py:453
  48.1 1.5 %collective-permute-start.10 = (f32[128,384]{1,0:T(8,128)S(1)}, f32[128,384]{1,0:T(8,128)S(1)}, u32[]{:S(2)}, u32[]{:S(2)}) collective-permute-start(f32[128,384]{1,0:T(8,128)S(1)} %shard_map.53.total), channel_id=1, source_target_pairs={{0,1},{1,0},{2,3},{3,2},{4,5},{5,4},{6,7},{7,6},{8,9},{9,8},{10,11... | collective-permute-start | bytes 589832 | tf_op jit(solution)/shard_map/ppermute | solution.py:457
  49.7 4.8 %collective-permute-start.11 = (s16[144,384]{1,0:T(8,128)(2,1)S(1)}, s16[144,384]{1,0:T(8,128)(2,1)S(1)}, u32[]{:S(2)}, u32[]{:S(2)}) collective-permute-start(s16[144,384]{1,0:T(8,128)(2,1)S(1)} %get-tuple-element.60), channel_id=1, source_target_pairs={{0,14},{1,13},{2,0},{3,15},{4,2},{5,1},{6,4},{7,3},{8,6},{9,5},{10... | collective-permute-start | bytes 331784 | tf_op jit(solution)/shard_map/ppermute | solution.py:453
  51.4 7.5 %collective-permute-start.12 = (s16[144,384]{1,0:T(8,128)(2,1)S(1)}, s16[144,384]{1,0:T(8,128)(2,1)S(1)}, u32[]{:S(2)}, u32[]{:S(2)}) collective-permute-start(s16[144,384]{1,0:T(8,128)(2,1)S(1)} %shard_map.57), channel_id=1, source_target_pairs={{0,2},{1,5},{2,4},{3,7},{4,6},{5,9},{6,8},{7,11},{8,10},{9,13},{10... | collective-permute-start | bytes 331784 | tf_op jit(solution)/shard_map/ppermute | solution.py:453
  59.0 1.5 %collective-permute-start.13 = (f32[128,384]{1,0:T(8,128)S(1)}, f32[128,384]{1,0:T(8,128)S(1)}, u32[]{:S(2)}, u32[]{:S(2)}) collective-permute-start(f32[128,384]{1,0:T(8,128)S(1)} %shard_map.58.total), channel_id=1, source_target_pairs={{0,1},{1,0},{2,3},{3,2},{4,5},{5,4},{6,7},{7,6},{8,9},{9,8},{10,11... | collective-permute-start | bytes 589832 | tf_op jit(solution)/shard_map/ppermute | solution.py:457
  60.7 4.8 %collective-permute-start.14 = (s16[144,384]{1,0:T(8,128)(2,1)S(1)}, s16[144,384]{1,0:T(8,128)(2,1)S(1)}, u32[]{:S(2)}, u32[]{:S(2)}) collective-permute-start(s16[144,384]{1,0:T(8,128)(2,1)S(1)} %get-tuple-element.63), channel_id=1, source_target_pairs={{0,14},{1,13},{2,0},{3,15},{4,2},{5,1},{6,4},{7,3},{8,6},{9,5},{10... | collective-permute-start | bytes 331784 | tf_op jit(solution)/shard_map/ppermute | solution.py:453
  66.9 2.2 %collective-permute-start.15 = (f32[104,128]{1,0:T(8,128)S(1)}, f32[104,128]{1,0:T(8,128)S(1)}, u32[]{:S(2)}, u32[]{:S(2)}) collective-permute-start(f32[104,128]{1,0:T(8,128)S(1)} %shard_map.62), channel_id=1, source_target_pairs={{0,1},{2,3},{4,5},{6,7},{8,9},{10,11},{12,13},{14,15},{16,17},{18,... | collective-permute-start | bytes 159752 | tf_op jit(solution)/shard_map/ppermute | solution.py:462
  69.1 0.7 collective-permute-start.16
  69.8 0.7 collective-permute-start.17
  70.5 0.7 collective-permute-start.18
  71.2 16.1 %collective-permute-start.19 = (f32[104,128]{1,0:T(8,128)S(1)}, f32[104,128]{1,0:T(8,128)S(1)}, u32[]{:S(2)}, u32[]{:S(2)}) collective-permute-start(f32[104,128]{1,0:T(8,128)S(1)} %add.32.refs_2_), channel_id=1, source_target_pairs={{1,0},{3,2},{5,4},{7,6},{9,8},{11,10},{13,12},{15,14},{17,16},{19,... | collective-permute-start | bytes 159752 | tf_op jit(solution)/shard_map/ppermute | solution.py:538

commit v16 on v14

--- a/solution.py
+++ b/solution.py
@@ -360,7 +360,6 @@
     base = inverse_factor(moments[0])
     right = dot(below(*moments[1:]), base, 1, 1)
     m1, m2, m3, m4, m5 = (dot(base, part(right, i)) for i in range(5))
-    y0, y1, y2 = (dot(base, part(data, i)) for i in range(3))
 
     by1 = dot(below(m1, m2, m3, m4), m1)
     square, m21, m31, m41 = (part(by1, i) for i in range(4))
@@ -437,12 +436,16 @@
     )
     norm = dot(power2, dot(gram, power2), 0, 0)
 
-    start = dot(power, below(y0, y1), 0, 0) - dot(dot(m1, bottom), y0, 0, 0)
-    image = dot(power, below(y1, y2), 0, 0) - dot(dot(m1, bottom), y1, 0, 0)
-    residue = dot(bottom, y1 - dot(m1, y0), 0, 0)
-    current = dot(factor, start)
-    vectors = below(current, dot(factor, residue), dot(factor, image) - dot(ritz, current))
-    return dot(inverse_factor(norm), dot(power2, vectors, 0, 0)) * math.sqrt(rows)
+    back = dot(m1, bottom)
+    of_top, of_bottom, of_back = (
+        dot(factor, dot(part, base, 0, 0)) for part in (top - back, bottom, back))
+    vectors = below(
+        beside(of_top, of_bottom, zero),
+        beside(-of_back, of_bottom, zero),
+        beside(-dot(ritz, of_top), of_top - dot(ritz, of_bottom), of_bottom),
+    )
+    mixed = dot(power2, vectors, 0, 0)
+    return dot(dot(inverse_factor(norm), mixed), data) * math.sqrt(rows)
 
 
 def dense_body(rows, core, index, mine, theirs, scaled, out):

time: 101 us -> 101 us (level)
  no operation moved by 1% of the time
where the time goes in v16:
time: 101 us
  waiting for transfers between devices  38.1 us (38%)
  Pallas kernels  31.7 us (31%)
  starting transfers between devices  26.1 us (26%)
  local copies, waits for them, and re-layouts  2.37 us (2%)
  between operations  1.56 us (2%)
    pallas_call x18, Pallas kernels, call(): pl.pallas_call(body, out_shape=[jax.ShapeDtypeStruct(shape, dtype) for sh...  31.7 us
    ppermute x6, waiting for transfers between devices, between_blocks(): return lax.ppermute(shard, ('blk', 'narrow'), pairs)  16 us
    ppermute x6, starting transfers between devices, between_blocks(): return lax.ppermute(shard, ('blk', 'narrow'), pairs)  15.2 us
    ppermute x3, waiting for transfers between devices, total_over_blocks(): lax.ppermute(values, 'blk', [(i, i ^ span) for i in range(blocks)])  11.9 us
    ppermute x4, starting transfers between devices, between_shards(): return lax.ppermute(shard, ('blk', 'narrow'), pairs)  7.24 us
    ppermute x7, waiting for transfers between devices, between_cores(): return lax.ppermute(shard, 'narrow', [(0, 1), (1, 0)])  5.78 us
    ppermute x4, waiting for transfers between devices, between_shards(): return lax.ppermute(shard, ('blk', 'narrow'), pairs)  4.44 us
    ppermute x7, starting transfers between devices, between_cores(): return lax.ppermute(shard, 'narrow', [(0, 1), (1, 0)])  3.03 us
  transfers between devices with their start and end apart: 20, of which 15 were waited for; matrix products, arithmetic and copies ran while one was open for 2% of the time, Pallas kernels for 9%

profile of v16, /device:TPU:0, one launch (start us, length us, event | category | flops | bytes accessed | tf_op | source)
XLA Modules:
  0.0 100.8 jit_solution(13947548167520866951)
XLA Ops:
  0.0 0.5 collective-permute-start.2
  0.5 2.5 %collective-permute-start = (bf16[384,768]{1,0:T(8,128)(2,1)}, bf16[384,768]{1,0:T(8,128)(2,1)S(1)}, u32[]{:S(2)}, u32[]{:S(2)}) collective-permute-start(bf16[384,768]{1,0:T(8,128)(2,1)} %own.1), channel_id=1, source_target_pairs={{2,0},{6,4},{10,8},{14,12},{1,13},{3,15},{5,1},{7,3},{9,5},{11,7},... | collective-permute-start | bytes 1769480 | tf_op jit(solution)/shard_map/ppermute | solution.py:495
  3.0 0.9 multiply_bitcast_fusion
  3.9 2.4 %collective-permute-start.1 = (f32[64,384]{1,0:T(8,128)S(1)}, f32[64,384]{1,0:T(8,128)S(1)}, u32[]{:S(2)}, u32[]{:S(2)}) collective-permute-start(f32[64,384]{1,0:T(8,128)S(1)} %multiply_bitcast_fusion), channel_id=1, source_target_pairs={{0,1},{1,0},{2,3},{3,2},{4,5},{5,4},{6,7},{7,6},{8,9},{9,8},{10,11... | collective-permute-start | bytes 294920 | tf_op jit(solution)/shard_map/ppermute | solution.py:465
  6.3 3.3 %collective-permute-start.3 = (bf16[384,768]{1,0:T(8,128)(2,1)}, bf16[384,768]{1,0:T(8,128)(2,1)S(1)}, u32[]{:S(2)}, u32[]{:S(2)}) collective-permute-start(bf16[384,768]{1,0:T(8,128)(2,1)} %own.1), channel_id=1, source_target_pairs={{3,0},{7,4},{11,8},{15,12},{0,13},{2,15},{4,1},{6,3},{8,5},{10,7},... | collective-permute-start | bytes 1769480 | tf_op jit(solution)/shard_map/ppermute | solution.py:495
  9.6 1.3 %dynamic_slice.3 = s32[1,1]{0,1:T(1,128)} dynamic-slice(s32[8,2]{0,1:T(2,128)} %param.5, s32[]{:T(128)S(6)} %select_n.13, s32[]{:T(128)S(6)} %select_n.14), dynamic_slice_sizes={1,1} | dynamic-slice | bytes 12 | tf_op jit(solution)/shard_map/dynamic_slice | solution.py:500
  11.6 1.9 %shard_map.46 = (bf16[768,384]{1,0:T(8,128)(2,1)S(1)}, bf16[768,384]{1,0:T(8,128)(2,1)S(1)}, f32[16,384]{1,0:T(8,128)S(1)}, f32[768,128]{1,0:T(8,128)S(1)}, bf16...) custom-call(bf16[384,768]{1,0:T(8,128)(2,1)S(1)} %copy-done, bf16[384,768]{1,0:T(8,128)(2,1)S(1)} %collective-permute-done.2.other), custom_call_target="tpu_custom_call" | custom-call | flops 2000000000 | bytes 1000000 | tf_op jit(solution)/shard_map/pallas_call | solution.py:32
  13.5 0.7 collective-permute-start.5
  14.2 4.4 %collective-permute-done.3.direct = bf16[384,768]{1,0:T(8,128)(2,1)S(1)} collective-permute-done((bf16[384,768]{1,0:T(8,128)(2,1)}, bf16[384,768]{1,0:T(8,128)(2,1)S(1)}, u32[]{:S(2)}, u32[]{:S(2)}) %collective-permute-start.3) | collective-permute-done | bytes 589856 | tf_op jit(solution)/shard_map/ppermute | solution.py:495
  18.6 0.7 collective-permute-start.4
  19.3 2.0 %shard_map.47 = (bf16[768,384]{1,0:T(8,128)(2,1)S(1)}, bf16[768,384]{1,0:T(8,128)(2,1)S(1)}, f32[16,384]{1,0:T(8,128)S(1)}, f32[8,384]{1,0:T(8,128)S(1)}) custom-call(f32[8,128]{1,0:T(8,128)S(1)} %broadcast_in_dim.22.keep, f32[8,128]{1,0:T(8,128)S(1)} %broadcast_in_dim.23.relays, f32[8,128]{1,0:T(8,128)S(1)} %get-tuple-element.40.token, ...), custom_call_target="tpu_custom_call" | custom-call | flops 2000000000 | bytes 1000000 | tf_op jit(solution)/shard_map/pallas_call | solution.py:32
  21.3 2.0 %shard_map.48 = (bf16[768,384]{1,0:T(8,128)(2,1)S(1)}, bf16[768,384]{1,0:T(8,128)(2,1)S(1)}, f32[16,384]{1,0:T(8,128)S(1)}, f32[8,384]{1,0:T(8,128)S(1)}) custom-call(f32[8,128]{1,0:T(8,128)S(1)} %broadcast_in_dim.22.keep, f32[8,128]{1,0:T(8,128)S(1)} %broadcast_in_dim.23.relays, f32[8,128]{1,0:T(8,128)S(1)} %get-tuple-element.40.token, ...), custom_call_target="tpu_custom_call" | custom-call | flops 2000000000 | bytes 1000000 | tf_op jit(solution)/shard_map/pallas_call | solution.py:32
  23.3 10.0 %collective-permute-start.6 = (f32[16,384]{1,0:T(8,128)S(1)}, f32[16,384]{1,0:T(8,128)S(1)}, u32[]{:S(2)}, u32[]{:S(2)}) collective-permute-start(f32[16,384]{1,0:T(8,128)S(1)} %pad_maximum_fusion.1), channel_id=1, source_target_pairs={{0,2},{1,5},{2,4},{3,7},{4,6},{5,9},{6,8},{7,11},{8,10},{9,13},{10... | collective-permute-start | bytes 73736 | tf_op jit(solution)/shard_map/ppermute | solution.py:461
  33.3 3.1 %collective-permute-done.6 = f32[16,384]{1,0:T(8,128)S(1)} collective-permute-done((f32[16,384]{1,0:T(8,128)S(1)}, f32[16,384]{1,0:T(8,128)S(1)}, u32[]{:S(2)}, u32[]{:S(2)}) %collective-permute-start.6) | collective-permute-done | bytes 24608 | tf_op jit(solution)/shard_map/ppermute | solution.py:461
  36.4 1.2 %collective-permute-done.7.other_sums = f32[16,384]{1,0:T(8,128)S(1)} collective-permute-done((f32[16,384]{1,0:T(8,128)S(1)}, f32[16,384]{1,0:T(8,128)S(1)}, u32[]{:S(2)}, u32[]{:S(2)}) %collective-permute-start.7) | collective-permute-done | bytes 24608 | tf_op jit(solution)/shard_map/ppermute | solution.py:465
  37.6 0.2 shard_map.49
  37.8 2.0 %collective-permute-start.8 = (s16[144,384]{1,0:T(8,128)(2,1)S(1)}, s16[144,384]{1,0:T(8,128)(2,1)S(1)}, u32[]{:S(2)}, u32[]{:S(2)}) collective-permute-start(s16[144,384]{1,0:T(8,128)(2,1)S(1)} %get-tuple-element.56), channel_id=1, source_target_pairs={{0,14},{1,13},{2,0},{3,15},{4,2},{5,1},{6,4},{7,3},{8,6},{9,5},{10... | collective-permute-start | bytes 331784 | tf_op jit(solution)/shard_map/ppermute | solution.py:461
  39.8 0.6 shard_map.52
  40.5 0.5 shard_map.50.product
  41.0 1.9 %collective-permute-done.8.near = s16[144,384]{1,0:T(8,128)(2,1)S(1)} collective-permute-done((s16[144,384]{1,0:T(8,128)(2,1)S(1)}, s16[144,384]{1,0:T(8,128)(2,1)S(1)}, u32[]{:S(2)}, u32[]{:S(2)}) %collective-permute-start.8) | collective-permute-done | bytes 110624 | tf_op jit(solution)/shard_map/ppermute | solution.py:461
  42.9 0.8 shard_map.51.total
  43.7 4.2 %collective-permute-done.9.behind = s16[144,384]{1,0:T(8,128)(2,1)S(1)} collective-permute-done((s16[144,384]{1,0:T(8,128)(2,1)S(1)}, s16[144,384]{1,0:T(8,128)(2,1)S(1)}, u32[]{:S(2)}, u32[]{:S(2)}) %collective-permute-start.9) | collective-permute-done | bytes 110624 | tf_op jit(solution)/shard_map/ppermute | solution.py:461
  47.9 0.1 shard_map.53.total
  48.1 1.4 %collective-permute-done.10.other_total = f32[128,384]{1,0:T(8,128)S(1)} collective-permute-done((f32[128,384]{1,0:T(8,128)S(1)}, f32[128,384]{1,0:T(8,128)S(1)}, u32[]{:S(2)}, u32[]{:S(2)}) %collective-permute-start.10) | collective-permute-done | bytes 196640 | tf_op jit(solution)/shard_map/ppermute | solution.py:465
  49.6 0.2 shard_map.54
  49.8 1.0 collective-permute-start.11
  50.8 0.6 shard_map.57
  51.4 1.1 %collective-permute-start.12 = (s16[144,384]{1,0:T(8,128)(2,1)S(1)}, s16[144,384]{1,0:T(8,128)(2,1)S(1)}, u32[]{:S(2)}, u32[]{:S(2)}) collective-permute-start(s16[144,384]{1,0:T(8,128)(2,1)S(1)} %shard_map.57), channel_id=1, source_target_pairs={{0,2},{1,5},{2,4},{3,7},{4,6},{5,9},{6,8},{7,11},{8,10},{9,13},{10... | collective-permute-start | bytes 331784 | tf_op jit(solution)/shard_map/ppermute | solution.py:461
  52.5 0.5 shard_map.55.product
  53.0 1.6 %collective-permute-done.11.near = s16[144,384]{1,0:T(8,128)(2,1)S(1)} collective-permute-done((s16[144,384]{1,0:T(8,128)(2,1)S(1)}, s16[144,384]{1,0:T(8,128)(2,1)S(1)}, u32[]{:S(2)}, u32[]{:S(2)}) %collective-permute-start.11) | collective-permute-done | bytes 110624 | tf_op jit(solution)/shard_map/ppermute | solution.py:461
  54.5 0.9 shard_map.56.total
  55.4 3.5 %collective-permute-done.12.behind = s16[144,384]{1,0:T(8,128)(2,1)S(1)} collective-permute-done((s16[144,384]{1,0:T(8,128)(2,1)S(1)}, s16[144,384]{1,0:T(8,128)(2,1)S(1)}, u32[]{:S(2)}, u32[]{:S(2)}) %collective-permute-start.12) | collective-permute-done | bytes 110624 | tf_op jit(solution)/shard_map/ppermute | solution.py:461
  58.9 0.1 shard_map.58.total
  59.1 1.4 %collective-permute-done.13.other_total = f32[128,384]{1,0:T(8,128)S(1)} collective-permute-done((f32[128,384]{1,0:T(8,128)S(1)}, f32[128,384]{1,0:T(8,128)S(1)}, u32[]{:S(2)}, u32[]{:S(2)}) %collective-permute-start.13) | collective-permute-done | bytes 196640 | tf_op jit(solution)/shard_map/ppermute | solution.py:465
  60.5 0.2 shard_map.59
  60.7 1.0 %collective-permute-start.14 = (s16[144,384]{1,0:T(8,128)(2,1)S(1)}, s16[144,384]{1,0:T(8,128)(2,1)S(1)}, u32[]{:S(2)}, u32[]{:S(2)}) collective-permute-start(s16[144,384]{1,0:T(8,128)(2,1)S(1)} %get-tuple-element.65), channel_id=1, source_target_pairs={{0,14},{1,13},{2,0},{3,15},{4,2},{5,1},{6,4},{7,3},{8,6},{9,5},{10... | collective-permute-start | bytes 331784 | tf_op jit(solution)/shard_map/ppermute | solution.py:461
  61.7 1.1 %copy-done.6 = bf16[768,384]{1,0:T(8,128)(2,1)S(1)} copy-done((bf16[768,384]{1,0:T(8,128)(2,1)S(1)}, bf16[768,384]{1,0:T(8,128)(2,1)}, u32[]{:S(2)}) %copy-start.6) | copy-done | bytes 589848
  62.8 0.5 shard_map.61.product
  63.3 0.5 shard_map.60
  63.8 1.8 %collective-permute-done.14.near = s16[144,384]{1,0:T(8,128)(2,1)S(1)} collective-permute-done((s16[144,384]{1,0:T(8,128)(2,1)S(1)}, s16[144,384]{1,0:T(8,128)(2,1)S(1)}, u32[]{:S(2)}, u32[]{:S(2)}) %collective-permute-start.14) | collective-permute-done | bytes 110624 | tf_op jit(solution)/shard_map/ppermute | solution.py:461
  65.6 1.5 %shard_map.62 = (f32[56,128]{1,0:T(8,128)S(1)}, f32[56,128]{1,0:T(8,128)S(1)}) custom-call(f32[8,128]{1,0:T(8,128)S(1)} %broadcast_in_dim.19.core.refs_0_, f32[320,64]{1,0:T(8,128)S(1)} %get-tuple-element.64.low, f32[128,384]{1,0:T(8,128)S(1)} %get-tuple-element.63.v2.vectors, f32[128,384]{1,0:T(8,128)S(1)} %shard_map.61.product, ...), custom_call_target="tpu_custom_call" | custom-call | flops 1000000000 | bytes 1000000 | tf_op jit(solution)/shard_map/pallas_call | solution.py:32
  67.2 1.2 %collective-permute-done.15 = f32[56,128]{1,0:T(8,128)S(1)} collective-permute-done((f32[56,128]{1,0:T(8,128)S(1)}, f32[56,128]{1,0:T(8,128)S(1)}, u32[]{:S(2)}, u32[]{:S(2)}) %collective-permute-start.15) | collective-permute-done | bytes 28704 | tf_op jit(solution)/shard_map/ppermute | solution.py:465
  68.4 3.9 %collective-permute-done.16 = f32[56,128]{1,0:T(8,128)S(1)} collective-permute-done((f32[56,128]{1,0:T(8,128)S(1)}, f32[56,128]{1,0:T(8,128)S(1)}, u32[]{:S(2)}, u32[]{:S(2)}) %collective-permute-start.16) | collective-permute-done | bytes 28704 | tf_op jit(solution)/shard_map/ppermute | solution.py:472
  72.3 3.9 %collective-permute-done.17 = f32[56,128]{1,0:T(8,128)S(1)} collective-permute-done((f32[56,128]{1,0:T(8,128)S(1)}, f32[56,128]{1,0:T(8,128)S(1)}, u32[]{:S(2)}, u32[]{:S(2)}) %collective-permute-start.17) | collective-permute-done | bytes 28704 | tf_op jit(solution)/shard_map/ppermute | solution.py:472
  76.1 0.6 collective-permute-start.18
  76.7 4.2 %collective-permute-done.18 = f32[56,128]{1,0:T(8,128)S(1)} collective-permute-done((f32[56,128]{1,0:T(8,128)S(1)}, f32[56,128]{1,0:T(8,128)S(1)}, u32[]{:S(2)}, u32[]{:S(2)}) %collective-permute-start.18) | collective-permute-done | bytes 28704 | tf_op jit(solution)/shard_map/ppermute | solution.py:472
  81.6 0.5 collective-permute-done.19.refs_3_
  82.1 18.7 %shard_map.63 = f32[64,384]{1,0:T(8,128)} custom-call(f32[8,128]{1,0:T(8,128)S(1)} %broadcast_in_dim.19.core.refs_0_, f32[8,128]{1,0:T(8,128)S(1)} %broadcast_in_dim.20.refs_1_, f32[56,128]{1,0:T(8,128)S(1)} %add.32.refs_2_, f32[56,128]{1,0:T(8,128)S(1)} %collective-permute-done.19.refs_3_, f32[192,384]{1,0:T(8,128)S(1)} %get-tuple-element.68.refs_4_), custom_call_target="tpu_custom_call" | custom-call | flops 20000000000 | bytes 1000000 | tf_op jit(solution)/shard_map/pallas_call | solution.py:32
  (37 shorter events, 0.4 us)
Async XLA Ops:
  0.0 11.6 %copy-start = (bf16[384,768]{1,0:T(8,128)(2,1)S(1)}, bf16[384,768]{1,0:T(8,128)(2,1)}, u32[]{:S(2)}) copy-start(bf16[384,768]{1,0:T(8,128)(2,1)} %own.1) | copy-start | bytes 1769476
  0.0 11.6 %collective-permute-start.2 = (bf16[384,768]{1,0:T(8,128)(2,1)}, bf16[384,768]{1,0:T(8,128)(2,1)S(1)}, u32[]{:S(2)}, u32[]{:S(2)}) collective-permute-start(bf16[384,768]{1,0:T(8,128)(2,1)} %own.1), channel_id=1, source_target_pairs={{0,1},{1,0},{2,3},{3,2},{4,5},{5,4},{6,7},{7,6},{8,9},{9,8},{10,11... | collective-permute-start | bytes 1769480 | tf_op jit(solution)/shard_map/ppermute | solution.py:465
  0.5 13.0 %collective-permute-start = (bf16[384,768]{1,0:T(8,128)(2,1)}, bf16[384,768]{1,0:T(8,128)(2,1)S(1)}, u32[]{:S(2)}, u32[]{:S(2)}) collective-permute-start(bf16[384,768]{1,0:T(8,128)(2,1)} %own.1), channel_id=1, source_target_pairs={{2,0},{6,4},{10,8},{14,12},{1,13},{3,15},{5,1},{7,3},{9,5},{11,7},... | collective-permute-start | bytes 1769480 | tf_op jit(solution)/shard_map/ppermute | solution.py:495
  3.9 7.6 %collective-permute-start.1 = (f32[64,384]{1,0:T(8,128)S(1)}, f32[64,384]{1,0:T(8,128)S(1)}, u32[]{:S(2)}, u32[]{:S(2)}) collective-permute-start(f32[64,384]{1,0:T(8,128)S(1)} %multiply_bitcast_fusion), channel_id=1, source_target_pairs={{0,1},{1,0},{2,3},{3,2},{4,5},{5,4},{6,7},{7,6},{8,9},{9,8},{10,11... | collective-permute-start | bytes 294920 | tf_op jit(solution)/shard_map/ppermute | solution.py:465
  6.3 12.4 %collective-permute-start.3 = (bf16[384,768]{1,0:T(8,128)(2,1)}, bf16[384,768]{1,0:T(8,128)(2,1)S(1)}, u32[]{:S(2)}, u32[]{:S(2)}) collective-permute-start(bf16[384,768]{1,0:T(8,128)(2,1)} %own.1), channel_id=1, source_target_pairs={{3,0},{7,4},{11,8},{15,12},{0,13},{2,15},{4,1},{6,3},{8,5},{10,7},... | collective-permute-start | bytes 1769480 | tf_op jit(solution)/shard_map/ppermute | solution.py:495
  13.4 39.0 %copy-start.3 = (bf16[768,384]{1,0:T(8,128)(2,1)}, bf16[768,384]{1,0:T(8,128)(2,1)S(1)}, u32[]{:S(2)}) copy-start(bf16[768,384]{1,0:T(8,128)(2,1)S(1)} %get-tuple-element.54.h0) | copy-start | bytes 1769476
  13.4 39.0 %copy-start.5 = (bf16[768,384]{1,0:T(8,128)(2,1)}, bf16[768,384]{1,0:T(8,128)(2,1)S(1)}, u32[]{:S(2)}) copy-start(bf16[768,384]{1,0:T(8,128)(2,1)S(1)} %get-tuple-element.55.l0) | copy-start | bytes 1769476
  13.5 5.8 %collective-permute-start.5 = (bf16[384,768]{1,0:T(8,128)(2,1)S(1)}, bf16[384,768]{1,0:T(8,128)(2,1)S(1)}, u32[]{:S(2)}, u32[]{:S(2)}) collective-permute-start(bf16[384,768]{1,0:T(8,128)(2,1)S(1)} %collective-permute-done.direct), channel_id=1, source_target_pairs={{2,14},{6,2},{10,6},{14,10},{18,30},{22,18},{26,22},{30,26}} | collective-permute-start | bytes 1769480 | tf_op jit(solution)/shard_map/ppermute | solution.py:495
  18.6 2.7 %collective-permute-start.4 = (bf16[384,768]{1,0:T(8,128)(2,1)S(1)}, bf16[384,768]{1,0:T(8,128)(2,1)S(1)}, u32[]{:S(2)}, u32[]{:S(2)}) collective-permute-start(bf16[384,768]{1,0:T(8,128)(2,1)S(1)} %collective-permute-done.direct), channel_id=1, source_target_pairs={{1,2},{5,6},{9,10},{13,14},{17,18},{21,22},{25,26},{29,30}} | collective-permute-start | bytes 1769480 | tf_op jit(solution)/shard_map/ppermute | solution.py:495
  23.3 31.2 %copy-start.1 = (bf16[768,384]{1,0:T(8,128)(2,1)}, bf16[768,384]{1,0:T(8,128)(2,1)S(1)}, u32[]{:S(2)}) copy-start(bf16[768,384]{1,0:T(8,128)(2,1)S(1)} %get-tuple-element.60.l2) | copy-start | bytes 1769476
  23.3 13.1 %collective-permute-start.6 = (f32[16,384]{1,0:T(8,128)S(1)}, f32[16,384]{1,0:T(8,128)S(1)}, u32[]{:S(2)}, u32[]{:S(2)}) collective-permute-start(f32[16,384]{1,0:T(8,128)S(1)} %pad_maximum_fusion.1), channel_id=1, source_target_pairs={{0,2},{1,5},{2,4},{3,7},{4,6},{5,9},{6,8},{7,11},{8,10},{9,13},{10... | collective-permute-start | bytes 73736 | tf_op jit(solution)/shard_map/ppermute | solution.py:461
  36.4 1.2 %collective-permute-start.7 = (f32[16,384]{1,0:T(8,128)S(1)}, f32[16,384]{1,0:T(8,128)S(1)}, u32[]{:S(2)}, u32[]{:S(2)}) collective-permute-start(f32[16,384]{1,0:T(8,128)S(1)} %add.28.sums), channel_id=1, source_target_pairs={{0,1},{1,0},{2,3},{3,2},{4,5},{5,4},{6,7},{7,6},{8,9},{9,8},{10,11... | collective-permute-start | bytes 73736 | tf_op jit(solution)/shard_map/ppermute | solution.py:465
  37.8 5.1 %collective-permute-start.8 = (s16[144,384]{1,0:T(8,128)(2,1)S(1)}, s16[144,384]{1,0:T(8,128)(2,1)S(1)}, u32[]{:S(2)}, u32[]{:S(2)}) collective-permute-start(s16[144,384]{1,0:T(8,128)(2,1)S(1)} %get-tuple-element.56), channel_id=1, source_target_pairs={{0,14},{1,13},{2,0},{3,15},{4,2},{5,1},{6,4},{7,3},{8,6},{9,5},{10... | collective-permute-start | bytes 331784 | tf_op jit(solution)/shard_map/ppermute | solution.py:461
  40.5 7.5 %collective-permute-start.9 = (s16[144,384]{1,0:T(8,128)(2,1)S(1)}, s16[144,384]{1,0:T(8,128)(2,1)S(1)}, u32[]{:S(2)}, u32[]{:S(2)}) collective-permute-start(s16[144,384]{1,0:T(8,128)(2,1)S(1)} %shard_map.52), channel_id=1, source_target_pairs={{0,2},{1,5},{2,4},{3,7},{4,6},{5,9},{6,8},{7,11},{8,10},{9,13},{10... | collective-permute-start | bytes 331784 | tf_op jit(solution)/shard_map/ppermute | solution.py:461
  48.1 1.5 %collective-permute-start.10 = (f32[128,384]{1,0:T(8,128)S(1)}, f32[128,384]{1,0:T(8,128)S(1)}, u32[]{:S(2)}, u32[]{:S(2)}) collective-permute-start(f32[128,384]{1,0:T(8,128)S(1)} %shard_map.53.total), channel_id=1, source_target_pairs={{0,1},{1,0},{2,3},{3,2},{4,5},{5,4},{6,7},{7,6},{8,9},{9,8},{10,11... | collective-permute-start | bytes 589832 | tf_op jit(solution)/shard_map/ppermute | solution.py:465
  49.8 4.8 %collective-permute-start.11 = (s16[144,384]{1,0:T(8,128)(2,1)S(1)}, s16[144,384]{1,0:T(8,128)(2,1)S(1)}, u32[]{:S(2)}, u32[]{:S(2)}) collective-permute-start(s16[144,384]{1,0:T(8,128)(2,1)S(1)} %get-tuple-element.62), channel_id=1, source_target_pairs={{0,14},{1,13},{2,0},{3,15},{4,2},{5,1},{6,4},{7,3},{8,6},{9,5},{10... | collective-permute-start | bytes 331784 | tf_op jit(solution)/shard_map/ppermute | solution.py:461
  51.4 7.5 %collective-permute-start.12 = (s16[144,384]{1,0:T(8,128)(2,1)S(1)}, s16[144,384]{1,0:T(8,128)(2,1)S(1)}, u32[]{:S(2)}, u32[]{:S(2)}) collective-permute-start(s16[144,384]{1,0:T(8,128)(2,1)S(1)} %shard_map.57), channel_id=1, source_target_pairs={{0,2},{1,5},{2,4},{3,7},{4,6},{5,9},{6,8},{7,11},{8,10},{9,13},{10... | collective-permute-start | bytes 331784 | tf_op jit(solution)/shard_map/ppermute | solution.py:461
  55.4 6.3 %copy-start.4 = (bf16[768,384]{1,0:T(8,128)(2,1)S(1)}, bf16[768,384]{1,0:T(8,128)(2,1)}, u32[]{:S(2)}) copy-start(bf16[768,384]{1,0:T(8,128)(2,1)} %copy-done.3) | copy-start | bytes 1769476
  59.0 1.5 %collective-permute-start.13 = (f32[128,384]{1,0:T(8,128)S(1)}, f32[128,384]{1,0:T(8,128)S(1)}, u32[]{:S(2)}, u32[]{:S(2)}) collective-permute-start(f32[128,384]{1,0:T(8,128)S(1)} %shard_map.58.total), channel_id=1, source_target_pairs={{0,1},{1,0},{2,3},{3,2},{4,5},{5,4},{6,7},{7,6},{8,9},{9,8},{10,11... | collective-permute-start | bytes 589832 | tf_op jit(solution)/shard_map/ppermute | solution.py:465
  60.7 5.0 %collective-permute-start.14 = (s16[144,384]{1,0:T(8,128)(2,1)S(1)}, s16[144,384]{1,0:T(8,128)(2,1)S(1)}, u32[]{:S(2)}, u32[]{:S(2)}) collective-permute-start(s16[144,384]{1,0:T(8,128)(2,1)S(1)} %get-tuple-element.65), channel_id=1, source_target_pairs={{0,14},{1,13},{2,0},{3,15},{4,2},{5,1},{6,4},{7,3},{8,6},{9,5},{10... | collective-permute-start | bytes 331784 | tf_op jit(solution)/shard_map/ppermute | solution.py:461
  61.7 1.1 %copy-start.6 = (bf16[768,384]{1,0:T(8,128)(2,1)S(1)}, bf16[768,384]{1,0:T(8,128)(2,1)}, u32[]{:S(2)}) copy-start(bf16[768,384]{1,0:T(8,128)(2,1)} %copy-done.5) | copy-start | bytes 1769476
  63.3 2.4 %copy-start.2 = (bf16[768,384]{1,0:T(8,128)(2,1)S(1)}, bf16[768,384]{1,0:T(8,128)(2,1)}, u32[]{:S(2)}) copy-start(bf16[768,384]{1,0:T(8,128)(2,1)} %copy-done.1) | copy-start | bytes 1769476
  67.1 1.3 %collective-permute-start.15 = (f32[56,128]{1,0:T(8,128)S(1)}, f32[56,128]{1,0:T(8,128)S(1)}, u32[]{:S(2)}, u32[]{:S(2)}) collective-permute-start(f32[56,128]{1,0:T(8,128)S(1)} %get-tuple-element.67), channel_id=1, source_target_pairs={{0,1},{1,0},{2,3},{3,2},{4,5},{5,4},{6,7},{7,6},{8,9},{9,8},{10,11... | collective-permute-start | bytes 86024 | tf_op jit(solution)/shard_map/ppermute | solution.py:465
  68.4 3.9 %collective-permute-start.16 = (f32[56,128]{1,0:T(8,128)S(1)}, f32[56,128]{1,0:T(8,128)S(1)}, u32[]{:S(2)}, u32[]{:S(2)}) collective-permute-start(f32[56,128]{1,0:T(8,128)S(1)} %add.29), channel_id=1, source_target_pairs={{0,2},{2,0},{4,6},{6,4},{8,10},{10,8},{12,14},{14,12},{1,3},{3,1},... | collective-permute-start | bytes 86024 | tf_op jit(solution)/shard_map/ppermute | solution.py:472
  72.3 3.9 %collective-permute-start.17 = (f32[56,128]{1,0:T(8,128)S(1)}, f32[56,128]{1,0:T(8,128)S(1)}, u32[]{:S(2)}, u32[]{:S(2)}) collective-permute-start(f32[56,128]{1,0:T(8,128)S(1)} %add.30), channel_id=1, source_target_pairs={{0,4},{2,6},{4,0},{6,2},{8,12},{10,14},{12,8},{14,10},{1,5},{3,7},... | collective-permute-start | bytes 86024 | tf_op jit(solution)/shard_map/ppermute | solution.py:472
  76.1 4.8 %collective-permute-start.18 = (f32[56,128]{1,0:T(8,128)S(1)}, f32[56,128]{1,0:T(8,128)S(1)}, u32[]{:S(2)}, u32[]{:S(2)}) collective-permute-start(f32[56,128]{1,0:T(8,128)S(1)} %add.31), channel_id=1, source_target_pairs={{0,8},{2,10},{4,12},{6,14},{8,0},{10,2},{12,4},{14,6},{1,9},{3,11}... | collective-permute-start | bytes 86024 | tf_op jit(solution)/shard_map/ppermute | solution.py:472
  80.9 1.2 %collective-permute-start.19 = (f32[56,128]{1,0:T(8,128)S(1)}, f32[56,128]{1,0:T(8,128)S(1)}, u32[]{:S(2)}, u32[]{:S(2)}) collective-permute-start(f32[56,128]{1,0:T(8,128)S(1)} %add.32.refs_2_), channel_id=1, source_target_pairs={{0,1},{1,0},{2,3},{3,2},{4,5},{5,4},{6,7},{7,6},{8,9},{9,8},{10,11... | collective-permute-start | bytes 86024 | tf_op jit(solution)/shard_map/ppermute | solution.py:465

commit v17 on v16

--- a/solution.py
+++ b/solution.py
@@ -260,6 +260,12 @@
     return jnp.broadcast_to(values[k:k + 1, :], values.shape)
 
 
+def reciprocal(values):
+    guess = pl.reciprocal(values, approx=True)
+    guess = guess * (2.0 - values * guess)
+    return guess * (2.0 - values * guess)
+
+
 def inverse_factor(matrix):
     size = matrix.shape[0]
     work = jnp.concatenate([matrix, unit(size, size)], axis=1)
@@ -276,7 +282,7 @@
         (a00,), (a10, a11), (a20, a21, a22), (a30, a31, a32, a33) = pivot
         u0, u1, u2, u3 = u = [sublane(blocks[top], r + j) for j in range(4)]
         det_a = a00 * a11 - a10 * a10
-        inv_a = 1.0 / det_a
+        inv_a = reciprocal(det_a)
         p00, p10, p11 = a11 * inv_a, a10 * inv_a, a00 * inv_a
         b00, b01 = a20 * p00 - a21 * p10, a21 * p11 - a20 * p10
         b10, b11 = a30 * p00 - a31 * p10, a31 * p11 - a30 * p10
@@ -284,7 +290,7 @@
         s10 = a32 - (b10 * a20 + b11 * a21)
         s11 = a33 - (b10 * a30 + b11 * a31)
         det_s = s00 * s11 - s10 * s10
-        inv_s = 1.0 / det_s
+        inv_s = reciprocal(det_s)
         q22, q32, q33 = s11 * inv_s, -s10 * inv_s, s00 * inv_s
         q20, q21 = -(q22 * b00 + q32 * b10), -(q22 * b01 + q32 * b11)
         q30, q31 = -(q32 * b00 + q33 * b10), -(q32 * b01 + q33 * b11)

time: 101 us -> 102 us (level)
  Pallas kernels: 31.7 us -> 33 us
    pallas_call x18, Pallas kernels: 31.7 us -> 33 us  [call(): pl.pallas_call(body, out_shape=[jax.ShapeDtypeStruct(shape, dtype) for sh...]
where the time goes in v17:
time: 102 us
  waiting for transfers between devices  38.1 us (37%)
  Pallas kernels  33 us (32%)
  starting transfers between devices  26.1 us (26%)
  local copies, waits for them, and re-layouts  2.37 us (2%)
  between operations  1.56 us (2%)
    pallas_call x18, Pallas kernels, call(): pl.pallas_call(body, out_shape=[jax.ShapeDtypeStruct(shape, dtype) for sh...  33 us
    ppermute x6, waiting for transfers between devices, between_blocks(): return lax.ppermute(shard, ('blk', 'narrow'), pairs)  16 us
    ppermute x6, starting transfers between devices, between_blocks(): return lax.ppermute(shard, ('blk', 'narrow'), pairs)  15.2 us
    ppermute x3, waiting for transfers between devices, total_over_blocks(): lax.ppermute(values, 'blk', [(i, i ^ span) for i in range(blocks)])  11.9 us
    ppermute x4, starting transfers between devices, between_shards(): return lax.ppermute(shard, ('blk', 'narrow'), pairs)  7.24 us
    ppermute x7, waiting for transfers between devices, between_cores(): return lax.ppermute(shard, 'narrow', [(0, 1), (1, 0)])  5.78 us
    ppermute x4, waiting for transfers between devices, between_shards(): return lax.ppermute(shard, ('blk', 'narrow'), pairs)  4.44 us
    ppermute x7, starting transfers between devices, between_cores(): return lax.ppermute(shard, 'narrow', [(0, 1), (1, 0)])  3.03 us
  transfers between devices with their start and end apart: 20, of which 15 were waited for; matrix products, arithmetic and copies ran while one was open for 2% of the time, Pallas kernels for 9%

profile of v17, /device:TPU:0, one launch (start us, length us, event | category | flops | bytes accessed | tf_op | source)
XLA Modules:
  0.0 102.1 jit_solution(14214443506001367671)
XLA Ops:
  0.0 0.5 collective-permute-start.2
  0.5 2.5 %collective-permute-start = (bf16[384,768]{1,0:T(8,128)(2,1)}, bf16[384,768]{1,0:T(8,128)(2,1)S(1)}, u32[]{:S(2)}, u32[]{:S(2)}) collective-permute-start(bf16[384,768]{1,0:T(8,128)(2,1)} %own.1), channel_id=1, source_target_pairs={{2,0},{6,4},{10,8},{14,12},{1,13},{3,15},{5,1},{7,3},{9,5},{11,7},... | collective-permute-start | bytes 1769480 | tf_op jit(solution)/shard_map/ppermute | solution.py:501
  3.0 0.9 multiply_bitcast_fusion
  3.9 2.4 %collective-permute-start.1 = (f32[64,384]{1,0:T(8,128)S(1)}, f32[64,384]{1,0:T(8,128)S(1)}, u32[]{:S(2)}, u32[]{:S(2)}) collective-permute-start(f32[64,384]{1,0:T(8,128)S(1)} %multiply_bitcast_fusion), channel_id=1, source_target_pairs={{0,1},{1,0},{2,3},{3,2},{4,5},{5,4},{6,7},{7,6},{8,9},{9,8},{10,11... | collective-permute-start | bytes 294920 | tf_op jit(solution)/shard_map/ppermute | solution.py:471
  6.3 3.3 %collective-permute-start.3 = (bf16[384,768]{1,0:T(8,128)(2,1)}, bf16[384,768]{1,0:T(8,128)(2,1)S(1)}, u32[]{:S(2)}, u32[]{:S(2)}) collective-permute-start(bf16[384,768]{1,0:T(8,128)(2,1)} %own.1), channel_id=1, source_target_pairs={{3,0},{7,4},{11,8},{15,12},{0,13},{2,15},{4,1},{6,3},{8,5},{10,7},... | collective-permute-start | bytes 1769480 | tf_op jit(solution)/shard_map/ppermute | solution.py:501
  9.6 1.3 %dynamic_slice.3 = s32[1,1]{0,1:T(1,128)} dynamic-slice(s32[8,2]{0,1:T(2,128)} %param.5, s32[]{:T(128)S(6)} %select_n.13, s32[]{:T(128)S(6)} %select_n.14), dynamic_slice_sizes={1,1} | dynamic-slice | bytes 12 | tf_op jit(solution)/shard_map/dynamic_slice | solution.py:506
  11.6 1.9 %shard_map.46 = (bf16[768,384]{1,0:T(8,128)(2,1)S(1)}, bf16[768,384]{1,0:T(8,128)(2,1)S(1)}, f32[16,384]{1,0:T(8,128)S(1)}, f32[768,128]{1,0:T(8,128)S(1)}, bf16...) custom-call(bf16[384,768]{1,0:T(8,128)(2,1)S(1)} %copy-done, bf16[384,768]{1,0:T(8,128)(2,1)S(1)} %collective-permute-done.2.other), custom_call_target="tpu_custom_call" | custom-call | flops 2000000000 | bytes 1000000 | tf_op jit(solution)/shard_map/pallas_call | solution.py:32
  13.5 0.7 collective-permute-start.5
  14.2 4.4 %collective-permute-done.3.direct = bf16[384,768]{1,0:T(8,128)(2,1)S(1)} collective-permute-done((bf16[384,768]{1,0:T(8,128)(2,1)}, bf16[384,768]{1,0:T(8,128)(2,1)S(1)}, u32[]{:S(2)}, u32[]{:S(2)}) %collective-permute-start.3) | collective-permute-done | bytes 589856 | tf_op jit(solution)/shard_map/ppermute | solution.py:501
  18.6 0.7 collective-permute-start.4
  19.3 2.0 %shard_map.47 = (bf16[768,384]{1,0:T(8,128)(2,1)S(1)}, bf16[768,384]{1,0:T(8,128)(2,1)S(1)}, f32[16,384]{1,0:T(8,128)S(1)}, f32[8,384]{1,0:T(8,128)S(1)}) custom-call(f32[8,128]{1,0:T(8,128)S(1)} %broadcast_in_dim.22.keep, f32[8,128]{1,0:T(8,128)S(1)} %broadcast_in_dim.23.relays, f32[8,128]{1,0:T(8,128)S(1)} %get-tuple-element.40.token, ...), custom_call_target="tpu_custom_call" | custom-call | flops 2000000000 | bytes 1000000 | tf_op jit(solution)/shard_map/pallas_call | solution.py:32
  21.3 2.0 %shard_map.48 = (bf16[768,384]{1,0:T(8,128)(2,1)S(1)}, bf16[768,384]{1,0:T(8,128)(2,1)S(1)}, f32[16,384]{1,0:T(8,128)S(1)}, f32[8,384]{1,0:T(8,128)S(1)}) custom-call(f32[8,128]{1,0:T(8,128)S(1)} %broadcast_in_dim.22.keep, f32[8,128]{1,0:T(8,128)S(1)} %broadcast_in_dim.23.relays, f32[8,128]{1,0:T(8,128)S(1)} %get-tuple-element.40.token, ...), custom_call_target="tpu_custom_call" | custom-call | flops 2000000000 | bytes 1000000 | tf_op jit(solution)/shard_map/pallas_call | solution.py:32
  23.3 10.0 %collective-permute-start.6 = (f32[16,384]{1,0:T(8,128)S(1)}, f32[16,384]{1,0:T(8,128)S(1)}, u32[]{:S(2)}, u32[]{:S(2)}) collective-permute-start(f32[16,384]{1,0:T(8,128)S(1)} %pad_maximum_fusion.1), channel_id=1, source_target_pairs={{0,2},{1,5},{2,4},{3,7},{4,6},{5,9},{6,8},{7,11},{8,10},{9,13},{10... | collective-permute-start | bytes 73736 | tf_op jit(solution)/shard_map/ppermute | solution.py:467
  33.3 3.1 %collective-permute-done.6 = f32[16,384]{1,0:T(8,128)S(1)} collective-permute-done((f32[16,384]{1,0:T(8,128)S(1)}, f32[16,384]{1,0:T(8,128)S(1)}, u32[]{:S(2)}, u32[]{:S(2)}) %collective-permute-start.6) | collective-permute-done | bytes 24608 | tf_op jit(solution)/shard_map/ppermute | solution.py:467
  36.4 1.2 %collective-permute-done.7.other_sums = f32[16,384]{1,0:T(8,128)S(1)} collective-permute-done((f32[16,384]{1,0:T(8,128)S(1)}, f32[16,384]{1,0:T(8,128)S(1)}, u32[]{:S(2)}, u32[]{:S(2)}) %collective-permute-start.7) | collective-permute-done | bytes 24608 | tf_op jit(solution)/shard_map/ppermute | solution.py:471
  37.6 0.2 shard_map.49
  37.8 2.0 %collective-permute-start.8 = (s16[144,384]{1,0:T(8,128)(2,1)S(1)}, s16[144,384]{1,0:T(8,128)(2,1)S(1)}, u32[]{:S(2)}, u32[]{:S(2)}) collective-permute-start(s16[144,384]{1,0:T(8,128)(2,1)S(1)} %get-tuple-element.56), channel_id=1, source_target_pairs={{0,14},{1,13},{2,0},{3,15},{4,2},{5,1},{6,4},{7,3},{8,6},{9,5},{10... | collective-permute-start | bytes 331784 | tf_op jit(solution)/shard_map/ppermute | solution.py:467
  39.8 0.6 shard_map.52
  40.5 0.5 shard_map.50.product
  41.0 1.9 %collective-permute-done.8.near = s16[144,384]{1,0:T(8,128)(2,1)S(1)} collective-permute-done((s16[144,384]{1,0:T(8,128)(2,1)S(1)}, s16[144,384]{1,0:T(8,128)(2,1)S(1)}, u32[]{:S(2)}, u32[]{:S(2)}) %collective-permute-start.8) | collective-permute-done | bytes 110624 | tf_op jit(solution)/shard_map/ppermute | solution.py:467
  42.9 0.8 shard_map.51.total
  43.7 4.2 %collective-permute-done.9.behind = s16[144,384]{1,0:T(8,128)(2,1)S(1)} collective-permute-done((s16[144,384]{1,0:T(8,128)(2,1)S(1)}, s16[144,384]{1,0:T(8,128)(2,1)S(1)}, u32[]{:S(2)}, u32[]{:S(2)}) %collective-permute-start.9) | collective-permute-done | bytes 110624 | tf_op jit(solution)/shard_map/ppermute | solution.py:467
  47.9 0.1 shard_map.53.total
  48.1 1.4 %collective-permute-done.10.other_total = f32[128,384]{1,0:T(8,128)S(1)} collective-permute-done((f32[128,384]{1,0:T(8,128)S(1)}, f32[128,384]{1,0:T(8,128)S(1)}, u32[]{:S(2)}, u32[]{:S(2)}) %collective-permute-start.10) | collective-permute-done | bytes 196640 | tf_op jit(solution)/shard_map/ppermute | solution.py:471
  49.6 0.2 shard_map.54
  49.8 1.0 collective-permute-start.11
  50.8 0.6 shard_map.57
  51.4 1.1 %collective-permute-start.12 = (s16[144,384]{1,0:T(8,128)(2,1)S(1)}, s16[144,384]{1,0:T(8,128)(2,1)S(1)}, u32[]{:S(2)}, u32[]{:S(2)}) collective-permute-start(s16[144,384]{1,0:T(8,128)(2,1)S(1)} %shard_map.57), channel_id=1, source_target_pairs={{0,2},{1,5},{2,4},{3,7},{4,6},{5,9},{6,8},{7,11},{8,10},{9,13},{10... | collective-permute-start | bytes 331784 | tf_op jit(solution)/shard_map/ppermute | solution.py:467
  52.5 0.5 shard_map.55.product
  53.0 1.6 %collective-permute-done.11.near = s16[144,384]{1,0:T(8,128)(2,1)S(1)} collective-permute-done((s16[144,384]{1,0:T(8,128)(2,1)S(1)}, s16[144,384]{1,0:T(8,128)(2,1)S(1)}, u32[]{:S(2)}, u32[]{:S(2)}) %collective-permute-start.11) | collective-permute-done | bytes 110624 | tf_op jit(solution)/shard_map/ppermute | solution.py:467
  54.5 0.9 shard_map.56.total
  55.4 3.5 %collective-permute-done.12.behind = s16[144,384]{1,0:T(8,128)(2,1)S(1)} collective-permute-done((s16[144,384]{1,0:T(8,128)(2,1)S(1)}, s16[144,384]{1,0:T(8,128)(2,1)S(1)}, u32[]{:S(2)}, u32[]{:S(2)}) %collective-permute-start.12) | collective-permute-done | bytes 110624 | tf_op jit(solution)/shard_map/ppermute | solution.py:467
  58.9 0.1 shard_map.58.total
  59.1 1.4 %collective-permute-done.13.other_total = f32[128,384]{1,0:T(8,128)S(1)} collective-permute-done((f32[128,384]{1,0:T(8,128)S(1)}, f32[128,384]{1,0:T(8,128)S(1)}, u32[]{:S(2)}, u32[]{:S(2)}) %collective-permute-start.13) | collective-permute-done | bytes 196640 | tf_op jit(solution)/shard_map/ppermute | solution.py:471
  60.5 0.2 shard_map.59
  60.7 1.0 %collective-permute-start.14 = (s16[144,384]{1,0:T(8,128)(2,1)S(1)}, s16[144,384]{1,0:T(8,128)(2,1)S(1)}, u32[]{:S(2)}, u32[]{:S(2)}) collective-permute-start(s16[144,384]{1,0:T(8,128)(2,1)S(1)} %get-tuple-element.65), channel_id=1, source_target_pairs={{0,14},{1,13},{2,0},{3,15},{4,2},{5,1},{6,4},{7,3},{8,6},{9,5},{10... | collective-permute-start | bytes 331784 | tf_op jit(solution)/shard_map/ppermute | solution.py:467
  61.7 1.1 %copy-done.6 = bf16[768,384]{1,0:T(8,128)(2,1)S(1)} copy-done((bf16[768,384]{1,0:T(8,128)(2,1)S(1)}, bf16[768,384]{1,0:T(8,128)(2,1)}, u32[]{:S(2)}) %copy-start.6) | copy-done | bytes 589848
  62.8 0.5 shard_map.61.product
  63.3 0.5 shard_map.60
  63.8 1.8 %collective-permute-done.14.near = s16[144,384]{1,0:T(8,128)(2,1)S(1)} collective-permute-done((s16[144,384]{1,0:T(8,128)(2,1)S(1)}, s16[144,384]{1,0:T(8,128)(2,1)S(1)}, u32[]{:S(2)}, u32[]{:S(2)}) %collective-permute-start.14) | collective-permute-done | bytes 110624 | tf_op jit(solution)/shard_map/ppermute | solution.py:467
  65.6 1.5 %shard_map.62 = (f32[56,128]{1,0:T(8,128)S(1)}, f32[56,128]{1,0:T(8,128)S(1)}) custom-call(f32[8,128]{1,0:T(8,128)S(1)} %broadcast_in_dim.19.core.refs_0_, f32[320,64]{1,0:T(8,128)S(1)} %get-tuple-element.64.low, f32[128,384]{1,0:T(8,128)S(1)} %get-tuple-element.63.v2.vectors, f32[128,384]{1,0:T(8,128)S(1)} %shard_map.61.product, ...), custom_call_target="tpu_custom_call" | custom-call | flops 1000000000 | bytes 1000000 | tf_op jit(solution)/shard_map/pallas_call | solution.py:32
  67.2 1.2 %collective-permute-done.15 = f32[56,128]{1,0:T(8,128)S(1)} collective-permute-done((f32[56,128]{1,0:T(8,128)S(1)}, f32[56,128]{1,0:T(8,128)S(1)}, u32[]{:S(2)}, u32[]{:S(2)}) %collective-permute-start.15) | collective-permute-done | bytes 28704 | tf_op jit(solution)/shard_map/ppermute | solution.py:471
  68.4 3.9 %collective-permute-done.16 = f32[56,128]{1,0:T(8,128)S(1)} collective-permute-done((f32[56,128]{1,0:T(8,128)S(1)}, f32[56,128]{1,0:T(8,128)S(1)}, u32[]{:S(2)}, u32[]{:S(2)}) %collective-permute-start.16) | collective-permute-done | bytes 28704 | tf_op jit(solution)/shard_map/ppermute | solution.py:478
  72.3 3.9 %collective-permute-done.17 = f32[56,128]{1,0:T(8,128)S(1)} collective-permute-done((f32[56,128]{1,0:T(8,128)S(1)}, f32[56,128]{1,0:T(8,128)S(1)}, u32[]{:S(2)}, u32[]{:S(2)}) %collective-permute-start.17) | collective-permute-done | bytes 28704 | tf_op jit(solution)/shard_map/ppermute | solution.py:478
  76.1 0.6 collective-permute-start.18
  76.7 4.2 %collective-permute-done.18 = f32[56,128]{1,0:T(8,128)S(1)} collective-permute-done((f32[56,128]{1,0:T(8,128)S(1)}, f32[56,128]{1,0:T(8,128)S(1)}, u32[]{:S(2)}, u32[]{:S(2)}) %collective-permute-start.18) | collective-permute-done | bytes 28704 | tf_op jit(solution)/shard_map/ppermute | solution.py:478
  81.6 0.5 collective-permute-done.19.refs_3_
  82.1 20.0 %shard_map.63 = f32[64,384]{1,0:T(8,128)} custom-call(f32[8,128]{1,0:T(8,128)S(1)} %broadcast_in_dim.19.core.refs_0_, f32[8,128]{1,0:T(8,128)S(1)} %broadcast_in_dim.20.refs_1_, f32[56,128]{1,0:T(8,128)S(1)} %add.32.refs_2_, f32[56,128]{1,0:T(8,128)S(1)} %collective-permute-done.19.refs_3_, f32[192,384]{1,0:T(8,128)S(1)} %get-tuple-element.68.refs_4_), custom_call_target="tpu_custom_call" | custom-call | flops 20000000000 | bytes 1000000 | tf_op jit(solution)/shard_map/pallas_call | solution.py:32
  (37 shorter events, 0.4 us)
Async XLA Ops:
  0.0 11.6 %copy-start = (bf16[384,768]{1,0:T(8,128)(2,1)S(1)}, bf16[384,768]{1,0:T(8,128)(2,1)}, u32[]{:S(2)}) copy-start(bf16[384,768]{1,0:T(8,128)(2,1)} %own.1) | copy-start | bytes 1769476
  0.0 11.6 %collective-permute-start.2 = (bf16[384,768]{1,0:T(8,128)(2,1)}, bf16[384,768]{1,0:T(8,128)(2,1)S(1)}, u32[]{:S(2)}, u32[]{:S(2)}) collective-permute-start(bf16[384,768]{1,0:T(8,128)(2,1)} %own.1), channel_id=1, source_target_pairs={{0,1},{1,0},{2,3},{3,2},{4,5},{5,4},{6,7},{7,6},{8,9},{9,8},{10,11... | collective-permute-start | bytes 1769480 | tf_op jit(solution)/shard_map/ppermute | solution.py:471
  0.5 13.0 %collective-permute-start = (bf16[384,768]{1,0:T(8,128)(2,1)}, bf16[384,768]{1,0:T(8,128)(2,1)S(1)}, u32[]{:S(2)}, u32[]{:S(2)}) collective-permute-start(bf16[384,768]{1,0:T(8,128)(2,1)} %own.1), channel_id=1, source_target_pairs={{2,0},{6,4},{10,8},{14,12},{1,13},{3,15},{5,1},{7,3},{9,5},{11,7},... | collective-permute-start | bytes 1769480 | tf_op jit(solution)/shard_map/ppermute | solution.py:501
  3.9 7.6 %collective-permute-start.1 = (f32[64,384]{1,0:T(8,128)S(1)}, f32[64,384]{1,0:T(8,128)S(1)}, u32[]{:S(2)}, u32[]{:S(2)}) collective-permute-start(f32[64,384]{1,0:T(8,128)S(1)} %multiply_bitcast_fusion), channel_id=1, source_target_pairs={{0,1},{1,0},{2,3},{3,2},{4,5},{5,4},{6,7},{7,6},{8,9},{9,8},{10,11... | collective-permute-start | bytes 294920 | tf_op jit(solution)/shard_map/ppermute | solution.py:471
  6.3 12.4 %collective-permute-start.3 = (bf16[384,768]{1,0:T(8,128)(2,1)}, bf16[384,768]{1,0:T(8,128)(2,1)S(1)}, u32[]{:S(2)}, u32[]{:S(2)}) collective-permute-start(bf16[384,768]{1,0:T(8,128)(2,1)} %own.1), channel_id=1, source_target_pairs={{3,0},{7,4},{11,8},{15,12},{0,13},{2,15},{4,1},{6,3},{8,5},{10,7},... | collective-permute-start | bytes 1769480 | tf_op jit(solution)/shard_map/ppermute | solution.py:501
  13.4 39.0 %copy-start.3 = (bf16[768,384]{1,0:T(8,128)(2,1)}, bf16[768,384]{1,0:T(8,128)(2,1)S(1)}, u32[]{:S(2)}) copy-start(bf16[768,384]{1,0:T(8,128)(2,1)S(1)} %get-tuple-element.54.h0) | copy-start | bytes 1769476
  13.4 39.0 %copy-start.5 = (bf16[768,384]{1,0:T(8,128)(2,1)}, bf16[768,384]{1,0:T(8,128)(2,1)S(1)}, u32[]{:S(2)}) copy-start(bf16[768,384]{1,0:T(8,128)(2,1)S(1)} %get-tuple-element.55.l0) | copy-start | bytes 1769476
  13.5 5.8 %collective-permute-start.5 = (bf16[384,768]{1,0:T(8,128)(2,1)S(1)}, bf16[384,768]{1,0:T(8,128)(2,1)S(1)}, u32[]{:S(2)}, u32[]{:S(2)}) collective-permute-start(bf16[384,768]{1,0:T(8,128)(2,1)S(1)} %collective-permute-done.direct), channel_id=1, source_target_pairs={{2,14},{6,2},{10,6},{14,10},{18,30},{22,18},{26,22},{30,26}} | collective-permute-start | bytes 1769480 | tf_op jit(solution)/shard_map/ppermute | solution.py:501
  18.6 2.7 %collective-permute-start.4 = (bf16[384,768]{1,0:T(8,128)(2,1)S(1)}, bf16[384,768]{1,0:T(8,128)(2,1)S(1)}, u32[]{:S(2)}, u32[]{:S(2)}) collective-permute-start(bf16[384,768]{1,0:T(8,128)(2,1)S(1)} %collective-permute-done.direct), channel_id=1, source_target_pairs={{1,2},{5,6},{9,10},{13,14},{17,18},{21,22},{25,26},{29,30}} | collective-permute-start | bytes 1769480 | tf_op jit(solution)/shard_map/ppermute | solution.py:501
  23.3 31.2 %copy-start.1 = (bf16[768,384]{1,0:T(8,128)(2,1)}, bf16[768,384]{1,0:T(8,128)(2,1)S(1)}, u32[]{:S(2)}) copy-start(bf16[768,384]{1,0:T(8,128)(2,1)S(1)} %get-tuple-element.60.l2) | copy-start | bytes 1769476
  23.3 13.1 %collective-permute-start.6 = (f32[16,384]{1,0:T(8,128)S(1)}, f32[16,384]{1,0:T(8,128)S(1)}, u32[]{:S(2)}, u32[]{:S(2)}) collective-permute-start(f32[16,384]{1,0:T(8,128)S(1)} %pad_maximum_fusion.1), channel_id=1, source_target_pairs={{0,2},{1,5},{2,4},{3,7},{4,6},{5,9},{6,8},{7,11},{8,10},{9,13},{10... | collective-permute-start | bytes 73736 | tf_op jit(solution)/shard_map/ppermute | solution.py:467
  36.4 1.2 %collective-permute-start.7 = (f32[16,384]{1,0:T(8,128)S(1)}, f32[16,384]{1,0:T(8,128)S(1)}, u32[]{:S(2)}, u32[]{:S(2)}) collective-permute-start(f32[16,384]{1,0:T(8,128)S(1)} %add.28.sums), channel_id=1, source_target_pairs={{0,1},{1,0},{2,3},{3,2},{4,5},{5,4},{6,7},{7,6},{8,9},{9,8},{10,11... | collective-permute-start | bytes 73736 | tf_op jit(solution)/shard_map/ppermute | solution.py:471
  37.8 5.1 %collective-permute-start.8 = (s16[144,384]{1,0:T(8,128)(2,1)S(1)}, s16[144,384]{1,0:T(8,128)(2,1)S(1)}, u32[]{:S(2)}, u32[]{:S(2)}) collective-permute-start(s16[144,384]{1,0:T(8,128)(2,1)S(1)} %get-tuple-element.56), channel_id=1, source_target_pairs={{0,14},{1,13},{2,0},{3,15},{4,2},{5,1},{6,4},{7,3},{8,6},{9,5},{10... | collective-permute-start | bytes 331784 | tf_op jit(solution)/shard_map/ppermute | solution.py:467
  40.5 7.5 %collective-permute-start.9 = (s16[144,384]{1,0:T(8,128)(2,1)S(1)}, s16[144,384]{1,0:T(8,128)(2,1)S(1)}, u32[]{:S(2)}, u32[]{:S(2)}) collective-permute-start(s16[144,384]{1,0:T(8,128)(2,1)S(1)} %shard_map.52), channel_id=1, source_target_pairs={{0,2},{1,5},{2,4},{3,7},{4,6},{5,9},{6,8},{7,11},{8,10},{9,13},{10... | collective-permute-start | bytes 331784 | tf_op jit(solution)/shard_map/ppermute | solution.py:467
  48.1 1.5 %collective-permute-start.10 = (f32[128,384]{1,0:T(8,128)S(1)}, f32[128,384]{1,0:T(8,128)S(1)}, u32[]{:S(2)}, u32[]{:S(2)}) collective-permute-start(f32[128,384]{1,0:T(8,128)S(1)} %shard_map.53.total), channel_id=1, source_target_pairs={{0,1},{1,0},{2,3},{3,2},{4,5},{5,4},{6,7},{7,6},{8,9},{9,8},{10,11... | collective-permute-start | bytes 589832 | tf_op jit(solution)/shard_map/ppermute | solution.py:471
  49.8 4.8 %collective-permute-start.11 = (s16[144,384]{1,0:T(8,128)(2,1)S(1)}, s16[144,384]{1,0:T(8,128)(2,1)S(1)}, u32[]{:S(2)}, u32[]{:S(2)}) collective-permute-start(s16[144,384]{1,0:T(8,128)(2,1)S(1)} %get-tuple-element.62), channel_id=1, source_target_pairs={{0,14},{1,13},{2,0},{3,15},{4,2},{5,1},{6,4},{7,3},{8,6},{9,5},{10... | collective-permute-start | bytes 331784 | tf_op jit(solution)/shard_map/ppermute | solution.py:467
  51.4 7.5 %collective-permute-start.12 = (s16[144,384]{1,0:T(8,128)(2,1)S(1)}, s16[144,384]{1,0:T(8,128)(2,1)S(1)}, u32[]{:S(2)}, u32[]{:S(2)}) collective-permute-start(s16[144,384]{1,0:T(8,128)(2,1)S(1)} %shard_map.57), channel_id=1, source_target_pairs={{0,2},{1,5},{2,4},{3,7},{4,6},{5,9},{6,8},{7,11},{8,10},{9,13},{10... | collective-permute-start | bytes 331784 | tf_op jit(solution)/shard_map/ppermute | solution.py:467
  55.4 6.3 %copy-start.4 = (bf16[768,384]{1,0:T(8,128)(2,1)S(1)}, bf16[768,384]{1,0:T(8,128)(2,1)}, u32[]{:S(2)}) copy-start(bf16[768,384]{1,0:T(8,128)(2,1)} %copy-done.3) | copy-start | bytes 1769476
  59.0 1.5 %collective-permute-start.13 = (f32[128,384]{1,0:T(8,128)S(1)}, f32[128,384]{1,0:T(8,128)S(1)}, u32[]{:S(2)}, u32[]{:S(2)}) collective-permute-start(f32[128,384]{1,0:T(8,128)S(1)} %shard_map.58.total), channel_id=1, source_target_pairs={{0,1},{1,0},{2,3},{3,2},{4,5},{5,4},{6,7},{7,6},{8,9},{9,8},{10,11... | collective-permute-start | bytes 589832 | tf_op jit(solution)/shard_map/ppermute | solution.py:471
  60.7 5.0 %collective-permute-start.14 = (s16[144,384]{1,0:T(8,128)(2,1)S(1)}, s16[144,384]{1,0:T(8,128)(2,1)S(1)}, u32[]{:S(2)}, u32[]{:S(2)}) collective-permute-start(s16[144,384]{1,0:T(8,128)(2,1)S(1)} %get-tuple-element.65), channel_id=1, source_target_pairs={{0,14},{1,13},{2,0},{3,15},{4,2},{5,1},{6,4},{7,3},{8,6},{9,5},{10... | collective-permute-start | bytes 331784 | tf_op jit(solution)/shard_map/ppermute | solution.py:467
  61.7 1.1 %copy-start.6 = (bf16[768,384]{1,0:T(8,128)(2,1)S(1)}, bf16[768,384]{1,0:T(8,128)(2,1)}, u32[]{:S(2)}) copy-start(bf16[768,384]{1,0:T(8,128)(2,1)} %copy-done.5) | copy-start | bytes 1769476
  63.3 2.4 %copy-start.2 = (bf16[768,384]{1,0:T(8,128)(2,1)S(1)}, bf16[768,384]{1,0:T(8,128)(2,1)}, u32[]{:S(2)}) copy-start(bf16[768,384]{1,0:T(8,128)(2,1)} %copy-done.1) | copy-start | bytes 1769476
  67.1 1.3 %collective-permute-start.15 = (f32[56,128]{1,0:T(8,128)S(1)}, f32[56,128]{1,0:T(8,128)S(1)}, u32[]{:S(2)}, u32[]{:S(2)}) collective-permute-start(f32[56,128]{1,0:T(8,128)S(1)} %get-tuple-element.67), channel_id=1, source_target_pairs={{0,1},{1,0},{2,3},{3,2},{4,5},{5,4},{6,7},{7,6},{8,9},{9,8},{10,11... | collective-permute-start | bytes 86024 | tf_op jit(solution)/shard_map/ppermute | solution.py:471
  68.4 3.9 %collective-permute-start.16 = (f32[56,128]{1,0:T(8,128)S(1)}, f32[56,128]{1,0:T(8,128)S(1)}, u32[]{:S(2)}, u32[]{:S(2)}) collective-permute-start(f32[56,128]{1,0:T(8,128)S(1)} %add.29), channel_id=1, source_target_pairs={{0,2},{2,0},{4,6},{6,4},{8,10},{10,8},{12,14},{14,12},{1,3},{3,1},... | collective-permute-start | bytes 86024 | tf_op jit(solution)/shard_map/ppermute | solution.py:478
  72.3 3.9 %collective-permute-start.17 = (f32[56,128]{1,0:T(8,128)S(1)}, f32[56,128]{1,0:T(8,128)S(1)}, u32[]{:S(2)}, u32[]{:S(2)}) collective-permute-start(f32[56,128]{1,0:T(8,128)S(1)} %add.30), channel_id=1, source_target_pairs={{0,4},{2,6},{4,0},{6,2},{8,12},{10,14},{12,8},{14,10},{1,5},{3,7},... | collective-permute-start | bytes 86024 | tf_op jit(solution)/shard_map/ppermute | solution.py:478
  76.1 4.8 %collective-permute-start.18 = (f32[56,128]{1,0:T(8,128)S(1)}, f32[56,128]{1,0:T(8,128)S(1)}, u32[]{:S(2)}, u32[]{:S(2)}) collective-permute-start(f32[56,128]{1,0:T(8,128)S(1)} %add.31), channel_id=1, source_target_pairs={{0,8},{2,10},{4,12},{6,14},{8,0},{10,2},{12,4},{14,6},{1,9},{3,11}... | collective-permute-start | bytes 86024 | tf_op jit(solution)/shard_map/ppermute | solution.py:478
  80.9 1.2 %collective-permute-start.19 = (f32[56,128]{1,0:T(8,128)S(1)}, f32[56,128]{1,0:T(8,128)S(1)}, u32[]{:S(2)}, u32[]{:S(2)}) collective-permute-start(f32[56,128]{1,0:T(8,128)S(1)} %add.32.refs_2_), channel_id=1, source_target_pairs={{0,1},{1,0},{2,3},{3,2},{4,5},{5,4},{6,7},{7,6},{8,9},{9,8},{10,11... | collective-permute-start | bytes 86024 | tf_op jit(solution)/shard_map/ppermute | solution.py:471
